TPU v7x, 32 devices: a whole 2x2x4 slice. The times are simulated.
32 devices in a mesh: dp: 8 (over z, x), blk: 4 (over y, core).
Axes of the slice: x: 2, y: 2, z: 4, core: 2. Of those that a mesh axis runs over, the one named last changes fastest.
Arguments:
- histories: bfloat16 [256, 128, 512], P(('dp', 'blk')), may hold values from -50 to 50
- lengths: int32 [256], P(('dp', 'blk')), may hold values from 1 to 128, as said below
- targets: int32 [256, 128], P(('dp', 'blk')), may hold values from 0 to 1023
- send_list: int32 [256], P(('dp', 'blk')), may hold values from 0 to 7, as said below
- w_in: bfloat16 [512, 2048], replicated, may hold values from -0.25 to 0.25
- w_out: bfloat16 [512, 512], replicated, may hold values from -0.25 to 0.25
- rel_bias: float32 [4, 128], replicated, may hold values from -4 to 4
- item_pool: bfloat16 [8192, 512], P(('dp', 'blk')), may hold values from -13 to 13
Outputs:
- row_loss: float32 [256, 128], P(('dp', 'blk'))
- pool_grad: float32 [8192, 512], P(('dp', 'blk'))
Inputs may be any that keep to these rules, and one draw needn't show every extreme that they name: `lengths`: some history has exactly 128 events in every draw. `send_list`: on each device a permutation of its 8 users; entry d + k names the user sent to slot k of data group d.
All inputs are finite; a program needn't handle non-finite values.
Results may differ from a plain program's by a relative error of at most 0.0095.
Values may be sent and summed in bfloat16 or wider, within the bound.
No kernel may reach another device: no remote copies, remote signals or barrier semaphores. Data moves between devices by JAX's collectives and lax.ppermute only.
A program may use at most 64 MiB of HBM per device.

v0:
```python
import math

import jax
import jax.numpy as jnp
from jax import lax
from jax.sharding import PartitionSpec as P

logit_scale = 20.0


def from_behind(array, axis, by):
    devices = lax.axis_size(axis)
    return lax.ppermute(array, axis, [(i, (i + by) % devices) for i in range(devices)])


def layer_norm(values, epsilon):
    center = values - jnp.mean(values, axis=-1, keepdims=True)
    spread = jnp.mean(center * center, axis=-1, keepdims=True)
    return center * lax.rsqrt(spread + epsilon)


def hstu_users(events, user_len, w_in, w_out, bias_full):
    user_count, length, feat_width = events.shape
    head_count = bias_full.shape[0]
    head_dim = feat_width // head_count
    per_block = math.gcd(user_count, max(1, 512 // length))
    places = jnp.arange(length)
    causal = (places[None, :] <= places[:, None])[None, None]

    def one_block(inputs):
        block_events, block_len = inputs
        flat_rows = block_events.reshape(per_block * length, feat_width)
        normed = layer_norm(flat_rows.astype(jnp.float32), 1e-05).astype(jnp.bfloat16)
        projected = jax.nn.silu(jnp.dot(normed, w_in, preferred_element_type=jnp.float32)).astype(
            jnp.bfloat16
        )
        projected = projected.reshape(per_block, length, 4, head_count, head_dim)
        gate_part = projected[:, :, 0]
        value_part = projected[:, :, 1]
        query_part = projected[:, :, 2]
        key_part = projected[:, :, 3]
        scores = jnp.einsum(
            "bihe,bjhe->bhij", query_part, key_part, preferred_element_type=jnp.float32
        )
        scores = scores / math.sqrt(head_dim) + bias_full[None]
        keep = causal & (places[None, None, None, :] < block_len[:, None, None, None])
        attn = jnp.where(keep, jax.nn.silu(scores), 0.0).astype(jnp.bfloat16)
        mixed = jnp.einsum("bhij,bjhe->bihe", attn, value_part, preferred_element_type=jnp.float32)
        mixed = mixed.reshape(per_block * length, feat_width)
        gate_flat = gate_part.reshape(per_block * length, feat_width).astype(jnp.float32)
        gated = (layer_norm(mixed, 1e-05) * gate_flat).astype(jnp.bfloat16)
        result = flat_rows.astype(jnp.float32) + jnp.dot(
            gated, w_out, preferred_element_type=jnp.float32
        )
        return result.astype(jnp.bfloat16).reshape(per_block, length, feat_width)

    blocks = events.reshape(user_count // per_block, per_block, length, feat_width)
    block_lens = user_len.reshape(user_count // per_block, per_block)
    finished = lax.map(one_block, (blocks, block_lens))
    return finished.reshape(user_count, length, feat_width)


def shards(histories, lengths, targets, send_list, w_in, w_out, rel_bias, item_pool):
    user_count, length, feat_width = histories.shape
    places = jnp.arange(length)
    distance = places[:, None] - places[None, :]
    one_hot = (distance[:, :, None] == places[None, None, :]).astype(jnp.float32)
    bias_full = jnp.einsum("hd,ijd->hij", rel_bias, one_hot, precision=lax.Precision.HIGHEST)
    routed_hist, routed_len, routed_tgt = (
        lax.all_to_all(histories[send_list], "dp", split_axis=0, concat_axis=0, tiled=True),
        lax.all_to_all(lengths[send_list], "dp", split_axis=0, concat_axis=0, tiled=True),
        lax.all_to_all(targets[send_list], "dp", split_axis=0, concat_axis=0, tiled=True),
    )
    layer_out = hstu_users(routed_hist, routed_len, w_in, w_out, bias_full)
    row_count = user_count * length
    flat_out = layer_out.reshape(row_count, feat_width).astype(jnp.float32)
    queries = (
        flat_out / jnp.sqrt(jnp.sum(flat_out * flat_out, axis=-1, keepdims=True) + 1e-06)
    ).astype(jnp.bfloat16)
    target_ids = routed_tgt.reshape(row_count)
    is_valid = (places[None, :] < routed_len[:, None]).reshape(row_count)
    pool_float = item_pool.astype(jnp.float32)
    item_norm = jnp.sqrt(jnp.sum(pool_float * pool_float, axis=-1, keepdims=True) + 1e-06)
    unit_rows = pool_float / item_norm
    unit_bf = unit_rows.astype(jnp.bfloat16)
    item_count = item_pool.shape[0]

    def block_logits(item_block, first_row):
        logits = logit_scale * lax.dot_general(
            queries, item_block, (((1,), (1,)), ((), ())), preferred_element_type=jnp.float32
        )
        is_target = target_ids[:, None] == first_row + jnp.arange(item_block.shape[0])[None, :]
        return (logits, is_target)

    logits, is_target = block_logits(
        lax.all_gather(unit_bf, "blk", axis=0, tiled=True), jnp.int32(0)
    )
    log_total = logit_scale + jnp.log(jnp.sum(jnp.exp(logits - logit_scale), axis=1))
    loop_size = lax.axis_size("blk")
    my_index = lax.axis_index("blk")
    visiting = unit_bf
    grad_acc = jnp.zeros((item_count, feat_width), jnp.float32)
    for turn_number in range(loop_size):
        owner_index = (my_index - turn_number) % loop_size
        grad_logits, grad_is_target = block_logits(visiting, owner_index * item_count)
        residual = (
            jnp.where(is_valid[:, None], jnp.exp(grad_logits - log_total[:, None]), 0.0)
            - jnp.where(is_valid[:, None] & grad_is_target, 1.0, 0.0)
        ).astype(jnp.bfloat16)
        grad_acc = grad_acc + logit_scale * lax.dot_general(
            residual, queries, (((0,), (0,)), ((), ())), preferred_element_type=jnp.float32
        )
        grad_acc = from_behind(grad_acc, "blk", 1)
        if turn_number + 1 < loop_size:
            visiting = from_behind(visiting, "blk", 1)
    row_loss = jnp.where(
        is_valid, log_total - jnp.sum(jnp.where(is_target, logits, 0.0), axis=1), 0.0
    ).reshape(user_count, length)
    pool_grad = (
        grad_acc - unit_rows * jnp.sum(unit_rows * grad_acc, axis=-1, keepdims=True)
    ) / item_norm
    return (row_loss, pool_grad)


def solution(mesh):
    placed = (
        P(("dp", "blk"), None, None),
        P(("dp", "blk")),
        P(("dp", "blk"), None),
        P(("dp", "blk")),
        P(),
        P(),
        P(),
        P(("dp", "blk"), None),
    )
    return jax.shard_map(
        shards,
        mesh=mesh,
        in_specs=placed,
        out_specs=(P(("dp", "blk"), None), P(("dp", "blk"), None)),
        check_vma=False,
    )
```

profile of v0, /device:TPU:0, one launch (start us, length us, event | category | flops | bytes accessed | tf_op | source)
XLA Modules:
  0.0 163.1 jit_solution(13419081882386657571)
XLA Ops:
  7.9 1.3 gather_fusion
  9.9 7.3 %all-to-all-start = ((s32[8,1,1]{2,1,0:T(1,128)}), s32[8,1,1]{2,1,0:T(1,128)S(1)}, u32[]{:S(2)}, u32[]{:S(2)}) async-start(s32[8,1,1]{2,1,0:T(1,128)} %copy.30), calls=%async_computation | async-start | bytes 8192 | tf_op jit(solution)/shard_map/all_to_all | solution.py:71
  17.2 1.6 gather_fusion.1
  18.8 4.8 %all-to-all-done = s32[8,1,1]{2,1,0:T(1,128)S(1)} async-done(((s32[8,1,1]{2,1,0:T(1,128)}), s32[8,1,1]{2,1,0:T(1,128)S(1)}, u32[]{:S(2)}, u32[]{:S(2)}) %all-to-all-start) | async-done | bytes 64 | tf_op jit(solution)/shard_map/all_to_all | solution.py:71
  23.6 3.6 %all-to-all-start.1 = ((bf16[8,128,512]{2,1,0:T(8,128)(2,1)}), bf16[8,128,512]{2,1,0:T(8,128)(2,1)S(1)}, u32[]{:S(2)}, u32[]{:S(2)}) async-start(bf16[8,128,512]{2,1,0:T(8,128)(2,1)} %gather_fusion.1), calls=%async_computation.1 | async-start | bytes 2097152 | tf_op jit(solution)/shard_map/all_to_all | solution.py:70
  27.3 0.8 fusion.108
  28.2 5.8 %fusion.52 = f32[4,128,128]{2,0,1:T(4,128)S(1)} fusion(s32[128,128]{1,0:T(8,128)S(1)} %iota_subtract_fusion, f32[4,128]{1,0:T(4,128)S(1)} %copy-done.9), kind=kOutput, calls=%fused_computation.90 | convolution fusion | flops 102760448 | bytes 329728 | tf_op jit(solution)/shard_map/hd,ijd->hij/dot_general | solution.py:68
  34.8 1.1 gather_fusion.2
  36.4 15.5 %all-to-all-done.1 = bf16[8,128,512]{2,1,0:T(8,128)(2,1)S(1)} async-done(((bf16[8,128,512]{2,1,0:T(8,128)(2,1)}), bf16[8,128,512]{2,1,0:T(8,128)(2,1)S(1)}, u32[]{:S(2)}, u32[]{:S(2)}) %all-to-all-start.1) | async-done | bytes 1048608 | tf_op jit(solution)/shard_map/all_to_all | solution.py:70
  51.8 3.4 %all-to-all-start.2 = ((s32[8,1,128]{2,1,0:T(1,128)}), s32[8,1,128]{2,1,0:T(1,128)S(1)}, u32[]{:S(2)}, u32[]{:S(2)}) async-start(s32[8,1,128]{2,1,0:T(1,128)} %bitcast.7), calls=%async_computation.2 | async-start | bytes 8192 | tf_op jit(solution)/shard_map/all_to_all | solution.py:72
  55.3 40.2 %while.11 = (s32[]{:T(128)}, bf16[2,4,128,512]{3,2,1,0:T(8,128)(2,1)}, bf16[2,4,128,512]{3,2,1,0:T(8,128)(2,1)S(1)}, bf16[512,2048]{1,0:T(8,128)(2,1)}, s32[2,4]...) while((s32[]{:T(128)}, ...), condition=%wide.region_5.6_spmd.clone, body=%wide.region_0.5_spmd.clone.sunk | while | flops 1489585664 | bytes 54994724 | solution.py:59
  56.2 1.0 copy-done.8
  57.3 3.0 %multiply_convert_fusion.2 = bf16[512,2048]{1,0:T(8,128)(2,1)} fusion(bf16[512,512]{1,0:T(8,128)(2,1)S(1)} %fusion.145, bf16[512,2048]{1,0:T(8,128)(2,1)S(1)} %copy-done.8), kind=kOutput, calls=%fused_computation.5.clone.1 | convolution fusion | flops 1078984704 | bytes 4718592 | tf_op jit(solution)/shard_map/while/body/eval_jaxpr/dot_general | solution.py:34
  60.3 3.2 %reshape.276 = bf16[4,128,4,4,128]{4,3,2,1,0:T(4,128)(2,1)S(1)} reshape(bf16[512,2048]{1,0:T(8,128)(2,1)} %multiply_convert_fusion.2) | data formatting | bytes 4194304 | tf_op jit(solution)/shard_map/while/body/eval_jaxpr/reshape | solution.py:37
  63.5 1.9 %fusion.146 = (bf16[4,128,1,4,128]{4,3,2,1,0:T(4,128)(2,1)}, f32[4,128,1,4,128]{4,3,2,1,0:T(4,128)}, bf16[4,128,1,4,128]{4,3,2,1,0:T(4,128)(2,1)}, bf16[4,128,1,4,128]{4,3,2,1,0:T(4,128)(2,1)}) fusion(bf16[4,128,4,4,128]{4,3,2,1,0:T(4,128)(2,1)S(1)} %reshape.276), kind=kLoop, calls=%fused_computation.163.clone.1 | loop fusion | flops 262144 | bytes 4718592 | tf_op jit(solution)/shard_map/while/body/eval_jaxpr/slice | solution.py:39
  65.5 1.3 copy.62
  66.9 2.2 %fusion.149 = (f32[4,128]{1,0:T(4,128)S(1)}, f32[4,128,4,128]{1,3,2,0:T(8,128)S(1)}) fusion(bf16[4,128,1,4,128]{4,3,2,1,0:T(4,128)(2,1)} %get-tuple-element.177, bf16[4,128,1,4,128]{4,3,2,1,0:T(4,128)(2,1)} %get-tuple-element.178, f32[4,128,128]{2,1,0:T(8,128)} %get-tuple-element.205, pred[4,128,128]{2,1,0:T(8,128)(4,1)S(1)} %broadcast_and_fusion.2, ...), kind=kOutput, calls=%fused_computation.164.clone.1 | convolution fusion | flops 136576512 | bytes 2951168 | tf_op jit(solution)/shard_map/while/body/eval_jaxpr/bhij,bjhe->bihe/dot_general | solution.py:48
  69.2 0.9 copy-done.4
  70.1 1.6 copy.63
  71.9 1.1 copy-done.3
  73.0 1.6 fusion.151
  74.5 0.8 constant_dynamic-update-slice_fusion.2
  76.4 1.0 copy-done.8
  77.4 3.0 %multiply_convert_fusion.2 = bf16[512,2048]{1,0:T(8,128)(2,1)} fusion(bf16[512,512]{1,0:T(8,128)(2,1)S(1)} %fusion.145, bf16[512,2048]{1,0:T(8,128)(2,1)S(1)} %copy-done.8), kind=kOutput, calls=%fused_computation.5.clone.1 | convolution fusion | flops 1078984704 | bytes 4718592 | tf_op jit(solution)/shard_map/while/body/eval_jaxpr/dot_general | solution.py:34
  80.4 3.2 %reshape.276 = bf16[4,128,4,4,128]{4,3,2,1,0:T(4,128)(2,1)S(1)} reshape(bf16[512,2048]{1,0:T(8,128)(2,1)} %multiply_convert_fusion.2) | data formatting | bytes 4194304 | tf_op jit(solution)/shard_map/while/body/eval_jaxpr/reshape | solution.py:37
  83.6 1.9 %fusion.146 = (bf16[4,128,1,4,128]{4,3,2,1,0:T(4,128)(2,1)}, f32[4,128,1,4,128]{4,3,2,1,0:T(4,128)}, bf16[4,128,1,4,128]{4,3,2,1,0:T(4,128)(2,1)}, bf16[4,128,1,4,128]{4,3,2,1,0:T(4,128)(2,1)}) fusion(bf16[4,128,4,4,128]{4,3,2,1,0:T(4,128)(2,1)S(1)} %reshape.276), kind=kLoop, calls=%fused_computation.163.clone.1 | loop fusion | flops 262144 | bytes 4718592 | tf_op jit(solution)/shard_map/while/body/eval_jaxpr/slice | solution.py:39
  85.6 1.3 copy.62
  87.0 2.2 %fusion.149 = (f32[4,128]{1,0:T(4,128)S(1)}, f32[4,128,4,128]{1,3,2,0:T(8,128)S(1)}) fusion(bf16[4,128,1,4,128]{4,3,2,1,0:T(4,128)(2,1)} %get-tuple-element.177, bf16[4,128,1,4,128]{4,3,2,1,0:T(4,128)(2,1)} %get-tuple-element.178, f32[4,128,128]{2,1,0:T(8,128)} %get-tuple-element.205, pred[4,128,128]{2,1,0:T(8,128)(4,1)S(1)} %broadcast_and_fusion.2, ...), kind=kOutput, calls=%fused_computation.164.clone.1 | convolution fusion | flops 136576512 | bytes 2951168 | tf_op jit(solution)/shard_map/while/body/eval_jaxpr/bhij,bjhe->bihe/dot_general | solution.py:48
  89.3 0.9 copy-done.4
  90.2 1.6 copy.63
  92.0 1.1 copy-done.3
  93.1 1.5 fusion.151
  94.6 0.9 constant_dynamic-update-slice_fusion.2
  95.5 1.5 multiply_reduce_fusion.2
  97.0 1.5 fusion.28
  98.6 3.0 %exponential_reduce_fusion = (f32[1024]{0:T(1024)S(1)}, f32[1024]{0:T(1024)S(1)}) fusion(s32[1024]{0:T(1024)S(1)} %bitcast.135, bf16[1024,512]{1,0:T(8,128)(2,1)S(1)} %fusion.28, bf16[1024,512]{1,0:T(8,128)(2,1)} %all-gather.2.cloned.1.call-done), kind=kOutput, calls=%fused_computation.54 | convolution fusion | flops 1080031232 | bytes 2109440 | tf_op jit(solution)/shard_map/dot_general | solution.py:89
  101.7 1.3 convolution_multiply_fusion.8
  103.0 1.6 collective-permute-start.1
  104.6 9.9 %collective-permute-done.1 = bf16[256,512]{1,0:T(8,128)(2,1)} collective-permute-done((bf16[256,512]{1,0:T(8,128)(2,1)S(1)}, bf16[256,512]{1,0:T(8,128)(2,1)}, u32[]{:S(2)}, u32[]{:S(2)}) %collective-permute-start.1) | collective-permute-done | bytes 262176 | tf_op jit(solution)/shard_map/ppermute | solution.py:13
  114.5 2.4 %fusion.49 = f32[256,512]{1,0:T(8,128)S(1)} fusion(f32[256,512]{1,0:T(8,128)} %collective-permute-done, bf16[1024,512]{1,0:T(8,128)(2,1)S(1)} %fusion.28, bf16[256,512]{1,0:T(8,128)(2,1)} %collective-permute-done.1, s32[256]{0:T(256)S(1)} %iota_add_fusion.2, f32[1024]{0:T(1024)S(1)} %log_add_fusion, pred[1024]{0:T(1024)(128)(4,1)S(1)} %fusion.94, ...), kind=kOutput, calls=%fused_computation.87 | convolution fusion | flops 539230208 | bytes 2369536 | tf_op jit(solution)/shard_map/dot_general | solution.py:110
  117.0 1.6 collective-permute-start.3
  118.6 9.8 %collective-permute-done.3 = bf16[256,512]{1,0:T(8,128)(2,1)S(1)} collective-permute-done((bf16[256,512]{1,0:T(8,128)(2,1)}, bf16[256,512]{1,0:T(8,128)(2,1)S(1)}, u32[]{:S(2)}, u32[]{:S(2)}) %collective-permute-start.3) | collective-permute-done | bytes 262176 | tf_op jit(solution)/shard_map/ppermute | solution.py:13
  128.4 3.1 %fusion.50 = f32[256,512]{1,0:T(8,128)} fusion(f32[256,512]{1,0:T(8,128)} %collective-permute-done.2, bf16[1024,512]{1,0:T(8,128)(2,1)S(1)} %fusion.28, bf16[256,512]{1,0:T(8,128)(2,1)S(1)} %collective-permute-done.3, s32[256]{0:T(256)S(1)} %iota_add_fusion.1, f32[1024]{0:T(1024)S(1)} %log_add_fusion, pred[1024]{0:T(1024)(128)(4,1)S(1)} %fusion.94, ...), kind=kOutput, calls=%fused_computation.88 | convolution fusion | flops 539230208 | bytes 2369536 | tf_op jit(solution)/shard_map/dot_general | solution.py:110
  131.5 1.6 collective-permute-start.5
  133.2 10.1 %collective-permute-done.5 = bf16[256,512]{1,0:T(8,128)(2,1)} collective-permute-done((bf16[256,512]{1,0:T(8,128)(2,1)S(1)}, bf16[256,512]{1,0:T(8,128)(2,1)}, u32[]{:S(2)}, u32[]{:S(2)}) %collective-permute-start.5) | collective-permute-done | bytes 262176 | tf_op jit(solution)/shard_map/ppermute | solution.py:13
  143.3 3.0 %fusion.51 = f32[256,512]{1,0:T(8,128)} fusion(f32[256,512]{1,0:T(8,128)S(1)} %collective-permute-done.4, bf16[1024,512]{1,0:T(8,128)(2,1)S(1)} %fusion.28, bf16[256,512]{1,0:T(8,128)(2,1)} %collective-permute-done.5, s32[256]{0:T(256)S(1)} %iota_add_fusion, f32[1024]{0:T(1024)S(1)} %log_add_fusion, pred[1024]{0:T(1024)(128)(4,1)S(1)} %fusion.94, ...), kind=kOutput, calls=%fused_computation.89 | convolution fusion | flops 539230208 | bytes 2369536 | tf_op jit(solution)/shard_map/dot_general | solution.py:110
  147.0 8.2 %collective-permute-done.6 = f32[256,512]{1,0:T(8,128)S(1)} collective-permute-done((f32[256,512]{1,0:T(8,128)}, f32[256,512]{1,0:T(8,128)S(1)}, u32[]{:S(2)}, u32[]{:S(2)}) %collective-permute-start.6) | collective-permute-done | bytes 524320 | tf_op jit(solution)/shard_map/ppermute | solution.py:13
  155.3 1.0 subtract_divide_fusion
  (80 shorter events, 6.6 us)
Async XLA Ops:
  7.2 10.0 %copy-start = (bf16[8,128,512]{2,1,0:T(8,128)(2,1)S(1)}, bf16[8,128,512]{2,1,0:T(8,128)(2,1)}, u32[]{:S(2)}) copy-start(bf16[8,128,512]{2,1,0:T(8,128)(2,1)} %param.10) | copy-start | bytes 3145732
  9.9 13.6 %all-to-all-start = ((s32[8,1,1]{2,1,0:T(1,128)}), s32[8,1,1]{2,1,0:T(1,128)S(1)}, u32[]{:S(2)}, u32[]{:S(2)}) async-start(s32[8,1,1]{2,1,0:T(1,128)} %copy.30), calls=%async_computation | async-start | bytes 8192 | tf_op jit(solution)/shard_map/all_to_all | solution.py:71
  17.2 10.0 %copy-start.5 = (bf16[256,512]{1,0:T(8,128)(2,1)S(1)}, bf16[256,512]{1,0:T(8,128)(2,1)}, u32[]{:S(2)}) copy-start(bf16[256,512]{1,0:T(8,128)(2,1)} %param.17) | copy-start | bytes 786436
  18.8 9.5 %copy-start.9 = (f32[4,128]{1,0:T(4,128)S(1)}, f32[4,128]{1,0:T(4,128)}, u32[]{:S(2)}) copy-start(f32[4,128]{1,0:T(4,128)} %param.16) | copy-start | bytes 6148
  23.6 28.3 %all-to-all-start.1 = ((bf16[8,128,512]{2,1,0:T(8,128)(2,1)}), bf16[8,128,512]{2,1,0:T(8,128)(2,1)S(1)}, u32[]{:S(2)}, u32[]{:S(2)}) async-start(bf16[8,128,512]{2,1,0:T(8,128)(2,1)} %gather_fusion.1), calls=%async_computation.1 | async-start | bytes 2097152 | tf_op jit(solution)/shard_map/all_to_all | solution.py:70
  27.1 7.7 %copy-start.7 = (s32[8,128]{1,0:T(8,128)S(1)}, s32[8,128]{1,0:T(8,128)}, u32[]{:S(2)}) copy-start(s32[8,128]{1,0:T(8,128)} %param.12) | copy-start | bytes 12292
  27.1 71.4 %all-gather.2.cloned.1.call-start = ((), (), s32[]{:S(2)}) async-start(), calls=%async_computation.3 | async-start | bytes 1310720 | tf_op jit(solution)/shard_map/all_gather | solution.py:96
  51.8 46.7 %all-to-all-start.2 = ((s32[8,1,128]{2,1,0:T(1,128)}), s32[8,1,128]{2,1,0:T(1,128)S(1)}, u32[]{:S(2)}, u32[]{:S(2)}) async-start(s32[8,1,128]{2,1,0:T(1,128)} %bitcast.7), calls=%async_computation.2 | async-start | bytes 8192 | tf_op jit(solution)/shard_map/all_to_all | solution.py:72
  55.3 1.0 copy-start.1
  55.3 2.0 %copy-start.8 = (bf16[512,2048]{1,0:T(8,128)(2,1)S(1)}, bf16[512,2048]{1,0:T(8,128)(2,1)}, u32[]{:S(2)}) copy-start(bf16[512,2048]{1,0:T(8,128)(2,1)} %get-tuple-element.203) | copy-start | bytes 6291460 | tf_op jit(solution)/shard_map/while
  69.1 1.0 copy-start.4
  69.1 2.7 %copy-start.2 = (bf16[2,4,128,512]{3,2,1,0:T(8,128)(2,1)S(1)}, bf16[2,4,128,512]{3,2,1,0:T(8,128)(2,1)}, u32[]{:S(2)}) copy-start(bf16[2,4,128,512]{3,2,1,0:T(8,128)(2,1)} %copy-done.1) | copy-start | bytes 3145732 | tf_op jit(solution)/shard_map/while
  71.8 1.2 copy-start.3
  75.4 1.0 copy-start.1
  75.4 2.0 %copy-start.8 = (bf16[512,2048]{1,0:T(8,128)(2,1)S(1)}, bf16[512,2048]{1,0:T(8,128)(2,1)}, u32[]{:S(2)}) copy-start(bf16[512,2048]{1,0:T(8,128)(2,1)} %get-tuple-element.203) | copy-start | bytes 6291460 | tf_op jit(solution)/shard_map/while
  89.2 1.0 copy-start.4
  89.2 2.7 %copy-start.2 = (bf16[2,4,128,512]{3,2,1,0:T(8,128)(2,1)S(1)}, bf16[2,4,128,512]{3,2,1,0:T(8,128)(2,1)}, u32[]{:S(2)}) copy-start(bf16[2,4,128,512]{3,2,1,0:T(8,128)(2,1)} %copy-done.1) | copy-start | bytes 3145732 | tf_op jit(solution)/shard_map/while
  91.9 1.2 copy-start.3
  98.6 3.1 %copy-start.6 = (bf16[256,512]{1,0:T(8,128)(2,1)S(1)}, bf16[256,512]{1,0:T(8,128)(2,1)}, u32[]{:S(2)}) copy-start(bf16[256,512]{1,0:T(8,128)(2,1)} %fusion.108) | copy-start | bytes 786436
  102.9 11.6 %collective-permute-start = (f32[256,512]{1,0:T(8,128)S(1)}, f32[256,512]{1,0:T(8,128)}, u32[]{:S(2)}, u32[]{:S(2)}) collective-permute-start(f32[256,512]{1,0:T(8,128)S(1)} %convolution_multiply_fusion.8), channel_id=1, source_target_pairs={{0,1},{1,2},{2,3},{3,0},{4,5},{5,6},{6,7},{7,4},{8,9},{9,10},{10,1... | collective-permute-start | bytes 1572872 | tf_op jit(solution)/shard_map/ppermute | solution.py:13
  103.0 11.5 %collective-permute-start.1 = (bf16[256,512]{1,0:T(8,128)(2,1)S(1)}, bf16[256,512]{1,0:T(8,128)(2,1)}, u32[]{:S(2)}, u32[]{:S(2)}) collective-permute-start(bf16[256,512]{1,0:T(8,128)(2,1)S(1)} %copy-done.6), channel_id=1, source_target_pairs={{0,1},{1,2},{2,3},{3,0},{4,5},{5,6},{6,7},{7,4},{8,9},{9,10},{10,1... | collective-permute-start | bytes 786440 | tf_op jit(solution)/shard_map/ppermute | solution.py:13
  116.9 11.5 %collective-permute-start.2 = (f32[256,512]{1,0:T(8,128)S(1)}, f32[256,512]{1,0:T(8,128)}, u32[]{:S(2)}, u32[]{:S(2)}) collective-permute-start(f32[256,512]{1,0:T(8,128)S(1)} %fusion.49), channel_id=1, source_target_pairs={{0,1},{1,2},{2,3},{3,0},{4,5},{5,6},{6,7},{7,4},{8,9},{9,10},{10,1... | collective-permute-start | bytes 1572872 | tf_op jit(solution)/shard_map/ppermute | solution.py:13
  117.0 11.4 %collective-permute-start.3 = (bf16[256,512]{1,0:T(8,128)(2,1)}, bf16[256,512]{1,0:T(8,128)(2,1)S(1)}, u32[]{:S(2)}, u32[]{:S(2)}) collective-permute-start(bf16[256,512]{1,0:T(8,128)(2,1)} %collective-permute-done.1), channel_id=1, source_target_pairs={{0,1},{1,2},{2,3},{3,0},{4,5},{5,6},{6,7},{7,4},{8,9},{9,10},{10,1... | collective-permute-start | bytes 786440 | tf_op jit(solution)/shard_map/ppermute | solution.py:13
  131.5 11.7 %collective-permute-start.4 = (f32[256,512]{1,0:T(8,128)}, f32[256,512]{1,0:T(8,128)S(1)}, u32[]{:S(2)}, u32[]{:S(2)}) collective-permute-start(f32[256,512]{1,0:T(8,128)} %fusion.50), channel_id=1, source_target_pairs={{0,1},{1,2},{2,3},{3,0},{4,5},{5,6},{6,7},{7,4},{8,9},{9,10},{10,1... | collective-permute-start | bytes 1572872 | tf_op jit(solution)/shard_map/ppermute | solution.py:13
  131.5 11.7 %collective-permute-start.5 = (bf16[256,512]{1,0:T(8,128)(2,1)S(1)}, bf16[256,512]{1,0:T(8,128)(2,1)}, u32[]{:S(2)}, u32[]{:S(2)}) collective-permute-start(bf16[256,512]{1,0:T(8,128)(2,1)S(1)} %collective-permute-done.3), channel_id=1, source_target_pairs={{0,1},{1,2},{2,3},{3,0},{4,5},{5,6},{6,7},{7,4},{8,9},{9,10},{10,1... | collective-permute-start | bytes 786440 | tf_op jit(solution)/shard_map/ppermute | solution.py:13
  146.3 8.8 %collective-permute-start.6 = (f32[256,512]{1,0:T(8,128)}, f32[256,512]{1,0:T(8,128)S(1)}, u32[]{:S(2)}, u32[]{:S(2)}) collective-permute-start(f32[256,512]{1,0:T(8,128)} %fusion.51), channel_id=1, source_target_pairs={{0,1},{1,2},{2,3},{3,0},{4,5},{5,6},{6,7},{7,4},{8,9},{9,10},{10,1... | collective-permute-start | bytes 1572872 | tf_op jit(solution)/shard_map/ppermute | solution.py:13
Sparse Core Ops, SparseCore 0:
  29.5 18.0 all-gather.1
where the time goes:
time: 164 us; the launch traced here: 163 us
  waiting for transfers between devices  58.2 us (35%)
  matrix products  32.2 us (20%)
  local copies, waits for them, and re-layouts  26.1 us (16%)
  starting transfers between devices  19.2 us (12%)
  between operations  14.2 us (9%)
  other arithmetic  12.9 us (8%)
    ppermute x7, waiting for transfers between devices, from_behind(): lax.ppermute(array, axis, [(i, (i + by) % devices) for i in range(devices)])  37.9 us
    all_to_all x1, waiting for transfers between devices, shards(): lax.all_to_all(histories[send_list], 'dp', split_axis=0, concat_axis=0, t...  15.5 us
    dot_general x4, matrix products, shards(): lax.dot_general(residual, queries, (((0,), (0,)), ((), ())), preferred_el...  9.83 us
    while x22, local copies, waits for them, and re-layouts  9.12 us
    all_to_all x1, starting transfers between devices, shards(): lax.all_to_all(lengths[send_list], 'dp', split_axis=0, concat_axis=0, til...  7.25 us
    reshape x2, local copies, waits for them, and re-layouts, one_block(): projected = projected.reshape(per_block, length, 4, head_count, head_dim)  6.45 us
    dot_general x2, matrix products, one_block(): jnp.dot(normed, w_in, preferred_element_type=jnp.float32)  6.07 us
    dot_general x1, matrix products, shards(): jnp.einsum('hd,ijd->hij', rel_bias, one_hot, precision=lax.Precision.HIGH...  5.83 us
  transfers between devices with their start and end apart: 11, of which 6 were waited for; matrix products, arithmetic and copies ran while one was open for 29% of the time, Pallas kernels for 0%

commit v1 on v0

v1 whole, which is shorter than its diff:
```python
import functools
import math

import jax
import jax.numpy as jnp
from jax import lax
from jax.experimental import pallas as pl
from jax.experimental.pallas import tpu as pltpu
from jax.sharding import PartitionSpec as P

logit_scale = 20.0
contract_last = (((1,), (1,)), ((), ()))


def swap(array, axis, bit):
    devices = lax.axis_size(axis)
    return lax.ppermute(array, axis, [(i, i ^ bit) for i in range(devices)])


def half_silu(half):
    return half + half * jnp.tanh(half)


def center_and_spread(values):
    center = values - jnp.mean(values, axis=-1, keepdims=True)
    return center, jnp.mean(center * center, axis=-1, keepdims=True)


def layer_rows(x, lens, w_in, w_out, bias_ref):
    length = bias_ref.shape[1]
    heads = bias_ref.shape[0]
    width = x.shape[1]
    hdim = width // heads
    center, spread = center_and_spread(x)
    half_normed = (center * (0.5 * lax.rsqrt(spread + 1e-05))).astype(jnp.bfloat16)
    parts = []
    for part in range(4):
        half = jnp.dot(
            half_normed, w_in[:, part * width : (part + 1) * width], preferred_element_type=jnp.float32
        )
        parts.append(half_silu(half).astype(jnp.bfloat16))
    gate, value, query, key = parts
    row = lax.broadcasted_iota(jnp.int32, (length, length), 0)
    col = lax.broadcasted_iota(jnp.int32, (length, length), 1)
    gated = []
    for u in range(len(lens)):
        rows = slice(u * length, (u + 1) * length)
        keep = (col <= row) & (col < lens[u])
        mixed = []
        for h in range(heads):
            cols = slice(h * hdim, (h + 1) * hdim)
            scores = lax.dot_general(
                query[rows, cols], key[rows, cols], contract_last, preferred_element_type=jnp.float32
            )
            attn = half_silu(scores * (0.5 / math.sqrt(hdim)) + bias_ref[h])
            attn = jnp.where(keep, attn, 0.0).astype(jnp.bfloat16)
            mixed.append(jnp.dot(attn, value[rows, cols], preferred_element_type=jnp.float32))
        center, spread = center_and_spread(jnp.concatenate(mixed, axis=1))
        normed = center * lax.rsqrt(spread + 1e-05)
        gated.append((normed * gate[rows].astype(jnp.float32)).astype(jnp.bfloat16))
    gated = jnp.concatenate(gated, axis=0)
    out = x + jnp.dot(gated, w_out[...], preferred_element_type=jnp.float32)
    out = out.astype(jnp.bfloat16).astype(jnp.float32)
    square = jnp.sum(out * out, axis=-1, keepdims=True)
    return (out * lax.rsqrt(square + 1e-06)).astype(jnp.bfloat16)


def users_kernel(
    per_step, blocks, scal_ref, x_ref, tgt_ref, w_in, w_out, rev_ref, unit_ref,
    loss_ref, own_ref, over_ref, side_ref, far_ref, acc_ref, bias_ref, exp_ref,
):
    step = pl.program_id(0)
    heads, length = rev_ref.shape
    width = x_ref.shape[-1]
    items = unit_ref.shape[0] // blocks

    @pl.when(step == 0)
    def _():
        acc_ref[...] = jnp.zeros_like(acc_ref)
        for h in range(heads):
            wide = jnp.broadcast_to(rev_ref[h : h + 1, :], (length, length))
            bias_ref[h] = 0.5 * pltpu.roll(wide, 0, 1, stride=1, stride_axis=0)

    lens = [scal_ref[blocks + step * per_step + u] for u in range(per_step)]
    x = x_ref[...].reshape(per_step * length, width).astype(jnp.float32)
    queries = layer_rows(x, lens, w_in, w_out, bias_ref)

    place = lax.broadcasted_iota(jnp.int32, (1, length), 1)
    valid = jnp.concatenate([place < lens[u] for u in range(per_step)], axis=1)
    target = jnp.concatenate(
        [tgt_ref[pl.ds(step * per_step + u, 1), :] for u in range(per_step)], axis=1
    )
    rows = per_step * length
    item_id = lax.broadcasted_iota(jnp.int32, (items, rows), 0)
    rate = logit_scale * math.log2(math.e)
    total = jnp.zeros((1, rows), jnp.float32)
    target_dot = jnp.zeros((1, rows), jnp.float32)
    for j in range(blocks):
        dots = lax.dot_general(
            unit_ref[j * items : (j + 1) * items], queries, contract_last, preferred_element_type=jnp.float32
        )
        exps = jnp.exp2(dots * rate - rate)
        exp_ref[j] = exps
        total += jnp.sum(exps, axis=0, keepdims=True)
        hit = item_id == target - j * items
        target_dot += jnp.sum(jnp.where(hit, dots, 0.0), axis=0, keepdims=True)
    log_total = logit_scale + jnp.log(total)
    loss = jnp.where(valid, log_total - logit_scale * target_dot, 0.0)
    for u in range(per_step):
        loss_ref[pl.ds(step * per_step + u, 1), :] = loss[:, u * length : (u + 1) * length]
    share = jnp.where(valid, 1.0 / total, 0.0)
    real_target = jnp.where(valid, target, -1)
    for j in range(blocks):
        hit = item_id == real_target - j * items
        residual = exp_ref[j] * share - jnp.where(hit, 1.0, 0.0)
        acc_ref[j] += jnp.dot(residual.astype(jnp.bfloat16), queries, preferred_element_type=jnp.float32)

    @pl.when(step == pl.num_programs(0) - 1)
    def _():
        own_ref[...] = acc_ref[scal_ref[0]]
        over_ref[...] = acc_ref[scal_ref[1]]
        side_ref[...] = acc_ref[scal_ref[2]].astype(jnp.bfloat16)
        far_ref[...] = acc_ref[scal_ref[3]].astype(jnp.bfloat16)


def users_call(events, lens, targets, w_in, w_out, reverse_bias, unit_all, block_ids):
    users, length, width = events.shape
    blocks = block_ids.shape[0]
    items = unit_all.shape[0] // blocks
    heads = reverse_bias.shape[0]
    per_step = 2 if users % 2 == 0 else 1
    whole = lambda *shape: pl.BlockSpec(shape, lambda s, scal: (0,) * len(shape))
    part = lambda dtype: jax.ShapeDtypeStruct((items, width), dtype)
    return pl.pallas_call(
        functools.partial(users_kernel, per_step, blocks),
        grid_spec=pltpu.PrefetchScalarGridSpec(
            num_scalar_prefetch=1,
            grid=(users // per_step,),
            in_specs=[
                pl.BlockSpec((per_step, length, width), lambda s, scal: (s, 0, 0)),
                whole(users, length),
                whole(*w_in.shape),
                whole(*w_out.shape),
                whole(*reverse_bias.shape),
                whole(*unit_all.shape),
            ],
            out_specs=[whole(users, length)] + [whole(items, width)] * 4,
            scratch_shapes=[
                pltpu.VMEM((blocks, items, width), jnp.float32),
                pltpu.VMEM((heads, length, length), jnp.float32),
                pltpu.VMEM((blocks, items, per_step * length), jnp.float32),
            ],
        ),
        out_shape=[
            jax.ShapeDtypeStruct((users, length), jnp.float32),
            part(jnp.float32),
            part(jnp.float32),
            part(jnp.bfloat16),
            part(jnp.bfloat16),
        ],
        compiler_params=pltpu.CompilerParams(vmem_limit_bytes=48 * 1024 * 1024),
        name="users",
    )(jnp.concatenate([block_ids, lens]), events, targets, w_in, w_out, reverse_bias, unit_all)


def shards(histories, lengths, targets, send_list, w_in, w_out, rel_bias, item_pool):
    user_count, length, feat_width = histories.shape
    pool_float = item_pool.astype(jnp.float32)
    item_norm = jnp.sqrt(jnp.sum(pool_float * pool_float, axis=-1, keepdims=True) + 1e-06)
    unit_rows = pool_float / item_norm
    unit_all = lax.all_gather(unit_rows.astype(jnp.bfloat16), "blk", axis=0, tiled=True)
    routed_hist = lax.all_to_all(histories[send_list], "dp", split_axis=0, concat_axis=0, tiled=True)
    groups = lax.axis_size("dp")
    numbers = jnp.concatenate([lengths[:, None], targets], axis=1)[send_list]
    numbers = lax.all_gather(numbers, "dp", axis=0, tiled=False)
    slots = user_count // groups
    numbers = lax.dynamic_slice_in_dim(numbers, lax.axis_index("dp") * slots, slots, axis=1)
    numbers = numbers.reshape(user_count, length + 1)
    routed_len, routed_tgt = numbers[:, 0], numbers[:, 1:]

    reverse_bias = jnp.roll(rel_bias[:, ::-1], 1, axis=1)
    mine = lax.axis_index("blk")
    block_ids = jnp.stack([mine, mine ^ 2, mine ^ 1, mine ^ 3]).astype(jnp.int32)
    row_loss, own, over, side, far = users_call(
        routed_hist, routed_len, routed_tgt, w_in, w_out, reverse_bias, unit_all, block_ids
    )
    over = over + swap(far, "blk", 1).astype(jnp.float32)
    own = own + swap(side, "blk", 1).astype(jnp.float32)
    item_sum = logit_scale * (own + swap(over.astype(jnp.bfloat16), "blk", 2).astype(jnp.float32))
    pool_grad = (
        item_sum - unit_rows * jnp.sum(unit_rows * item_sum, axis=-1, keepdims=True)
    ) / item_norm
    return (row_loss, pool_grad)


def solution(mesh):
    placed = (
        P(("dp", "blk"), None, None),
        P(("dp", "blk")),
        P(("dp", "blk"), None),
        P(("dp", "blk")),
        P(),
        P(),
        P(),
        P(("dp", "blk"), None),
    )
    return jax.shard_map(
        shards,
        mesh=mesh,
        in_specs=placed,
        out_specs=(P(("dp", "blk"), None), P(("dp", "blk"), None)),
        check_vma=False,
    )
```

time: 164 us -> 101 us (0.62)
  waiting for transfers between devices: 58.2 us -> 7.87 us
  blocking collectives: 0 us -> 43.8 us
  matrix products: 32.2 us -> 0 us
  local copies, waits for them, and re-layouts: 26.1 us -> 4.47 us
  Pallas kernels: 0 us -> 17.9 us
  other arithmetic: 12.9 us -> 3.23 us
  starting transfers between devices: 19.2 us -> 9.53 us
    all_gather x0 -> x1, blocking collectives: none -> 43.8 us  [shards(): numbers = lax.all_gather(numbers, 'dp', axis=0, tiled=False)]
    dot_general x12 -> x0, matrix products: 32.2 us -> none  [the longest x4 9.83 us: shards(): lax.dot_general(residual, queries, (((0,), (0,)), ((), ())), preferred_el...]
    ppermute x7 -> x3, waiting for transfers between devices: 37.9 us -> 7.85 us  [swap(): return lax.ppermute(array, axis, [(i, i ^ bit) for i in range(devices)])]
    pallas_call x0 -> x1, Pallas kernels: none -> 17.9 us  [users_call(): pl.pallas_call(functools.partial(users_kernel, per_step, blocks), grid_sp...]
    all_to_all x1, waiting for transfers between devices: 15.5 us -> 0.01 us  [shards(): lax.all_to_all(histories[send_list], 'dp', split_axis=0, concat_axis=0, t...]
    all_to_all x2 -> x0, starting transfers between devices: 10.7 us -> none  [the longest x1 7.25 us: shards(): lax.all_to_all(lengths[send_list], 'dp', split_axis=0, concat_axis=0, til...]
    while x22 -> x0, local copies, waits for them, and re-layouts: 9.12 us -> none
    reshape x3 -> x0, local copies, waits for them, and re-layouts: 6.53 us -> none  [the longest x2 6.45 us: one_block(): projected = projected.reshape(per_block, length, 4, head_count, head_dim)]
  transfers between devices with their start and end apart: 11 -> 5, of which waited for: 6 -> 2; matrix products, arithmetic and copies ran while one was open for 29% -> 2% of each run, Pallas kernels for 0% -> 0%
where the time goes in v1:
time: 101 us
  blocking collectives  43.8 us (43%)
  Pallas kernels  17.9 us (18%)
  between operations  14.1 us (14%)
  starting transfers between devices  9.53 us (9%)
  waiting for transfers between devices  7.87 us (8%)
  local copies, waits for them, and re-layouts  4.47 us (4%)
  other arithmetic  3.23 us (3%)
    all_gather x1, blocking collectives, shards(): numbers = lax.all_gather(numbers, 'dp', axis=0, tiled=False)  43.8 us
    pallas_call x1, Pallas kernels, users_call(): pl.pallas_call(functools.partial(users_kernel, per_step, blocks), grid_sp...  17.9 us
    ppermute x3, waiting for transfers between devices, swap(): return lax.ppermute(array, axis, [(i, i ^ bit) for i in range(devices)])  7.85 us
    all_to_all x1, starting transfers between devices, shards(): lax.all_to_all(histories[send_list], 'dp', split_axis=0, concat_axis=0, t...  7.4 us
    ppermute x3, starting transfers between devices, swap(): return lax.ppermute(array, axis, [(i, i ^ bit) for i in range(devices)])  2.09 us
  transfers between devices with their start and end apart: 5, of which 2 were waited for; matrix products, arithmetic and copies ran while one was open for 2% of the time, Pallas kernels for 0%

profile of v1, /device:TPU:0, one launch (start us, length us, event | category | flops | bytes accessed | tf_op | source)
XLA Modules:
  0.0 100.9 jit_solution(2386949527567499328)
XLA Ops:
  7.2 0.0 copy-start
  7.2 0.7 compare_select_fusion
  7.9 0.5 copy-done
  8.4 0.0 copy-start.3
  8.4 1.6 %gather_fusion.1 = bf16[8,128,512]{2,1,0:T(8,128)(2,1)} fusion(bf16[8,128,512]{2,1,0:T(8,128)(2,1)S(1)} %copy-done, s32[1024]{0:T(1024)S(1)} %pad_clamp_fusion), kind=kCustom, calls=%fused_computation.1 | custom fusion | bytes 2097184 | tf_op jit(solution)/shard_map/gather | solution.py:172
  10.1 0.0 copy-start.4
  10.1 0.0 copy-start.6
  10.1 0.0 copy-start.5
  10.1 0.0 copy-start.2
  10.1 7.4 %all-to-all-start = ((bf16[8,128,512]{2,1,0:T(8,128)(2,1)}), bf16[8,128,512]{2,1,0:T(8,128)(2,1)S(1)}, u32[]{:S(2)}, u32[]{:S(2)}) async-start(bf16[8,128,512]{2,1,0:T(8,128)(2,1)} %gather_fusion.1), calls=%async_computation | async-start | bytes 2097152 | tf_op jit(solution)/shard_map/all_to_all | solution.py:172
  17.5 0.0 all-gather.3.cloned.1.call-start
  17.5 0.0 copy-done.3
  17.5 0.1 fusion
  17.7 0.8 fusion.1
  18.5 0.0 all-gather.3.cloned.1.call-update
  18.5 0.0 copy-done.4
  18.5 0.1 slice.21
  18.6 0.1 slice.22
  18.7 0.0 copy-done.6
  18.7 0.1 copy.12
  18.8 0.0 copy-done.5
  18.8 0.1 pad_add_fusion
  18.9 0.6 gather_fusion
  19.4 43.8 %all-gather = s32[64,129]{1,0:T(8,128)S(1)} all-gather(s32[8,129]{1,0:T(8,128)S(1)} %gather_fusion), channel_id=2, replica_groups=mesh['dp'=8,'blk'=4] {'dp'}, dimensions={0}, use_global_device_ids=true | all-gather | bytes 37152 | tf_op jit(solution)/shard_map/all_gather | solution.py:175
  63.3 0.1 slice.28.tgt_ref
  63.3 0.1 slice_reduce_fusion
  63.4 0.1 concatenate.11.scal_ref
  63.5 0.1 pad_maximum_fusion.rev_ref
  63.6 0.0 all-gather.3.cloned.1.call-done.unit_ref
  63.6 0.0 all-to-all-done.x_ref
  63.6 0.0 copy-done.2
  63.6 0.0 copy-start.1
  63.6 1.2 %copy-done.1 = bf16[1024,512]{1,0:T(8,128)(2,1)S(1)} copy-done((bf16[1024,512]{1,0:T(8,128)(2,1)S(1)}, bf16[1024,512]{1,0:T(8,128)(2,1)}, u32[]{:S(2)}) %copy-start.1) | copy-done | bytes 1048600
  64.8 17.9 %users.1 = (f32[8,128]{1,0:T(8,128)}, f32[256,512]{1,0:T(8,128)S(1)}, f32[256,512]{1,0:T(8,128)S(1)}, bf16[256,512]{1,0:T(8,128)(2,1)S(1)}, bf16[256,512]{1,0:T(8,128)(2,1)S(1)}) custom-call(s32[12]{0:T(128)S(1)} %concatenate.11.scal_ref, bf16[8,128,512]{2,1,0:T(8,128)(2,1)S(1)} %all-to-all-done.x_ref, s32[8,128]{1,0:T(8,128)S(1)} %slice.28.tgt_ref, ...), custom_call_target="tpu_custom_call" | custom-call | tf_op jit(solution)/shard_map/users/pallas_call | solution.py:134
  82.7 0.0 collective-permute-start.1
  82.7 0.5 collective-permute-start
  83.2 1.0 %collective-permute-done.1 = bf16[256,512]{1,0:T(8,128)(2,1)S(1)} collective-permute-done((bf16[256,512]{1,0:T(8,128)(2,1)S(1)}, bf16[256,512]{1,0:T(8,128)(2,1)S(1)}, u32[]{:S(2)}, u32[]{:S(2)}) %collective-permute-start.1) | collective-permute-done | bytes 262176 | tf_op jit(solution)/shard_map/ppermute | solution.py:17
  84.2 0.1 add_convert_fusion
  84.3 1.6 %collective-permute-start.2 = (bf16[256,512]{1,0:T(8,128)(2,1)S(1)}, bf16[256,512]{1,0:T(8,128)(2,1)S(1)}, u32[]{:S(2)}, u32[]{:S(2)}) collective-permute-start(bf16[256,512]{1,0:T(8,128)(2,1)S(1)} %add_convert_fusion), channel_id=1, source_target_pairs={{0,2},{1,3},{2,0},{3,1},{4,6},{5,7},{6,4},{7,5},{8,10},{9,11},{10,... | collective-permute-start | bytes 786440 | tf_op jit(solution)/shard_map/ppermute | solution.py:17
  85.9 0.0 collective-permute-done
  85.9 6.8 %collective-permute-done.2 = bf16[256,512]{1,0:T(8,128)(2,1)S(1)} collective-permute-done((bf16[256,512]{1,0:T(8,128)(2,1)S(1)}, bf16[256,512]{1,0:T(8,128)(2,1)S(1)}, u32[]{:S(2)}, u32[]{:S(2)}) %collective-permute-start.2) | collective-permute-done | bytes 262176 | tf_op jit(solution)/shard_map/ppermute | solution.py:17
  92.7 0.3 multiply_reduce_fusion
  93.0 1.0 %subtract_divide_fusion = f32[256,512]{1,0:T(8,128)} fusion(f32[256]{0:T(256)S(1)} %multiply_reduce_fusion, f32[256]{0:T(256)S(1)} %add_sqrt_fusion, bf16[256,512]{1,0:T(8,128)(2,1)S(1)} %collective-permute-done.2, f32[256,512]{1,0:T(8,128)S(1)} %get-tuple-element.8, bf16[256,512]{1,0:T(8,128)(2,1)S(1)} %collective-permute-done, bf16[256,512]{1,0:T(8,128)(2,1)S(1)} %copy-done.3), kind=kLoop, calls=%fused_computation.5 | loop fusion | flops 1310720 | bytes 1837056 | tf_op jit(solution)/shard_map/div | solution.py:190
  (4 shorter events, 0.0 us)
Async XLA Ops:
  7.2 1.2 %copy-start = (bf16[8,128,512]{2,1,0:T(8,128)(2,1)S(1)}, bf16[8,128,512]{2,1,0:T(8,128)(2,1)}, u32[]{:S(2)}) copy-start(bf16[8,128,512]{2,1,0:T(8,128)(2,1)} %param.8) | copy-start | bytes 3145732
  8.4 9.1 %copy-start.3 = (bf16[256,512]{1,0:T(8,128)(2,1)S(1)}, bf16[256,512]{1,0:T(8,128)(2,1)}, u32[]{:S(2)}) copy-start(bf16[256,512]{1,0:T(8,128)(2,1)} %param.15) | copy-start | bytes 786436
  10.1 8.5 %copy-start.4 = (f32[4,128]{1,0:T(4,128)S(1)}, f32[4,128]{1,0:T(4,128)}, u32[]{:S(2)}) copy-start(f32[4,128]{1,0:T(4,128)} %param.14) | copy-start | bytes 6148
  10.1 8.6 %copy-start.6 = (s32[8]{0:T(128)S(1)}, s32[8]{0:T(128)}, u32[]{:S(2)}) copy-start(s32[8]{0:T(128)} %param.9) | copy-start | bytes 100
  10.1 8.7 %copy-start.5 = (s32[8,128]{1,0:T(8,128)S(1)}, s32[8,128]{1,0:T(8,128)}, u32[]{:S(2)}) copy-start(s32[8,128]{1,0:T(8,128)} %param.10) | copy-start | bytes 12292
  10.1 53.5 %copy-start.2 = (bf16[512,512]{1,0:T(8,128)(2,1)S(1)}, bf16[512,512]{1,0:T(8,128)(2,1)}, u32[]{:S(2)}) copy-start(bf16[512,512]{1,0:T(8,128)(2,1)} %w_out.1) | copy-start | bytes 1572868
  10.1 53.5 %all-to-all-start = ((bf16[8,128,512]{2,1,0:T(8,128)(2,1)}), bf16[8,128,512]{2,1,0:T(8,128)(2,1)S(1)}, u32[]{:S(2)}, u32[]{:S(2)}) async-start(bf16[8,128,512]{2,1,0:T(8,128)(2,1)} %gather_fusion.1), calls=%async_computation | async-start | bytes 2097152 | tf_op jit(solution)/shard_map/all_to_all | solution.py:172
  17.5 46.1 %all-gather.3.cloned.1.call-start = ((), (), s32[]{:S(2)}) async-start(), calls=%async_computation.1 | async-start | bytes 1310720 | tf_op jit(solution)/shard_map/all_gather | solution.py:171
  63.6 1.2 %copy-start.1 = (bf16[1024,512]{1,0:T(8,128)(2,1)S(1)}, bf16[1024,512]{1,0:T(8,128)(2,1)}, u32[]{:S(2)}) copy-start(bf16[1024,512]{1,0:T(8,128)(2,1)} %all-gather.3.cloned.1.call-done.unit_ref) | copy-start | bytes 3145732
  82.7 1.5 %collective-permute-start.1 = (bf16[256,512]{1,0:T(8,128)(2,1)S(1)}, bf16[256,512]{1,0:T(8,128)(2,1)S(1)}, u32[]{:S(2)}, u32[]{:S(2)}) collective-permute-start(bf16[256,512]{1,0:T(8,128)(2,1)S(1)} %get-tuple-element.11), channel_id=1, source_target_pairs={{0,1},{1,0},{2,3},{3,2},{4,5},{5,4},{6,7},{7,6},{8,9},{9,8},{10,11... | collective-permute-start | bytes 786440 | tf_op jit(solution)/shard_map/ppermute | solution.py:17
  82.7 3.2 %collective-permute-start = (bf16[256,512]{1,0:T(8,128)(2,1)S(1)}, bf16[256,512]{1,0:T(8,128)(2,1)S(1)}, u32[]{:S(2)}, u32[]{:S(2)}) collective-permute-start(bf16[256,512]{1,0:T(8,128)(2,1)S(1)} %get-tuple-element.9), channel_id=1, source_target_pairs={{0,1},{1,0},{2,3},{3,2},{4,5},{5,4},{6,7},{7,6},{8,9},{9,8},{10,11... | collective-permute-start | bytes 786440 | tf_op jit(solution)/shard_map/ppermute | solution.py:17
  84.3 8.4 %collective-permute-start.2 = (bf16[256,512]{1,0:T(8,128)(2,1)S(1)}, bf16[256,512]{1,0:T(8,128)(2,1)S(1)}, u32[]{:S(2)}, u32[]{:S(2)}) collective-permute-start(bf16[256,512]{1,0:T(8,128)(2,1)S(1)} %add_convert_fusion), channel_id=1, source_target_pairs={{0,2},{1,3},{2,0},{3,1},{4,6},{5,7},{6,4},{7,5},{8,10},{9,11},{10,... | collective-permute-start | bytes 786440 | tf_op jit(solution)/shard_map/ppermute | solution.py:17
Sparse Core Ops, SparseCore 0:
  20.4 18.1 all-gather.2

commit v2 on v1

v2 whole, which is shorter than its diff:
```python
import functools
import math

import jax
import jax.numpy as jnp
from jax import lax
from jax.experimental import pallas as pl
from jax.experimental.pallas import tpu as pltpu
from jax.sharding import PartitionSpec as P

logit_scale = 20.0
contract_last = (((1,), (1,)), ((), ()))


def swap(array, axis, bit):
    devices = lax.axis_size(axis)
    return lax.ppermute(array, axis, [(i, i ^ bit) for i in range(devices)])


def from_behind(array, axis, by):
    devices = lax.axis_size(axis)
    return lax.ppermute(array, axis, [(i, (i + by) % devices) for i in range(devices)])


def half_silu(half):
    return half + half * jnp.tanh(half)


def center_and_spread(values):
    center = values - jnp.mean(values, axis=-1, keepdims=True)
    return center, jnp.mean(center * center, axis=-1, keepdims=True)


def layer_kernel(order, scal_ref, *refs):
    count = len(order)
    x_refs, (w_in, w_out, bias_in), q_refs = refs[:count], refs[count : count + 3], refs[count + 3 :]
    heads, length = bias_in.shape
    width = w_out.shape[0]
    hdim = width // heads
    users = scal_ref.shape[0] // 3
    lens = [scal_ref[2 * users + scal_ref[users + scal_ref[k]]] for k in order]

    x = jnp.concatenate([ref[0] for ref in x_refs], axis=0).astype(jnp.float32)
    center, spread = center_and_spread(x)
    half_normed = (center * (0.5 * lax.rsqrt(spread + 1e-05))).astype(jnp.bfloat16)
    parts = []
    for part in range(4):
        half = jnp.dot(
            half_normed, w_in[:, part * width : (part + 1) * width], preferred_element_type=jnp.float32
        )
        parts.append(half_silu(half).astype(jnp.bfloat16))
    gate, value, query, key = parts
    row = lax.broadcasted_iota(jnp.int32, (length, length), 0)
    col = lax.broadcasted_iota(jnp.int32, (length, length), 1)
    half_bias = []
    for h in range(heads):
        wide = jnp.broadcast_to(0.5 * bias_in[h : h + 1, :], (length, length))
        half_bias.append(pltpu.roll(wide, 0, 1, stride=1, stride_axis=0).T)
    gated = []
    for u in range(count):
        rows = slice(u * length, (u + 1) * length)
        keep = (col <= row) & (col < lens[u])
        mixed = []
        for h in range(heads):
            cols = slice(h * hdim, (h + 1) * hdim)
            scores = lax.dot_general(
                query[rows, cols], key[rows, cols], contract_last, preferred_element_type=jnp.float32
            )
            attn = half_silu(scores * (0.5 / math.sqrt(hdim)) + half_bias[h])
            attn = jnp.where(keep, attn, 0.0).astype(jnp.bfloat16)
            mixed.append(jnp.dot(attn, value[rows, cols], preferred_element_type=jnp.float32))
        center, spread = center_and_spread(jnp.concatenate(mixed, axis=1))
        normed = center * lax.rsqrt(spread + 1e-05)
        gated.append((normed * gate[rows].astype(jnp.float32)).astype(jnp.bfloat16))
    gated = jnp.concatenate(gated, axis=0)
    out = x + jnp.dot(gated, w_out[...], preferred_element_type=jnp.float32)
    out = out.astype(jnp.bfloat16).astype(jnp.float32)
    square = jnp.sum(out * out, axis=-1, keepdims=True)
    queries = (out * lax.rsqrt(square + 1e-06)).astype(jnp.bfloat16)
    for u in range(count):
        q_refs[u][...] = queries[u * length : (u + 1) * length]


def layer_call(scalars, order, histories, w_in, w_out, rel_bias):
    users, length, width = histories.shape
    fixed = lambda array: pl.BlockSpec(array.shape, lambda s, scal: (0,) * array.ndim)

    def event_spec(k):
        return pl.BlockSpec((1, length, width), lambda s, scal: (scal[users + scal[k]], 0, 0))

    return pl.pallas_call(
        functools.partial(layer_kernel, order),
        grid_spec=pltpu.PrefetchScalarGridSpec(
            num_scalar_prefetch=1,
            grid=(1,),
            in_specs=[event_spec(k) for k in order] + [fixed(w_in), fixed(w_out), fixed(rel_bias)],
            out_specs=[pl.BlockSpec((length, width), lambda s, scal: (0, 0)) for _ in order],
        ),
        out_shape=[jax.ShapeDtypeStruct((length, width), jnp.bfloat16) for _ in order],
        compiler_params=pltpu.CompilerParams(vmem_limit_bytes=24 * 1024 * 1024),
        name="layer",
    )(scalars, *([histories] * len(order)), w_in, w_out, rel_bias)


def loss_kernel(places, blocks, first, last, scal_ref, *refs):
    count = len(places)
    q_refs, (num_ref, unit_ref) = refs[:count], refs[count : count + 2]
    refs = refs[count + 2 :]
    if not first:
        (acc_in, loss_in), refs = refs[:2], refs[2:]
    loss_ref, sum_refs, exp_ref = refs[0], refs[1:-1], refs[-1]
    length, width = q_refs[0].shape
    items = unit_ref.shape[0] // blocks
    rows = count * length

    queries = jnp.concatenate([ref[...] for ref in q_refs], axis=0)
    spots = [scal_ref[blocks + k] for k in places]
    numbers = [num_ref[spot] for spot in spots]
    target = jnp.concatenate([number[1:2, :] for number in numbers], axis=1)
    place = lax.broadcasted_iota(jnp.int32, (1, length), 1)
    valid = jnp.concatenate([place < number[0:1, :] for number in numbers], axis=1)
    item_id = lax.broadcasted_iota(jnp.int32, (items, rows), 0)
    rate = logit_scale * math.log2(math.e)
    total = jnp.zeros((1, rows), jnp.float32)
    target_dot = jnp.zeros((1, rows), jnp.float32)
    for j in range(blocks):
        dots = lax.dot_general(
            unit_ref[j * items : (j + 1) * items], queries, contract_last, preferred_element_type=jnp.float32
        )
        exps = jnp.exp2(dots * rate - rate)
        exp_ref[j] = exps
        total += jnp.sum(exps, axis=0, keepdims=True)
        hit = item_id == target - j * items
        target_dot += jnp.sum(jnp.where(hit, dots, 0.0), axis=0, keepdims=True)
    log_total = logit_scale + jnp.log(total)
    loss = jnp.where(valid, log_total - logit_scale * target_dot, 0.0)
    if first:
        loss_ref[...] = jnp.zeros_like(loss_ref)
    else:
        loss_ref[...] = loss_in[...]
    for u in range(count):
        loss_ref[pl.ds(spots[u], 1), :] = loss[:, u * length : (u + 1) * length]
    share = jnp.where(valid, 1.0 / total, 0.0)
    real_target = jnp.where(valid, target, -1)

    def block_sum(j):
        hit = item_id == real_target - j * items
        residual = exp_ref[j] * share - jnp.where(hit, 1.0, 0.0)
        part = jnp.dot(residual.astype(jnp.bfloat16), queries, preferred_element_type=jnp.float32)
        return part if first else part + acc_in[j]

    for k in range(blocks):
        if last:
            sum_refs[k][...] = block_sum(scal_ref[k]).astype(sum_refs[k].dtype)
        else:
            sum_refs[0][k] = block_sum(k)


def loss_call(scalars, places, queries, numbers, unit_all, blocks, carried, last):
    users, _, length = numbers.shape
    width = unit_all.shape[1]
    items = unit_all.shape[0] // blocks
    fixed = lambda array: pl.BlockSpec(array.shape, lambda s, scal: (0,) * array.ndim)
    if last:
        sums = [
            jax.ShapeDtypeStruct((items, width), jnp.float32 if k < blocks // 2 else jnp.bfloat16)
            for k in range(blocks)
        ]
    else:
        sums = [jax.ShapeDtypeStruct((blocks, items, width), jnp.float32)]
    outs = [jax.ShapeDtypeStruct((users, length), jnp.float32)] + sums
    arrays = [*queries, numbers, unit_all, *carried]
    return pl.pallas_call(
        functools.partial(loss_kernel, places, blocks, not carried, last),
        grid_spec=pltpu.PrefetchScalarGridSpec(
            num_scalar_prefetch=1,
            grid=(1,),
            in_specs=[fixed(array) for array in arrays],
            out_specs=[fixed(out) for out in outs],
            scratch_shapes=[pltpu.VMEM((blocks, items, len(places) * length), jnp.float32)],
        ),
        out_shape=outs,
        compiler_params=pltpu.CompilerParams(vmem_limit_bytes=24 * 1024 * 1024),
        name="loss",
    )(scalars, *arrays)


def shards(histories, lengths, targets, send_list, w_in, w_out, rel_bias, item_pool):
    user_count, length, feat_width = histories.shape
    groups, blocks = lax.axis_size("dp"), lax.axis_size("blk")
    slots = user_count // groups
    group, mine = lax.axis_index("dp"), lax.axis_index("blk")

    work = sorted(
        ((shift, slot) for shift in range(groups) for slot in range(slots)),
        key=lambda pair: (pair[0] == 0, abs(pair[0] - groups / 2)),
    )
    shifts = jnp.array([pair[0] for pair in work], jnp.int32)
    slot_of = jnp.array([pair[1] for pair in work], jnp.int32)
    sent = ((group + shifts) % groups) * slots + slot_of
    scalars = jnp.concatenate([sent, send_list, lengths])

    pool_float = item_pool.astype(jnp.float32)
    item_norm = jnp.sqrt(jnp.sum(pool_float * pool_float, axis=-1, keepdims=True) + 1e-06)
    unit_rows = pool_float / item_norm
    unit_all = lax.all_gather(unit_rows.astype(jnp.bfloat16), "blk", axis=0, tiled=True)

    pair = 2 if user_count % 2 == 0 else 1
    arrived = [None] * user_count
    for at in range(0, user_count, pair):
        order = tuple(range(at, at + pair))
        for k, queries in zip(order, layer_call(scalars, order, histories, w_in, w_out, rel_bias)):
            arrived[k] = queries if work[k][0] == 0 else from_behind(queries, "dp", work[k][0])

    numbers = jnp.stack([jnp.broadcast_to(lengths[:, None], targets.shape), targets], axis=1)[send_list]
    numbers = lax.all_to_all(numbers, "dp", split_axis=0, concat_axis=0, tiled=True)

    came = ((group - shifts) % groups) * slots + slot_of
    block_ids = jnp.stack([mine, mine ^ 2, mine ^ 1, mine ^ 3]).astype(jnp.int32)
    scalars = jnp.concatenate([block_ids, came])
    turns = [user_count - 1, *range(user_count - 1)]
    carried = ()
    for at in range(0, user_count, pair):
        places = tuple(turns[at : at + pair])
        last = at + pair >= user_count
        outs = loss_call(
            scalars, places, [arrived[k] for k in places], numbers, unit_all, blocks, carried, last
        )
        carried = (outs[1], outs[0])
    row_loss, own, over, side, far = outs
    over = over + swap(far, "blk", 1).astype(jnp.float32)
    own = own + swap(side, "blk", 1).astype(jnp.float32)
    item_sum = logit_scale * (own + swap(over.astype(jnp.bfloat16), "blk", 2).astype(jnp.float32))
    pool_grad = (
        item_sum - unit_rows * jnp.sum(unit_rows * item_sum, axis=-1, keepdims=True)
    ) / item_norm
    return (row_loss, pool_grad)


def solution(mesh):
    placed = (
        P(("dp", "blk"), None, None),
        P(("dp", "blk")),
        P(("dp", "blk"), None),
        P(("dp", "blk")),
        P(),
        P(),
        P(),
        P(("dp", "blk"), None),
    )
    return jax.shard_map(
        shards,
        mesh=mesh,
        in_specs=placed,
        out_specs=(P(("dp", "blk"), None), P(("dp", "blk"), None)),
        check_vma=False,
    )
```

time: 101 us -> 88.7 us (0.88)
  blocking collectives: 43.8 us -> 0 us
  starting transfers between devices: 9.53 us -> 24.6 us
  local copies, waits for them, and re-layouts: 4.47 us -> 11.4 us
  Pallas kernels: 17.9 us -> 24.3 us
  other arithmetic: 3.23 us -> 5.69 us
    all_gather x1 -> x0, blocking collectives: 43.8 us -> none  [shards(): numbers = lax.all_gather(numbers, 'dp', axis=0, tiled=False)]
    ppermute x0 -> x7, starting transfers between devices: none -> 18.9 us  [from_behind(): lax.ppermute(array, axis, [(i, (i + by) % devices) for i in range(devices)])]
    unnamed x15 -> x38, local copies, waits for them, and re-layouts: 1.73 us -> 10.1 us
    pallas_call x1 -> x8, Pallas kernels: 17.9 us -> 24.3 us  [the longest x4 15.8 us: layer_call(): pl.pallas_call(functools.partial(layer_kernel, order), grid_spec=pltpu.Pr...]
    all_to_all x1, starting transfers between devices: 7.4 us -> 3.61 us  [shards(): lax.all_to_all(numbers, 'dp', split_axis=0, concat_axis=0, tiled=True)]
    gather x2 -> x1, local copies, waits for them, and re-layouts: 2.21 us -> 1.15 us  [shards(): jnp.stack([jnp.broadcast_to(lengths[:, None], targets.shape), targets], a...]
  transfers between devices with their start and end apart: 5 -> 12, of which waited for: 2 -> 2; matrix products, arithmetic and copies ran while one was open for 2% -> 3% of each run, Pallas kernels for 0% -> 25%
where the time goes in v2:
time: 88.7 us; the launch traced here: 88.1 us
  starting transfers between devices  24.6 us (28%)
  Pallas kernels  24.3 us (27%)
  between operations  14.2 us (16%)
  local copies, waits for them, and re-layouts  11.4 us (13%)
  waiting for transfers between devices  7.89 us (9%)
  other arithmetic  5.69 us (6%)
    ppermute x7, starting transfers between devices, from_behind(): lax.ppermute(array, axis, [(i, (i + by) % devices) for i in range(devices)])  18.9 us
    pallas_call x4, Pallas kernels, layer_call(): pl.pallas_call(functools.partial(layer_kernel, order), grid_spec=pltpu.Pr...  15.8 us
    unnamed x38, local copies, waits for them, and re-layouts  10.1 us
    pallas_call x4, Pallas kernels, loss_call(): pl.pallas_call(functools.partial(loss_kernel, places, blocks, not carried...  8.42 us
    ppermute x3, waiting for transfers between devices, swap(): return lax.ppermute(array, axis, [(i, i ^ bit) for i in range(devices)])  7.85 us
    all_to_all x1, starting transfers between devices, shards(): lax.all_to_all(numbers, 'dp', split_axis=0, concat_axis=0, tiled=True)  3.61 us
    ppermute x3, starting transfers between devices, swap(): return lax.ppermute(array, axis, [(i, i ^ bit) for i in range(devices)])  2.09 us
  transfers between devices with their start and end apart: 12, of which 2 were waited for; matrix products, arithmetic and copies ran while one was open for 3% of the time, Pallas kernels for 25%

profile of v2, /device:TPU:0, one launch (start us, length us, event | category | flops | bytes accessed | tf_op | source)
XLA Modules:
  0.0 88.1 jit_solution(16449192686108981523)
XLA Ops:
  7.2 0.0 all-gather.2.cloned.1.call-start
  7.2 1.1 %fusion = f32[256]{0:T(256)S(1)} fusion(bf16[256,512]{1,0:T(8,128)(2,1)} %param.17), kind=kLoop, calls=%fused_computation.3 | loop fusion | flops 392960 | bytes 263168 | tf_op jit(solution)/shard_map/reduce_sum | solution.py:204
  8.3 0.5 copy-done.13
  8.8 1.8 %fusion.3 = bf16[256,512]{1,0:T(8,128)(2,1)} fusion(f32[256]{0:T(256)S(1)} %add_sqrt_fusion, bf16[256,512]{1,0:T(8,128)(2,1)} %param.17), kind=kLoop, calls=%fused_computation.21 | loop fusion | flops 393216 | bytes 525312 | tf_op jit(solution)/shard_map/convert_element_type | solution.py:206
  10.6 0.0 all-gather.2.cloned.1.call-update
  10.6 0.7 and_select_fusion
  11.3 0.7 pad_add_fusion.1.scal_ref
  12.1 1.2 %copy-done = bf16[8,128,512]{2,1,0:T(8,128)(2,1)S(1)} copy-done((bf16[8,128,512]{2,1,0:T(8,128)(2,1)S(1)}, bf16[8,128,512]{2,1,0:T(8,128)(2,1)}, u32[]{:S(2)}) %copy-start) | copy-done | bytes 1048600
  13.3 1.6 %copy-done.2 = bf16[512,2048]{1,0:T(8,128)(2,1)S(1)} copy-done((bf16[512,2048]{1,0:T(8,128)(2,1)S(1)}, bf16[512,2048]{1,0:T(8,128)(2,1)}, u32[]{:S(2)}) %copy-start.2) | copy-done | bytes 2097176
  14.9 1.0 %copy-done.6 = bf16[512,512]{1,0:T(8,128)(2,1)S(1)} copy-done((bf16[512,512]{1,0:T(8,128)(2,1)S(1)}, bf16[512,512]{1,0:T(8,128)(2,1)}, u32[]{:S(2)}) %copy-start.6) | copy-done | bytes 524312
  15.9 0.7 copy-done.10
  16.6 4.0 %layer.7 = (bf16[128,512]{1,0:T(8,128)(2,1)}, bf16[128,512]{1,0:T(8,128)(2,1)}) custom-call(s32[24]{0:T(128)S(1)} %pad_add_fusion.1.scal_ref, bf16[8,128,512]{2,1,0:T(8,128)(2,1)S(1)} %copy-done, bf16[8,128,512]{2,1,0:T(8,128)(2,1)S(1)} %copy-done, bf16[512,2048]{1,0:T(8,128)(2,1)S(1)} %copy-done.2, bf16[512,512]{1,0:T(8,128)(2,1)S(1)} %copy-done.6, ...), custom_call_target="tpu_custom_call" | custom-call | tf_op jit(solution)/shard_map/layer/pallas_call | solution.py:91
  20.6 4.0 %collective-permute-start.6 = (bf16[128,512]{1,0:T(8,128)(2,1)}, bf16[128,512]{1,0:T(8,128)(2,1)S(1)}, u32[]{:S(2)}, u32[]{:S(2)}) collective-permute-start(bf16[128,512]{1,0:T(8,128)(2,1)} %get-tuple-element.28), channel_id=1, source_target_pairs={{0,16},{4,20},{8,24},{12,28},{16,0},{20,4},{24,8},{28,12},{1,17},{... | collective-permute-start | bytes 393224 | tf_op jit(solution)/shard_map/ppermute | solution.py:22
  24.6 2.5 %collective-permute-start.4 = (bf16[128,512]{1,0:T(8,128)(2,1)}, bf16[128,512]{1,0:T(8,128)(2,1)S(1)}, u32[]{:S(2)}, u32[]{:S(2)}) collective-permute-start(bf16[128,512]{1,0:T(8,128)(2,1)} %get-tuple-element.25), channel_id=1, source_target_pairs={{0,12},{4,16},{8,20},{12,24},{16,28},{20,0},{24,4},{28,8},{1,13},{... | collective-permute-start | bytes 393224 | tf_op jit(solution)/shard_map/ppermute | solution.py:22
  27.2 0.1 stack_broadcast_in_dim.2
  27.3 1.2 %gather_fusion = s32[8,2,128]{2,1,0:T(2,128)} fusion(s32[8,2,128]{2,1,0:T(2,128)S(1)} %pad_add_fusion, s32[1024]{0:T(1024)S(1)} %pad_clamp_fusion), kind=kCustom, calls=%fused_computation | custom fusion | bytes 16416 | tf_op jit(solution)/shard_map/gather | solution.py:215
  28.4 3.6 %all-to-all-start = ((s32[8,2,128]{2,1,0:T(2,128)}), s32[8,2,128]{2,1,0:T(2,128)S(1)}, u32[]{:S(2)}, u32[]{:S(2)}) async-start(s32[8,2,128]{2,1,0:T(2,128)} %gather_fusion), calls=%async_computation | async-start | bytes 16384 | tf_op jit(solution)/shard_map/all_to_all | solution.py:216
  32.0 0.0 copy-start.7
  32.1 1.0 %copy-done.7 = bf16[512,512]{1,0:T(8,128)(2,1)S(1)} copy-done((bf16[512,512]{1,0:T(8,128)(2,1)S(1)}, bf16[512,512]{1,0:T(8,128)(2,1)}, u32[]{:S(2)}) %copy-start.7) | copy-done | bytes 524312
  33.1 4.0 %layer.6 = (bf16[128,512]{1,0:T(8,128)(2,1)}, bf16[128,512]{1,0:T(8,128)(2,1)}) custom-call(s32[24]{0:T(128)S(1)} %pad_add_fusion.1.scal_ref, bf16[8,128,512]{2,1,0:T(8,128)(2,1)S(1)} %copy-done.1, bf16[8,128,512]{2,1,0:T(8,128)(2,1)S(1)} %copy-done.1, bf16[512,2048]{1,0:T(8,128)(2,1)S(1)} %copy-done.3, bf16[512,512]{1,0:T(8,128)(2,1)S(1)} %copy-done.7, ...), custom_call_target="tpu_custom_call" | custom-call | tf_op jit(solution)/shard_map/layer/pallas_call | solution.py:91
  37.1 3.8 %collective-permute-start.5 = (bf16[128,512]{1,0:T(8,128)(2,1)}, bf16[128,512]{1,0:T(8,128)(2,1)}, u32[]{:S(2)}, u32[]{:S(2)}) collective-permute-start(bf16[128,512]{1,0:T(8,128)(2,1)} %get-tuple-element.26), channel_id=1, source_target_pairs={{0,20},{4,24},{8,28},{12,0},{16,4},{20,8},{24,12},{28,16},{1,21},{... | collective-permute-start | bytes 393224 | tf_op jit(solution)/shard_map/ppermute | solution.py:22
  40.9 1.5 %collective-permute-start.2 = (bf16[128,512]{1,0:T(8,128)(2,1)}, bf16[128,512]{1,0:T(8,128)(2,1)S(1)}, u32[]{:S(2)}, u32[]{:S(2)}) collective-permute-start(bf16[128,512]{1,0:T(8,128)(2,1)} %get-tuple-element.23), channel_id=1, source_target_pairs={{0,8},{4,12},{8,16},{12,20},{16,24},{20,28},{24,0},{28,4},{1,9},{5... | collective-permute-start | bytes 393224 | tf_op jit(solution)/shard_map/ppermute | solution.py:22
  42.3 4.0 %layer.4 = (bf16[128,512]{1,0:T(8,128)(2,1)}, bf16[128,512]{1,0:T(8,128)(2,1)}) custom-call(s32[24]{0:T(128)S(1)} %pad_add_fusion.1.scal_ref, bf16[8,128,512]{2,1,0:T(8,128)(2,1)S(1)} %copy-done.1, bf16[8,128,512]{2,1,0:T(8,128)(2,1)S(1)} %copy-done.1, bf16[512,2048]{1,0:T(8,128)(2,1)S(1)} %copy-done.3, bf16[512,512]{1,0:T(8,128)(2,1)S(1)} %copy-done.7, ...), custom_call_target="tpu_custom_call" | custom-call | tf_op jit(solution)/shard_map/layer/pallas_call | solution.py:91
  46.3 2.4 %collective-permute-start.3 = (bf16[128,512]{1,0:T(8,128)(2,1)}, bf16[128,512]{1,0:T(8,128)(2,1)}, u32[]{:S(2)}, u32[]{:S(2)}) collective-permute-start(bf16[128,512]{1,0:T(8,128)(2,1)} %get-tuple-element.24), channel_id=1, source_target_pairs={{0,24},{4,28},{8,0},{12,4},{16,8},{20,12},{24,16},{28,20},{1,25},{... | collective-permute-start | bytes 393224 | tf_op jit(solution)/shard_map/ppermute | solution.py:22
  48.7 3.9 %layer.5 = (bf16[128,512]{1,0:T(8,128)(2,1)}, bf16[128,512]{1,0:T(8,128)(2,1)S(1)}) custom-call(s32[24]{0:T(128)S(1)} %pad_add_fusion.1.scal_ref, bf16[8,128,512]{2,1,0:T(8,128)(2,1)S(1)} %copy-done.1, bf16[8,128,512]{2,1,0:T(8,128)(2,1)S(1)} %copy-done.1, bf16[512,2048]{1,0:T(8,128)(2,1)S(1)} %copy-done.3, bf16[512,512]{1,0:T(8,128)(2,1)S(1)} %copy-done.7, ...), custom_call_target="tpu_custom_call" | custom-call | tf_op jit(solution)/shard_map/layer/pallas_call | solution.py:91
  52.6 0.6 copy-done.8
  53.3 1.5 %collective-permute-start = (bf16[128,512]{1,0:T(8,128)(2,1)}, bf16[128,512]{1,0:T(8,128)(2,1)S(1)}, u32[]{:S(2)}, u32[]{:S(2)}) collective-permute-start(bf16[128,512]{1,0:T(8,128)(2,1)} %get-tuple-element.21), channel_id=1, source_target_pairs={{0,4},{4,8},{8,12},{12,16},{16,20},{20,24},{24,28},{28,0},{1,5},{5... | collective-permute-start | bytes 393224 | tf_op jit(solution)/shard_map/ppermute | solution.py:22
  54.7 0.0 collective-permute-done.4.refs_0_
  54.7 3.3 %collective-permute-start.1 = (bf16[128,512]{1,0:T(8,128)(2,1)}, bf16[128,512]{1,0:T(8,128)(2,1)S(1)}, u32[]{:S(2)}, u32[]{:S(2)}) collective-permute-start(bf16[128,512]{1,0:T(8,128)(2,1)} %get-tuple-element.22), channel_id=1, source_target_pairs={{0,28},{4,0},{8,4},{12,8},{16,12},{20,16},{24,20},{28,24},{1,29},{... | collective-permute-start | bytes 393224 | tf_op jit(solution)/shard_map/ppermute | solution.py:22
  58.0 0.1 concatenate.6.scal_ref
  58.1 0.0 all-to-all-done.refs_2_
  58.1 1.2 %copy-done.4 = bf16[1024,512]{1,0:T(8,128)(2,1)S(1)} copy-done((bf16[1024,512]{1,0:T(8,128)(2,1)S(1)}, bf16[1024,512]{1,0:T(8,128)(2,1)}, u32[]{:S(2)}) %copy-start.4) | copy-done | bytes 1048600
  59.3 0.9 %copy-done.9 = bf16[128,512]{1,0:T(8,128)(2,1)S(1)} copy-done((bf16[128,512]{1,0:T(8,128)(2,1)S(1)}, bf16[128,512]{1,0:T(8,128)(2,1)}, u32[]{:S(2)}) %copy-start.9) | copy-done | bytes 131096
  60.2 1.5 %loss.4 = (f32[8,128]{1,0:T(8,128)S(1)}, f32[4,256,512]{2,1,0:T(8,128)S(1)}) custom-call(s32[12]{0:T(128)S(1)} %concatenate.6.scal_ref, bf16[128,512]{1,0:T(8,128)(2,1)S(1)} %copy-done.9, bf16[128,512]{1,0:T(8,128)(2,1)S(1)} %collective-permute-done.6.refs_1_, s32[8,2,128]{2,1,0:T(2,128)S(1)} %all-to-all-done.refs_2_, bf16[1024,512]{1,0:T(8,128)(2,1)S(1)} %copy-done.4), custom_call_target="tpu_custom_call" | custom-call | tf_op jit(solution)/shard_map/loss/pallas_call | solution.py:173
  61.8 1.2 %copy-done.5 = bf16[1024,512]{1,0:T(8,128)(2,1)S(1)} copy-done((bf16[1024,512]{1,0:T(8,128)(2,1)S(1)}, bf16[1024,512]{1,0:T(8,128)(2,1)}, u32[]{:S(2)}) %copy-start.5) | copy-done | bytes 1048600
  63.0 2.5 %loss.5 = (f32[8,128]{1,0:T(8,128)S(1)}, f32[4,256,512]{2,1,0:T(8,128)S(1)}) custom-call(s32[12]{0:T(128)S(1)} %concatenate.6.scal_ref, bf16[128,512]{1,0:T(8,128)(2,1)S(1)} %collective-permute-done.4.refs_0_, bf16[128,512]{1,0:T(8,128)(2,1)} %collective-permute-done.5.refs_1_, s32[8,2,128]{2,1,0:T(2,128)S(1)} %all-to-all-done.refs_2_, ...), custom_call_target="tpu_custom_call" | custom-call | tf_op jit(solution)/shard_map/loss/pallas_call | solution.py:173
  65.5 0.0 collective-permute-done.2.refs_0_
  65.5 2.5 %loss.6 = (f32[8,128]{1,0:T(8,128)S(1)}, f32[4,256,512]{2,1,0:T(8,128)S(1)}) custom-call(s32[12]{0:T(128)S(1)} %concatenate.6.scal_ref, bf16[128,512]{1,0:T(8,128)(2,1)S(1)} %collective-permute-done.2.refs_0_, bf16[128,512]{1,0:T(8,128)(2,1)} %collective-permute-done.3.refs_1_, s32[8,2,128]{2,1,0:T(2,128)S(1)} %all-to-all-done.refs_2_, ...), custom_call_target="tpu_custom_call" | custom-call | tf_op jit(solution)/shard_map/loss/pallas_call | solution.py:173
  68.0 0.0 collective-permute-done.1.refs_1_
  68.0 0.0 copy-start.12
  68.0 1.9 %loss.7 = (f32[8,128]{1,0:T(8,128)}, f32[256,512]{1,0:T(8,128)S(1)}, f32[256,512]{1,0:T(8,128)S(1)}, bf16[256,512]{1,0:T(8,128)(2,1)S(1)}, bf16[256,512]{1,0:T(8,128)(2,1)S(1)}) custom-call(s32[12]{0:T(128)S(1)} %concatenate.6.scal_ref, bf16[128,512]{1,0:T(8,128)(2,1)S(1)} %collective-permute-done.refs_0_, ...), custom_call_target="tpu_custom_call" | custom-call | tf_op jit(solution)/shard_map/loss/pallas_call | solution.py:173
  70.0 0.5 collective-permute-start.7
  70.5 1.0 %collective-permute-done.8 = bf16[256,512]{1,0:T(8,128)(2,1)S(1)} collective-permute-done((bf16[256,512]{1,0:T(8,128)(2,1)S(1)}, bf16[256,512]{1,0:T(8,128)(2,1)S(1)}, u32[]{:S(2)}, u32[]{:S(2)}) %collective-permute-start.8) | collective-permute-done | bytes 262176 | tf_op jit(solution)/shard_map/ppermute | solution.py:17
  71.5 0.1 add_convert_fusion
  71.6 1.6 %collective-permute-start.9 = (bf16[256,512]{1,0:T(8,128)(2,1)S(1)}, bf16[256,512]{1,0:T(8,128)(2,1)S(1)}, u32[]{:S(2)}, u32[]{:S(2)}) collective-permute-start(bf16[256,512]{1,0:T(8,128)(2,1)S(1)} %add_convert_fusion), channel_id=1, source_target_pairs={{0,2},{1,3},{2,0},{3,1},{4,6},{5,7},{6,4},{7,5},{8,10},{9,11},{10,... | collective-permute-start | bytes 786440 | tf_op jit(solution)/shard_map/ppermute | solution.py:17
  73.2 6.8 %collective-permute-done.9 = bf16[256,512]{1,0:T(8,128)(2,1)S(1)} collective-permute-done((bf16[256,512]{1,0:T(8,128)(2,1)S(1)}, bf16[256,512]{1,0:T(8,128)(2,1)S(1)}, u32[]{:S(2)}, u32[]{:S(2)}) %collective-permute-start.9) | collective-permute-done | bytes 262176 | tf_op jit(solution)/shard_map/ppermute | solution.py:17
  80.0 0.3 multiply_reduce_fusion
  80.3 1.0 %subtract_divide_fusion = f32[256,512]{1,0:T(8,128)} fusion(f32[256]{0:T(256)S(1)} %multiply_reduce_fusion, f32[256]{0:T(256)S(1)} %copy-done.14, bf16[256,512]{1,0:T(8,128)(2,1)S(1)} %collective-permute-done.9, f32[256,512]{1,0:T(8,128)S(1)} %get-tuple-element.36, bf16[256,512]{1,0:T(8,128)(2,1)S(1)} %collective-permute-done.7, ...), kind=kLoop, calls=%fused_computation.4 | loop fusion | flops 1310720 | bytes 1837056 | tf_op jit(solution)/shard_map/div | solution.py:234
  (38 shorter events, 0.1 us)
Async XLA Ops:
  7.2 50.9 %all-gather.2.cloned.1.call-start = ((), (), s32[]{:S(2)}) async-start(), calls=%async_computation.1 | async-start | bytes 1310720 | tf_op jit(solution)/shard_map/all_gather | solution.py:206
  8.3 0.5 copy-start.13
  12.0 1.2 %copy-start = (bf16[8,128,512]{2,1,0:T(8,128)(2,1)S(1)}, bf16[8,128,512]{2,1,0:T(8,128)(2,1)}, u32[]{:S(2)}) copy-start(bf16[8,128,512]{2,1,0:T(8,128)(2,1)} %refs_1_.7) | copy-start | bytes 3145732
  13.3 1.6 %copy-start.2 = (bf16[512,2048]{1,0:T(8,128)(2,1)S(1)}, bf16[512,2048]{1,0:T(8,128)(2,1)}, u32[]{:S(2)}) copy-start(bf16[512,2048]{1,0:T(8,128)(2,1)} %refs_2_.7) | copy-start | bytes 6291460
  14.9 1.0 %copy-start.6 = (bf16[512,512]{1,0:T(8,128)(2,1)S(1)}, bf16[512,512]{1,0:T(8,128)(2,1)}, u32[]{:S(2)}) copy-start(bf16[512,512]{1,0:T(8,128)(2,1)} %refs_3_.7) | copy-start | bytes 1572868
  15.9 0.7 copy-start.10
  16.6 10.6 %copy-start.17 = (s32[8]{0:T(128)S(1)}, s32[8]{0:T(128)}, u32[]{:S(2)}) copy-start(s32[8]{0:T(128)} %param.13) | copy-start | bytes 100
  16.6 10.6 %copy-start.16 = (s32[8]{0:T(128)S(1)}, s32[8]{0:T(128)}, u32[]{:S(2)}) copy-start(s32[8]{0:T(128)} %param.11) | copy-start | bytes 100
  16.6 10.6 %copy-start.15 = (s32[8,128]{1,0:T(8,128)S(1)}, s32[8,128]{1,0:T(8,128)}, u32[]{:S(2)}) copy-start(s32[8,128]{1,0:T(8,128)} %param.12) | copy-start | bytes 12292
  16.6 15.4 %copy-start.1 = (bf16[8,128,512]{2,1,0:T(8,128)(2,1)S(1)}, bf16[8,128,512]{2,1,0:T(8,128)(2,1)}, u32[]{:S(2)}) copy-start(bf16[8,128,512]{2,1,0:T(8,128)(2,1)} %refs_1_.7) | copy-start | bytes 3145732
  16.6 15.4 %copy-start.3 = (bf16[512,2048]{1,0:T(8,128)(2,1)S(1)}, bf16[512,2048]{1,0:T(8,128)(2,1)}, u32[]{:S(2)}) copy-start(bf16[512,2048]{1,0:T(8,128)(2,1)} %refs_2_.7) | copy-start | bytes 6291460
  16.6 15.4 %copy-start.11 = (f32[4,128]{1,0:T(4,128)S(1)}, f32[4,128]{1,0:T(4,128)}, u32[]{:S(2)}) copy-start(f32[4,128]{1,0:T(4,128)} %refs_4_.7) | copy-start | bytes 6148
  20.6 32.7 %collective-permute-start.6 = (bf16[128,512]{1,0:T(8,128)(2,1)}, bf16[128,512]{1,0:T(8,128)(2,1)S(1)}, u32[]{:S(2)}, u32[]{:S(2)}) collective-permute-start(bf16[128,512]{1,0:T(8,128)(2,1)} %get-tuple-element.28), channel_id=1, source_target_pairs={{0,16},{4,20},{8,24},{12,28},{16,0},{20,4},{24,8},{28,12},{1,17},{... | collective-permute-start | bytes 393224 | tf_op jit(solution)/shard_map/ppermute | solution.py:22
  24.6 30.1 %collective-permute-start.4 = (bf16[128,512]{1,0:T(8,128)(2,1)}, bf16[128,512]{1,0:T(8,128)(2,1)S(1)}, u32[]{:S(2)}, u32[]{:S(2)}) collective-permute-start(bf16[128,512]{1,0:T(8,128)(2,1)} %get-tuple-element.25), channel_id=1, source_target_pairs={{0,12},{4,16},{8,20},{12,24},{16,28},{20,0},{24,4},{28,8},{1,13},{... | collective-permute-start | bytes 393224 | tf_op jit(solution)/shard_map/ppermute | solution.py:22
  28.4 29.7 %all-to-all-start = ((s32[8,2,128]{2,1,0:T(2,128)}), s32[8,2,128]{2,1,0:T(2,128)S(1)}, u32[]{:S(2)}, u32[]{:S(2)}) async-start(s32[8,2,128]{2,1,0:T(2,128)} %gather_fusion), calls=%async_computation | async-start | bytes 16384 | tf_op jit(solution)/shard_map/all_to_all | solution.py:216
  32.0 1.0 %copy-start.7 = (bf16[512,512]{1,0:T(8,128)(2,1)S(1)}, bf16[512,512]{1,0:T(8,128)(2,1)}, u32[]{:S(2)}) copy-start(bf16[512,512]{1,0:T(8,128)(2,1)} %refs_3_.7) | copy-start | bytes 1572868
  37.1 24.7 %collective-permute-start.5 = (bf16[128,512]{1,0:T(8,128)(2,1)}, bf16[128,512]{1,0:T(8,128)(2,1)}, u32[]{:S(2)}, u32[]{:S(2)}) collective-permute-start(bf16[128,512]{1,0:T(8,128)(2,1)} %get-tuple-element.26), channel_id=1, source_target_pairs={{0,20},{4,24},{8,28},{12,0},{16,4},{20,8},{24,12},{28,16},{1,21},{... | collective-permute-start | bytes 393224 | tf_op jit(solution)/shard_map/ppermute | solution.py:22
  40.9 24.6 %collective-permute-start.2 = (bf16[128,512]{1,0:T(8,128)(2,1)}, bf16[128,512]{1,0:T(8,128)(2,1)S(1)}, u32[]{:S(2)}, u32[]{:S(2)}) collective-permute-start(bf16[128,512]{1,0:T(8,128)(2,1)} %get-tuple-element.23), channel_id=1, source_target_pairs={{0,8},{4,12},{8,16},{12,20},{16,24},{20,28},{24,0},{28,4},{1,9},{5... | collective-permute-start | bytes 393224 | tf_op jit(solution)/shard_map/ppermute | solution.py:22
  46.3 11.7 %copy-start.18 = (s32[8]{0:T(128)S(1)}, s32[8]{0:T(128)}, u32[]{:S(2)}) copy-start(s32[8]{0:T(128)} %constant.53) | copy-start | bytes 100
  46.3 19.2 %collective-permute-start.3 = (bf16[128,512]{1,0:T(8,128)(2,1)}, bf16[128,512]{1,0:T(8,128)(2,1)}, u32[]{:S(2)}, u32[]{:S(2)}) collective-permute-start(bf16[128,512]{1,0:T(8,128)(2,1)} %get-tuple-element.24), channel_id=1, source_target_pairs={{0,24},{4,28},{8,0},{12,4},{16,8},{20,12},{24,16},{28,20},{1,25},{... | collective-permute-start | bytes 393224 | tf_op jit(solution)/shard_map/ppermute | solution.py:22
  52.6 0.6 copy-start.8
  53.3 14.7 %collective-permute-start = (bf16[128,512]{1,0:T(8,128)(2,1)}, bf16[128,512]{1,0:T(8,128)(2,1)S(1)}, u32[]{:S(2)}, u32[]{:S(2)}) collective-permute-start(bf16[128,512]{1,0:T(8,128)(2,1)} %get-tuple-element.21), channel_id=1, source_target_pairs={{0,4},{4,8},{8,12},{12,16},{16,20},{20,24},{24,28},{28,0},{1,5},{5... | collective-permute-start | bytes 393224 | tf_op jit(solution)/shard_map/ppermute | solution.py:22
  54.7 13.3 %collective-permute-start.1 = (bf16[128,512]{1,0:T(8,128)(2,1)}, bf16[128,512]{1,0:T(8,128)(2,1)S(1)}, u32[]{:S(2)}, u32[]{:S(2)}) collective-permute-start(bf16[128,512]{1,0:T(8,128)(2,1)} %get-tuple-element.22), channel_id=1, source_target_pairs={{0,28},{4,0},{8,4},{12,8},{16,12},{20,16},{24,20},{28,24},{1,29},{... | collective-permute-start | bytes 393224 | tf_op jit(solution)/shard_map/ppermute | solution.py:22
  58.1 1.2 %copy-start.4 = (bf16[1024,512]{1,0:T(8,128)(2,1)S(1)}, bf16[1024,512]{1,0:T(8,128)(2,1)}, u32[]{:S(2)}) copy-start(bf16[1024,512]{1,0:T(8,128)(2,1)} %all-gather.2.cloned.1.call-done.refs_3_) | copy-start | bytes 3145732
  59.3 0.9 %copy-start.9 = (bf16[128,512]{1,0:T(8,128)(2,1)S(1)}, bf16[128,512]{1,0:T(8,128)(2,1)}, u32[]{:S(2)}) copy-start(bf16[128,512]{1,0:T(8,128)(2,1)} %copy-done.8) | copy-start | bytes 393220
  61.8 1.2 %copy-start.5 = (bf16[1024,512]{1,0:T(8,128)(2,1)S(1)}, bf16[1024,512]{1,0:T(8,128)(2,1)}, u32[]{:S(2)}) copy-start(bf16[1024,512]{1,0:T(8,128)(2,1)} %all-gather.2.cloned.1.call-done.refs_3_) | copy-start | bytes 3145732
  68.0 12.0 %copy-start.12 = (bf16[256,512]{1,0:T(8,128)(2,1)S(1)}, bf16[256,512]{1,0:T(8,128)(2,1)}, u32[]{:S(2)}) copy-start(bf16[256,512]{1,0:T(8,128)(2,1)} %param.17) | copy-start | bytes 786436
  68.0 12.0 %copy-start.14 = (f32[256]{0:T(256)S(1)}, f32[256]{0:T(256)}, u32[]{:S(2)}) copy-start(f32[256]{0:T(256)} %copy-done.13) | copy-start | bytes 3076
  70.0 1.5 %collective-permute-start.8 = (bf16[256,512]{1,0:T(8,128)(2,1)S(1)}, bf16[256,512]{1,0:T(8,128)(2,1)S(1)}, u32[]{:S(2)}, u32[]{:S(2)}) collective-permute-start(bf16[256,512]{1,0:T(8,128)(2,1)S(1)} %get-tuple-element.39), channel_id=1, source_target_pairs={{0,1},{1,0},{2,3},{3,2},{4,5},{5,4},{6,7},{7,6},{8,9},{9,8},{10,11... | collective-permute-start | bytes 786440 | tf_op jit(solution)/shard_map/ppermute | solution.py:17
  70.0 3.2 %collective-permute-start.7 = (bf16[256,512]{1,0:T(8,128)(2,1)S(1)}, bf16[256,512]{1,0:T(8,128)(2,1)S(1)}, u32[]{:S(2)}, u32[]{:S(2)}) collective-permute-start(bf16[256,512]{1,0:T(8,128)(2,1)S(1)} %get-tuple-element.37), channel_id=1, source_target_pairs={{0,1},{1,0},{2,3},{3,2},{4,5},{5,4},{6,7},{7,6},{8,9},{9,8},{10,11... | collective-permute-start | bytes 786440 | tf_op jit(solution)/shard_map/ppermute | solution.py:17
  71.6 8.4 %collective-permute-start.9 = (bf16[256,512]{1,0:T(8,128)(2,1)S(1)}, bf16[256,512]{1,0:T(8,128)(2,1)S(1)}, u32[]{:S(2)}, u32[]{:S(2)}) collective-permute-start(bf16[256,512]{1,0:T(8,128)(2,1)S(1)} %add_convert_fusion), channel_id=1, source_target_pairs={{0,2},{1,3},{2,0},{3,1},{4,6},{5,7},{6,4},{7,5},{8,10},{9,11},{10,... | collective-permute-start | bytes 786440 | tf_op jit(solution)/shard_map/ppermute | solution.py:17
Sparse Core Ops, SparseCore 0:
  10.7 19.4 all-gather.1

commit v3 on v1

v3 whole, which is shorter than its diff:
```python
import functools
import math

import jax
import jax.numpy as jnp
from jax import lax
from jax.experimental import pallas as pl
from jax.experimental.pallas import tpu as pltpu
from jax.sharding import PartitionSpec as P

logit_scale = 20.0
contract_last = (((1,), (1,)), ((), ()))
tile = 256
chunk = 16


def swap(array, axis, bit):
    devices = lax.axis_size(axis)
    return lax.ppermute(array, axis, [(i, i ^ bit) for i in range(devices)])


def half_silu(half):
    return half + half * jnp.tanh(half)


def center_and_spread(values):
    center = values - jnp.mean(values, axis=-1, keepdims=True)
    return center, jnp.mean(center * center, axis=-1, keepdims=True)


def pick_kernel(list_ref, from_ref, to_ref, sems):
    copies = [
        pltpu.make_async_copy(from_ref.at[list_ref[k]], to_ref.at[k], sems.at[k])
        for k in range(to_ref.shape[0])
    ]
    for copy in copies:
        copy.start()
    for copy in copies:
        copy.wait()


def pick(array, entries):
    return pl.pallas_call(
        pick_kernel,
        grid_spec=pltpu.PrefetchScalarGridSpec(
            num_scalar_prefetch=1,
            grid=(1,),
            in_specs=[pl.BlockSpec(memory_space=pltpu.HBM)],
            out_specs=pl.BlockSpec(memory_space=pl.ANY),
            scratch_shapes=[pltpu.SemaphoreType.DMA(entries.shape)],
        ),
        out_shape=jax.ShapeDtypeStruct(entries.shape + array.shape[1:], array.dtype),
        name="pick",
    )(entries, array)


def users_kernel(
    per_step, blocks, scal_ref, x_ref, tgt_ref, w_in, w_out, bias_in, unit_ref,
    loss_ref, own_ref, over_ref, side_ref, far_ref,
    acc, bias, exp_ref, events, gate, value, query, key, mixed, packed_tgt, packed_loss,
):
    step = pl.program_id(0)
    heads, length = bias_in.shape
    width = x_ref.shape[-1]
    hdim = width // heads
    half = length // 2
    items = unit_ref.shape[0] // blocks

    @pl.when(step == 0)
    def _():
        acc[...] = jnp.zeros_like(acc)
        for h in range(heads):
            wide = jnp.broadcast_to(0.5 * bias_in[h : h + 1, :], (length, length))
            bias[h] = pltpu.roll(wide, 0, 1, stride=1, stride_axis=0).T

    lens = [scal_ref[blocks + step * per_step + u] for u in range(per_step)]
    starts, end = [], 0
    for u in range(per_step):
        starts.append(pl.multiple_of(end, chunk) if u else 0)
        end = end + (lens[u] + chunk - 1) // chunk * chunk
    end = pl.multiple_of(end, chunk)
    tiles = (end + tile - 1) // tile
    covered = pl.multiple_of(tiles * tile, tile)

    place = lax.broadcasted_iota(jnp.int32, (1, length), 1)
    packed_tgt[...] = jnp.full_like(packed_tgt, -1)
    for u in range(per_step):
        events[pl.ds(starts[u], length), :] = x_ref[u]
        wanted = jnp.where(place < lens[u], tgt_ref[pl.ds(step * per_step + u, 1), :], -1)
        line, turn = starts[u] // length, lax.rem(starts[u], length)
        turned = pltpu.roll(wanted, turn, 1)
        packed_tgt[pl.ds(line, 1), :] = jnp.where(place >= turn, turned, packed_tgt[pl.ds(line, 1), :])
        packed_tgt[pl.ds(line + 1, 1), :] = jnp.where(
            place < turn, turned, packed_tgt[pl.ds(line + 1, 1), :]
        )
    events[pl.ds(end, tile), :] = jnp.zeros((tile, width), events.dtype)
    last_tile = pl.multiple_of(covered - tile, tile)
    mixed[pl.ds(last_tile, tile), :] = jnp.zeros((tile, width), mixed.dtype)
    for part in (value, query, key):
        part[pl.ds(covered, length), :] = jnp.zeros((length, width), part.dtype)

    def project(t, _):
        rows = pl.ds(pl.multiple_of(t * tile, tile), tile)
        center, spread = center_and_spread(events[rows, :].astype(jnp.float32))
        half_normed = (center * (0.5 * lax.rsqrt(spread + 1e-05))).astype(jnp.bfloat16)
        for index, part in enumerate((gate, value, query, key)):
            halves = jnp.dot(
                half_normed, w_in[:, index * width : (index + 1) * width], preferred_element_type=jnp.float32
            )
            part[rows, :] = half_silu(halves).astype(jnp.bfloat16)
        return 0

    lax.fori_loop(0, tiles, project, 0)

    def attend(u, first, count, seen):
        rows, sources = pl.ds(starts[u] + first, count), pl.ds(starts[u], seen)
        row = first + lax.broadcasted_iota(jnp.int32, (count, seen), 0)
        col = lax.broadcasted_iota(jnp.int32, (count, seen), 1)
        keep = (col <= row) & (col < lens[u])
        for h in range(heads):
            cols = slice(h * hdim, (h + 1) * hdim)
            scores = lax.dot_general(
                query[rows, cols], key[sources, cols], contract_last, preferred_element_type=jnp.float32
            )
            attn = half_silu(
                scores * (0.5 / math.sqrt(hdim)) + bias[h, first : first + count, :seen]
            )
            attn = jnp.where(keep, attn, 0.0).astype(jnp.bfloat16)
            mixed[rows, cols] = jnp.dot(attn, value[sources, cols], preferred_element_type=jnp.float32)

    for u in range(per_step):
        pl.when(lens[u] > half)(functools.partial(attend, u, half, length - half, length))
    for u in range(per_step):
        attend(u, 0, half, half)

    item_id = lax.broadcasted_iota(jnp.int32, (items, tile), 0)
    rate = logit_scale * math.log2(math.e)
    lines = tile // length

    def score(t, _):
        rows = pl.ds(pl.multiple_of(t * tile, tile), tile)
        center, spread = center_and_spread(mixed[rows, :])
        normed = center * lax.rsqrt(spread + 1e-05)
        gated = (normed * gate[rows, :].astype(jnp.float32)).astype(jnp.bfloat16)
        out = events[rows, :].astype(jnp.float32) + jnp.dot(
            gated, w_out[...], preferred_element_type=jnp.float32
        )
        out = out.astype(jnp.bfloat16).astype(jnp.float32)
        square = jnp.sum(out * out, axis=-1, keepdims=True)
        queries = (out * lax.rsqrt(square + 1e-06)).astype(jnp.bfloat16)

        target = jnp.concatenate([packed_tgt[pl.ds(t * lines + k, 1), :] for k in range(lines)], axis=1)
        total = jnp.zeros((1, tile), jnp.float32)
        target_dot = jnp.zeros((1, tile), jnp.float32)
        for j in range(blocks):
            dots = lax.dot_general(
                unit_ref[j * items : (j + 1) * items], queries, contract_last,
                preferred_element_type=jnp.float32,
            )
            exps = jnp.exp2(dots * rate - rate)
            exp_ref[j] = exps
            total += jnp.sum(exps, axis=0, keepdims=True)
            hit = item_id == target - j * items
            target_dot += jnp.sum(jnp.where(hit, dots, 0.0), axis=0, keepdims=True)
        loss = logit_scale + jnp.log(total) - logit_scale * target_dot
        for k in range(lines):
            packed_loss[pl.ds(t * lines + k, 1), :] = loss[:, k * length : (k + 1) * length]
        share = jnp.where(target >= 0, 1.0 / total, 0.0)
        for j in range(blocks):
            hit = item_id == target - j * items
            residual = exp_ref[j] * share - jnp.where(hit, 1.0, 0.0)
            acc[j] += jnp.dot(residual.astype(jnp.bfloat16), queries, preferred_element_type=jnp.float32)
        return 0

    lax.fori_loop(0, tiles, score, 0)

    for u in range(per_step):
        line, turn = starts[u] // length, lax.rem(starts[u], length)
        back = lax.rem(length - turn, length)
        near = pltpu.roll(packed_loss[pl.ds(line, 1), :], back, 1)
        rest = pltpu.roll(packed_loss[pl.ds(line + 1, 1), :], back, 1)
        loss = jnp.where(place < length - turn, near, rest)
        loss_ref[pl.ds(step * per_step + u, 1), :] = jnp.where(place < lens[u], loss, 0.0)

    @pl.when(step == pl.num_programs(0) - 1)
    def _():
        own_ref[...] = acc[scal_ref[0]]
        over_ref[...] = acc[scal_ref[1]]
        side_ref[...] = acc[scal_ref[2]].astype(jnp.bfloat16)
        far_ref[...] = acc[scal_ref[3]].astype(jnp.bfloat16)


def users_call(events, lens, targets, w_in, w_out, rel_bias, unit_all, block_ids):
    users, length, width = events.shape
    blocks = block_ids.shape[0]
    items = unit_all.shape[0] // blocks
    heads = rel_bias.shape[0]
    per_step = math.gcd(users, 8)
    rows = per_step * length
    lines = -(-(rows // length + 1) // 8) * 8
    whole = lambda *shape: pl.BlockSpec(shape, lambda s, scal: (0,) * len(shape))
    part = lambda dtype: jax.ShapeDtypeStruct((items, width), dtype)
    return pl.pallas_call(
        functools.partial(users_kernel, per_step, blocks),
        grid_spec=pltpu.PrefetchScalarGridSpec(
            num_scalar_prefetch=1,
            grid=(users // per_step,),
            in_specs=[
                pl.BlockSpec((per_step, length, width), lambda s, scal: (s, 0, 0)),
                whole(users, length),
                whole(*w_in.shape),
                whole(*w_out.shape),
                whole(*rel_bias.shape),
                whole(*unit_all.shape),
            ],
            out_specs=[whole(users, length)] + [whole(items, width)] * 4,
            scratch_shapes=[
                pltpu.VMEM((blocks, items, width), jnp.float32),
                pltpu.VMEM((heads, length, length), jnp.float32),
                pltpu.VMEM((blocks, items, tile), jnp.float32),
                pltpu.VMEM((rows + tile, width), jnp.bfloat16),
            ]
            + [pltpu.VMEM((rows + tile, width), jnp.bfloat16)] * 4
            + [
                pltpu.VMEM((rows + tile, width), jnp.float32),
                pltpu.VMEM((lines, length), jnp.int32),
                pltpu.VMEM((lines, length), jnp.float32),
            ],
        ),
        out_shape=[
            jax.ShapeDtypeStruct((users, length), jnp.float32),
            part(jnp.float32),
            part(jnp.float32),
            part(jnp.bfloat16),
            part(jnp.bfloat16),
        ],
        compiler_params=pltpu.CompilerParams(vmem_limit_bytes=44 * 1024 * 1024),
        name="users",
    )(jnp.concatenate([block_ids, lens]), events, targets, w_in, w_out, rel_bias, unit_all)


def gather_all(array, axis):
    devices, index = lax.axis_size(axis), lax.axis_index(axis)
    array, bit = array[None], 1
    while bit < devices:
        other = swap(array, axis, bit)
        upper = (index & bit) != 0
        array = jnp.concatenate([jnp.where(upper, other, array), jnp.where(upper, array, other)], axis=0)
        bit *= 2
    return array


def shards(histories, lengths, targets, send_list, w_in, w_out, rel_bias, item_pool):
    user_count, length, feat_width = histories.shape
    groups = lax.axis_size("dp")
    slots = user_count // groups
    picked = pick(histories, send_list)
    numbers = jnp.stack([jnp.broadcast_to(lengths[:, None], targets.shape), targets], axis=1)
    picked, numbers = lax.optimization_barrier((picked, numbers))
    routed_hist = lax.all_to_all(picked, "dp", split_axis=0, concat_axis=0, tiled=True)

    pool_float = item_pool.astype(jnp.float32)
    item_norm = jnp.sqrt(jnp.sum(pool_float * pool_float, axis=-1, keepdims=True) + 1e-06)
    unit_rows = pool_float / item_norm
    unit_all = lax.all_gather(unit_rows.astype(jnp.bfloat16), "blk", axis=0, tiled=True)

    numbers = gather_all(numbers[send_list], "dp")
    numbers = lax.dynamic_slice_in_dim(numbers, lax.axis_index("dp") * slots, slots, axis=1)
    numbers = numbers.reshape(user_count, 2, length)

    mine = lax.axis_index("blk")
    block_ids = jnp.stack([mine, mine ^ 2, mine ^ 1, mine ^ 3]).astype(jnp.int32)
    row_loss, own, over, side, far = users_call(
        routed_hist, numbers[:, 0, 0], numbers[:, 1], w_in, w_out, rel_bias, unit_all, block_ids
    )
    over = over + swap(far, "blk", 1).astype(jnp.float32)
    own = own + swap(side, "blk", 1).astype(jnp.float32)
    item_sum = logit_scale * (own + swap(over.astype(jnp.bfloat16), "blk", 2).astype(jnp.float32))
    pool_grad = (
        item_sum - unit_rows * jnp.sum(unit_rows * item_sum, axis=-1, keepdims=True)
    ) / item_norm
    return (row_loss, pool_grad)


def solution(mesh):
    placed = (
        P(("dp", "blk"), None, None),
        P(("dp", "blk")),
        P(("dp", "blk"), None),
        P(("dp", "blk")),
        P(),
        P(),
        P(),
        P(("dp", "blk"), None),
    )
    return jax.shard_map(
        shards,
        mesh=mesh,
        in_specs=placed,
        out_specs=(P(("dp", "blk"), None), P(("dp", "blk"), None)),
        check_vma=False,
    )
```

time: 101 us -> 111 us (1.099)
  blocking collectives: 43.8 us -> 0 us
  Pallas kernels: 17.9 us -> 46.8 us
  waiting for transfers between devices: 7.87 us -> 24 us
  starting transfers between devices: 9.53 us -> 18.8 us
    all_gather x1 -> x0, blocking collectives: 43.8 us -> none  [shards(): numbers = lax.all_gather(numbers, 'dp', axis=0, tiled=False)]
    pallas_call x0 -> x1, Pallas kernels: none -> 33.7 us  [pick(): pl.pallas_call(pick_kernel, grid_spec=pltpu.PrefetchScalarGridSpec(num_sc...]
    ppermute x3 -> x6, waiting for transfers between devices: 7.85 us -> 24 us  [swap(): return lax.ppermute(array, axis, [(i, i ^ bit) for i in range(devices)])]
    ppermute x3 -> x6, starting transfers between devices: 2.09 us -> 11.4 us  [swap(): return lax.ppermute(array, axis, [(i, i ^ bit) for i in range(devices)])]
    pallas_call x1, Pallas kernels: 17.9 us -> 13.1 us  [users_call(): pl.pallas_call(functools.partial(users_kernel, per_step, blocks), grid_sp...]
    gather x2 -> x1, local copies, waits for them, and re-layouts: 2.21 us -> 0.58 us  [shards(): numbers = gather_all(numbers[send_list], 'dp')]
    unnamed x15 -> x12, local copies, waits for them, and re-layouts: 1.73 us -> 2.28 us
  transfers between devices with their start and end apart: 5 -> 8, of which waited for: 2 -> 5; matrix products, arithmetic and copies ran while one was open for 2% -> 2% of each run, Pallas kernels for 0% -> 0%
where the time goes in v3:
time: 111 us
  Pallas kernels  46.8 us (42%)
  waiting for transfers between devices  24 us (22%)
  starting transfers between devices  18.8 us (17%)
  between operations  14.2 us (13%)
  local copies, waits for them, and re-layouts  3.79 us (3%)
  other arithmetic  3.13 us (3%)
    pallas_call x1, Pallas kernels, pick(): pl.pallas_call(pick_kernel, grid_spec=pltpu.PrefetchScalarGridSpec(num_sc...  33.7 us
    ppermute x6, waiting for transfers between devices, swap(): return lax.ppermute(array, axis, [(i, i ^ bit) for i in range(devices)])  24 us
    pallas_call x1, Pallas kernels, users_call(): pl.pallas_call(functools.partial(users_kernel, per_step, blocks), grid_sp...  13.1 us
    ppermute x6, starting transfers between devices, swap(): return lax.ppermute(array, axis, [(i, i ^ bit) for i in range(devices)])  11.4 us
    all_to_all x1, starting transfers between devices, shards(): lax.all_to_all(picked, 'dp', split_axis=0, concat_axis=0, tiled=True)  7.4 us
    unnamed x12, local copies, waits for them, and re-layouts  2.28 us
  transfers between devices with their start and end apart: 8, of which 5 were waited for; matrix products, arithmetic and copies ran while one was open for 2% of the time, Pallas kernels for 0%

profile of v3, /device:TPU:0, one launch (start us, length us, event | category | flops | bytes accessed | tf_op | source)
XLA Modules:
  0.0 110.8 jit_solution(7206983929190296993)
XLA Ops:
  7.2 0.7 stack_broadcast_in_dim.2
  7.9 0.7 pad_add_fusion.2
  8.6 0.0 copy-start.4
  8.6 33.7 %pick.1 = bf16[8,128,512]{2,1,0:T(8,128)(2,1)} custom-call(s32[8]{0:T(128)} %list_ref.1, bf16[8,128,512]{2,1,0:T(8,128)(2,1)} %from_ref.1), custom_call_target="tpu_custom_call" | custom-call | tf_op jit(solution)/shard_map/pick/pallas_call | solution.py:43
  42.3 0.0 copy-start.5
  42.4 0.0 copy-start
  42.4 0.0 copy-start.3
  42.4 7.4 %all-to-all-start = ((bf16[8,128,512]{2,1,0:T(8,128)(2,1)}), bf16[8,128,512]{2,1,0:T(8,128)(2,1)S(1)}, u32[]{:S(2)}, u32[]{:S(2)}) async-start(bf16[8,128,512]{2,1,0:T(8,128)(2,1)} %pick.1), calls=%async_computation | async-start | bytes 2097152 | tf_op jit(solution)/shard_map/all_to_all | solution.py:260
  49.8 0.0 all-gather.2.cloned.1.call-start
  49.8 0.0 copy-done.4
  49.8 0.1 fusion
  50.0 0.8 fusion.2
  50.8 0.0 all-gather.2.cloned.1.call-update
  50.8 0.0 copy-done.5
  50.9 0.6 gather_fusion
  51.4 2.0 %collective-permute-start = (s32[1,8,2,128]{3,2,1,0:T(2,128)S(1)}, s32[1,8,2,128]{3,2,1,0:T(2,128)S(1)}, u32[]{:S(2)}, u32[]{:S(2)}) collective-permute-start(s32[1,8,2,128]{3,2,1,0:T(2,128)S(1)} %bitcast.15), channel_id=1, source_target_pairs={{0,4},{4,0},{8,12},{12,8},{16,20},{20,16},{24,28},{28,24},{1,5},{5... | collective-permute-start | bytes 24584 | tf_op jit(solution)/shard_map/ppermute | solution.py:19
  53.5 3.5 %collective-permute-done = s32[1,8,2,128]{3,2,1,0:T(2,128)S(1)} collective-permute-done((s32[1,8,2,128]{3,2,1,0:T(2,128)S(1)}, s32[1,8,2,128]{3,2,1,0:T(2,128)S(1)}, u32[]{:S(2)}, u32[]{:S(2)}) %collective-permute-start) | collective-permute-done | bytes 8224 | tf_op jit(solution)/shard_map/ppermute | solution.py:19
  57.0 3.4 %collective-permute-start.1 = (s32[2,8,2,128]{3,2,1,0:T(2,128)S(1)}, s32[2,8,2,128]{3,2,1,0:T(2,128)S(1)}, u32[]{:S(2)}, u32[]{:S(2)}) collective-permute-start(s32[2,8,2,128]{3,2,1,0:T(2,128)S(1)} %pad_add_fusion.1), channel_id=1, source_target_pairs={{0,8},{4,12},{8,0},{12,4},{16,24},{20,28},{24,16},{28,20},{1,9},{5... | collective-permute-start | bytes 49160 | tf_op jit(solution)/shard_map/ppermute | solution.py:19
  60.4 6.8 %collective-permute-done.1 = s32[2,8,2,128]{3,2,1,0:T(2,128)S(1)} collective-permute-done((s32[2,8,2,128]{3,2,1,0:T(2,128)S(1)}, s32[2,8,2,128]{3,2,1,0:T(2,128)S(1)}, u32[]{:S(2)}, u32[]{:S(2)}) %collective-permute-start.1) | collective-permute-done | bytes 16416 | tf_op jit(solution)/shard_map/ppermute | solution.py:19
  67.2 4.6 %collective-permute-start.2 = (s32[4,8,2,128]{3,2,1,0:T(2,128)S(1)}, s32[4,8,2,128]{3,2,1,0:T(2,128)S(1)}, u32[]{:S(2)}, u32[]{:S(2)}) collective-permute-start(s32[4,8,2,128]{3,2,1,0:T(2,128)S(1)} %pad_add_fusion), channel_id=1, source_target_pairs={{0,16},{4,20},{8,24},{12,28},{16,0},{20,4},{24,8},{28,12},{1,17},{... | collective-permute-start | bytes 98312 | tf_op jit(solution)/shard_map/ppermute | solution.py:19
  71.9 5.1 %collective-permute-done.2 = s32[4,8,2,128]{3,2,1,0:T(2,128)S(1)} collective-permute-done((s32[4,8,2,128]{3,2,1,0:T(2,128)S(1)}, s32[4,8,2,128]{3,2,1,0:T(2,128)S(1)}, u32[]{:S(2)}, u32[]{:S(2)}) %collective-permute-start.2) | collective-permute-done | bytes 32800 | tf_op jit(solution)/shard_map/ppermute | solution.py:19
  77.0 0.1 slice_reduce_fusion
  77.1 0.1 concatenate.15.scal_ref
  77.2 0.0 all-gather.2.cloned.1.call-done.unit_ref
  77.2 0.0 all-to-all-done.x_ref
  77.2 0.0 copy-done
  77.2 0.0 copy-done.3
  77.2 0.0 copy-start.1
  77.3 1.2 %copy-done.1 = bf16[1024,512]{1,0:T(8,128)(2,1)S(1)} copy-done((bf16[1024,512]{1,0:T(8,128)(2,1)S(1)}, bf16[1024,512]{1,0:T(8,128)(2,1)}, u32[]{:S(2)}) %copy-start.1) | copy-done | bytes 1048600
  78.5 0.0 copy-start.2
  78.5 1.0 copy-done.2
  79.5 13.1 %users.1 = (f32[8,128]{1,0:T(8,128)}, f32[256,512]{1,0:T(8,128)S(1)}, f32[256,512]{1,0:T(8,128)S(1)}, bf16[256,512]{1,0:T(8,128)(2,1)S(1)}, bf16[256,512]{1,0:T(8,128)(2,1)S(1)}) custom-call(s32[12]{0:T(128)S(1)} %concatenate.15.scal_ref, bf16[8,128,512]{2,1,0:T(8,128)(2,1)S(1)} %all-to-all-done.x_ref, s32[8,128]{1,0:T(8,128)S(1)} %slice_bitcast_fusion.tgt_ref, ...), custom_call_target="tpu_custom_call" | custom-call | tf_op jit(solution)/shard_map/users/pallas_call | solution.py:203
  92.6 0.0 collective-permute-start.4
  92.6 0.5 collective-permute-start.3
  93.1 1.0 collective-permute-done.4
  94.2 0.1 add_convert_fusion
  94.2 0.8 collective-permute-start.5
  95.1 0.0 collective-permute-done.3
  95.1 7.6 %collective-permute-done.5 = bf16[256,512]{1,0:T(8,128)(2,1)S(1)} collective-permute-done((bf16[256,512]{1,0:T(8,128)(2,1)S(1)}, bf16[256,512]{1,0:T(8,128)(2,1)S(1)}, u32[]{:S(2)}, u32[]{:S(2)}) %collective-permute-start.5) | collective-permute-done | bytes 262176 | tf_op jit(solution)/shard_map/ppermute | solution.py:19
  102.6 0.3 multiply_reduce_fusion
  102.9 1.0 subtract_divide_fusion
  (11 shorter events, 0.1 us)
Async XLA Ops:
  8.6 41.2 %copy-start.4 = (bf16[256,512]{1,0:T(8,128)(2,1)S(1)}, bf16[256,512]{1,0:T(8,128)(2,1)}, u32[]{:S(2)}) copy-start(bf16[256,512]{1,0:T(8,128)(2,1)} %param.15) | copy-start | bytes 786436
  42.3 8.5 %copy-start.5 = (s32[8]{0:T(128)S(1)}, s32[8]{0:T(128)}, u32[]{:S(2)}) copy-start(s32[8]{0:T(128)} %list_ref.1) | copy-start | bytes 100
  42.4 34.9 %copy-start = (bf16[512,2048]{1,0:T(8,128)(2,1)S(1)}, bf16[512,2048]{1,0:T(8,128)(2,1)}, u32[]{:S(2)}) copy-start(bf16[512,2048]{1,0:T(8,128)(2,1)} %w_in.1) | copy-start | bytes 6291460
  42.4 34.9 %copy-start.3 = (f32[4,128]{1,0:T(4,128)S(1)}, f32[4,128]{1,0:T(4,128)}, u32[]{:S(2)}) copy-start(f32[4,128]{1,0:T(4,128)} %bias_in.1) | copy-start | bytes 6148
  42.4 34.8 %all-to-all-start = ((bf16[8,128,512]{2,1,0:T(8,128)(2,1)}), bf16[8,128,512]{2,1,0:T(8,128)(2,1)S(1)}, u32[]{:S(2)}, u32[]{:S(2)}) async-start(bf16[8,128,512]{2,1,0:T(8,128)(2,1)} %pick.1), calls=%async_computation | async-start | bytes 2097152 | tf_op jit(solution)/shard_map/all_to_all | solution.py:260
  49.8 27.4 %all-gather.2.cloned.1.call-start = ((), (), s32[]{:S(2)}) async-start(), calls=%async_computation.1 | async-start | bytes 1310720 | tf_op jit(solution)/shard_map/all_gather | solution.py:265
  51.4 5.5 %collective-permute-start = (s32[1,8,2,128]{3,2,1,0:T(2,128)S(1)}, s32[1,8,2,128]{3,2,1,0:T(2,128)S(1)}, u32[]{:S(2)}, u32[]{:S(2)}) collective-permute-start(s32[1,8,2,128]{3,2,1,0:T(2,128)S(1)} %bitcast.15), channel_id=1, source_target_pairs={{0,4},{4,0},{8,12},{12,8},{16,20},{20,16},{24,28},{28,24},{1,5},{5... | collective-permute-start | bytes 24584 | tf_op jit(solution)/shard_map/ppermute | solution.py:19
  57.0 10.3 %collective-permute-start.1 = (s32[2,8,2,128]{3,2,1,0:T(2,128)S(1)}, s32[2,8,2,128]{3,2,1,0:T(2,128)S(1)}, u32[]{:S(2)}, u32[]{:S(2)}) collective-permute-start(s32[2,8,2,128]{3,2,1,0:T(2,128)S(1)} %pad_add_fusion.1), channel_id=1, source_target_pairs={{0,8},{4,12},{8,0},{12,4},{16,24},{20,28},{24,16},{28,20},{1,9},{5... | collective-permute-start | bytes 49160 | tf_op jit(solution)/shard_map/ppermute | solution.py:19
  67.2 9.7 %collective-permute-start.2 = (s32[4,8,2,128]{3,2,1,0:T(2,128)S(1)}, s32[4,8,2,128]{3,2,1,0:T(2,128)S(1)}, u32[]{:S(2)}, u32[]{:S(2)}) collective-permute-start(s32[4,8,2,128]{3,2,1,0:T(2,128)S(1)} %pad_add_fusion), channel_id=1, source_target_pairs={{0,16},{4,20},{8,24},{12,28},{16,0},{20,4},{24,8},{28,12},{1,17},{... | collective-permute-start | bytes 98312 | tf_op jit(solution)/shard_map/ppermute | solution.py:19
  77.2 1.2 %copy-start.1 = (bf16[1024,512]{1,0:T(8,128)(2,1)S(1)}, bf16[1024,512]{1,0:T(8,128)(2,1)}, u32[]{:S(2)}) copy-start(bf16[1024,512]{1,0:T(8,128)(2,1)} %all-gather.2.cloned.1.call-done.unit_ref) | copy-start | bytes 3145732
  78.5 1.0 copy-start.2
  92.6 1.5 %collective-permute-start.4 = (bf16[256,512]{1,0:T(8,128)(2,1)S(1)}, bf16[256,512]{1,0:T(8,128)(2,1)S(1)}, u32[]{:S(2)}, u32[]{:S(2)}) collective-permute-start(bf16[256,512]{1,0:T(8,128)(2,1)S(1)} %get-tuple-element.15), channel_id=1, source_target_pairs={{0,1},{1,0},{2,3},{3,2},{4,5},{5,4},{6,7},{7,6},{8,9},{9,8},{10,11... | collective-permute-start | bytes 786440 | tf_op jit(solution)/shard_map/ppermute | solution.py:19
  92.6 2.5 %collective-permute-start.3 = (bf16[256,512]{1,0:T(8,128)(2,1)S(1)}, bf16[256,512]{1,0:T(8,128)(2,1)S(1)}, u32[]{:S(2)}, u32[]{:S(2)}) collective-permute-start(bf16[256,512]{1,0:T(8,128)(2,1)S(1)} %get-tuple-element.13), channel_id=1, source_target_pairs={{0,1},{1,0},{2,3},{3,2},{4,5},{5,4},{6,7},{7,6},{8,9},{9,8},{10,11... | collective-permute-start | bytes 786440 | tf_op jit(solution)/shard_map/ppermute | solution.py:19
  94.2 8.4 %collective-permute-start.5 = (bf16[256,512]{1,0:T(8,128)(2,1)S(1)}, bf16[256,512]{1,0:T(8,128)(2,1)S(1)}, u32[]{:S(2)}, u32[]{:S(2)}) collective-permute-start(bf16[256,512]{1,0:T(8,128)(2,1)S(1)} %add_convert_fusion), channel_id=1, source_target_pairs={{0,2},{1,3},{2,0},{3,1},{4,6},{5,7},{6,4},{7,5},{8,10},{9,11},{10,... | collective-permute-start | bytes 786440 | tf_op jit(solution)/shard_map/ppermute | solution.py:19
Sparse Core Ops, SparseCore 0:
  52.8 18.1 all-gather.1

commit v4 on v3

v4 whole, which is shorter than its diff:
```python
import functools
import math

import jax
import jax.numpy as jnp
from jax import lax
from jax.experimental import pallas as pl
from jax.experimental.pallas import tpu as pltpu
from jax.sharding import PartitionSpec as P

logit_scale = 20.0
contract_last = (((1,), (1,)), ((), ()))
tile = 256
chunk = 16
number_rows = 8


def swap(array, axis, bit):
    devices = lax.axis_size(axis)
    return lax.ppermute(array, axis, [(i, i ^ bit) for i in range(devices)])


def half_silu(half):
    return half + half * jnp.tanh(half)


def center_and_spread(values):
    center = values - jnp.mean(values, axis=-1, keepdims=True)
    return center, jnp.mean(center * center, axis=-1, keepdims=True)


def pack_kernel(list_ref, len_ref, from_ref, tgt_ref, to_ref, buffer, in_sems, out_sems):
    users, _, width = to_ref.shape
    length = from_ref.shape[1]
    copies_in = [
        pltpu.make_async_copy(from_ref.at[list_ref[k]], buffer.at[k, pl.ds(0, length)], in_sems.at[k])
        for k in range(users)
    ]
    copies_out = [pltpu.make_async_copy(buffer.at[k], to_ref.at[k], out_sems.at[k]) for k in range(users)]
    for copy in copies_in:
        copy.start()
    shape = (number_rows, length)
    for k in range(users):
        target = tgt_ref[pl.ds(list_ref[k], 1), :]
        digits = [jnp.full((1, length), len_ref[list_ref[k]], jnp.int32), target // 256, target % 256]
        lanes = [jnp.broadcast_to(digit.astype(jnp.float32), shape) for digit in digits]
        lanes += [jnp.zeros(shape, jnp.float32)] * (width // length - 3)
        buffer[k, length:, :] = jnp.concatenate(lanes, axis=1).astype(jnp.bfloat16)
    for k in range(users):
        copies_in[k].wait()
        copies_out[k].start()
    for copy in copies_out:
        copy.wait()


def pack(histories, lengths, targets, entries):
    users, length, width = histories.shape
    shape = (users, length + number_rows, width)
    return pl.pallas_call(
        pack_kernel,
        grid_spec=pltpu.PrefetchScalarGridSpec(
            num_scalar_prefetch=2,
            grid=(1,),
            in_specs=[
                pl.BlockSpec(memory_space=pl.ANY),
                pl.BlockSpec(targets.shape, lambda s, entries, lens: (0, 0)),
            ],
            out_specs=pl.BlockSpec(memory_space=pl.ANY),
            scratch_shapes=[
                pltpu.VMEM(shape, jnp.bfloat16),
                pltpu.SemaphoreType.DMA((users,)),
                pltpu.SemaphoreType.DMA((users,)),
            ],
        ),
        out_shape=jax.ShapeDtypeStruct(shape, jnp.bfloat16),
        compiler_params=pltpu.CompilerParams(vmem_limit_bytes=16 * 1024 * 1024),
        name="pack",
    )(entries, lengths, histories, targets)


def users_kernel(
    blocks, len_ref, block_ref, x_any, w_in_any, w_out_any, bias_in, unit_any,
    loss_ref, own_ref, over_ref, side_ref, far_ref,
    acc, bias, x_ref, w_in, w_out, unit_ref, exp_ref, residual, events, starts_ref, key, value,
    packed_tgt, packed_loss, x_sems, w_sems,
):
    step = pl.program_id(0)
    heads, length = bias_in.shape
    per_step, _, width = x_ref.shape
    hdim = width // heads
    items = unit_ref.shape[0] // blocks
    lines = tile // length

    x_copies = [
        pltpu.make_async_copy(x_any.at[step * per_step + u], x_ref.at[u], x_sems.at[u])
        for u in range(per_step)
    ]
    w_copies = [
        pltpu.make_async_copy(w_in_any, w_in, w_sems.at[0]),
        pltpu.make_async_copy(w_out_any, w_out, w_sems.at[1]),
        pltpu.make_async_copy(unit_any, unit_ref, w_sems.at[2]),
    ]
    for copy in x_copies:
        copy.start()

    @pl.when(step == 0)
    def _():
        for copy in w_copies:
            copy.start()
        acc[...] = jnp.zeros_like(acc)
        for h in range(heads):
            wide = jnp.broadcast_to(0.5 * bias_in[h : h + 1, :], (length, length))
            turned = pltpu.roll(wide, 0, 1, stride=1, stride_axis=0).T
            bias[h] = jnp.concatenate([turned, turned], axis=1)

    lens = [len_ref[step * per_step + u] for u in range(per_step)]
    starts, end = [], 0
    for u in range(per_step):
        starts.append(pl.multiple_of(end, chunk) if u else 0)
        end = end + (lens[u] + chunk - 1) // chunk * chunk
    end = pl.multiple_of(end, chunk)
    tiles = (end + tile - 1) // tile

    place = lax.broadcasted_iota(jnp.int32, (1, length), 1)
    packed_tgt[...] = jnp.full_like(packed_tgt, -1)
    key[:length, :] = jnp.zeros((length, width), key.dtype)
    value[:length, :] = jnp.zeros((length, width), value.dtype)
    for u in range(per_step):
        starts_ref[pl.ds(starts[u], length), :] = jnp.full((length, length), starts[u], jnp.int32)
    for copy in x_copies:
        copy.wait()
    for u in range(per_step):
        events[pl.ds(starts[u], length), :] = x_ref[u, :length, :]
        digits = x_ref[u, length:, :].astype(jnp.float32)
        target = digits[:1, length : 2 * length] * 256.0 + digits[:1, 2 * length : 3 * length]
        wanted = jnp.where(place < lens[u], target.astype(jnp.int32), -1)
        line, turn = starts[u] // length + 1, lax.rem(starts[u], length)
        turned = pltpu.roll(wanted, turn, 1)
        packed_tgt[pl.ds(line, 1), :] = jnp.where(place >= turn, turned, packed_tgt[pl.ds(line, 1), :])
        packed_tgt[pl.ds(line + 1, 1), :] = jnp.where(
            place < turn, turned, packed_tgt[pl.ds(line + 1, 1), :]
        )
    events[pl.ds(end, tile), :] = jnp.zeros((tile, width), events.dtype)

    @pl.when(step == 0)
    def _():
        for copy in w_copies:
            copy.wait()

    row = lax.broadcasted_iota(jnp.int32, (length, length), 0)
    col = lax.broadcasted_iota(jnp.int32, (length, length), 1)
    item_id = lax.broadcasted_iota(jnp.int32, (items, tile), 0)
    rate = logit_scale * math.log2(math.e)

    def one_tile(t, _):
        first = pl.multiple_of(t * tile, tile)
        x = events[pl.ds(first, tile), :].astype(jnp.float32)
        center, spread = center_and_spread(x)
        half_normed = (center * (0.5 * lax.rsqrt(spread + 1e-05))).astype(jnp.bfloat16)
        gate, values, query, keys = [
            half_silu(
                jnp.dot(
                    half_normed, w_in[:, part * width : (part + 1) * width],
                    preferred_element_type=jnp.float32,
                )
            ).astype(jnp.bfloat16)
            for part in range(4)
        ]
        key[pl.ds(first + length, tile), :] = keys
        value[pl.ds(first + length, tile), :] = values
        mixed = []
        for k in range(lines):
            base = pl.multiple_of(first + k * length, length)
            sources = pl.ds(base, 2 * length)
            start = starts_ref[pl.ds(base, length), :]
            ahead = packed_tgt[pl.ds(t * lines + k, 1), :] >= 0
            here = packed_tgt[pl.ds(t * lines + k + 1, 1), :] >= 0
            keep_ahead = (base - length + col >= start) & ahead
            keep_here = (col <= row) & (base + col >= start) & here
            keep = jnp.concatenate([keep_ahead, keep_here], axis=1)
            by_head = []
            for h in range(heads):
                cols = slice(h * hdim, (h + 1) * hdim)
                scores = lax.dot_general(
                    query[k * length : (k + 1) * length, cols], key[sources, cols], contract_last,
                    preferred_element_type=jnp.float32,
                )
                attn = half_silu(scores * (0.5 / math.sqrt(hdim)) + bias[h])
                attn = jnp.where(keep, attn, 0.0).astype(jnp.bfloat16)
                by_head.append(jnp.dot(attn, value[sources, cols], preferred_element_type=jnp.float32))
            mixed.append(jnp.concatenate(by_head, axis=1))
        center, spread = center_and_spread(jnp.concatenate(mixed, axis=0))
        normed = center * lax.rsqrt(spread + 1e-05)
        gated = (normed * gate.astype(jnp.float32)).astype(jnp.bfloat16)
        out = x + jnp.dot(gated, w_out[...], preferred_element_type=jnp.float32)
        out = out.astype(jnp.bfloat16).astype(jnp.float32)
        square = jnp.sum(out * out, axis=-1, keepdims=True)
        queries = (out * lax.rsqrt(square + 1e-06)).astype(jnp.bfloat16)

        target = jnp.concatenate(
            [packed_tgt[pl.ds(t * lines + k + 1, 1), :] for k in range(lines)], axis=1
        )
        dots = lax.dot_general(
            unit_ref[...], queries, contract_last, preferred_element_type=jnp.float32
        )
        total = jnp.zeros((1, tile), jnp.float32)
        target_dot = jnp.zeros((1, tile), jnp.float32)
        for j in range(blocks):
            part = dots[j * items : (j + 1) * items]
            exps = jnp.exp2(part * rate - rate)
            exp_ref[j] = exps
            total += jnp.sum(exps, axis=0, keepdims=True)
            hit = item_id == target - j * items
            target_dot += jnp.sum(jnp.where(hit, part, 0.0), axis=0, keepdims=True)
        loss = logit_scale + jnp.log(total) - logit_scale * target_dot
        for k in range(lines):
            packed_loss[pl.ds(t * lines + k, 1), :] = loss[:, k * length : (k + 1) * length]
        share = jnp.where(target >= 0, 1.0 / total, 0.0)
        for j in range(blocks):
            hit = item_id == target - j * items
            left = exp_ref[j] * share - jnp.where(hit, 1.0, 0.0)
            residual[j * items : (j + 1) * items, :] = left.astype(jnp.bfloat16)
        acc[...] += jnp.dot(residual[...], queries, preferred_element_type=jnp.float32)
        return 0

    lax.fori_loop(0, tiles, one_tile, 0)

    for u in range(per_step):
        line, turn = starts[u] // length, lax.rem(starts[u], length)
        back = lax.rem(length - turn, length)
        near = pltpu.roll(packed_loss[pl.ds(line, 1), :], back, 1)
        rest = pltpu.roll(packed_loss[pl.ds(line + 1, 1), :], back, 1)
        loss = jnp.where(place < length - turn, near, rest)
        loss_ref[pl.ds(step * per_step + u, 1), :] = jnp.where(place < lens[u], loss, 0.0)

    @pl.when(step == pl.num_programs(0) - 1)
    def _():
        for k, out_ref in enumerate((own_ref, over_ref, side_ref, far_ref)):
            rows = pl.ds(pl.multiple_of(block_ref[k] * items, items), items)
            out_ref[...] = acc[rows, :].astype(out_ref.dtype)


def users_call(packed, lens, w_in, w_out, rel_bias, unit_all, block_ids):
    users, packed_rows, width = packed.shape
    heads, length = rel_bias.shape
    blocks = block_ids.shape[0]
    items = unit_all.shape[0] // blocks
    per_step = math.gcd(users, 8)
    rows = per_step * length
    lines = -(-(rows // length + 2) // 8) * 8
    whole = lambda *shape: pl.BlockSpec(shape, lambda s, lens, ids: (0,) * len(shape))
    anywhere = pl.BlockSpec(memory_space=pl.ANY)
    part = lambda dtype: jax.ShapeDtypeStruct((items, width), dtype)
    return pl.pallas_call(
        functools.partial(users_kernel, blocks),
        grid_spec=pltpu.PrefetchScalarGridSpec(
            num_scalar_prefetch=2,
            grid=(users // per_step,),
            in_specs=[anywhere, anywhere, anywhere, whole(heads, length), anywhere],
            out_specs=[whole(users, length)] + [whole(items, width)] * 4,
            scratch_shapes=[
                pltpu.VMEM((blocks * items, width), jnp.float32),
                pltpu.VMEM((heads, length, 2 * length), jnp.float32),
                pltpu.VMEM((per_step, packed_rows, width), jnp.bfloat16),
                pltpu.VMEM(w_in.shape, jnp.bfloat16),
                pltpu.VMEM(w_out.shape, jnp.bfloat16),
                pltpu.VMEM(unit_all.shape, jnp.bfloat16),
                pltpu.VMEM((blocks, items, tile), jnp.float32),
                pltpu.VMEM((blocks * items, tile), jnp.bfloat16),
                pltpu.VMEM((rows + tile, width), jnp.bfloat16),
                pltpu.VMEM((rows + tile, length), jnp.int32),
                pltpu.VMEM((length + rows + tile, width), jnp.bfloat16),
                pltpu.VMEM((length + rows + tile, width), jnp.bfloat16),
                pltpu.VMEM((lines, length), jnp.int32),
                pltpu.VMEM((lines, length), jnp.float32),
                pltpu.SemaphoreType.DMA((per_step,)),
                pltpu.SemaphoreType.DMA((3,)),
            ],
        ),
        out_shape=[
            jax.ShapeDtypeStruct((users, length), jnp.float32),
            part(jnp.float32),
            part(jnp.float32),
            part(jnp.bfloat16),
            part(jnp.bfloat16),
        ],
        compiler_params=pltpu.CompilerParams(vmem_limit_bytes=36 * 1024 * 1024),
        name="users",
    )(lens, block_ids, packed, w_in, w_out, rel_bias, unit_all)


def shards(histories, lengths, targets, send_list, w_in, w_out, rel_bias, item_pool):
    length = histories.shape[1]
    packed = pack(histories, lengths, targets, send_list)
    packed = lax.all_to_all(packed, "dp", split_axis=0, concat_axis=0, tiled=True)

    pool_float = item_pool.astype(jnp.float32)
    item_norm = jnp.sqrt(jnp.sum(pool_float * pool_float, axis=-1, keepdims=True) + 1e-06)
    unit_rows = pool_float / item_norm
    unit_all = lax.all_gather(unit_rows.astype(jnp.bfloat16), "blk", axis=0, tiled=True)

    mine = lax.axis_index("blk")
    block_ids = jnp.stack([mine, mine ^ 2, mine ^ 1, mine ^ 3]).astype(jnp.int32)
    lens = packed[:, length, 0].astype(jnp.int32)
    row_loss, own, over, side, far = users_call(packed, lens, w_in, w_out, rel_bias, unit_all, block_ids)
    over = over + swap(far, "blk", 1).astype(jnp.float32)
    own = own + swap(side, "blk", 1).astype(jnp.float32)
    item_sum = logit_scale * (own + swap(over.astype(jnp.bfloat16), "blk", 2).astype(jnp.float32))
    pool_grad = (
        item_sum - unit_rows * jnp.sum(unit_rows * item_sum, axis=-1, keepdims=True)
    ) / item_norm
    return (row_loss, pool_grad)


def solution(mesh):
    placed = (
        P(("dp", "blk"), None, None),
        P(("dp", "blk")),
        P(("dp", "blk"), None),
        P(("dp", "blk")),
        P(),
        P(),
        P(),
        P(("dp", "blk"), None),
    )
    return jax.shard_map(
        shards,
        mesh=mesh,
        in_specs=placed,
        out_specs=(P(("dp", "blk"), None), P(("dp", "blk"), None)),
        check_vma=False,
    )
```

time: 111 us -> 79.8 us (0.72)
  Pallas kernels: 46.8 us -> 13.6 us
  waiting for transfers between devices: 24 us -> 33.9 us
  starting transfers between devices: 18.8 us -> 9.58 us
  local copies, waits for them, and re-layouts: 3.79 us -> 5.49 us
    pallas_call x2, Pallas kernels: 46.8 us -> 13.6 us  [the longest x1 10.6 us: users_call(): pl.pallas_call(functools.partial(users_kernel, blocks), grid_spec=pltpu.P...]
    all_to_all x1, waiting for transfers between devices: 0.01 us -> 26 us  [shards(): lax.all_to_all(packed, 'dp', split_axis=0, concat_axis=0, tiled=True)]
    ppermute x6 -> x3, waiting for transfers between devices: 24 us -> 7.85 us  [swap(): return lax.ppermute(array, axis, [(i, i ^ bit) for i in range(devices)])]
    ppermute x6 -> x3, starting transfers between devices: 11.4 us -> 2.15 us  [swap(): return lax.ppermute(array, axis, [(i, i ^ bit) for i in range(devices)])]
    unnamed x12 -> x18, local copies, waits for them, and re-layouts: 2.28 us -> 5.49 us
  transfers between devices with their start and end apart: 8 -> 5, of which waited for: 5 -> 3; matrix products, arithmetic and copies ran while one was open for 2% -> 2% of each run, Pallas kernels for 0% -> 0%
where the time goes in v4:
time: 79.8 us; the launch traced here: 79.4 us
  waiting for transfers between devices  33.9 us (42%)
  between operations  14.1 us (18%)
  Pallas kernels  13.6 us (17%)
  starting transfers between devices  9.58 us (12%)
  local copies, waits for them, and re-layouts  5.49 us (7%)
  other arithmetic  2.65 us (3%)
    all_to_all x1, waiting for transfers between devices, shards(): lax.all_to_all(packed, 'dp', split_axis=0, concat_axis=0, tiled=True)  26 us
    pallas_call x1, Pallas kernels, users_call(): pl.pallas_call(functools.partial(users_kernel, blocks), grid_spec=pltpu.P...  10.6 us
    ppermute x3, waiting for transfers between devices, swap(): return lax.ppermute(array, axis, [(i, i ^ bit) for i in range(devices)])  7.85 us
    all_to_all x1, starting transfers between devices, shards(): lax.all_to_all(packed, 'dp', split_axis=0, concat_axis=0, tiled=True)  7.4 us
    unnamed x18, local copies, waits for them, and re-layouts  5.49 us
    pallas_call x1, Pallas kernels, pack(): pl.pallas_call(pack_kernel, grid_spec=pltpu.PrefetchScalarGridSpec(num_sc...  3.07 us
    ppermute x3, starting transfers between devices, swap(): return lax.ppermute(array, axis, [(i, i ^ bit) for i in range(devices)])  2.15 us
  transfers between devices with their start and end apart: 5, of which 3 were waited for; matrix products, arithmetic and copies ran while one was open for 2% of the time, Pallas kernels for 0%

profile of v4, /device:TPU:0, one launch (start us, length us, event | category | flops | bytes accessed | tf_op | source)
XLA Modules:
  0.0 79.4 jit_solution(17394647368229137293)
XLA Ops:
  7.2 0.0 copy-start.2
  7.2 1.2 %copy-done.2 = bf16[8,128,512]{2,1,0:T(8,128)(2,1)S(1)} copy-done((bf16[8,128,512]{2,1,0:T(8,128)(2,1)S(1)}, bf16[8,128,512]{2,1,0:T(8,128)(2,1)}, u32[]{:S(2)}) %copy-start.2) | copy-done | bytes 1048600
  8.4 0.0 copy-start.4
  8.4 0.7 copy-done.4
  9.1 0.0 copy-start.6
  9.1 0.7 copy-done.6
  9.7 0.0 copy-start.7
  9.7 0.7 copy-done.7
  10.4 0.0 copy-start.8
  10.4 3.1 %pack.1 = bf16[8,136,512]{2,1,0:T(8,128)(2,1)} custom-call(s32[8]{0:T(128)S(1)} %copy-done.6, s32[8]{0:T(128)S(1)} %copy-done.7, bf16[8,128,512]{2,1,0:T(8,128)(2,1)S(1)} %copy-done.2, s32[8,128]{1,0:T(8,128)S(1)} %copy-done.4), custom_call_target="tpu_custom_call" | custom-call | tf_op jit(solution)/shard_map/pack/pallas_call | solution.py:59
  13.5 0.0 copy-start
  13.5 0.0 copy-start.5
  13.5 7.4 %all-to-all-start = ((bf16[8,136,512]{2,1,0:T(8,128)(2,1)}), bf16[8,136,512]{2,1,0:T(8,128)(2,1)S(1)}, u32[]{:S(2)}, u32[]{:S(2)}) async-start(bf16[8,136,512]{2,1,0:T(8,128)(2,1)} %pack.1), calls=%async_computation | async-start | bytes 2228224 | tf_op jit(solution)/shard_map/all_to_all | solution.py:295
  20.9 0.0 all-gather.2.cloned.1.call-start
  20.9 0.0 copy-done.8
  20.9 0.1 fusion
  21.1 0.8 %fusion.2 = bf16[256,512]{1,0:T(8,128)(2,1)} fusion(f32[256]{0:T(256)S(1)} %add_sqrt_fusion, bf16[256,512]{1,0:T(8,128)(2,1)S(1)} %copy-done.8), kind=kLoop, calls=%fused_computation.11 | loop fusion | flops 393216 | bytes 525312 | tf_op jit(solution)/shard_map/convert_element_type | solution.py:300
  21.9 0.0 all-gather.2.cloned.1.call-update
  21.9 0.1 pad_add_fusion.block_ref
  22.0 26.0 %all-to-all-done.x_any = bf16[8,136,512]{2,1,0:T(8,128)(2,1)S(1)} async-done(((bf16[8,136,512]{2,1,0:T(8,128)(2,1)}), bf16[8,136,512]{2,1,0:T(8,128)(2,1)S(1)}, u32[]{:S(2)}, u32[]{:S(2)}) %all-to-all-start) | async-done | bytes 1114144 | tf_op jit(solution)/shard_map/all_to_all | solution.py:295
  48.1 0.2 fusion.1.len_ref
  48.3 0.0 all-gather.2.cloned.1.call-done.unit_any
  48.3 0.0 copy-done
  48.3 0.0 copy-done.5
  48.3 0.0 copy-start.1
  48.4 1.2 %copy-done.1 = bf16[1024,512]{1,0:T(8,128)(2,1)S(1)} copy-done((bf16[1024,512]{1,0:T(8,128)(2,1)S(1)}, bf16[1024,512]{1,0:T(8,128)(2,1)}, u32[]{:S(2)}) %copy-start.1) | copy-done | bytes 1048600
  49.6 0.0 copy-start.3
  49.6 1.0 %copy-done.3 = bf16[512,512]{1,0:T(8,128)(2,1)S(1)} copy-done((bf16[512,512]{1,0:T(8,128)(2,1)S(1)}, bf16[512,512]{1,0:T(8,128)(2,1)}, u32[]{:S(2)}) %copy-start.3) | copy-done | bytes 524312
  50.6 10.6 %users.1 = (f32[8,128]{1,0:T(8,128)}, f32[256,512]{1,0:T(8,128)S(1)}, f32[256,512]{1,0:T(8,128)S(1)}, bf16[256,512]{1,0:T(8,128)(2,1)S(1)}, bf16[256,512]{1,0:T(8,128)(2,1)S(1)}) custom-call(s32[8]{0:T(128)S(1)} %fusion.1.len_ref, s32[4]{0:T(128)S(1)} %pad_add_fusion.block_ref, bf16[8,136,512]{2,1,0:T(8,128)(2,1)S(1)} %all-to-all-done.x_any, ...), custom_call_target="tpu_custom_call" | custom-call | tf_op jit(solution)/shard_map/users/pallas_call | solution.py:254
  61.2 0.1 collective-permute-start.1
  61.3 0.5 collective-permute-start
  61.8 1.0 %collective-permute-done.1 = bf16[256,512]{1,0:T(8,128)(2,1)S(1)} collective-permute-done((bf16[256,512]{1,0:T(8,128)(2,1)S(1)}, bf16[256,512]{1,0:T(8,128)(2,1)S(1)}, u32[]{:S(2)}, u32[]{:S(2)}) %collective-permute-start.1) | collective-permute-done | bytes 262176 | tf_op jit(solution)/shard_map/ppermute | solution.py:20
  62.8 0.1 add_convert_fusion
  62.9 1.6 %collective-permute-start.2 = (bf16[256,512]{1,0:T(8,128)(2,1)S(1)}, bf16[256,512]{1,0:T(8,128)(2,1)S(1)}, u32[]{:S(2)}, u32[]{:S(2)}) collective-permute-start(bf16[256,512]{1,0:T(8,128)(2,1)S(1)} %add_convert_fusion), channel_id=1, source_target_pairs={{0,2},{1,3},{2,0},{3,1},{4,6},{5,7},{6,4},{7,5},{8,10},{9,11},{10,... | collective-permute-start | bytes 786440 | tf_op jit(solution)/shard_map/ppermute | solution.py:20
  64.4 0.0 collective-permute-done
  64.4 6.8 %collective-permute-done.2 = bf16[256,512]{1,0:T(8,128)(2,1)S(1)} collective-permute-done((bf16[256,512]{1,0:T(8,128)(2,1)S(1)}, bf16[256,512]{1,0:T(8,128)(2,1)S(1)}, u32[]{:S(2)}, u32[]{:S(2)}) %collective-permute-start.2) | collective-permute-done | bytes 262176 | tf_op jit(solution)/shard_map/ppermute | solution.py:20
  71.3 0.3 multiply_reduce_fusion
  71.5 1.0 %subtract_divide_fusion = f32[256,512]{1,0:T(8,128)} fusion(f32[256]{0:T(256)S(1)} %multiply_reduce_fusion, f32[256]{0:T(256)S(1)} %add_sqrt_fusion, bf16[256,512]{1,0:T(8,128)(2,1)S(1)} %collective-permute-done.2, f32[256,512]{1,0:T(8,128)S(1)} %get-tuple-element.8, bf16[256,512]{1,0:T(8,128)(2,1)S(1)} %collective-permute-done, bf16[256,512]{1,0:T(8,128)(2,1)S(1)} %copy-done.8), kind=kLoop, calls=%fused_computation.3 | loop fusion | flops 1310720 | bytes 1837056 | tf_op jit(solution)/shard_map/div | solution.py:309
  (1 shorter events, 0.0 us)
Async XLA Ops:
  7.2 1.2 %copy-start.2 = (bf16[8,128,512]{2,1,0:T(8,128)(2,1)S(1)}, bf16[8,128,512]{2,1,0:T(8,128)(2,1)}, u32[]{:S(2)}) copy-start(bf16[8,128,512]{2,1,0:T(8,128)(2,1)} %from_ref.1) | copy-start | bytes 3145732
  8.4 0.7 copy-start.4
  9.1 0.7 copy-start.6
  9.7 0.7 copy-start.7
  10.4 10.5 %copy-start.8 = (bf16[256,512]{1,0:T(8,128)(2,1)S(1)}, bf16[256,512]{1,0:T(8,128)(2,1)}, u32[]{:S(2)}) copy-start(bf16[256,512]{1,0:T(8,128)(2,1)} %param.15) | copy-start | bytes 786436
  13.5 34.9 %copy-start = (bf16[512,2048]{1,0:T(8,128)(2,1)S(1)}, bf16[512,2048]{1,0:T(8,128)(2,1)}, u32[]{:S(2)}) copy-start(bf16[512,2048]{1,0:T(8,128)(2,1)} %w_in_any.1) | copy-start | bytes 6291460
  13.5 34.9 %copy-start.5 = (f32[4,128]{1,0:T(4,128)S(1)}, f32[4,128]{1,0:T(4,128)}, u32[]{:S(2)}) copy-start(f32[4,128]{1,0:T(4,128)} %bias_in.1) | copy-start | bytes 6148
  13.5 34.6 %all-to-all-start = ((bf16[8,136,512]{2,1,0:T(8,128)(2,1)}), bf16[8,136,512]{2,1,0:T(8,128)(2,1)S(1)}, u32[]{:S(2)}, u32[]{:S(2)}) async-start(bf16[8,136,512]{2,1,0:T(8,128)(2,1)} %pack.1), calls=%async_computation | async-start | bytes 2228224 | tf_op jit(solution)/shard_map/all_to_all | solution.py:295
  20.9 27.4 %all-gather.2.cloned.1.call-start = ((), (), s32[]{:S(2)}) async-start(), calls=%async_computation.1 | async-start | bytes 1310720 | tf_op jit(solution)/shard_map/all_gather | solution.py:300
  48.3 1.2 %copy-start.1 = (bf16[1024,512]{1,0:T(8,128)(2,1)S(1)}, bf16[1024,512]{1,0:T(8,128)(2,1)}, u32[]{:S(2)}) copy-start(bf16[1024,512]{1,0:T(8,128)(2,1)} %all-gather.2.cloned.1.call-done.unit_any) | copy-start | bytes 3145732
  49.6 1.0 %copy-start.3 = (bf16[512,512]{1,0:T(8,128)(2,1)S(1)}, bf16[512,512]{1,0:T(8,128)(2,1)}, u32[]{:S(2)}) copy-start(bf16[512,512]{1,0:T(8,128)(2,1)} %w_out_any.1) | copy-start | bytes 1572868
  61.2 1.6 %collective-permute-start.1 = (bf16[256,512]{1,0:T(8,128)(2,1)S(1)}, bf16[256,512]{1,0:T(8,128)(2,1)S(1)}, u32[]{:S(2)}, u32[]{:S(2)}) collective-permute-start(bf16[256,512]{1,0:T(8,128)(2,1)S(1)} %get-tuple-element.11), channel_id=1, source_target_pairs={{0,1},{1,0},{2,3},{3,2},{4,5},{5,4},{6,7},{7,6},{8,9},{9,8},{10,11... | collective-permute-start | bytes 786440 | tf_op jit(solution)/shard_map/ppermute | solution.py:20
  61.3 3.2 %collective-permute-start = (bf16[256,512]{1,0:T(8,128)(2,1)S(1)}, bf16[256,512]{1,0:T(8,128)(2,1)S(1)}, u32[]{:S(2)}, u32[]{:S(2)}) collective-permute-start(bf16[256,512]{1,0:T(8,128)(2,1)S(1)} %get-tuple-element.9), channel_id=1, source_target_pairs={{0,1},{1,0},{2,3},{3,2},{4,5},{5,4},{6,7},{7,6},{8,9},{9,8},{10,11... | collective-permute-start | bytes 786440 | tf_op jit(solution)/shard_map/ppermute | solution.py:20
  62.9 8.4 %collective-permute-start.2 = (bf16[256,512]{1,0:T(8,128)(2,1)S(1)}, bf16[256,512]{1,0:T(8,128)(2,1)S(1)}, u32[]{:S(2)}, u32[]{:S(2)}) collective-permute-start(bf16[256,512]{1,0:T(8,128)(2,1)S(1)} %add_convert_fusion), channel_id=1, source_target_pairs={{0,2},{1,3},{2,0},{3,1},{4,6},{5,7},{6,4},{7,5},{8,10},{9,11},{10,... | collective-permute-start | bytes 786440 | tf_op jit(solution)/shard_map/ppermute | solution.py:20
Sparse Core Ops, SparseCore 0:
  23.9 18.1 all-gather.1

commit v5 on v4

--- a/solution.py
+++ b/solution.py
@@ -20,6 +20,10 @@
     return lax.ppermute(array, axis, [(i, i ^ bit) for i in range(devices)])
 
 
+def in_hbm(array):
+    return pltpu.with_memory_space_constraint(array, pltpu.HBM)
+
+
 def half_silu(half):
     return half + half * jnp.tanh(half)
 
@@ -29,53 +33,83 @@
     return center, jnp.mean(center * center, axis=-1, keepdims=True)
 
 
-def pack_kernel(list_ref, len_ref, from_ref, tgt_ref, to_ref, buffer, in_sems, out_sems):
-    users, _, width = to_ref.shape
-    length = from_ref.shape[1]
+def pack_kernel(
+    list_any, len_any, from_any, tgt_any, pool_any, to_any, unit_any,
+    entries, lens, targets, pool, unit, buffer, sems, in_sems, out_sems,
+):
+    users = buffer.shape[0]
+    _, length, width = from_any.shape
+    pieces = width // length
+    small = [
+        pltpu.make_async_copy(source, target, sems.at[k])
+        for k, (source, target) in enumerate(
+            ((list_any, entries), (len_any, lens), (tgt_any, targets), (pool_any, pool))
+        )
+    ]
+    for copy in small:
+        copy.start()
+    small[0].wait()
     copies_in = [
-        pltpu.make_async_copy(from_ref.at[list_ref[k]], buffer.at[k, pl.ds(0, length)], in_sems.at[k])
+        [
+            pltpu.make_async_copy(
+                from_any.at[entries[k], :, pl.ds(c * length, length)],
+                buffer.at[k, pl.ds(c * length, length)],
+                in_sems.at[k, c],
+            )
+            for c in range(pieces)
+        ]
         for k in range(users)
     ]
-    copies_out = [pltpu.make_async_copy(buffer.at[k], to_ref.at[k], out_sems.at[k]) for k in range(users)]
-    for copy in copies_in:
-        copy.start()
-    shape = (number_rows, length)
+    for copies in copies_in:
+        for copy in copies:
+            copy.start()
+    small[3].wait()
+    rows = pool[...].astype(jnp.float32)
+    unit[...] = (rows * lax.rsqrt(jnp.sum(rows * rows, axis=-1, keepdims=True) + 1e-06)).astype(jnp.bfloat16)
+    unit_out = pltpu.make_async_copy(unit, unit_any, sems.at[4])
+    unit_out.start()
+    small[1].wait()
+    small[2].wait()
+    row = lax.broadcasted_iota(jnp.int32, (number_rows, length), 0)
     for k in range(users):
-        target = tgt_ref[pl.ds(list_ref[k], 1), :]
-        digits = [jnp.full((1, length), len_ref[list_ref[k]], jnp.int32), target // 256, target % 256]
-        lanes = [jnp.broadcast_to(digit.astype(jnp.float32), shape) for digit in digits]
-        lanes += [jnp.zeros(shape, jnp.float32)] * (width // length - 3)
-        buffer[k, length:, :] = jnp.concatenate(lanes, axis=1).astype(jnp.bfloat16)
+        target = targets[pl.ds(entries[k], 1), :]
+        numbers = jnp.where(row == 0, lens[entries[k]], jnp.where(row == 1, target // 256, target % 256))
+        buffer[k, width:, :] = numbers.astype(jnp.float32).astype(jnp.bfloat16)
+    copies_out = [pltpu.make_async_copy(buffer.at[k], to_any.at[k], out_sems.at[k]) for k in range(users)]
     for k in range(users):
-        copies_in[k].wait()
+        for copy in copies_in[k]:
+            copy.wait()
         copies_out[k].start()
+    unit_out.wait()
     for copy in copies_out:
         copy.wait()
 
 
-def pack(histories, lengths, targets, entries):
+def pack(histories, lengths, targets, entries, item_pool):
     users, length, width = histories.shape
-    shape = (users, length + number_rows, width)
+    shape = (users, width + number_rows, length)
     return pl.pallas_call(
         pack_kernel,
-        grid_spec=pltpu.PrefetchScalarGridSpec(
-            num_scalar_prefetch=2,
-            grid=(1,),
-            in_specs=[
-                pl.BlockSpec(memory_space=pl.ANY),
-                pl.BlockSpec(targets.shape, lambda s, entries, lens: (0, 0)),
-            ],
-            out_specs=pl.BlockSpec(memory_space=pl.ANY),
-            scratch_shapes=[
-                pltpu.VMEM(shape, jnp.bfloat16),
-                pltpu.SemaphoreType.DMA((users,)),
-                pltpu.SemaphoreType.DMA((users,)),
-            ],
-        ),
-        out_shape=jax.ShapeDtypeStruct(shape, jnp.bfloat16),
+        in_specs=[pl.BlockSpec(memory_space=pltpu.HBM)] * 5,
+        out_specs=[pl.BlockSpec(memory_space=pltpu.HBM)] * 2,
+        scratch_shapes=[
+            pltpu.SMEM(entries.shape, jnp.int32),
+            pltpu.SMEM(lengths.shape, jnp.int32),
+            pltpu.VMEM(targets.shape, jnp.int32),
+            pltpu.VMEM(item_pool.shape, jnp.bfloat16),
+            pltpu.VMEM(item_pool.shape, jnp.bfloat16),
+            pltpu.VMEM(shape, jnp.bfloat16),
+            pltpu.SemaphoreType.DMA((5,)),
+            pltpu.SemaphoreType.DMA((users, width // length)),
+            pltpu.SemaphoreType.DMA((users,)),
+        ],
+        out_shape=[
+            jax.ShapeDtypeStruct(shape, jnp.bfloat16),
+            jax.ShapeDtypeStruct(item_pool.shape, jnp.bfloat16),
+        ],
         compiler_params=pltpu.CompilerParams(vmem_limit_bytes=16 * 1024 * 1024),
         name="pack",
-    )(entries, lengths, histories, targets)
+    )(*[in_hbm(array) for array in (entries, lengths, histories, targets, item_pool)])
 
 
 def users_kernel(
@@ -86,7 +120,8 @@
 ):
     step = pl.program_id(0)
     heads, length = bias_in.shape
-    per_step, _, width = x_ref.shape
+    per_step = x_ref.shape[0]
+    width = w_out.shape[0]
     hdim = width // heads
     items = unit_ref.shape[0] // blocks
     lines = tile // length
@@ -130,9 +165,10 @@
     for copy in x_copies:
         copy.wait()
     for u in range(per_step):
-        events[pl.ds(starts[u], length), :] = x_ref[u, :length, :]
-        digits = x_ref[u, length:, :].astype(jnp.float32)
-        target = digits[:1, length : 2 * length] * 256.0 + digits[:1, 2 * length : 3 * length]
+        for c in range(0, width, length):
+            events[pl.ds(starts[u], length), c : c + length] = x_ref[u, c : c + length, :]
+        digits = x_ref[u, width:, :].astype(jnp.float32)
+        target = digits[1:2, :] * 256.0 + digits[2:3, :]
         wanted = jnp.where(place < lens[u], target.astype(jnp.int32), -1)
         line, turn = starts[u] // length + 1, lax.rem(starts[u], length)
         turned = pltpu.roll(wanted, turn, 1)
@@ -241,27 +277,27 @@
 
 
 def users_call(packed, lens, w_in, w_out, rel_bias, unit_all, block_ids):
-    users, packed_rows, width = packed.shape
-    heads, length = rel_bias.shape
+    users, packed_rows, length = packed.shape
+    heads, width = rel_bias.shape[0], w_out.shape[0]
     blocks = block_ids.shape[0]
     items = unit_all.shape[0] // blocks
     per_step = math.gcd(users, 8)
     rows = per_step * length
     lines = -(-(rows // length + 2) // 8) * 8
     whole = lambda *shape: pl.BlockSpec(shape, lambda s, lens, ids: (0,) * len(shape))
-    anywhere = pl.BlockSpec(memory_space=pl.ANY)
+    anywhere, hbm = pl.BlockSpec(memory_space=pl.ANY), pl.BlockSpec(memory_space=pltpu.HBM)
     part = lambda dtype: jax.ShapeDtypeStruct((items, width), dtype)
     return pl.pallas_call(
         functools.partial(users_kernel, blocks),
         grid_spec=pltpu.PrefetchScalarGridSpec(
             num_scalar_prefetch=2,
             grid=(users // per_step,),
-            in_specs=[anywhere, anywhere, anywhere, whole(heads, length), anywhere],
+            in_specs=[anywhere, anywhere, hbm, whole(heads, length), hbm],
             out_specs=[whole(users, length)] + [whole(items, width)] * 4,
             scratch_shapes=[
                 pltpu.VMEM((blocks * items, width), jnp.float32),
                 pltpu.VMEM((heads, length, 2 * length), jnp.float32),
-                pltpu.VMEM((per_step, packed_rows, width), jnp.bfloat16),
+                pltpu.VMEM((per_step, packed_rows, length), jnp.bfloat16),
                 pltpu.VMEM(w_in.shape, jnp.bfloat16),
                 pltpu.VMEM(w_out.shape, jnp.bfloat16),
                 pltpu.VMEM(unit_all.shape, jnp.bfloat16),
@@ -286,22 +322,21 @@
         ],
         compiler_params=pltpu.CompilerParams(vmem_limit_bytes=36 * 1024 * 1024),
         name="users",
-    )(lens, block_ids, packed, w_in, w_out, rel_bias, unit_all)
+    )(lens, block_ids, packed, w_in, in_hbm(w_out), rel_bias, in_hbm(unit_all))
 
 
 def shards(histories, lengths, targets, send_list, w_in, w_out, rel_bias, item_pool):
-    length = histories.shape[1]
-    packed = pack(histories, lengths, targets, send_list)
+    packed, unit_bf = pack(histories, lengths, targets, send_list, item_pool)
     packed = lax.all_to_all(packed, "dp", split_axis=0, concat_axis=0, tiled=True)
+    unit_all = lax.all_gather(unit_bf, "blk", axis=0, tiled=True)
 
     pool_float = item_pool.astype(jnp.float32)
     item_norm = jnp.sqrt(jnp.sum(pool_float * pool_float, axis=-1, keepdims=True) + 1e-06)
     unit_rows = pool_float / item_norm
-    unit_all = lax.all_gather(unit_rows.astype(jnp.bfloat16), "blk", axis=0, tiled=True)
 
     mine = lax.axis_index("blk")
     block_ids = jnp.stack([mine, mine ^ 2, mine ^ 1, mine ^ 3]).astype(jnp.int32)
-    lens = packed[:, length, 0].astype(jnp.int32)
+    lens = packed[:, histories.shape[2], 0].astype(jnp.int32)
     row_loss, own, over, side, far = users_call(packed, lens, w_in, w_out, rel_bias, unit_all, block_ids)
     over = over + swap(far, "blk", 1).astype(jnp.float32)
     own = own + swap(side, "blk", 1).astype(jnp.float32)

time: 79.8 us -> 74.9 us (0.939)
  local copies, waits for them, and re-layouts: 5.49 us -> 0.98 us
  starting transfers between devices: 9.58 us -> 13 us
  Pallas kernels: 13.6 us -> 11.1 us
  other arithmetic: 2.65 us -> 1.78 us
    unnamed x18 -> x8, local copies, waits for them, and re-layouts: 5.49 us -> 0.98 us
    ppermute x3, starting transfers between devices: 2.15 us -> 5.61 us  [swap(): return lax.ppermute(array, axis, [(i, i ^ bit) for i in range(devices)])]
    pallas_call x1, Pallas kernels: 10.6 us -> 7.81 us  [users_call(): pl.pallas_call(functools.partial(users_kernel, blocks), grid_spec=pltpu.P...]
    convert_element_type x2 -> x1, other arithmetic: 1.07 us -> 0.24 us  [shards(): lens = packed[:, histories.shape[2], 0].astype(jnp.int32)]
  transfers between devices with their start and end apart: 5 -> 5, of which waited for: 3 -> 3; matrix products, arithmetic and copies ran while one was open for 2% -> 1% of each run, Pallas kernels for 0% -> 0%
where the time goes in v5:
time: 74.9 us; the launch traced here: 74.5 us
  waiting for transfers between devices  33.5 us (45%)
  between operations  14.1 us (19%)
  starting transfers between devices  13 us (17%)
  Pallas kernels  11.1 us (15%)
  other arithmetic  1.78 us (2%)
  local copies, waits for them, and re-layouts  0.98 us (1%)
    all_to_all x1, waiting for transfers between devices, shards(): lax.all_to_all(packed, 'dp', split_axis=0, concat_axis=0, tiled=True)  25.3 us
    pallas_call x1, Pallas kernels, users_call(): pl.pallas_call(functools.partial(users_kernel, blocks), grid_spec=pltpu.P...  7.81 us
    ppermute x3, waiting for transfers between devices, swap(): return lax.ppermute(array, axis, [(i, i ^ bit) for i in range(devices)])  7.54 us
    all_to_all x1, starting transfers between devices, shards(): lax.all_to_all(packed, 'dp', split_axis=0, concat_axis=0, tiled=True)  7.38 us
    ppermute x3, starting transfers between devices, swap(): return lax.ppermute(array, axis, [(i, i ^ bit) for i in range(devices)])  5.61 us
    pallas_call x1, Pallas kernels, pack(): pl.pallas_call(pack_kernel, in_specs=[pl.BlockSpec(memory_space=pltpu.HBM...  3.25 us
  transfers between devices with their start and end apart: 5, of which 3 were waited for; matrix products, arithmetic and copies ran while one was open for 1% of the time, Pallas kernels for 0%

profile of v5, /device:TPU:0, one launch (start us, length us, event | category | flops | bytes accessed | tf_op | source)
XLA Modules:
  0.0 74.5 jit_solution(4004435206804636899)
XLA Ops:
  7.2 3.2 %pack.1 = (bf16[8,520,128]{2,1,0:T(8,128)(2,1)S(1)}, bf16[256,512]{1,0:T(8,128)(2,1)}) custom-call(s32[8]{0:T(128)} %list_any.1, s32[8]{0:T(128)} %len_any.1, bf16[8,128,512]{2,1,0:T(8,128)(2,1)} %from_any.1, s32[8,128]{1,0:T(8,128)} %tgt_any.1, bf16[256,512]{1,0:T(8,128)(2,1)} %pool_any.1), custom_call_target="tpu_custom_call" | custom-call | tf_op jit(solution)/shard_map/pack/pallas_call | solution.py:91
  10.4 0.0 copy-start.1
  10.4 1.0 %copy-done.1 = bf16[8,520,128]{2,1,0:T(8,128)(2,1)} copy-done((bf16[8,520,128]{2,1,0:T(8,128)(2,1)}, bf16[8,520,128]{2,1,0:T(8,128)(2,1)S(1)}, u32[]{:S(2)}) %copy-start.1) | copy-done | bytes 1064984
  11.4 0.0 copy-start
  11.4 0.0 copy-start.2
  11.4 7.4 %all-to-all-start = ((bf16[8,520,128]{2,1,0:T(8,128)(2,1)}), bf16[8,520,128]{2,1,0:T(8,128)(2,1)S(1)}, u32[]{:S(2)}, u32[]{:S(2)}) async-start(bf16[8,520,128]{2,1,0:T(8,128)(2,1)} %copy-done.1), calls=%async_computation | async-start | bytes 2129920 | tf_op jit(solution)/shard_map/all_to_all | solution.py:330
  18.8 0.0 all-gather.2.cloned.1.call-start
  18.8 0.7 all-gather.2.cloned.1.call-update
  19.5 0.1 pad_add_fusion.block_ref
  19.6 25.3 %all-to-all-done.x_any = bf16[8,520,128]{2,1,0:T(8,128)(2,1)S(1)} async-done(((bf16[8,520,128]{2,1,0:T(8,128)(2,1)}), bf16[8,520,128]{2,1,0:T(8,128)(2,1)S(1)}, u32[]{:S(2)}, u32[]{:S(2)}) %all-to-all-start) | async-done | bytes 1064992 | tf_op jit(solution)/shard_map/all_to_all | solution.py:330
  44.9 0.2 fusion.1.len_ref
  45.1 0.0 all-gather.2.cloned.1.call-done.unit_any
  45.2 0.0 copy-done
  45.2 0.0 copy-done.2
  45.2 7.8 %users.1 = (f32[8,128]{1,0:T(8,128)}, f32[256,512]{1,0:T(8,128)S(1)}, f32[256,512]{1,0:T(8,128)S(1)}, bf16[256,512]{1,0:T(8,128)(2,1)S(1)}, bf16[256,512]{1,0:T(8,128)(2,1)S(1)}) custom-call(s32[8]{0:T(128)S(1)} %fusion.1.len_ref, s32[4]{0:T(128)S(1)} %pad_add_fusion.block_ref, bf16[8,520,128]{2,1,0:T(8,128)(2,1)S(1)} %all-to-all-done.x_any, ...), custom_call_target="tpu_custom_call" | custom-call | tf_op jit(solution)/shard_map/users/pallas_call | solution.py:290
  53.0 0.0 copy-start.3
  53.0 2.0 %collective-permute-start.1 = (bf16[256,512]{1,0:T(8,128)(2,1)S(1)}, bf16[256,512]{1,0:T(8,128)(2,1)S(1)}, u32[]{:S(2)}, u32[]{:S(2)}) collective-permute-start(bf16[256,512]{1,0:T(8,128)(2,1)S(1)} %get-tuple-element.15), channel_id=1, source_target_pairs={{0,1},{1,0},{2,3},{3,2},{4,5},{5,4},{6,7},{7,6},{8,9},{9,8},{10,11... | collective-permute-start | bytes 786440 | tf_op jit(solution)/shard_map/ppermute | solution.py:20
  55.0 0.1 collective-permute-start
  55.1 1.1 %collective-permute-done.1 = bf16[256,512]{1,0:T(8,128)(2,1)S(1)} collective-permute-done((bf16[256,512]{1,0:T(8,128)(2,1)S(1)}, bf16[256,512]{1,0:T(8,128)(2,1)S(1)}, u32[]{:S(2)}, u32[]{:S(2)}) %collective-permute-start.1) | collective-permute-done | bytes 262176 | tf_op jit(solution)/shard_map/ppermute | solution.py:20
  56.1 0.1 add_convert_fusion
  56.2 3.6 %collective-permute-start.2 = (bf16[256,512]{1,0:T(8,128)(2,1)S(1)}, bf16[256,512]{1,0:T(8,128)(2,1)S(1)}, u32[]{:S(2)}, u32[]{:S(2)}) collective-permute-start(bf16[256,512]{1,0:T(8,128)(2,1)S(1)} %add_convert_fusion), channel_id=1, source_target_pairs={{0,2},{1,3},{2,0},{3,1},{4,6},{5,7},{6,4},{7,5},{8,10},{9,11},{10,... | collective-permute-start | bytes 786440 | tf_op jit(solution)/shard_map/ppermute | solution.py:20
  59.8 0.0 copy-done.3
  59.8 0.1 fusion
  59.9 0.0 collective-permute-done
  59.9 6.5 %collective-permute-done.2 = bf16[256,512]{1,0:T(8,128)(2,1)S(1)} collective-permute-done((bf16[256,512]{1,0:T(8,128)(2,1)S(1)}, bf16[256,512]{1,0:T(8,128)(2,1)S(1)}, u32[]{:S(2)}, u32[]{:S(2)}) %collective-permute-start.2) | collective-permute-done | bytes 262176 | tf_op jit(solution)/shard_map/ppermute | solution.py:20
  66.4 0.3 multiply_reduce_fusion
  66.7 1.0 %subtract_divide_fusion = f32[256,512]{1,0:T(8,128)} fusion(bf16[256,512]{1,0:T(8,128)(2,1)S(1)} %copy-done.3, f32[256]{0:T(256)S(1)} %multiply_reduce_fusion, f32[256]{0:T(256)S(1)} %add_sqrt_fusion, bf16[256,512]{1,0:T(8,128)(2,1)S(1)} %collective-permute-done.2, f32[256,512]{1,0:T(8,128)S(1)} %get-tuple-element.12, ...), kind=kLoop, calls=%fused_computation.3 | loop fusion | flops 1310720 | bytes 1837056 | tf_op jit(solution)/shard_map/div | solution.py:344
  (1 shorter events, 0.0 us)
Async XLA Ops:
  10.4 1.0 %copy-start.1 = (bf16[8,520,128]{2,1,0:T(8,128)(2,1)}, bf16[8,520,128]{2,1,0:T(8,128)(2,1)S(1)}, u32[]{:S(2)}) copy-start(bf16[8,520,128]{2,1,0:T(8,128)(2,1)S(1)} %get-tuple-element.9) | copy-start | bytes 3194884
  11.4 33.8 %copy-start = (bf16[512,2048]{1,0:T(8,128)(2,1)S(1)}, bf16[512,2048]{1,0:T(8,128)(2,1)}, u32[]{:S(2)}) copy-start(bf16[512,2048]{1,0:T(8,128)(2,1)} %w_in_any.1) | copy-start | bytes 6291460
  11.4 33.8 %copy-start.2 = (f32[4,128]{1,0:T(4,128)S(1)}, f32[4,128]{1,0:T(4,128)}, u32[]{:S(2)}) copy-start(f32[4,128]{1,0:T(4,128)} %bias_in.1) | copy-start | bytes 6148
  11.4 33.5 %all-to-all-start = ((bf16[8,520,128]{2,1,0:T(8,128)(2,1)}), bf16[8,520,128]{2,1,0:T(8,128)(2,1)S(1)}, u32[]{:S(2)}, u32[]{:S(2)}) async-start(bf16[8,520,128]{2,1,0:T(8,128)(2,1)} %copy-done.1), calls=%async_computation | async-start | bytes 2129920 | tf_op jit(solution)/shard_map/all_to_all | solution.py:330
  18.8 26.4 %all-gather.2.cloned.1.call-start = ((), (), s32[]{:S(2)}) async-start(), calls=%async_computation.1 | async-start | bytes 1310720 | tf_op jit(solution)/shard_map/all_gather | solution.py:331
  53.0 6.8 %copy-start.3 = (bf16[256,512]{1,0:T(8,128)(2,1)S(1)}, bf16[256,512]{1,0:T(8,128)(2,1)}, u32[]{:S(2)}) copy-start(bf16[256,512]{1,0:T(8,128)(2,1)} %pool_any.1) | copy-start | bytes 786436
  53.0 3.1 %collective-permute-start.1 = (bf16[256,512]{1,0:T(8,128)(2,1)S(1)}, bf16[256,512]{1,0:T(8,128)(2,1)S(1)}, u32[]{:S(2)}, u32[]{:S(2)}) collective-permute-start(bf16[256,512]{1,0:T(8,128)(2,1)S(1)} %get-tuple-element.15), channel_id=1, source_target_pairs={{0,1},{1,0},{2,3},{3,2},{4,5},{5,4},{6,7},{7,6},{8,9},{9,8},{10,11... | collective-permute-start | bytes 786440 | tf_op jit(solution)/shard_map/ppermute | solution.py:20
  55.0 5.0 %collective-permute-start = (bf16[256,512]{1,0:T(8,128)(2,1)S(1)}, bf16[256,512]{1,0:T(8,128)(2,1)S(1)}, u32[]{:S(2)}, u32[]{:S(2)}) collective-permute-start(bf16[256,512]{1,0:T(8,128)(2,1)S(1)} %get-tuple-element.13), channel_id=1, source_target_pairs={{0,1},{1,0},{2,3},{3,2},{4,5},{5,4},{6,7},{7,6},{8,9},{9,8},{10,11... | collective-permute-start | bytes 786440 | tf_op jit(solution)/shard_map/ppermute | solution.py:20
  56.2 10.2 %collective-permute-start.2 = (bf16[256,512]{1,0:T(8,128)(2,1)S(1)}, bf16[256,512]{1,0:T(8,128)(2,1)S(1)}, u32[]{:S(2)}, u32[]{:S(2)}) collective-permute-start(bf16[256,512]{1,0:T(8,128)(2,1)S(1)} %add_convert_fusion), channel_id=1, source_target_pairs={{0,2},{1,3},{2,0},{3,1},{4,6},{5,7},{6,4},{7,5},{8,10},{9,11},{10,... | collective-permute-start | bytes 786440 | tf_op jit(solution)/shard_map/ppermute | solution.py:20
Sparse Core Ops, SparseCore 0:
  21.8 18.1 all-gather.1

commit v6 on v5

--- a/solution.py
+++ b/solution.py
@@ -10,7 +10,7 @@
 
 logit_scale = 20.0
 contract_last = (((1,), (1,)), ((), ()))
-tile = 256
+tile = 512
 chunk = 16
 number_rows = 8
 
@@ -37,8 +37,7 @@
     list_any, len_any, from_any, tgt_any, pool_any, to_any, unit_any,
     entries, lens, targets, pool, unit, buffer, sems, in_sems, out_sems,
 ):
-    users = buffer.shape[0]
-    _, length, width = from_any.shape
+    users, length, width = from_any.shape
     pieces = width // length
     small = [
         pltpu.make_async_copy(source, target, sems.at[k])
@@ -48,17 +47,16 @@
     ]
     for copy in small:
         copy.start()
-    small[0].wait()
     copies_in = [
         [
             pltpu.make_async_copy(
-                from_any.at[entries[k], :, pl.ds(c * length, length)],
-                buffer.at[k, pl.ds(c * length, length)],
-                in_sems.at[k, c],
+                from_any.at[u, :, pl.ds(c * length, length)],
+                buffer.at[u, pl.ds(c * length, length)],
+                in_sems.at[u, c],
             )
             for c in range(pieces)
         ]
-        for k in range(users)
+        for u in range(users)
     ]
     for copies in copies_in:
         for copy in copies:
@@ -71,15 +69,19 @@
     small[1].wait()
     small[2].wait()
     row = lax.broadcasted_iota(jnp.int32, (number_rows, length), 0)
-    for k in range(users):
-        target = targets[pl.ds(entries[k], 1), :]
-        numbers = jnp.where(row == 0, lens[entries[k]], jnp.where(row == 1, target // 256, target % 256))
-        buffer[k, width:, :] = numbers.astype(jnp.float32).astype(jnp.bfloat16)
-    copies_out = [pltpu.make_async_copy(buffer.at[k], to_any.at[k], out_sems.at[k]) for k in range(users)]
-    for k in range(users):
-        for copy in copies_in[k]:
+    for u in range(users):
+        target = targets[u : u + 1, :]
+        numbers = jnp.where(row == 0, lens[u], jnp.where(row == 1, target // 256, target % 256))
+        buffer[u, width:, :] = numbers.astype(jnp.float32).astype(jnp.bfloat16)
+    small[0].wait()
+    for copies in copies_in:
+        for copy in copies:
             copy.wait()
-        copies_out[k].start()
+    copies_out = [
+        pltpu.make_async_copy(buffer.at[entries[k]], to_any.at[k], out_sems.at[k]) for k in range(users)
+    ]
+    for copy in copies_out:
+        copy.start()
     unit_out.wait()
     for copy in copies_out:
         copy.wait()
@@ -104,8 +106,8 @@
             pltpu.SemaphoreType.DMA((users,)),
         ],
         out_shape=[
-            jax.ShapeDtypeStruct(shape, jnp.bfloat16),
-            jax.ShapeDtypeStruct(item_pool.shape, jnp.bfloat16),
+            pltpu.HBM(shape, jnp.bfloat16),
+            pltpu.HBM(item_pool.shape, jnp.bfloat16),
         ],
         compiler_params=pltpu.CompilerParams(vmem_limit_bytes=16 * 1024 * 1024),
         name="pack",
@@ -113,40 +115,59 @@
 
 
 def users_kernel(
-    blocks, len_ref, block_ref, x_any, w_in_any, w_out_any, bias_in, unit_any,
+    blocks, per_step, len_ref, block_ref, x_ref, w_in, w_out, bias_in, unit_any,
     loss_ref, own_ref, over_ref, side_ref, far_ref,
-    acc, bias, x_ref, w_in, w_out, unit_ref, exp_ref, residual, events, starts_ref, key, value,
-    packed_tgt, packed_loss, x_sems, w_sems,
+    acc, bias, exp_ref, residual, events, starts_ref, key, value, packed_tgt, packed_loss,
+    unit_ref, unit_sems,
 ):
-    step = pl.program_id(0)
     heads, length = bias_in.shape
-    per_step = x_ref.shape[0]
+    items = unit_ref.shape[0] // blocks
+    unit_copies = [
+        pltpu.make_async_copy(
+            unit_any.at[pl.ds(k * items, items)], unit_ref.at[pl.ds(k * items, items)], unit_sems.at[k]
+        )
+        for k in range(blocks)
+    ]
+    for copy in unit_copies:
+        copy.start()
+    acc[...] = jnp.zeros_like(acc)
+    for h in range(heads):
+        wide = jnp.broadcast_to(0.5 * bias_in[h : h + 1, :], (length, length))
+        turned = pltpu.roll(wide, 0, 1, stride=1, stride_axis=0).T
+        bias[h] = jnp.concatenate([turned, turned], axis=1)
+
+    def units_arrive():
+        for copy in unit_copies:
+            copy.wait()
+
+    def one_step(step, _):
+        users_step(
+            step, units_arrive if steps == 1 else None, blocks, per_step, len_ref, x_ref, w_in, w_out, unit_ref, loss_ref,
+            acc, bias, exp_ref, residual, events, starts_ref, key, value, packed_tgt, packed_loss,
+        )
+        return 0
+
+    steps = x_ref.shape[0] // per_step
+    if steps == 1:
+        one_step(0, 0)
+    else:
+        units_arrive()
+        lax.fori_loop(0, steps, one_step, 0)
+
+    for k, out_ref in enumerate((own_ref, over_ref, side_ref, far_ref)):
+        rows = pl.ds(pl.multiple_of(block_ref[k] * items, items), items)
+        out_ref[...] = acc[rows, :].astype(out_ref.dtype)
+
+
+def users_step(
+    step, units_arrive, blocks, per_step, len_ref, x_ref, w_in, w_out, unit_ref, loss_ref,
+    acc, bias, exp_ref, residual, events, starts_ref, key, value, packed_tgt, packed_loss,
+):
+    heads, length, _ = bias.shape
     width = w_out.shape[0]
     hdim = width // heads
     items = unit_ref.shape[0] // blocks
     lines = tile // length
-
-    x_copies = [
-        pltpu.make_async_copy(x_any.at[step * per_step + u], x_ref.at[u], x_sems.at[u])
-        for u in range(per_step)
-    ]
-    w_copies = [
-        pltpu.make_async_copy(w_in_any, w_in, w_sems.at[0]),
-        pltpu.make_async_copy(w_out_any, w_out, w_sems.at[1]),
-        pltpu.make_async_copy(unit_any, unit_ref, w_sems.at[2]),
-    ]
-    for copy in x_copies:
-        copy.start()
-
-    @pl.when(step == 0)
-    def _():
-        for copy in w_copies:
-            copy.start()
-        acc[...] = jnp.zeros_like(acc)
-        for h in range(heads):
-            wide = jnp.broadcast_to(0.5 * bias_in[h : h + 1, :], (length, length))
-            turned = pltpu.roll(wide, 0, 1, stride=1, stride_axis=0).T
-            bias[h] = jnp.concatenate([turned, turned], axis=1)
 
     lens = [len_ref[step * per_step + u] for u in range(per_step)]
     starts, end = [], 0
@@ -162,12 +183,10 @@
     value[:length, :] = jnp.zeros((length, width), value.dtype)
     for u in range(per_step):
         starts_ref[pl.ds(starts[u], length), :] = jnp.full((length, length), starts[u], jnp.int32)
-    for copy in x_copies:
-        copy.wait()
     for u in range(per_step):
         for c in range(0, width, length):
-            events[pl.ds(starts[u], length), c : c + length] = x_ref[u, c : c + length, :]
-        digits = x_ref[u, width:, :].astype(jnp.float32)
+            events[pl.ds(starts[u], length), c : c + length] = x_ref[step * per_step + u, c : c + length, :]
+        digits = x_ref[step * per_step + u, width:, :].astype(jnp.float32)
         target = digits[1:2, :] * 256.0 + digits[2:3, :]
         wanted = jnp.where(place < lens[u], target.astype(jnp.int32), -1)
         line, turn = starts[u] // length + 1, lax.rem(starts[u], length)
@@ -178,11 +197,8 @@
         )
     events[pl.ds(end, tile), :] = jnp.zeros((tile, width), events.dtype)
 
-    @pl.when(step == 0)
-    def _():
-        for copy in w_copies:
-            copy.wait()
-
+    if units_arrive:
+        units_arrive()
     row = lax.broadcasted_iota(jnp.int32, (length, length), 0)
     col = lax.broadcasted_iota(jnp.int32, (length, length), 1)
     item_id = lax.broadcasted_iota(jnp.int32, (items, tile), 0)
@@ -269,50 +285,36 @@
         loss = jnp.where(place < length - turn, near, rest)
         loss_ref[pl.ds(step * per_step + u, 1), :] = jnp.where(place < lens[u], loss, 0.0)
 
-    @pl.when(step == pl.num_programs(0) - 1)
-    def _():
-        for k, out_ref in enumerate((own_ref, over_ref, side_ref, far_ref)):
-            rows = pl.ds(pl.multiple_of(block_ref[k] * items, items), items)
-            out_ref[...] = acc[rows, :].astype(out_ref.dtype)
-
 
 def users_call(packed, lens, w_in, w_out, rel_bias, unit_all, block_ids):
-    users, packed_rows, length = packed.shape
+    users, _, length = packed.shape
     heads, width = rel_bias.shape[0], w_out.shape[0]
     blocks = block_ids.shape[0]
     items = unit_all.shape[0] // blocks
     per_step = math.gcd(users, 8)
-    rows = per_step * length
+    rows = -(-per_step * length // tile) * tile
     lines = -(-(rows // length + 2) // 8) * 8
-    whole = lambda *shape: pl.BlockSpec(shape, lambda s, lens, ids: (0,) * len(shape))
-    anywhere, hbm = pl.BlockSpec(memory_space=pl.ANY), pl.BlockSpec(memory_space=pltpu.HBM)
-    part = lambda dtype: jax.ShapeDtypeStruct((items, width), dtype)
+    scalar, whole = pl.BlockSpec(memory_space=pltpu.SMEM), pl.BlockSpec(memory_space=pltpu.VMEM)
+    part = lambda dtype: pltpu.VMEM((items, width), dtype)
+    in_vmem = lambda array: pltpu.with_memory_space_constraint(array, pltpu.VMEM)
     return pl.pallas_call(
-        functools.partial(users_kernel, blocks),
-        grid_spec=pltpu.PrefetchScalarGridSpec(
-            num_scalar_prefetch=2,
-            grid=(users // per_step,),
-            in_specs=[anywhere, anywhere, hbm, whole(heads, length), hbm],
-            out_specs=[whole(users, length)] + [whole(items, width)] * 4,
-            scratch_shapes=[
-                pltpu.VMEM((blocks * items, width), jnp.float32),
-                pltpu.VMEM((heads, length, 2 * length), jnp.float32),
-                pltpu.VMEM((per_step, packed_rows, length), jnp.bfloat16),
-                pltpu.VMEM(w_in.shape, jnp.bfloat16),
-                pltpu.VMEM(w_out.shape, jnp.bfloat16),
-                pltpu.VMEM(unit_all.shape, jnp.bfloat16),
-                pltpu.VMEM((blocks, items, tile), jnp.float32),
-                pltpu.VMEM((blocks * items, tile), jnp.bfloat16),
-                pltpu.VMEM((rows + tile, width), jnp.bfloat16),
-                pltpu.VMEM((rows + tile, length), jnp.int32),
-                pltpu.VMEM((length + rows + tile, width), jnp.bfloat16),
-                pltpu.VMEM((length + rows + tile, width), jnp.bfloat16),
-                pltpu.VMEM((lines, length), jnp.int32),
-                pltpu.VMEM((lines, length), jnp.float32),
-                pltpu.SemaphoreType.DMA((per_step,)),
-                pltpu.SemaphoreType.DMA((3,)),
-            ],
-        ),
+        functools.partial(users_kernel, blocks, per_step),
+        in_specs=[scalar, scalar, whole, whole, whole, whole, pl.BlockSpec(memory_space=pltpu.HBM)],
+        out_specs=[whole] * 5,
+        scratch_shapes=[
+            pltpu.VMEM((blocks * items, width), jnp.float32),
+            pltpu.VMEM((heads, length, 2 * length), jnp.float32),
+            pltpu.VMEM((blocks, items, tile), jnp.float32),
+            pltpu.VMEM((blocks * items, tile), jnp.bfloat16),
+            pltpu.VMEM((rows + tile, width), jnp.bfloat16),
+            pltpu.VMEM((rows + tile, length), jnp.int32),
+            pltpu.VMEM((length + rows + tile, width), jnp.bfloat16),
+            pltpu.VMEM((length + rows + tile, width), jnp.bfloat16),
+            pltpu.VMEM((lines, length), jnp.int32),
+            pltpu.VMEM((lines, length), jnp.float32),
+            pltpu.VMEM(unit_all.shape, jnp.bfloat16),
+            pltpu.SemaphoreType.DMA((blocks,)),
+        ],
         out_shape=[
             jax.ShapeDtypeStruct((users, length), jnp.float32),
             part(jnp.float32),
@@ -320,9 +322,9 @@
             part(jnp.bfloat16),
             part(jnp.bfloat16),
         ],
-        compiler_params=pltpu.CompilerParams(vmem_limit_bytes=36 * 1024 * 1024),
+        compiler_params=pltpu.CompilerParams(vmem_limit_bytes=32 * 1024 * 1024),
         name="users",
-    )(lens, block_ids, packed, w_in, in_hbm(w_out), rel_bias, in_hbm(unit_all))
+    )(lens, block_ids, *[in_vmem(array) for array in (packed, w_in, w_out, rel_bias)], in_hbm(unit_all))
 
 
 def shards(histories, lengths, targets, send_list, w_in, w_out, rel_bias, item_pool):

time: 74.9 us -> 71.3 us (0.952)
  starting transfers between devices: 13 us -> 9.59 us
    ppermute x3, starting transfers between devices: 5.61 us -> 2.16 us  [swap(): return lax.ppermute(array, axis, [(i, i ^ bit) for i in range(devices)])]
where the time goes in v6:
time: 71.3 us; the launch traced here: 71 us
  waiting for transfers between devices  33.7 us (47%)
  between operations  14.1 us (20%)
  Pallas kernels  10.7 us (15%)
  starting transfers between devices  9.59 us (13%)
  other arithmetic  1.83 us (3%)
  local copies, waits for them, and re-layouts  1.06 us (1%)
    all_to_all x1, waiting for transfers between devices, shards(): lax.all_to_all(packed, 'dp', split_axis=0, concat_axis=0, tiled=True)  25.3 us
    ppermute x3, waiting for transfers between devices, swap(): return lax.ppermute(array, axis, [(i, i ^ bit) for i in range(devices)])  7.69 us
    pallas_call x1, Pallas kernels, users_call(): pl.pallas_call(functools.partial(users_kernel, blocks, per_step), in_spec...  7.69 us
    all_to_all x1, starting transfers between devices, shards(): lax.all_to_all(packed, 'dp', split_axis=0, concat_axis=0, tiled=True)  7.4 us
    pallas_call x1, Pallas kernels, pack(): pl.pallas_call(pack_kernel, in_specs=[pl.BlockSpec(memory_space=pltpu.HBM...  3.01 us
    ppermute x3, starting transfers between devices, swap(): return lax.ppermute(array, axis, [(i, i ^ bit) for i in range(devices)])  2.16 us
  transfers between devices with their start and end apart: 5, of which 3 were waited for; matrix products, arithmetic and copies ran while one was open for 1% of the time, Pallas kernels for 0%

profile of v6, /device:TPU:0, one launch (start us, length us, event | category | flops | bytes accessed | tf_op | source)
XLA Modules:
  0.0 71.0 jit_solution(11678611551109720938)
XLA Ops:
  7.2 3.0 %pack.1 = (bf16[8,520,128]{2,1,0:T(8,128)(2,1)}, bf16[256,512]{1,0:T(8,128)(2,1)}) custom-call(s32[8]{0:T(128)} %list_any.1, s32[8]{0:T(128)} %len_any.1, bf16[8,128,512]{2,1,0:T(8,128)(2,1)} %from_any.1, s32[8,128]{1,0:T(8,128)} %tgt_any.1, bf16[256,512]{1,0:T(8,128)(2,1)} %pool_any.1), custom_call_target="tpu_custom_call" | custom-call | tf_op jit(solution)/shard_map/pack/pallas_call | solution.py:93
  10.2 0.0 copy-start
  10.2 0.0 copy-start.2
  10.2 7.4 %all-to-all-start = ((bf16[8,520,128]{2,1,0:T(8,128)(2,1)}), bf16[8,520,128]{2,1,0:T(8,128)(2,1)S(1)}, u32[]{:S(2)}, u32[]{:S(2)}) async-start(bf16[8,520,128]{2,1,0:T(8,128)(2,1)} %get-tuple-element.9), calls=%async_computation | async-start | bytes 2129920 | tf_op jit(solution)/shard_map/all_to_all | solution.py:332
  17.6 0.0 all-gather.2.cloned.1.call-start
  17.6 0.7 all-gather.2.cloned.1.call-update
  18.3 0.1 pad_add_fusion.block_ref
  18.4 25.3 %all-to-all-done.x_ref = bf16[8,520,128]{2,1,0:T(8,128)(2,1)S(1)} async-done(((bf16[8,520,128]{2,1,0:T(8,128)(2,1)}), bf16[8,520,128]{2,1,0:T(8,128)(2,1)S(1)}, u32[]{:S(2)}, u32[]{:S(2)}) %all-to-all-start) | async-done | bytes 1064992 | tf_op jit(solution)/shard_map/all_to_all | solution.py:332
  43.7 0.2 fusion.1.len_ref
  44.0 0.0 all-gather.2.cloned.1.call-done.unit_any
  44.0 0.0 copy-done
  44.0 0.0 copy-done.2
  44.0 0.0 copy-start.1
  44.0 1.0 %copy-done.1 = bf16[512,512]{1,0:T(8,128)(2,1)S(1)} copy-done((bf16[512,512]{1,0:T(8,128)(2,1)S(1)}, bf16[512,512]{1,0:T(8,128)(2,1)}, u32[]{:S(2)}) %copy-start.1) | copy-done | bytes 524312
  45.0 7.7 %users.1 = (f32[8,128]{1,0:T(8,128)}, f32[256,512]{1,0:T(8,128)S(1)}, f32[256,512]{1,0:T(8,128)S(1)}, bf16[256,512]{1,0:T(8,128)(2,1)S(1)}, bf16[256,512]{1,0:T(8,128)(2,1)S(1)}) custom-call(s32[8]{0:T(128)S(1)} %fusion.1.len_ref, s32[4]{0:T(128)S(1)} %pad_add_fusion.block_ref, bf16[8,520,128]{2,1,0:T(8,128)(2,1)S(1)} %all-to-all-done.x_ref, ...), custom_call_target="tpu_custom_call" | custom-call | tf_op jit(solution)/shard_map/users/pallas_call | solution.py:300
  52.8 0.0 copy-start.3
  52.8 0.1 collective-permute-start.1
  52.8 0.5 collective-permute-start
  53.3 1.0 %collective-permute-done.1 = bf16[256,512]{1,0:T(8,128)(2,1)S(1)} collective-permute-done((bf16[256,512]{1,0:T(8,128)(2,1)S(1)}, bf16[256,512]{1,0:T(8,128)(2,1)S(1)}, u32[]{:S(2)}, u32[]{:S(2)}) %collective-permute-start.1) | collective-permute-done | bytes 262176 | tf_op jit(solution)/shard_map/ppermute | solution.py:20
  54.4 0.1 add_convert_fusion
  54.4 1.6 %collective-permute-start.2 = (bf16[256,512]{1,0:T(8,128)(2,1)S(1)}, bf16[256,512]{1,0:T(8,128)(2,1)S(1)}, u32[]{:S(2)}, u32[]{:S(2)}) collective-permute-start(bf16[256,512]{1,0:T(8,128)(2,1)S(1)} %add_convert_fusion), channel_id=1, source_target_pairs={{0,2},{1,3},{2,0},{3,1},{4,6},{5,7},{6,4},{7,5},{8,10},{9,11},{10,... | collective-permute-start | bytes 786440 | tf_op jit(solution)/shard_map/ppermute | solution.py:20
  56.0 0.0 copy-done.3
  56.0 0.1 fusion
  56.2 0.0 collective-permute-done
  56.2 6.7 %collective-permute-done.2 = bf16[256,512]{1,0:T(8,128)(2,1)S(1)} collective-permute-done((bf16[256,512]{1,0:T(8,128)(2,1)S(1)}, bf16[256,512]{1,0:T(8,128)(2,1)S(1)}, u32[]{:S(2)}, u32[]{:S(2)}) %collective-permute-start.2) | collective-permute-done | bytes 262176 | tf_op jit(solution)/shard_map/ppermute | solution.py:20
  62.9 0.3 multiply_reduce_fusion
  63.1 1.0 %subtract_divide_fusion = f32[256,512]{1,0:T(8,128)} fusion(bf16[256,512]{1,0:T(8,128)(2,1)S(1)} %copy-done.3, f32[256]{0:T(256)S(1)} %multiply_reduce_fusion, f32[256]{0:T(256)S(1)} %add_sqrt_fusion, bf16[256,512]{1,0:T(8,128)(2,1)S(1)} %collective-permute-done.2, f32[256,512]{1,0:T(8,128)S(1)} %get-tuple-element.12, ...), kind=kLoop, calls=%fused_computation.3 | loop fusion | flops 1310720 | bytes 1837056 | tf_op jit(solution)/shard_map/div | solution.py:346
  (1 shorter events, 0.0 us)
Async XLA Ops:
  10.2 33.8 %copy-start = (bf16[512,2048]{1,0:T(8,128)(2,1)S(1)}, bf16[512,2048]{1,0:T(8,128)(2,1)}, u32[]{:S(2)}) copy-start(bf16[512,2048]{1,0:T(8,128)(2,1)} %w_in.1) | copy-start | bytes 6291460
  10.2 33.8 %copy-start.2 = (f32[4,128]{1,0:T(4,128)S(1)}, f32[4,128]{1,0:T(4,128)}, u32[]{:S(2)}) copy-start(f32[4,128]{1,0:T(4,128)} %bias_in.1) | copy-start | bytes 6148
  10.2 33.5 %all-to-all-start = ((bf16[8,520,128]{2,1,0:T(8,128)(2,1)}), bf16[8,520,128]{2,1,0:T(8,128)(2,1)S(1)}, u32[]{:S(2)}, u32[]{:S(2)}) async-start(bf16[8,520,128]{2,1,0:T(8,128)(2,1)} %get-tuple-element.9), calls=%async_computation | async-start | bytes 2129920 | tf_op jit(solution)/shard_map/all_to_all | solution.py:332
  17.6 26.4 %all-gather.2.cloned.1.call-start = ((), (), s32[]{:S(2)}) async-start(), calls=%async_computation.1 | async-start | bytes 1310720 | tf_op jit(solution)/shard_map/all_gather | solution.py:333
  44.0 1.0 %copy-start.1 = (bf16[512,512]{1,0:T(8,128)(2,1)S(1)}, bf16[512,512]{1,0:T(8,128)(2,1)}, u32[]{:S(2)}) copy-start(bf16[512,512]{1,0:T(8,128)(2,1)} %w_out.1) | copy-start | bytes 1572868
  52.8 3.3 %copy-start.3 = (bf16[256,512]{1,0:T(8,128)(2,1)S(1)}, bf16[256,512]{1,0:T(8,128)(2,1)}, u32[]{:S(2)}) copy-start(bf16[256,512]{1,0:T(8,128)(2,1)} %pool_any.1) | copy-start | bytes 786436
  52.8 1.6 %collective-permute-start.1 = (bf16[256,512]{1,0:T(8,128)(2,1)S(1)}, bf16[256,512]{1,0:T(8,128)(2,1)S(1)}, u32[]{:S(2)}, u32[]{:S(2)}) collective-permute-start(bf16[256,512]{1,0:T(8,128)(2,1)S(1)} %get-tuple-element.15), channel_id=1, source_target_pairs={{0,1},{1,0},{2,3},{3,2},{4,5},{5,4},{6,7},{7,6},{8,9},{9,8},{10,11... | collective-permute-start | bytes 786440 | tf_op jit(solution)/shard_map/ppermute | solution.py:20
  52.8 3.3 %collective-permute-start = (bf16[256,512]{1,0:T(8,128)(2,1)S(1)}, bf16[256,512]{1,0:T(8,128)(2,1)S(1)}, u32[]{:S(2)}, u32[]{:S(2)}) collective-permute-start(bf16[256,512]{1,0:T(8,128)(2,1)S(1)} %get-tuple-element.13), channel_id=1, source_target_pairs={{0,1},{1,0},{2,3},{3,2},{4,5},{5,4},{6,7},{7,6},{8,9},{9,8},{10,11... | collective-permute-start | bytes 786440 | tf_op jit(solution)/shard_map/ppermute | solution.py:20
  54.4 8.4 %collective-permute-start.2 = (bf16[256,512]{1,0:T(8,128)(2,1)S(1)}, bf16[256,512]{1,0:T(8,128)(2,1)S(1)}, u32[]{:S(2)}, u32[]{:S(2)}) collective-permute-start(bf16[256,512]{1,0:T(8,128)(2,1)S(1)} %add_convert_fusion), channel_id=1, source_target_pairs={{0,2},{1,3},{2,0},{3,1},{4,6},{5,7},{6,4},{7,5},{8,10},{9,11},{10,... | collective-permute-start | bytes 786440 | tf_op jit(solution)/shard_map/ppermute | solution.py:20
Sparse Core Ops, SparseCore 0:
  20.6 18.1 all-gather.1

commit v7 on v6

v7 whole, which is shorter than its diff:
```python
import functools
import math

import jax
import jax.numpy as jnp
from jax import lax
from jax.experimental import pallas as pl
from jax.experimental.pallas import tpu as pltpu
from jax.sharding import PartitionSpec as P

logit_scale = 20.0
contract_last = (((1,), (1,)), ((), ()))
tile = 256
chunk = 16
number_rows = 8


def swap(array, axis, bit):
    devices = lax.axis_size(axis)
    return lax.ppermute(array, axis, [(i, i ^ bit) for i in range(devices)])


def from_behind(array, axis, by):
    devices = lax.axis_size(axis)
    return lax.ppermute(array, axis, [(i, (i + by) % devices) for i in range(devices)])


def in_vmem(array):
    return pltpu.with_memory_space_constraint(array, pltpu.VMEM)


def in_hbm(array):
    return pltpu.with_memory_space_constraint(array, pltpu.HBM)


def half_silu(half):
    return half + half * jnp.tanh(half)


def center_and_spread(values):
    center = values - jnp.mean(values, axis=-1, keepdims=True)
    return center, jnp.mean(center * center, axis=-1, keepdims=True)


def pack_kernel(
    work, groups, group_ref, list_any, len_any, from_any, tgt_any, pool_any, *refs,
):
    users = from_any.shape[0]
    to_refs, unit_any = refs[:users], refs[users]
    entries, lens, targets, pool, unit, buffer, sems, in_sems, out_sems = refs[users + 1 :]
    users, length, width = from_any.shape
    pieces = width // length
    small = [
        pltpu.make_async_copy(source, target, sems.at[k])
        for k, (source, target) in enumerate(
            ((list_any, entries), (len_any, lens), (tgt_any, targets), (pool_any, pool))
        )
    ]
    for copy in small:
        copy.start()
    copies_in = [
        [
            pltpu.make_async_copy(
                from_any.at[u, :, pl.ds(c * length, length)],
                buffer.at[u, pl.ds(c * length, length)],
                in_sems.at[u, c],
            )
            for c in range(pieces)
        ]
        for u in range(users)
    ]
    for copies in copies_in:
        for copy in copies:
            copy.start()
    small[3].wait()
    rows = pool[...].astype(jnp.float32)
    unit[...] = (rows * lax.rsqrt(jnp.sum(rows * rows, axis=-1, keepdims=True) + 1e-06)).astype(jnp.bfloat16)
    unit_out = pltpu.make_async_copy(unit, unit_any, sems.at[4])
    unit_out.start()
    small[1].wait()
    small[2].wait()
    row = lax.broadcasted_iota(jnp.int32, (number_rows, length), 0)
    for u in range(users):
        target = targets[u : u + 1, :]
        numbers = jnp.where(row == 0, lens[u], jnp.where(row == 1, target // 256, target % 256))
        buffer[u, width:, :] = numbers.astype(jnp.float32).astype(jnp.bfloat16)
    small[0].wait()
    copies_out = []
    for k, (shift, slot) in enumerate(work):
        user = entries[(group_ref[0] + shift) % groups * (users // groups) + slot]
        for c in range(pieces):
            pltpu.make_async_copy(
                from_any.at[user, :, pl.ds(c * length, length)],
                buffer.at[user, pl.ds(c * length, length)],
                in_sems.at[user, c],
            ).wait()
        copies_out.append(pltpu.make_async_copy(buffer.at[user], to_refs[k], out_sems.at[k]))
        copies_out[k].start()
    unit_out.wait()
    for copy in copies_out:
        copy.wait()


def pack(histories, lengths, targets, entries, item_pool, work, groups, group):
    users, length, width = histories.shape
    shape = (users, width + number_rows, length)
    hbm = pl.BlockSpec(memory_space=pltpu.HBM)
    return pl.pallas_call(
        functools.partial(pack_kernel, work, groups),
        in_specs=[pl.BlockSpec(memory_space=pltpu.SMEM)] + [hbm] * 5,
        out_specs=[hbm] * (users + 1),
        scratch_shapes=[
            pltpu.SMEM(entries.shape, jnp.int32),
            pltpu.SMEM(lengths.shape, jnp.int32),
            pltpu.VMEM(targets.shape, jnp.int32),
            pltpu.VMEM(item_pool.shape, jnp.bfloat16),
            pltpu.VMEM(item_pool.shape, jnp.bfloat16),
            pltpu.VMEM(shape, jnp.bfloat16),
            pltpu.SemaphoreType.DMA((5,)),
            pltpu.SemaphoreType.DMA((users, width // length)),
            pltpu.SemaphoreType.DMA((users,)),
        ],
        out_shape=[pltpu.HBM(shape[1:], jnp.bfloat16)] * users + [pltpu.HBM(item_pool.shape, jnp.bfloat16)],
        compiler_params=pltpu.CompilerParams(vmem_limit_bytes=16 * 1024 * 1024),
        name="pack",
    )(group, *[in_hbm(array) for array in (entries, lengths, histories, targets, item_pool)])


def users_kernel(
    places, blocks, first, last, id_ref, w_in, w_out, bias_in, *refs,
):
    count = len(places)
    x_refs, unit_refs, refs = refs[:count], refs[count : count + blocks], refs[count + blocks :]
    if not first:
        loss_in, sums_in, refs = refs[0], refs[1 : 1 + blocks], refs[1 + blocks :]
    loss_ref, out_refs, refs = refs[0], refs[1 : 1 + blocks], refs[1 + blocks :]
    wide_sums, bias, scratch = refs[0], refs[1], refs[2:]
    heads, length = bias_in.shape
    sums = [
        ref if ref.dtype == jnp.float32 else wide_sums.at[k - blocks // 2] for k, ref in enumerate(out_refs)
    ]
    loss_ref[...] = jnp.zeros_like(loss_ref) if first else loss_in[...]
    for k in range(blocks):
        sums[k][...] = jnp.zeros_like(sums[k]) if first else sums_in[k][...]
    for h in range(heads):
        wide = jnp.broadcast_to(0.5 * bias_in[h : h + 1, :], (length, length))
        turned = pltpu.roll(wide, 0, 1, stride=1, stride_axis=0).T
        bias[h] = jnp.concatenate([turned, turned], axis=1)
    for at in range(0, count, 8):
        users_step(
            x_refs[at : at + 8], [id_ref[blocks + k] for k in places[at : at + 8]],
            [id_ref[k] for k in range(blocks)], w_in, w_out, unit_refs, loss_ref, sums, bias, *scratch,
        )
    for k in range(blocks):
        if sums[k] is not out_refs[k]:
            out_refs[k][...] = sums[k][...].astype(out_refs[k].dtype)


def users_step(
    x_refs, spots, block_ids, w_in, w_out, unit_refs, loss_ref, sums, bias,
    exp_ref, residual, events, starts_ref, key, value, packed_tgt, packed_loss,
):
    heads, length, _ = bias.shape
    width = w_out.shape[0]
    hdim = width // heads
    items = unit_refs[0].shape[0]
    lines = tile // length
    per_step = len(x_refs)

    digits = [ref[width:, :].astype(jnp.float32) for ref in x_refs]
    lens = [jnp.max(digit[:1, :]).astype(jnp.int32) for digit in digits]
    starts, end = [], 0
    for u in range(per_step):
        starts.append(pl.multiple_of(end, chunk) if u else 0)
        end = end + (lens[u] + chunk - 1) // chunk * chunk
    end = pl.multiple_of(end, chunk)
    tiles = (end + tile - 1) // tile

    place = lax.broadcasted_iota(jnp.int32, (1, length), 1)
    packed_tgt[...] = jnp.full_like(packed_tgt, -1)
    key[:length, :] = jnp.zeros((length, width), key.dtype)
    value[:length, :] = jnp.zeros((length, width), value.dtype)
    for u in range(per_step):
        starts_ref[pl.ds(starts[u], length), :] = jnp.full((length, length), starts[u], jnp.int32)
    for u in range(per_step):
        for c in range(0, width, length):
            events[pl.ds(starts[u], length), c : c + length] = x_refs[u][c : c + length, :]
        target = digits[u][1:2, :] * 256.0 + digits[u][2:3, :]
        wanted = jnp.where(place < lens[u], target.astype(jnp.int32), -1)
        line, turn = starts[u] // length + 1, lax.rem(starts[u], length)
        turned = pltpu.roll(wanted, turn, 1)
        packed_tgt[pl.ds(line, 1), :] = jnp.where(place >= turn, turned, packed_tgt[pl.ds(line, 1), :])
        packed_tgt[pl.ds(line + 1, 1), :] = jnp.where(
            place < turn, turned, packed_tgt[pl.ds(line + 1, 1), :]
        )
    events[pl.ds(end, tile), :] = jnp.zeros((tile, width), events.dtype)

    row = lax.broadcasted_iota(jnp.int32, (length, length), 0)
    col = lax.broadcasted_iota(jnp.int32, (length, length), 1)
    item_id = lax.broadcasted_iota(jnp.int32, (items, tile), 0)
    rate = logit_scale * math.log2(math.e)

    def one_tile(t, _):
        first = pl.multiple_of(t * tile, tile)
        x = events[pl.ds(first, tile), :].astype(jnp.float32)
        center, spread = center_and_spread(x)
        half_normed = (center * (0.5 * lax.rsqrt(spread + 1e-05))).astype(jnp.bfloat16)
        gate, values, query, keys = [
            half_silu(
                jnp.dot(
                    half_normed, w_in[:, part * width : (part + 1) * width],
                    preferred_element_type=jnp.float32,
                )
            ).astype(jnp.bfloat16)
            for part in range(4)
        ]
        key[pl.ds(first + length, tile), :] = keys
        value[pl.ds(first + length, tile), :] = values
        mixed = []
        for k in range(lines):
            base = pl.multiple_of(first + k * length, length)
            sources = pl.ds(base, 2 * length)
            start = starts_ref[pl.ds(base, length), :]
            ahead = packed_tgt[pl.ds(t * lines + k, 1), :] >= 0
            here = packed_tgt[pl.ds(t * lines + k + 1, 1), :] >= 0
            keep_ahead = (base - length + col >= start) & ahead
            keep_here = (col <= row) & (base + col >= start) & here
            keep = jnp.concatenate([keep_ahead, keep_here], axis=1)
            by_head = []
            for h in range(heads):
                cols = slice(h * hdim, (h + 1) * hdim)
                scores = lax.dot_general(
                    query[k * length : (k + 1) * length, cols], key[sources, cols], contract_last,
                    preferred_element_type=jnp.float32,
                )
                attn = half_silu(scores * (0.5 / math.sqrt(hdim)) + bias[h])
                attn = jnp.where(keep, attn, 0.0).astype(jnp.bfloat16)
                by_head.append(jnp.dot(attn, value[sources, cols], preferred_element_type=jnp.float32))
            mixed.append(jnp.concatenate(by_head, axis=1))
        center, spread = center_and_spread(jnp.concatenate(mixed, axis=0))
        normed = center * lax.rsqrt(spread + 1e-05)
        gated = (normed * gate.astype(jnp.float32)).astype(jnp.bfloat16)
        out = x + jnp.dot(gated, w_out[...], preferred_element_type=jnp.float32)
        out = out.astype(jnp.bfloat16).astype(jnp.float32)
        square = jnp.sum(out * out, axis=-1, keepdims=True)
        queries = (out * lax.rsqrt(square + 1e-06)).astype(jnp.bfloat16)

        target = jnp.concatenate(
            [packed_tgt[pl.ds(t * lines + k + 1, 1), :] for k in range(lines)], axis=1
        )
        total = jnp.zeros((1, tile), jnp.float32)
        target_dot = jnp.zeros((1, tile), jnp.float32)
        for j, block in enumerate(block_ids):
            dots = lax.dot_general(
                unit_refs[j][...], queries, contract_last, preferred_element_type=jnp.float32
            )
            exps = jnp.exp2(dots * rate - rate)
            exp_ref[j] = exps
            total += jnp.sum(exps, axis=0, keepdims=True)
            hit = item_id == target - block * items
            target_dot += jnp.sum(jnp.where(hit, dots, 0.0), axis=0, keepdims=True)
        loss = logit_scale + jnp.log(total) - logit_scale * target_dot
        for k in range(lines):
            packed_loss[pl.ds(t * lines + k, 1), :] = loss[:, k * length : (k + 1) * length]
        share = jnp.where(target >= 0, 1.0 / total, 0.0)
        for j, block in enumerate(block_ids):
            hit = item_id == target - block * items
            left = exp_ref[j] * share - jnp.where(hit, 1.0, 0.0)
            residual[j] = left.astype(jnp.bfloat16)
        for j in range(len(block_ids)):
            sums[j][...] += jnp.dot(residual[j], queries, preferred_element_type=jnp.float32)
        return 0

    lax.fori_loop(0, tiles, one_tile, 0)

    for u in range(per_step):
        line, turn = starts[u] // length, lax.rem(starts[u], length)
        back = lax.rem(length - turn, length)
        near = pltpu.roll(packed_loss[pl.ds(line, 1), :], back, 1)
        rest = pltpu.roll(packed_loss[pl.ds(line + 1, 1), :], back, 1)
        loss = jnp.where(place < length - turn, near, rest)
        loss_ref[pl.ds(spots[u], 1), :] = jnp.where(place < lens[u], loss, 0.0)


def users_call(ids, places, users, packed, units, w_in, w_out, rel_bias, carried, last):
    heads, length = rel_bias.shape
    width = w_out.shape[0]
    blocks = len(units)
    items = units[0].shape[0]
    rows = -(-min(len(places), 8) * length // tile) * tile
    lines = -(-(rows // length + 2) // 8) * 8
    whole = pl.BlockSpec(memory_space=pltpu.VMEM)
    arrays = [w_in, w_out, rel_bias, *packed, *units, *carried]
    narrow = lambda k: last and k >= blocks // 2
    return pl.pallas_call(
        functools.partial(users_kernel, places, blocks, not carried, last),
        in_specs=[pl.BlockSpec(memory_space=pltpu.SMEM)] + [whole] * len(arrays),
        out_specs=[whole] * (1 + blocks),
        scratch_shapes=[
            pltpu.VMEM((blocks // 2, items, width), jnp.float32),
            pltpu.VMEM((heads, length, 2 * length), jnp.float32),
            pltpu.VMEM((blocks, items, tile), jnp.float32),
            pltpu.VMEM((blocks, items, tile), jnp.bfloat16),
            pltpu.VMEM((rows + tile, width), jnp.bfloat16),
            pltpu.VMEM((rows + tile, length), jnp.int32),
            pltpu.VMEM((length + rows + tile, width), jnp.bfloat16),
            pltpu.VMEM((length + rows + tile, width), jnp.bfloat16),
            pltpu.VMEM((lines, length), jnp.int32),
            pltpu.VMEM((lines, length), jnp.float32),
        ],
        out_shape=[pltpu.VMEM((users, length), jnp.float32)]
        + [
            pltpu.VMEM((items, width), jnp.bfloat16 if narrow(k) else jnp.float32) for k in range(blocks)
        ],
        compiler_params=pltpu.CompilerParams(vmem_limit_bytes=24 * 1024 * 1024),
        name="users",
    )(ids, *[in_vmem(array) for array in arrays])


def shards(histories, lengths, targets, send_list, w_in, w_out, rel_bias, item_pool):
    user_count = histories.shape[0]
    groups = lax.axis_size("dp")
    slots = user_count // groups
    group, mine = lax.axis_index("dp").astype(jnp.int32), lax.axis_index("blk").astype(jnp.int32)

    work = sorted(
        ((shift, slot) for shift in range(groups) for slot in range(slots)),
        key=lambda pair: (pair[0] != 0, abs(pair[0] - groups / 2)),
    )
    *packed, unit = pack(
        histories, lengths, targets, send_list, item_pool, work, groups, group.reshape(1)
    )
    over_unit = swap(unit, "blk", 2)
    packed = [
        users if shift == 0 else from_behind(users, "dp", shift) for users, (shift, _) in zip(packed, work)
    ]
    units = [unit, over_unit, swap(unit, "blk", 1), swap(over_unit, "blk", 1)]

    pool_float = item_pool.astype(jnp.float32)
    item_norm = jnp.sqrt(jnp.sum(pool_float * pool_float, axis=-1, keepdims=True) + 1e-06)
    unit_rows = pool_float / item_norm

    came = [((group - shift) % groups) * slots + slot for shift, slot in work]
    ids = jnp.stack([mine, mine ^ 2, mine ^ 1, mine ^ 3, *came])
    half = user_count // 2
    order = tuple(range(user_count))
    carried = users_call(
        ids, order[:half], user_count, packed[:half], units, w_in, w_out, rel_bias, (), False
    )
    row_loss, own, over, side, far = users_call(
        ids, order[half:], user_count, packed[half:], units, w_in, w_out, rel_bias, carried, True
    )
    over = over + swap(far, "blk", 1).astype(jnp.float32)
    own = own + swap(side, "blk", 1).astype(jnp.float32)
    item_sum = logit_scale * (own + swap(over.astype(jnp.bfloat16), "blk", 2).astype(jnp.float32))
    pool_grad = (
        item_sum - unit_rows * jnp.sum(unit_rows * item_sum, axis=-1, keepdims=True)
    ) / item_norm
    return (row_loss, pool_grad)


def solution(mesh):
    placed = (
        P(("dp", "blk"), None, None),
        P(("dp", "blk")),
        P(("dp", "blk"), None),
        P(("dp", "blk")),
        P(),
        P(),
        P(),
        P(("dp", "blk"), None),
    )
    return jax.shard_map(
        shards,
        mesh=mesh,
        in_specs=placed,
        out_specs=(P(("dp", "blk"), None), P(("dp", "blk"), None)),
        check_vma=False,
    )
```

time: 71.3 us -> 60.6 us (0.85); the launches traced: 71 us -> 61.3 us
  waiting for transfers between devices: 33.7 us -> 17.4 us
  starting transfers between devices: 9.59 us -> 24.4 us
  between operations: 14.1 us -> 0.76 us
  local copies, waits for them, and re-layouts: 1.06 us -> 5.86 us
    all_to_all x1 -> x0, waiting for transfers between devices: 25.3 us -> none  [shards(): lax.all_to_all(packed, 'dp', split_axis=0, concat_axis=0, tiled=True)]
    ppermute x0 -> x7, starting transfers between devices: none -> 17.1 us  [from_behind(): lax.ppermute(array, axis, [(i, (i + by) % devices) for i in range(devices)])]
    ppermute x0 -> x7, waiting for transfers between devices: none -> 10.4 us  [from_behind(): lax.ppermute(array, axis, [(i, (i + by) % devices) for i in range(devices)])]
    all_to_all x1 -> x0, starting transfers between devices: 7.4 us -> none  [shards(): lax.all_to_all(packed, 'dp', split_axis=0, concat_axis=0, tiled=True)]
    ppermute x3 -> x6, starting transfers between devices: 2.16 us -> 7.26 us  [swap(): return lax.ppermute(array, axis, [(i, i ^ bit) for i in range(devices)])]
    unnamed x8 -> x19, local copies, waits for them, and re-layouts: 1.06 us -> 5.78 us
    ppermute x3 -> x6, waiting for transfers between devices: 7.69 us -> 6.99 us  [swap(): return lax.ppermute(array, axis, [(i, i ^ bit) for i in range(devices)])]
    pallas_call x2 -> x3, Pallas kernels: 10.7 us -> 11.3 us  [the longest x2 8.33 us: users_call(): pl.pallas_call(functools.partial(users_kernel, places, blocks, not carrie...]
  transfers between devices with their start and end apart: 5 -> 13, of which waited for: 3 -> 5; matrix products, arithmetic and copies ran while one was open for 1% -> 1% of each run, Pallas kernels for 0% -> 7%
where the time goes in v7:
time: 60.6 us; the launch traced here: 61.3 us
  starting transfers between devices  24.4 us (40%)
  waiting for transfers between devices  17.4 us (29%)
  Pallas kernels  11.3 us (19%)
  local copies, waits for them, and re-layouts  5.86 us (10%)
  other arithmetic  1.51 us (2%)
  between operations  0.76 us (1%)
    ppermute x7, starting transfers between devices, from_behind(): lax.ppermute(array, axis, [(i, (i + by) % devices) for i in range(devices)])  17.1 us
    ppermute x7, waiting for transfers between devices, from_behind(): lax.ppermute(array, axis, [(i, (i + by) % devices) for i in range(devices)])  10.4 us
    pallas_call x2, Pallas kernels, users_call(): pl.pallas_call(functools.partial(users_kernel, places, blocks, not carrie...  8.33 us
    ppermute x6, starting transfers between devices, swap(): return lax.ppermute(array, axis, [(i, i ^ bit) for i in range(devices)])  7.26 us
    ppermute x6, waiting for transfers between devices, swap(): return lax.ppermute(array, axis, [(i, i ^ bit) for i in range(devices)])  6.99 us
    unnamed x19, local copies, waits for them, and re-layouts  5.78 us
    pallas_call x1, Pallas kernels, pack(): pl.pallas_call(functools.partial(pack_kernel, work, groups), in_specs=[pl...  3 us
  transfers between devices with their start and end apart: 13, of which 5 were waited for; matrix products, arithmetic and copies ran while one was open for 1% of the time, Pallas kernels for 7%

profile of v7, /device:TPU:0, one launch (start us, length us, event | category | flops | bytes accessed | tf_op | source)
XLA Modules:
  0.0 61.3 jit_solution(10412756334583400724)
XLA Ops:
  0.6 3.0 %pack.1 = (bf16[520,128]{1,0:T(8,128)(2,1)}, bf16[520,128]{1,0:T(8,128)(2,1)}, bf16[520,128]{1,0:T(8,128)(2,1)}, bf16[520,128]{1,0:T(8,128)(2,1)}, bf16[520,128]...) custom-call(s32[1]{0:T(128)} %bitcast.12.group_ref, ...), custom_call_target="tpu_custom_call" | custom-call | tf_op jit(solution)/shard_map/pack/pallas_call | solution.py:108
  3.6 3.0 %collective-permute-start.4 = (bf16[256,512]{1,0:T(8,128)(2,1)}, bf16[256,512]{1,0:T(8,128)(2,1)S(1)}, u32[]{:S(2)}, u32[]{:S(2)}) collective-permute-start(bf16[256,512]{1,0:T(8,128)(2,1)} %get-tuple-element.25.refs_4_), channel_id=1, source_target_pairs={{0,2},{1,3},{2,0},{3,1},{4,6},{5,7},{6,4},{7,5},{8,10},{9,11},{10,... | collective-permute-start | bytes 786440 | tf_op jit(solution)/shard_map/ppermute | solution.py:20
  6.7 0.0 collective-permute-start.5
  6.7 2.6 %collective-permute-start.7 = (bf16[520,128]{1,0:T(8,128)(2,1)}, bf16[520,128]{1,0:T(8,128)(2,1)S(1)}, u32[]{:S(2)}, u32[]{:S(2)}) collective-permute-start(bf16[520,128]{1,0:T(8,128)(2,1)} %get-tuple-element.27), channel_id=1, source_target_pairs={{0,16},{4,20},{8,24},{12,28},{16,0},{20,4},{24,8},{28,12},{1,17},{... | collective-permute-start | bytes 399368 | tf_op jit(solution)/shard_map/ppermute | solution.py:25
  9.3 2.5 %collective-permute-start.8 = (bf16[520,128]{1,0:T(8,128)(2,1)}, bf16[520,128]{1,0:T(8,128)(2,1)S(1)}, u32[]{:S(2)}, u32[]{:S(2)}) collective-permute-start(bf16[520,128]{1,0:T(8,128)(2,1)} %get-tuple-element.28), channel_id=1, source_target_pairs={{0,12},{4,16},{8,20},{12,24},{16,28},{20,0},{24,4},{28,8},{1,13},{... | collective-permute-start | bytes 399368 | tf_op jit(solution)/shard_map/ppermute | solution.py:25
  11.8 1.3 %collective-permute-start.9 = (bf16[520,128]{1,0:T(8,128)(2,1)}, bf16[520,128]{1,0:T(8,128)(2,1)S(1)}, u32[]{:S(2)}, u32[]{:S(2)}) collective-permute-start(bf16[520,128]{1,0:T(8,128)(2,1)} %get-tuple-element.29), channel_id=1, source_target_pairs={{0,20},{4,24},{8,28},{12,0},{16,4},{20,8},{24,12},{28,16},{1,21},{... | collective-permute-start | bytes 399368 | tf_op jit(solution)/shard_map/ppermute | solution.py:25
  13.1 0.1 collective-permute-done.4.refs_5_
  13.2 0.0 collective-permute-start.6
  13.2 9.5 %collective-permute-done.7.refs_1_ = bf16[520,128]{1,0:T(8,128)(2,1)S(1)} collective-permute-done((bf16[520,128]{1,0:T(8,128)(2,1)}, bf16[520,128]{1,0:T(8,128)(2,1)S(1)}, u32[]{:S(2)}, u32[]{:S(2)}) %collective-permute-start.7) | collective-permute-done | bytes 133152 | tf_op jit(solution)/shard_map/ppermute | solution.py:25
  22.7 0.0 collective-permute-start
  22.7 0.9 %collective-permute-done.8.refs_2_ = bf16[520,128]{1,0:T(8,128)(2,1)S(1)} collective-permute-done((bf16[520,128]{1,0:T(8,128)(2,1)}, bf16[520,128]{1,0:T(8,128)(2,1)S(1)}, u32[]{:S(2)}, u32[]{:S(2)}) %collective-permute-start.8) | collective-permute-done | bytes 133152 | tf_op jit(solution)/shard_map/ppermute | solution.py:25
  23.6 6.0 %collective-permute-start.1 = (bf16[520,128]{1,0:T(8,128)(2,1)}, bf16[520,128]{1,0:T(8,128)(2,1)S(1)}, u32[]{:S(2)}, u32[]{:S(2)}) collective-permute-start(bf16[520,128]{1,0:T(8,128)(2,1)} %get-tuple-element.22), channel_id=1, source_target_pairs={{0,24},{4,28},{8,0},{12,4},{16,8},{20,12},{24,16},{28,20},{1,25},{... | collective-permute-start | bytes 399368 | tf_op jit(solution)/shard_map/ppermute | solution.py:25
  29.6 0.0 collective-permute-done.9.refs_3_
  29.6 0.0 collective-permute-start.2
  29.6 0.0 collective-permute-done.5.refs_6_
  29.6 4.7 %collective-permute-start.3 = (bf16[520,128]{1,0:T(8,128)(2,1)}, bf16[520,128]{1,0:T(8,128)(2,1)S(1)}, u32[]{:S(2)}, u32[]{:S(2)}) collective-permute-start(bf16[520,128]{1,0:T(8,128)(2,1)} %get-tuple-element.24), channel_id=1, source_target_pairs={{0,28},{4,0},{8,4},{12,8},{16,12},{20,16},{24,20},{28,24},{1,29},{... | collective-permute-start | bytes 399368 | tf_op jit(solution)/shard_map/ppermute | solution.py:25
  34.3 0.1 stack.51.id_ref
  34.4 0.0 collective-permute-done.6.refs_7_
  34.4 0.0 copy-start
  34.5 1.6 %copy-done = bf16[512,2048]{1,0:T(8,128)(2,1)S(1)} copy-done((bf16[512,2048]{1,0:T(8,128)(2,1)S(1)}, bf16[512,2048]{1,0:T(8,128)(2,1)}, u32[]{:S(2)}) %copy-start) | copy-done | bytes 2097176
  36.0 0.0 copy-start.2
  36.0 1.0 %copy-done.2 = bf16[512,512]{1,0:T(8,128)(2,1)S(1)} copy-done((bf16[512,512]{1,0:T(8,128)(2,1)S(1)}, bf16[512,512]{1,0:T(8,128)(2,1)}, u32[]{:S(2)}) %copy-start.2) | copy-done | bytes 524312
  37.1 0.0 copy-start.4
  37.1 0.9 %copy-done.4 = bf16[256,512]{1,0:T(8,128)(2,1)S(1)} copy-done((bf16[256,512]{1,0:T(8,128)(2,1)S(1)}, bf16[256,512]{1,0:T(8,128)(2,1)}, u32[]{:S(2)}) %copy-start.4) | copy-done | bytes 262168
  38.0 0.9 %copy-done.6 = bf16[520,128]{1,0:T(8,128)(2,1)S(1)} copy-done((bf16[520,128]{1,0:T(8,128)(2,1)S(1)}, bf16[520,128]{1,0:T(8,128)(2,1)}, u32[]{:S(2)}) %copy-start.6) | copy-done | bytes 133144
  38.9 0.7 %copy-done.7 = f32[4,128]{1,0:T(4,128)S(1)} copy-done((f32[4,128]{1,0:T(4,128)S(1)}, f32[4,128]{1,0:T(4,128)}, u32[]{:S(2)}) %copy-start.7) | copy-done | bytes 2072
  39.6 4.2 %users.2 = (f32[8,128]{1,0:T(8,128)S(1)}, f32[256,512]{1,0:T(8,128)S(1)}, f32[256,512]{1,0:T(8,128)S(1)}, f32[256,512]{1,0:T(8,128)S(1)}, f32[256,512]{1,0:T(8,128)S(1)}) custom-call(s32[12]{0:T(128)S(1)} %stack.51.id_ref, bf16[512,2048]{1,0:T(8,128)(2,1)S(1)} %copy-done, bf16[512,512]{1,0:T(8,128)(2,1)S(1)} %copy-done.2, f32[4,128]{1,0:T(4,128)S(1)} %copy-done.7, ...), custom_call_target="tpu_custom_call" | custom-call | tf_op jit(solution)/shard_map/users/pallas_call | solution.py:295
  43.8 0.0 collective-permute-done.refs_0_
  43.8 0.0 collective-permute-done.1.refs_1_
  43.8 0.0 collective-permute-done.2.refs_2_
  43.8 0.0 collective-permute-done.3.refs_3_
  43.8 0.0 copy-done.1
  43.8 0.0 copy-done.3
  43.8 0.0 copy-done.5
  43.9 0.0 copy-start.8
  43.9 4.2 %users.3 = (f32[8,128]{1,0:T(8,128)S(1)}, f32[256,512]{1,0:T(8,128)S(1)}, f32[256,512]{1,0:T(8,128)S(1)}, bf16[256,512]{1,0:T(8,128)(2,1)S(1)}, bf16[256,512]{1,0:T(8,128)(2,1)S(1)}) custom-call(s32[12]{0:T(128)S(1)} %stack.51.id_ref, bf16[512,2048]{1,0:T(8,128)(2,1)S(1)} %copy-done.1, bf16[512,512]{1,0:T(8,128)(2,1)S(1)} %copy-done.3, ...), custom_call_target="tpu_custom_call" | custom-call | tf_op jit(solution)/shard_map/users/pallas_call | solution.py:295
  48.0 0.1 collective-permute-start.11
  48.1 0.5 collective-permute-start.10
  48.6 1.0 %collective-permute-done.11 = bf16[256,512]{1,0:T(8,128)(2,1)S(1)} collective-permute-done((bf16[256,512]{1,0:T(8,128)(2,1)S(1)}, bf16[256,512]{1,0:T(8,128)(2,1)S(1)}, u32[]{:S(2)}, u32[]{:S(2)}) %collective-permute-start.11) | collective-permute-done | bytes 262176 | tf_op jit(solution)/shard_map/ppermute | solution.py:20
  49.6 0.1 add_convert_fusion
  49.7 3.7 %collective-permute-start.12 = (bf16[256,512]{1,0:T(8,128)(2,1)S(1)}, bf16[256,512]{1,0:T(8,128)(2,1)S(1)}, u32[]{:S(2)}, u32[]{:S(2)}) collective-permute-start(bf16[256,512]{1,0:T(8,128)(2,1)S(1)} %add_convert_fusion), channel_id=1, source_target_pairs={{0,2},{1,3},{2,0},{3,1},{4,6},{5,7},{6,4},{7,5},{8,10},{9,11},{10,... | collective-permute-start | bytes 786440 | tf_op jit(solution)/shard_map/ppermute | solution.py:20
  53.4 0.0 copy-done.8
  53.4 0.1 fusion
  53.5 0.6 copy.10
  54.1 0.0 collective-permute-done.10
  54.1 5.9 %collective-permute-done.12 = bf16[256,512]{1,0:T(8,128)(2,1)S(1)} collective-permute-done((bf16[256,512]{1,0:T(8,128)(2,1)S(1)}, bf16[256,512]{1,0:T(8,128)(2,1)S(1)}, u32[]{:S(2)}, u32[]{:S(2)}) %collective-permute-start.12) | collective-permute-done | bytes 262176 | tf_op jit(solution)/shard_map/ppermute | solution.py:20
  60.0 0.3 multiply_reduce_fusion
  60.2 1.0 %subtract_divide_fusion = f32[256,512]{1,0:T(8,128)} fusion(bf16[256,512]{1,0:T(8,128)(2,1)S(1)} %copy-done.8, f32[256]{0:T(256)S(1)} %multiply_reduce_fusion, f32[256]{0:T(256)S(1)} %add_sqrt_fusion, bf16[256,512]{1,0:T(8,128)(2,1)S(1)} %collective-permute-done.12, f32[256,512]{1,0:T(8,128)S(1)} %get-tuple-element.36, ...), kind=kLoop, calls=%fused_computation.3 | loop fusion | flops 1310720 | bytes 1837056 | tf_op jit(solution)/shard_map/div | solution.py:356
  (6 shorter events, 0.0 us)
Async XLA Ops:
  3.6 9.5 %collective-permute-start.4 = (bf16[256,512]{1,0:T(8,128)(2,1)}, bf16[256,512]{1,0:T(8,128)(2,1)S(1)}, u32[]{:S(2)}, u32[]{:S(2)}) collective-permute-start(bf16[256,512]{1,0:T(8,128)(2,1)} %get-tuple-element.25.refs_4_), channel_id=1, source_target_pairs={{0,2},{1,3},{2,0},{3,1},{4,6},{5,7},{6,4},{7,5},{8,10},{9,11},{10,... | collective-permute-start | bytes 786440 | tf_op jit(solution)/shard_map/ppermute | solution.py:20
  6.7 22.9 %collective-permute-start.5 = (bf16[256,512]{1,0:T(8,128)(2,1)}, bf16[256,512]{1,0:T(8,128)(2,1)S(1)}, u32[]{:S(2)}, u32[]{:S(2)}) collective-permute-start(bf16[256,512]{1,0:T(8,128)(2,1)} %get-tuple-element.25.refs_4_), channel_id=1, source_target_pairs={{0,1},{1,0},{2,3},{3,2},{4,5},{5,4},{6,7},{7,6},{8,9},{9,8},{10,11... | collective-permute-start | bytes 786440 | tf_op jit(solution)/shard_map/ppermute | solution.py:20
  6.7 16.0 %collective-permute-start.7 = (bf16[520,128]{1,0:T(8,128)(2,1)}, bf16[520,128]{1,0:T(8,128)(2,1)S(1)}, u32[]{:S(2)}, u32[]{:S(2)}) collective-permute-start(bf16[520,128]{1,0:T(8,128)(2,1)} %get-tuple-element.27), channel_id=1, source_target_pairs={{0,16},{4,20},{8,24},{12,28},{16,0},{20,4},{24,8},{28,12},{1,17},{... | collective-permute-start | bytes 399368 | tf_op jit(solution)/shard_map/ppermute | solution.py:25
  9.3 14.3 %collective-permute-start.8 = (bf16[520,128]{1,0:T(8,128)(2,1)}, bf16[520,128]{1,0:T(8,128)(2,1)S(1)}, u32[]{:S(2)}, u32[]{:S(2)}) collective-permute-start(bf16[520,128]{1,0:T(8,128)(2,1)} %get-tuple-element.28), channel_id=1, source_target_pairs={{0,12},{4,16},{8,20},{12,24},{16,28},{20,0},{24,4},{28,8},{1,13},{... | collective-permute-start | bytes 399368 | tf_op jit(solution)/shard_map/ppermute | solution.py:25
  11.8 17.8 %collective-permute-start.9 = (bf16[520,128]{1,0:T(8,128)(2,1)}, bf16[520,128]{1,0:T(8,128)(2,1)S(1)}, u32[]{:S(2)}, u32[]{:S(2)}) collective-permute-start(bf16[520,128]{1,0:T(8,128)(2,1)} %get-tuple-element.29), channel_id=1, source_target_pairs={{0,20},{4,24},{8,28},{12,0},{16,4},{20,8},{24,12},{28,16},{1,21},{... | collective-permute-start | bytes 399368 | tf_op jit(solution)/shard_map/ppermute | solution.py:25
  13.2 21.2 %collective-permute-start.6 = (bf16[256,512]{1,0:T(8,128)(2,1)S(1)}, bf16[256,512]{1,0:T(8,128)(2,1)S(1)}, u32[]{:S(2)}, u32[]{:S(2)}) collective-permute-start(bf16[256,512]{1,0:T(8,128)(2,1)S(1)} %collective-permute-done.4.refs_5_), channel_id=1, source_target_pairs={{0,1},{1,0},{2,3},{3,2},{4,5},{5,4},{6,7},{7,6},{8,9},{9,8},{10,11... | collective-permute-start | bytes 786440 | tf_op jit(solution)/shard_map/ppermute | solution.py:20
  22.7 21.1 %collective-permute-start = (bf16[520,128]{1,0:T(8,128)(2,1)}, bf16[520,128]{1,0:T(8,128)(2,1)S(1)}, u32[]{:S(2)}, u32[]{:S(2)}) collective-permute-start(bf16[520,128]{1,0:T(8,128)(2,1)} %get-tuple-element.21), channel_id=1, source_target_pairs={{0,8},{4,12},{8,16},{12,20},{16,24},{20,28},{24,0},{28,4},{1,9},{5... | collective-permute-start | bytes 399368 | tf_op jit(solution)/shard_map/ppermute | solution.py:25
  23.6 20.2 %collective-permute-start.1 = (bf16[520,128]{1,0:T(8,128)(2,1)}, bf16[520,128]{1,0:T(8,128)(2,1)S(1)}, u32[]{:S(2)}, u32[]{:S(2)}) collective-permute-start(bf16[520,128]{1,0:T(8,128)(2,1)} %get-tuple-element.22), channel_id=1, source_target_pairs={{0,24},{4,28},{8,0},{12,4},{16,8},{20,12},{24,16},{28,20},{1,25},{... | collective-permute-start | bytes 399368 | tf_op jit(solution)/shard_map/ppermute | solution.py:25
  29.6 14.2 %collective-permute-start.2 = (bf16[520,128]{1,0:T(8,128)(2,1)}, bf16[520,128]{1,0:T(8,128)(2,1)S(1)}, u32[]{:S(2)}, u32[]{:S(2)}) collective-permute-start(bf16[520,128]{1,0:T(8,128)(2,1)} %get-tuple-element.23), channel_id=1, source_target_pairs={{0,4},{4,8},{8,12},{12,16},{16,20},{20,24},{24,28},{28,0},{1,5},{5... | collective-permute-start | bytes 399368 | tf_op jit(solution)/shard_map/ppermute | solution.py:25
  29.6 14.2 %collective-permute-start.3 = (bf16[520,128]{1,0:T(8,128)(2,1)}, bf16[520,128]{1,0:T(8,128)(2,1)S(1)}, u32[]{:S(2)}, u32[]{:S(2)}) collective-permute-start(bf16[520,128]{1,0:T(8,128)(2,1)} %get-tuple-element.24), channel_id=1, source_target_pairs={{0,28},{4,0},{8,4},{12,8},{16,12},{20,16},{24,20},{28,24},{1,29},{... | collective-permute-start | bytes 399368 | tf_op jit(solution)/shard_map/ppermute | solution.py:25
  34.4 1.6 %copy-start = (bf16[512,2048]{1,0:T(8,128)(2,1)S(1)}, bf16[512,2048]{1,0:T(8,128)(2,1)}, u32[]{:S(2)}) copy-start(bf16[512,2048]{1,0:T(8,128)(2,1)} %w_in.3) | copy-start | bytes 6291460
  36.0 1.0 %copy-start.2 = (bf16[512,512]{1,0:T(8,128)(2,1)S(1)}, bf16[512,512]{1,0:T(8,128)(2,1)}, u32[]{:S(2)}) copy-start(bf16[512,512]{1,0:T(8,128)(2,1)} %w_out.3) | copy-start | bytes 1572868
  37.1 0.9 %copy-start.4 = (bf16[256,512]{1,0:T(8,128)(2,1)S(1)}, bf16[256,512]{1,0:T(8,128)(2,1)}, u32[]{:S(2)}) copy-start(bf16[256,512]{1,0:T(8,128)(2,1)} %get-tuple-element.25.refs_4_) | copy-start | bytes 786436
  38.0 0.9 %copy-start.6 = (bf16[520,128]{1,0:T(8,128)(2,1)S(1)}, bf16[520,128]{1,0:T(8,128)(2,1)}, u32[]{:S(2)}) copy-start(bf16[520,128]{1,0:T(8,128)(2,1)} %get-tuple-element.26.refs_0_) | copy-start | bytes 399364
  38.9 0.7 %copy-start.7 = (f32[4,128]{1,0:T(4,128)S(1)}, f32[4,128]{1,0:T(4,128)}, u32[]{:S(2)}) copy-start(f32[4,128]{1,0:T(4,128)} %bias_in.3) | copy-start | bytes 6148
  39.6 4.2 %copy-start.1 = (bf16[512,2048]{1,0:T(8,128)(2,1)S(1)}, bf16[512,2048]{1,0:T(8,128)(2,1)}, u32[]{:S(2)}) copy-start(bf16[512,2048]{1,0:T(8,128)(2,1)} %w_in.3) | copy-start | bytes 6291460
  39.6 4.2 %copy-start.3 = (bf16[512,512]{1,0:T(8,128)(2,1)S(1)}, bf16[512,512]{1,0:T(8,128)(2,1)}, u32[]{:S(2)}) copy-start(bf16[512,512]{1,0:T(8,128)(2,1)} %w_out.3) | copy-start | bytes 1572868
  39.6 4.2 %copy-start.5 = (bf16[256,512]{1,0:T(8,128)(2,1)S(1)}, bf16[256,512]{1,0:T(8,128)(2,1)}, u32[]{:S(2)}) copy-start(bf16[256,512]{1,0:T(8,128)(2,1)} %get-tuple-element.25.refs_4_) | copy-start | bytes 786436
  43.9 9.5 %copy-start.8 = (bf16[256,512]{1,0:T(8,128)(2,1)S(1)}, bf16[256,512]{1,0:T(8,128)(2,1)}, u32[]{:S(2)}) copy-start(bf16[256,512]{1,0:T(8,128)(2,1)} %pool_any.1) | copy-start | bytes 786436
  48.0 1.6 %collective-permute-start.11 = (bf16[256,512]{1,0:T(8,128)(2,1)S(1)}, bf16[256,512]{1,0:T(8,128)(2,1)S(1)}, u32[]{:S(2)}, u32[]{:S(2)}) collective-permute-start(bf16[256,512]{1,0:T(8,128)(2,1)S(1)} %get-tuple-element.39), channel_id=1, source_target_pairs={{0,1},{1,0},{2,3},{3,2},{4,5},{5,4},{6,7},{7,6},{8,9},{9,8},{10,11... | collective-permute-start | bytes 786440 | tf_op jit(solution)/shard_map/ppermute | solution.py:20
  48.1 6.0 %collective-permute-start.10 = (bf16[256,512]{1,0:T(8,128)(2,1)S(1)}, bf16[256,512]{1,0:T(8,128)(2,1)S(1)}, u32[]{:S(2)}, u32[]{:S(2)}) collective-permute-start(bf16[256,512]{1,0:T(8,128)(2,1)S(1)} %get-tuple-element.37), channel_id=1, source_target_pairs={{0,1},{1,0},{2,3},{3,2},{4,5},{5,4},{6,7},{7,6},{8,9},{9,8},{10,11... | collective-permute-start | bytes 786440 | tf_op jit(solution)/shard_map/ppermute | solution.py:20
  49.7 10.3 %collective-permute-start.12 = (bf16[256,512]{1,0:T(8,128)(2,1)S(1)}, bf16[256,512]{1,0:T(8,128)(2,1)S(1)}, u32[]{:S(2)}, u32[]{:S(2)}) collective-permute-start(bf16[256,512]{1,0:T(8,128)(2,1)S(1)} %add_convert_fusion), channel_id=1, source_target_pairs={{0,2},{1,3},{2,0},{3,1},{4,6},{5,7},{6,4},{7,5},{8,10},{9,11},{10,... | collective-permute-start | bytes 786440 | tf_op jit(solution)/shard_map/ppermute | solution.py:20

commit v8 on v7

--- a/solution.py
+++ b/solution.py
@@ -20,11 +20,6 @@
     return lax.ppermute(array, axis, [(i, i ^ bit) for i in range(devices)])
 
 
-def from_behind(array, axis, by):
-    devices = lax.axis_size(axis)
-    return lax.ppermute(array, axis, [(i, (i + by) % devices) for i in range(devices)])
-
-
 def in_vmem(array):
     return pltpu.with_memory_space_constraint(array, pltpu.VMEM)
 
@@ -43,11 +38,9 @@
 
 
 def pack_kernel(
-    work, groups, group_ref, list_any, len_any, from_any, tgt_any, pool_any, *refs,
+    group_ref, list_any, len_any, from_any, tgt_any, pool_any, to_any, own_any, unit_any,
+    entries, lens, targets, pool, unit, buffer, sems, in_sems, out_sems, own_sems,
 ):
-    users = from_any.shape[0]
-    to_refs, unit_any = refs[:users], refs[users]
-    entries, lens, targets, pool, unit, buffer, sems, in_sems, out_sems = refs[users + 1 :]
     users, length, width = from_any.shape
     pieces = width // length
     small = [
@@ -86,29 +79,38 @@
         buffer[u, width:, :] = numbers.astype(jnp.float32).astype(jnp.bfloat16)
     small[0].wait()
     copies_out = []
-    for k, (shift, slot) in enumerate(work):
-        user = entries[(group_ref[0] + shift) % groups * (users // groups) + slot]
+    for k in range(users):
+        user = entries[k]
         for c in range(pieces):
             pltpu.make_async_copy(
                 from_any.at[user, :, pl.ds(c * length, length)],
                 buffer.at[user, pl.ds(c * length, length)],
                 in_sems.at[user, c],
             ).wait()
-        copies_out.append(pltpu.make_async_copy(buffer.at[user], to_refs[k], out_sems.at[k]))
+        copies_out.append(pltpu.make_async_copy(buffer.at[user], to_any.at[k], out_sems.at[k]))
         copies_out[k].start()
+    own_slots = own_any.shape[0]
+    copies_own = [
+        pltpu.make_async_copy(
+            buffer.at[entries[group_ref[0] * own_slots + k]], own_any.at[k], own_sems.at[k]
+        )
+        for k in range(own_slots)
+    ]
+    for copy in copies_own:
+        copy.start()
     unit_out.wait()
-    for copy in copies_out:
+    for copy in copies_out + copies_own:
         copy.wait()
 
 
-def pack(histories, lengths, targets, entries, item_pool, work, groups, group):
+def pack(histories, lengths, targets, entries, item_pool, group, own_slots):
     users, length, width = histories.shape
     shape = (users, width + number_rows, length)
     hbm = pl.BlockSpec(memory_space=pltpu.HBM)
     return pl.pallas_call(
-        functools.partial(pack_kernel, work, groups),
+        pack_kernel,
         in_specs=[pl.BlockSpec(memory_space=pltpu.SMEM)] + [hbm] * 5,
-        out_specs=[hbm] * (users + 1),
+        out_specs=[hbm] * 3,
         scratch_shapes=[
             pltpu.SMEM(entries.shape, jnp.int32),
             pltpu.SMEM(lengths.shape, jnp.int32),
@@ -119,18 +121,21 @@
             pltpu.SemaphoreType.DMA((5,)),
             pltpu.SemaphoreType.DMA((users, width // length)),
             pltpu.SemaphoreType.DMA((users,)),
+            pltpu.SemaphoreType.DMA((own_slots,)),
         ],
-        out_shape=[pltpu.HBM(shape[1:], jnp.bfloat16)] * users + [pltpu.HBM(item_pool.shape, jnp.bfloat16)],
+        out_shape=[
+            pltpu.HBM(shape, jnp.bfloat16),
+            pltpu.HBM((own_slots,) + shape[1:], jnp.bfloat16),
+            pltpu.HBM(item_pool.shape, jnp.bfloat16),
+        ],
         compiler_params=pltpu.CompilerParams(vmem_limit_bytes=16 * 1024 * 1024),
         name="pack",
     )(group, *[in_hbm(array) for array in (entries, lengths, histories, targets, item_pool)])
 
 
-def users_kernel(
-    places, blocks, first, last, id_ref, w_in, w_out, bias_in, *refs,
-):
-    count = len(places)
-    x_refs, unit_refs, refs = refs[:count], refs[count : count + blocks], refs[count + blocks :]
+def users_kernel(blocks, own_slots, first, id_ref, x_ref, w_in, w_out, bias_in, *refs):
+    count = x_ref.shape[0]
+    unit_refs, refs = refs[:blocks], refs[blocks:]
     if not first:
         loss_in, sums_in, refs = refs[0], refs[1 : 1 + blocks], refs[1 + blocks :]
     loss_ref, out_refs, refs = refs[0], refs[1 : 1 + blocks], refs[1 + blocks :]
@@ -146,9 +151,13 @@
         wide = jnp.broadcast_to(0.5 * bias_in[h : h + 1, :], (length, length))
         turned = pltpu.roll(wide, 0, 1, stride=1, stride_axis=0).T
         bias[h] = jnp.concatenate([turned, turned], axis=1)
+    own = id_ref[blocks]
     for at in range(0, count, 8):
+        users = range(at, min(at + 8, count))
         users_step(
-            x_refs[at : at + 8], [id_ref[blocks + k] for k in places[at : at + 8]],
+            [x_ref.at[u] for u in users],
+            [own + u if first else u for u in users],
+            [1 if first else jnp.where((u >= own) & (u < own + own_slots), 0, 1) for u in users],
             [id_ref[k] for k in range(blocks)], w_in, w_out, unit_refs, loss_ref, sums, bias, *scratch,
         )
     for k in range(blocks):
@@ -157,24 +166,23 @@
 
 
 def users_step(
-    x_refs, spots, block_ids, w_in, w_out, unit_refs, loss_ref, sums, bias,
+    x_refs, spots, to_do, block_ids, w_in, w_out, unit_refs, loss_ref, sums, bias,
     exp_ref, residual, events, starts_ref, key, value, packed_tgt, packed_loss,
 ):
     heads, length, _ = bias.shape
     width = w_out.shape[0]
     hdim = width // heads
     items = unit_refs[0].shape[0]
-    lines = tile // length
     per_step = len(x_refs)
 
     digits = [ref[width:, :].astype(jnp.float32) for ref in x_refs]
-    lens = [jnp.max(digit[:1, :]).astype(jnp.int32) for digit in digits]
+    lens = [jnp.max(digit[:1, :]).astype(jnp.int32) * flag for digit, flag in zip(digits, to_do)]
     starts, end = [], 0
     for u in range(per_step):
         starts.append(pl.multiple_of(end, chunk) if u else 0)
         end = end + (lens[u] + chunk - 1) // chunk * chunk
     end = pl.multiple_of(end, chunk)
-    tiles = (end + tile - 1) // tile
+    strips = (end + length - 1) // length
 
     place = lax.broadcasted_iota(jnp.int32, (1, length), 1)
     packed_tgt[...] = jnp.full_like(packed_tgt, -1)
@@ -197,11 +205,12 @@
 
     row = lax.broadcasted_iota(jnp.int32, (length, length), 0)
     col = lax.broadcasted_iota(jnp.int32, (length, length), 1)
-    item_id = lax.broadcasted_iota(jnp.int32, (items, tile), 0)
     rate = logit_scale * math.log2(math.e)
 
-    def one_tile(t, _):
-        first = pl.multiple_of(t * tile, tile)
+    def one_tile(strip, lines):
+        tile = lines * length
+        first = pl.multiple_of(strip * length, length)
+        item_id = lax.broadcasted_iota(jnp.int32, (items, tile), 0)
         x = events[pl.ds(first, tile), :].astype(jnp.float32)
         center, spread = center_and_spread(x)
         half_normed = (center * (0.5 * lax.rsqrt(spread + 1e-05))).astype(jnp.bfloat16)
@@ -221,8 +230,8 @@
             base = pl.multiple_of(first + k * length, length)
             sources = pl.ds(base, 2 * length)
             start = starts_ref[pl.ds(base, length), :]
-            ahead = packed_tgt[pl.ds(t * lines + k, 1), :] >= 0
-            here = packed_tgt[pl.ds(t * lines + k + 1, 1), :] >= 0
+            ahead = packed_tgt[pl.ds(strip + k, 1), :] >= 0
+            here = packed_tgt[pl.ds(strip + k + 1, 1), :] >= 0
             keep_ahead = (base - length + col >= start) & ahead
             keep_here = (col <= row) & (base + col >= start) & here
             keep = jnp.concatenate([keep_ahead, keep_here], axis=1)
@@ -246,7 +255,7 @@
         queries = (out * lax.rsqrt(square + 1e-06)).astype(jnp.bfloat16)
 
         target = jnp.concatenate(
-            [packed_tgt[pl.ds(t * lines + k + 1, 1), :] for k in range(lines)], axis=1
+            [packed_tgt[pl.ds(strip + k + 1, 1), :] for k in range(lines)], axis=1
         )
         total = jnp.zeros((1, tile), jnp.float32)
         target_dot = jnp.zeros((1, tile), jnp.float32)
@@ -255,23 +264,28 @@
                 unit_refs[j][...], queries, contract_last, preferred_element_type=jnp.float32
             )
             exps = jnp.exp2(dots * rate - rate)
-            exp_ref[j] = exps
+            exp_ref[j, :, :tile] = exps
             total += jnp.sum(exps, axis=0, keepdims=True)
             hit = item_id == target - block * items
             target_dot += jnp.sum(jnp.where(hit, dots, 0.0), axis=0, keepdims=True)
         loss = logit_scale + jnp.log(total) - logit_scale * target_dot
         for k in range(lines):
-            packed_loss[pl.ds(t * lines + k, 1), :] = loss[:, k * length : (k + 1) * length]
+            packed_loss[pl.ds(strip + k, 1), :] = loss[:, k * length : (k + 1) * length]
         share = jnp.where(target >= 0, 1.0 / total, 0.0)
         for j, block in enumerate(block_ids):
             hit = item_id == target - block * items
-            left = exp_ref[j] * share - jnp.where(hit, 1.0, 0.0)
-            residual[j] = left.astype(jnp.bfloat16)
+            left = exp_ref[j, :, :tile] * share - jnp.where(hit, 1.0, 0.0)
+            residual[j, :, :tile] = left.astype(jnp.bfloat16)
         for j in range(len(block_ids)):
-            sums[j][...] += jnp.dot(residual[j], queries, preferred_element_type=jnp.float32)
+            sums[j][...] += jnp.dot(residual[j, :, :tile], queries, preferred_element_type=jnp.float32)
+
+    def full_tile(t, _):
+        one_tile(t * (tile // length), tile // length)
         return 0
 
-    lax.fori_loop(0, tiles, one_tile, 0)
+    full = strips // (tile // length)
+    lax.fori_loop(0, full, full_tile, 0)
+    pl.when(strips % (tile // length) != 0)(lambda: one_tile(full * (tile // length), 1))
 
     for u in range(per_step):
         line, turn = starts[u] // length, lax.rem(starts[u], length)
@@ -279,21 +293,21 @@
         near = pltpu.roll(packed_loss[pl.ds(line, 1), :], back, 1)
         rest = pltpu.roll(packed_loss[pl.ds(line + 1, 1), :], back, 1)
         loss = jnp.where(place < length - turn, near, rest)
-        loss_ref[pl.ds(spots[u], 1), :] = jnp.where(place < lens[u], loss, 0.0)
-
-
-def users_call(ids, places, users, packed, units, w_in, w_out, rel_bias, carried, last):
+        loss_ref[pl.ds(spots[u], 1), :] += jnp.where(place < lens[u], loss, 0.0)
+
+
+def users_call(ids, users, packed, units, w_in, w_out, rel_bias, own_slots, carried):
     heads, length = rel_bias.shape
     width = w_out.shape[0]
     blocks = len(units)
     items = units[0].shape[0]
-    rows = -(-min(len(places), 8) * length // tile) * tile
+    rows = -(-min(packed.shape[0], 8) * length // tile) * tile
     lines = -(-(rows // length + 2) // 8) * 8
     whole = pl.BlockSpec(memory_space=pltpu.VMEM)
-    arrays = [w_in, w_out, rel_bias, *packed, *units, *carried]
-    narrow = lambda k: last and k >= blocks // 2
+    arrays = [packed, w_in, w_out, rel_bias, *units, *carried]
+    dtype_of = lambda k: jnp.bfloat16 if carried and k >= blocks // 2 else jnp.float32
     return pl.pallas_call(
-        functools.partial(users_kernel, places, blocks, not carried, last),
+        functools.partial(users_kernel, blocks, own_slots, not carried),
         in_specs=[pl.BlockSpec(memory_space=pltpu.SMEM)] + [whole] * len(arrays),
         out_specs=[whole] * (1 + blocks),
         scratch_shapes=[
@@ -309,9 +323,7 @@
             pltpu.VMEM((lines, length), jnp.float32),
         ],
         out_shape=[pltpu.VMEM((users, length), jnp.float32)]
-        + [
-            pltpu.VMEM((items, width), jnp.bfloat16 if narrow(k) else jnp.float32) for k in range(blocks)
-        ],
+        + [pltpu.VMEM((items, width), dtype_of(k)) for k in range(blocks)],
         compiler_params=pltpu.CompilerParams(vmem_limit_bytes=24 * 1024 * 1024),
         name="users",
     )(ids, *[in_vmem(array) for array in arrays])
@@ -319,36 +331,23 @@
 
 def shards(histories, lengths, targets, send_list, w_in, w_out, rel_bias, item_pool):
     user_count = histories.shape[0]
-    groups = lax.axis_size("dp")
-    slots = user_count // groups
+    own_slots = user_count // lax.axis_size("dp")
     group, mine = lax.axis_index("dp").astype(jnp.int32), lax.axis_index("blk").astype(jnp.int32)
-
-    work = sorted(
-        ((shift, slot) for shift in range(groups) for slot in range(slots)),
-        key=lambda pair: (pair[0] != 0, abs(pair[0] - groups / 2)),
+    packed, own_users, unit = pack(
+        histories, lengths, targets, send_list, item_pool, group.reshape(1), own_slots
     )
-    *packed, unit = pack(
-        histories, lengths, targets, send_list, item_pool, work, groups, group.reshape(1)
-    )
+    routed = lax.all_to_all(packed, "dp", split_axis=0, concat_axis=0, tiled=True)
     over_unit = swap(unit, "blk", 2)
-    packed = [
-        users if shift == 0 else from_behind(users, "dp", shift) for users, (shift, _) in zip(packed, work)
-    ]
     units = [unit, over_unit, swap(unit, "blk", 1), swap(over_unit, "blk", 1)]
 
     pool_float = item_pool.astype(jnp.float32)
     item_norm = jnp.sqrt(jnp.sum(pool_float * pool_float, axis=-1, keepdims=True) + 1e-06)
     unit_rows = pool_float / item_norm
 
-    came = [((group - shift) % groups) * slots + slot for shift, slot in work]
-    ids = jnp.stack([mine, mine ^ 2, mine ^ 1, mine ^ 3, *came])
-    half = user_count // 2
-    order = tuple(range(user_count))
-    carried = users_call(
-        ids, order[:half], user_count, packed[:half], units, w_in, w_out, rel_bias, (), False
-    )
+    ids = jnp.stack([mine, mine ^ 2, mine ^ 1, mine ^ 3, group * own_slots])
+    carried = users_call(ids, user_count, own_users, units, w_in, w_out, rel_bias, own_slots, ())
     row_loss, own, over, side, far = users_call(
-        ids, order[half:], user_count, packed[half:], units, w_in, w_out, rel_bias, carried, True
+        ids, user_count, routed, units, w_in, w_out, rel_bias, own_slots, carried
     )
     over = over + swap(far, "blk", 1).astype(jnp.float32)
     own = own + swap(side, "blk", 1).astype(jnp.float32)

time: 60.6 us -> 61.2 us (level)
  the two profiles are of different devices: /device:TPU:0 before, /device:TPU:6 now
where the time goes in v8:
time: 61.2 us; the launch traced here: 60.6 us
  waiting for transfers between devices  22 us (36%)
  local copies, waits for them, and re-layouts  14.6 us (24%)
  Pallas kernels  14.2 us (23%)
  starting transfers between devices  7.63 us (12%)
  other arithmetic  1.47 us (2%)
  between operations  0.75 us (1%)
    ppermute x6, waiting for transfers between devices, swap(): return lax.ppermute(array, axis, [(i, i ^ bit) for i in range(devices)])  16.7 us
    unnamed x39, local copies, waits for them, and re-layouts  14.5 us
    pallas_call x2, Pallas kernels, users_call(): pl.pallas_call(functools.partial(users_kernel, blocks, own_slots, not car...  11.1 us
    all_to_all x1, starting transfers between devices, shards(): lax.all_to_all(packed, 'dp', split_axis=0, concat_axis=0, tiled=True)  6.48 us
    all_to_all x1, waiting for transfers between devices, shards(): lax.all_to_all(packed, 'dp', split_axis=0, concat_axis=0, tiled=True)  5.3 us
    pallas_call x1, Pallas kernels, pack(): pl.pallas_call(pack_kernel, in_specs=[pl.BlockSpec(memory_space=pltpu.SME...  3.05 us
  transfers between devices with their start and end apart: 7, of which 5 were waited for; matrix products, arithmetic and copies ran while one was open for 1% of the time, Pallas kernels for 6%

profile of v8, /device:TPU:6, one launch (start us, length us, event | category | flops | bytes accessed | tf_op | source)
XLA Modules:
  0.0 60.6 jit_solution(3316986129339736379)
XLA Ops:
  0.6 3.0 %pack.1 = (bf16[8,520,128]{2,1,0:T(8,128)(2,1)}, bf16[1,520,128]{2,1,0:T(8,128)(2,1)}, bf16[256,512]{1,0:T(8,128)(2,1)}) custom-call(s32[1]{0:T(128)} %bitcast.4.group_ref, s32[8]{0:T(128)} %list_any.1, s32[8]{0:T(128)} %len_any.1, bf16[8,128,512]{2,1,0:T(8,128)(2,1)} %from_any.1, s32[8,128]{1,0:T(8,128)} %tgt_any.1, bf16[256,512]{1,0:T(8,128)(2,1)} %pool_any.1), custom_call_target="tpu_custom_call" | custom-call | tf_op jit(solution)/shard_map/pack/pallas_call | solution.py:110
  3.7 0.0 copy-start
  3.7 0.0 copy-start.17
  3.7 6.5 %all-to-all-start = ((bf16[8,520,128]{2,1,0:T(8,128)(2,1)}), bf16[8,520,128]{2,1,0:T(8,128)(2,1)S(1)}, u32[]{:S(2)}, u32[]{:S(2)}) async-start(bf16[8,520,128]{2,1,0:T(8,128)(2,1)} %get-tuple-element.15), calls=%async_computation | async-start | bytes 2129920 | tf_op jit(solution)/shard_map/all_to_all | solution.py:339
  10.2 0.5 collective-permute-start
  10.7 0.0 collective-permute-start.1
  10.7 7.2 %collective-permute-done.refs_1_ = bf16[256,512]{1,0:T(8,128)(2,1)S(1)} collective-permute-done((bf16[256,512]{1,0:T(8,128)(2,1)}, bf16[256,512]{1,0:T(8,128)(2,1)S(1)}, u32[]{:S(2)}, u32[]{:S(2)}) %collective-permute-start) | collective-permute-done | bytes 262176 | tf_op jit(solution)/shard_map/ppermute | solution.py:20
  17.9 0.0 collective-permute-start.2
  17.9 0.0 copy-start.5
  17.9 0.7 %copy-done.5 = bf16[256,512]{1,0:T(8,128)(2,1)} copy-done((bf16[256,512]{1,0:T(8,128)(2,1)}, bf16[256,512]{1,0:T(8,128)(2,1)S(1)}, u32[]{:S(2)}) %copy-start.5) | copy-done | bytes 262168
  18.6 0.1 stack.23.id_ref
  18.7 0.0 collective-permute-done.1.refs_2_
  18.7 0.9 %collective-permute-done.2.refs_3_ = bf16[256,512]{1,0:T(8,128)(2,1)} collective-permute-done((bf16[256,512]{1,0:T(8,128)(2,1)S(1)}, bf16[256,512]{1,0:T(8,128)(2,1)}, u32[]{:S(2)}, u32[]{:S(2)}) %collective-permute-start.2) | collective-permute-done | bytes 262176 | tf_op jit(solution)/shard_map/ppermute | solution.py:20
  19.6 0.0 copy-done
  19.6 0.0 copy-done.17
  19.6 0.0 copy-start.1
  19.6 1.0 %copy-done.1 = bf16[512,512]{1,0:T(8,128)(2,1)S(1)} copy-done((bf16[512,512]{1,0:T(8,128)(2,1)S(1)}, bf16[512,512]{1,0:T(8,128)(2,1)}, u32[]{:S(2)}) %copy-start.1) | copy-done | bytes 524312
  20.6 0.9 %copy-done.3 = bf16[256,512]{1,0:T(8,128)(2,1)S(1)} copy-done((bf16[256,512]{1,0:T(8,128)(2,1)S(1)}, bf16[256,512]{1,0:T(8,128)(2,1)}, u32[]{:S(2)}) %copy-start.3) | copy-done | bytes 262168
  21.6 0.9 %copy-done.6 = bf16[256,512]{1,0:T(8,128)(2,1)S(1)} copy-done((bf16[256,512]{1,0:T(8,128)(2,1)S(1)}, bf16[256,512]{1,0:T(8,128)(2,1)}, u32[]{:S(2)}) %copy-start.6) | copy-done | bytes 262168
  22.5 0.9 %copy-done.16 = bf16[1,520,128]{2,1,0:T(8,128)(2,1)S(1)} copy-done((bf16[1,520,128]{2,1,0:T(8,128)(2,1)S(1)}, bf16[1,520,128]{2,1,0:T(8,128)(2,1)}, u32[]{:S(2)}) %copy-start.16) | copy-done | bytes 133144
  23.4 3.8 %users.2 = (f32[8,128]{1,0:T(8,128)S(1)}, f32[256,512]{1,0:T(8,128)S(1)}, f32[256,512]{1,0:T(8,128)S(1)}, f32[256,512]{1,0:T(8,128)S(1)}, f32[256,512]{1,0:T(8,128)S(1)}) custom-call(s32[5]{0:T(128)S(1)} %stack.23.id_ref, bf16[1,520,128]{2,1,0:T(8,128)(2,1)S(1)} %copy-done.16, bf16[512,2048]{1,0:T(8,128)(2,1)S(1)} %copy-done, ...), custom_call_target="tpu_custom_call" | custom-call | tf_op jit(solution)/shard_map/users/pallas_call | solution.py:309
  27.2 0.0 copy-start.8
  27.2 0.8 %copy-done.8 = f32[256,512]{1,0:T(8,128)} copy-done((f32[256,512]{1,0:T(8,128)}, f32[256,512]{1,0:T(8,128)S(1)}, u32[]{:S(2)}) %copy-start.8) | copy-done | bytes 524312
  28.0 0.8 %copy-done.10 = f32[256,512]{1,0:T(8,128)} copy-done((f32[256,512]{1,0:T(8,128)}, f32[256,512]{1,0:T(8,128)S(1)}, u32[]{:S(2)}) %copy-start.10) | copy-done | bytes 524312
  28.8 0.8 %copy-done.12 = f32[256,512]{1,0:T(8,128)} copy-done((f32[256,512]{1,0:T(8,128)}, f32[256,512]{1,0:T(8,128)S(1)}, u32[]{:S(2)}) %copy-start.12) | copy-done | bytes 524312
  29.6 0.8 %copy-done.14 = f32[256,512]{1,0:T(8,128)} copy-done((f32[256,512]{1,0:T(8,128)}, f32[256,512]{1,0:T(8,128)S(1)}, u32[]{:S(2)}) %copy-start.14) | copy-done | bytes 524312
  30.4 5.3 %all-to-all-done.x_ref = bf16[8,520,128]{2,1,0:T(8,128)(2,1)S(1)} async-done(((bf16[8,520,128]{2,1,0:T(8,128)(2,1)}), bf16[8,520,128]{2,1,0:T(8,128)(2,1)S(1)}, u32[]{:S(2)}, u32[]{:S(2)}) %all-to-all-start) | async-done | bytes 1064992 | tf_op jit(solution)/shard_map/all_to_all | solution.py:339
  35.7 0.0 copy-done.4
  35.7 1.0 %copy-done.2 = bf16[512,512]{1,0:T(8,128)(2,1)S(1)} copy-done((bf16[512,512]{1,0:T(8,128)(2,1)S(1)}, bf16[512,512]{1,0:T(8,128)(2,1)}, u32[]{:S(2)}) %copy-start.2) | copy-done | bytes 524312
  36.8 0.9 %copy-done.7 = bf16[256,512]{1,0:T(8,128)(2,1)S(1)} copy-done((bf16[256,512]{1,0:T(8,128)(2,1)S(1)}, bf16[256,512]{1,0:T(8,128)(2,1)}, u32[]{:S(2)}) %copy-start.7) | copy-done | bytes 262168
  37.7 1.0 %copy-done.9 = f32[256,512]{1,0:T(8,128)S(1)} copy-done((f32[256,512]{1,0:T(8,128)S(1)}, f32[256,512]{1,0:T(8,128)}, u32[]{:S(2)}) %copy-start.9) | copy-done | bytes 524312
  38.8 1.0 %copy-done.11 = f32[256,512]{1,0:T(8,128)S(1)} copy-done((f32[256,512]{1,0:T(8,128)S(1)}, f32[256,512]{1,0:T(8,128)}, u32[]{:S(2)}) %copy-start.11) | copy-done | bytes 524312
  39.8 1.0 %copy-done.13 = f32[256,512]{1,0:T(8,128)S(1)} copy-done((f32[256,512]{1,0:T(8,128)S(1)}, f32[256,512]{1,0:T(8,128)}, u32[]{:S(2)}) %copy-start.13) | copy-done | bytes 524312
  40.8 1.0 %copy-done.15 = f32[256,512]{1,0:T(8,128)S(1)} copy-done((f32[256,512]{1,0:T(8,128)S(1)}, f32[256,512]{1,0:T(8,128)}, u32[]{:S(2)}) %copy-start.15) | copy-done | bytes 524312
  41.9 7.3 %users.3 = (f32[8,128]{1,0:T(8,128)S(1)}, f32[256,512]{1,0:T(8,128)S(1)}, f32[256,512]{1,0:T(8,128)S(1)}, bf16[256,512]{1,0:T(8,128)(2,1)S(1)}, bf16[256,512]{1,0:T(8,128)(2,1)S(1)}) custom-call(s32[5]{0:T(128)S(1)} %stack.23.id_ref, bf16[8,520,128]{2,1,0:T(8,128)(2,1)S(1)} %all-to-all-done.x_ref, bf16[512,2048]{1,0:T(8,128)(2,1)S(1)} %copy-done, ...), custom_call_target="tpu_custom_call" | custom-call | tf_op jit(solution)/shard_map/users/pallas_call | solution.py:309
  49.2 0.0 copy-start.18
  49.2 0.1 collective-permute-start.4
  49.3 0.5 collective-permute-start.3
  49.8 1.0 %collective-permute-done.4 = bf16[256,512]{1,0:T(8,128)(2,1)S(1)} collective-permute-done((bf16[256,512]{1,0:T(8,128)(2,1)S(1)}, bf16[256,512]{1,0:T(8,128)(2,1)S(1)}, u32[]{:S(2)}, u32[]{:S(2)}) %collective-permute-start.4) | collective-permute-done | bytes 262176 | tf_op jit(solution)/shard_map/ppermute | solution.py:20
  50.8 0.1 add_convert_fusion
  50.9 0.1 collective-permute-start.5
  51.0 0.0 copy-done.18
  51.0 0.1 fusion
  51.1 0.6 copy.10
  51.7 0.0 collective-permute-done.3
  51.7 7.6 %collective-permute-done.5 = bf16[256,512]{1,0:T(8,128)(2,1)S(1)} collective-permute-done((bf16[256,512]{1,0:T(8,128)(2,1)S(1)}, bf16[256,512]{1,0:T(8,128)(2,1)S(1)}, u32[]{:S(2)}, u32[]{:S(2)}) %collective-permute-start.5) | collective-permute-done | bytes 262176 | tf_op jit(solution)/shard_map/ppermute | solution.py:20
  59.3 0.3 multiply_reduce_fusion
  59.6 1.0 %subtract_divide_fusion = f32[256,512]{1,0:T(8,128)} fusion(bf16[256,512]{1,0:T(8,128)(2,1)S(1)} %copy-done.18, f32[256]{0:T(256)S(1)} %multiply_reduce_fusion, f32[256]{0:T(256)S(1)} %add_sqrt_fusion, bf16[256,512]{1,0:T(8,128)(2,1)S(1)} %collective-permute-done.5, f32[256,512]{1,0:T(8,128)S(1)} %get-tuple-element.24, ...), kind=kLoop, calls=%fused_computation.3 | loop fusion | flops 1310720 | bytes 1837056 | tf_op jit(solution)/shard_map/div | solution.py:355
  (14 shorter events, 0.0 us)
Async XLA Ops:
  3.7 15.9 %copy-start = (bf16[512,2048]{1,0:T(8,128)(2,1)S(1)}, bf16[512,2048]{1,0:T(8,128)(2,1)}, u32[]{:S(2)}) copy-start(bf16[512,2048]{1,0:T(8,128)(2,1)} %w_in.3) | copy-start | bytes 6291460
  3.7 15.9 %copy-start.17 = (f32[4,128]{1,0:T(4,128)S(1)}, f32[4,128]{1,0:T(4,128)}, u32[]{:S(2)}) copy-start(f32[4,128]{1,0:T(4,128)} %bias_in.3) | copy-start | bytes 6148
  3.7 32.0 %all-to-all-start = ((bf16[8,520,128]{2,1,0:T(8,128)(2,1)}), bf16[8,520,128]{2,1,0:T(8,128)(2,1)S(1)}, u32[]{:S(2)}, u32[]{:S(2)}) async-start(bf16[8,520,128]{2,1,0:T(8,128)(2,1)} %get-tuple-element.15), calls=%async_computation | async-start | bytes 2129920 | tf_op jit(solution)/shard_map/all_to_all | solution.py:339
  10.2 7.7 %collective-permute-start = (bf16[256,512]{1,0:T(8,128)(2,1)}, bf16[256,512]{1,0:T(8,128)(2,1)S(1)}, u32[]{:S(2)}, u32[]{:S(2)}) collective-permute-start(bf16[256,512]{1,0:T(8,128)(2,1)} %get-tuple-element.16.refs_0_), channel_id=1, source_target_pairs={{0,2},{1,3},{2,0},{3,1},{4,6},{5,7},{6,4},{7,5},{8,10},{9,11},{10,... | collective-permute-start | bytes 786440 | tf_op jit(solution)/shard_map/ppermute | solution.py:20
  10.7 8.0 %collective-permute-start.1 = (bf16[256,512]{1,0:T(8,128)(2,1)}, bf16[256,512]{1,0:T(8,128)(2,1)}, u32[]{:S(2)}, u32[]{:S(2)}) collective-permute-start(bf16[256,512]{1,0:T(8,128)(2,1)} %get-tuple-element.16.refs_0_), channel_id=1, source_target_pairs={{0,1},{1,0},{2,3},{3,2},{4,5},{5,4},{6,7},{7,6},{8,9},{9,8},{10,11... | collective-permute-start | bytes 786440 | tf_op jit(solution)/shard_map/ppermute | solution.py:20
  17.9 1.7 %collective-permute-start.2 = (bf16[256,512]{1,0:T(8,128)(2,1)S(1)}, bf16[256,512]{1,0:T(8,128)(2,1)}, u32[]{:S(2)}, u32[]{:S(2)}) collective-permute-start(bf16[256,512]{1,0:T(8,128)(2,1)S(1)} %collective-permute-done.refs_1_), channel_id=1, source_target_pairs={{0,1},{1,0},{2,3},{3,2},{4,5},{5,4},{6,7},{7,6},{8,9},{9,8},{10,11... | collective-permute-start | bytes 786440 | tf_op jit(solution)/shard_map/ppermute | solution.py:20
  17.9 0.7 %copy-start.5 = (bf16[256,512]{1,0:T(8,128)(2,1)}, bf16[256,512]{1,0:T(8,128)(2,1)S(1)}, u32[]{:S(2)}) copy-start(bf16[256,512]{1,0:T(8,128)(2,1)S(1)} %collective-permute-done.refs_1_) | copy-start | bytes 786436
  19.6 1.0 %copy-start.1 = (bf16[512,512]{1,0:T(8,128)(2,1)S(1)}, bf16[512,512]{1,0:T(8,128)(2,1)}, u32[]{:S(2)}) copy-start(bf16[512,512]{1,0:T(8,128)(2,1)} %w_out.3) | copy-start | bytes 1572868
  20.6 0.9 %copy-start.3 = (bf16[256,512]{1,0:T(8,128)(2,1)S(1)}, bf16[256,512]{1,0:T(8,128)(2,1)}, u32[]{:S(2)}) copy-start(bf16[256,512]{1,0:T(8,128)(2,1)} %get-tuple-element.16.refs_0_) | copy-start | bytes 786436
  21.6 0.9 %copy-start.6 = (bf16[256,512]{1,0:T(8,128)(2,1)S(1)}, bf16[256,512]{1,0:T(8,128)(2,1)}, u32[]{:S(2)}) copy-start(bf16[256,512]{1,0:T(8,128)(2,1)} %copy-done.5) | copy-start | bytes 786436
  22.5 0.9 %copy-start.16 = (bf16[1,520,128]{2,1,0:T(8,128)(2,1)S(1)}, bf16[1,520,128]{2,1,0:T(8,128)(2,1)}, u32[]{:S(2)}) copy-start(bf16[1,520,128]{2,1,0:T(8,128)(2,1)} %get-tuple-element.17.x_ref) | copy-start | bytes 399364
  23.4 12.3 %copy-start.4 = (bf16[256,512]{1,0:T(8,128)(2,1)S(1)}, bf16[256,512]{1,0:T(8,128)(2,1)}, u32[]{:S(2)}) copy-start(bf16[256,512]{1,0:T(8,128)(2,1)} %get-tuple-element.16.refs_0_) | copy-start | bytes 786436
  27.2 0.8 %copy-start.8 = (f32[256,512]{1,0:T(8,128)}, f32[256,512]{1,0:T(8,128)S(1)}, u32[]{:S(2)}) copy-start(f32[256,512]{1,0:T(8,128)S(1)} %get-tuple-element.19.refs_5_) | copy-start | bytes 1572868
  28.0 0.8 %copy-start.10 = (f32[256,512]{1,0:T(8,128)}, f32[256,512]{1,0:T(8,128)S(1)}, u32[]{:S(2)}) copy-start(f32[256,512]{1,0:T(8,128)S(1)} %get-tuple-element.20.refs_6_) | copy-start | bytes 1572868
  28.8 0.8 %copy-start.12 = (f32[256,512]{1,0:T(8,128)}, f32[256,512]{1,0:T(8,128)S(1)}, u32[]{:S(2)}) copy-start(f32[256,512]{1,0:T(8,128)S(1)} %get-tuple-element.21.refs_7_) | copy-start | bytes 1572868
  29.6 0.8 %copy-start.14 = (f32[256,512]{1,0:T(8,128)}, f32[256,512]{1,0:T(8,128)S(1)}, u32[]{:S(2)}) copy-start(f32[256,512]{1,0:T(8,128)S(1)} %get-tuple-element.22.refs_8_) | copy-start | bytes 1572868
  35.7 1.0 %copy-start.2 = (bf16[512,512]{1,0:T(8,128)(2,1)S(1)}, bf16[512,512]{1,0:T(8,128)(2,1)}, u32[]{:S(2)}) copy-start(bf16[512,512]{1,0:T(8,128)(2,1)} %w_out.3) | copy-start | bytes 1572868
  36.8 0.9 %copy-start.7 = (bf16[256,512]{1,0:T(8,128)(2,1)S(1)}, bf16[256,512]{1,0:T(8,128)(2,1)}, u32[]{:S(2)}) copy-start(bf16[256,512]{1,0:T(8,128)(2,1)} %copy-done.5) | copy-start | bytes 786436
  37.7 1.0 %copy-start.9 = (f32[256,512]{1,0:T(8,128)S(1)}, f32[256,512]{1,0:T(8,128)}, u32[]{:S(2)}) copy-start(f32[256,512]{1,0:T(8,128)} %copy-done.8) | copy-start | bytes 1572868
  38.8 1.0 %copy-start.11 = (f32[256,512]{1,0:T(8,128)S(1)}, f32[256,512]{1,0:T(8,128)}, u32[]{:S(2)}) copy-start(f32[256,512]{1,0:T(8,128)} %copy-done.10) | copy-start | bytes 1572868
  39.8 1.0 %copy-start.13 = (f32[256,512]{1,0:T(8,128)S(1)}, f32[256,512]{1,0:T(8,128)}, u32[]{:S(2)}) copy-start(f32[256,512]{1,0:T(8,128)} %copy-done.12) | copy-start | bytes 1572868
  40.8 1.0 %copy-start.15 = (f32[256,512]{1,0:T(8,128)S(1)}, f32[256,512]{1,0:T(8,128)}, u32[]{:S(2)}) copy-start(f32[256,512]{1,0:T(8,128)} %copy-done.14) | copy-start | bytes 1572868
  49.2 1.8 %copy-start.18 = (bf16[256,512]{1,0:T(8,128)(2,1)S(1)}, bf16[256,512]{1,0:T(8,128)(2,1)}, u32[]{:S(2)}) copy-start(bf16[256,512]{1,0:T(8,128)(2,1)} %pool_any.1) | copy-start | bytes 786436
  49.2 1.6 %collective-permute-start.4 = (bf16[256,512]{1,0:T(8,128)(2,1)S(1)}, bf16[256,512]{1,0:T(8,128)(2,1)S(1)}, u32[]{:S(2)}, u32[]{:S(2)}) collective-permute-start(bf16[256,512]{1,0:T(8,128)(2,1)S(1)} %get-tuple-element.27), channel_id=1, source_target_pairs={{0,1},{1,0},{2,3},{3,2},{4,5},{5,4},{6,7},{7,6},{8,9},{9,8},{10,11... | collective-permute-start | bytes 786440 | tf_op jit(solution)/shard_map/ppermute | solution.py:20
  49.3 2.4 %collective-permute-start.3 = (bf16[256,512]{1,0:T(8,128)(2,1)S(1)}, bf16[256,512]{1,0:T(8,128)(2,1)S(1)}, u32[]{:S(2)}, u32[]{:S(2)}) collective-permute-start(bf16[256,512]{1,0:T(8,128)(2,1)S(1)} %get-tuple-element.25), channel_id=1, source_target_pairs={{0,1},{1,0},{2,3},{3,2},{4,5},{5,4},{6,7},{7,6},{8,9},{9,8},{10,11... | collective-permute-start | bytes 786440 | tf_op jit(solution)/shard_map/ppermute | solution.py:20
  50.9 8.4 %collective-permute-start.5 = (bf16[256,512]{1,0:T(8,128)(2,1)S(1)}, bf16[256,512]{1,0:T(8,128)(2,1)S(1)}, u32[]{:S(2)}, u32[]{:S(2)}) collective-permute-start(bf16[256,512]{1,0:T(8,128)(2,1)S(1)} %add_convert_fusion), channel_id=1, source_target_pairs={{0,2},{1,3},{2,0},{3,1},{4,6},{5,7},{6,4},{7,5},{8,10},{9,11},{10,... | collective-permute-start | bytes 786440 | tf_op jit(solution)/shard_map/ppermute | solution.py:20

commit v9 on v7

--- a/solution.py
+++ b/solution.py
@@ -75,8 +75,11 @@
     small[3].wait()
     rows = pool[...].astype(jnp.float32)
     unit[...] = (rows * lax.rsqrt(jnp.sum(rows * rows, axis=-1, keepdims=True) + 1e-06)).astype(jnp.bfloat16)
-    unit_out = pltpu.make_async_copy(unit, unit_any, sems.at[4])
-    unit_out.start()
+    units_out = [
+        pltpu.make_async_copy(unit, unit_any.at[k], sems.at[4 + k]) for k in range(unit_any.shape[0])
+    ]
+    for copy in units_out:
+        copy.start()
     small[1].wait()
     small[2].wait()
     row = lax.broadcasted_iota(jnp.int32, (number_rows, length), 0)
@@ -96,12 +99,11 @@
             ).wait()
         copies_out.append(pltpu.make_async_copy(buffer.at[user], to_refs[k], out_sems.at[k]))
         copies_out[k].start()
-    unit_out.wait()
-    for copy in copies_out:
+    for copy in units_out + copies_out:
         copy.wait()
 
 
-def pack(histories, lengths, targets, entries, item_pool, work, groups, group):
+def pack(histories, lengths, targets, entries, item_pool, work, groups, group, blocks):
     users, length, width = histories.shape
     shape = (users, width + number_rows, length)
     hbm = pl.BlockSpec(memory_space=pltpu.HBM)
@@ -116,44 +118,67 @@
             pltpu.VMEM(item_pool.shape, jnp.bfloat16),
             pltpu.VMEM(item_pool.shape, jnp.bfloat16),
             pltpu.VMEM(shape, jnp.bfloat16),
-            pltpu.SemaphoreType.DMA((5,)),
+            pltpu.SemaphoreType.DMA((4 + blocks,)),
             pltpu.SemaphoreType.DMA((users, width // length)),
             pltpu.SemaphoreType.DMA((users,)),
         ],
-        out_shape=[pltpu.HBM(shape[1:], jnp.bfloat16)] * users + [pltpu.HBM(item_pool.shape, jnp.bfloat16)],
+        out_shape=[pltpu.HBM(shape[1:], jnp.bfloat16)] * users
+        + [pltpu.HBM((blocks,) + item_pool.shape, jnp.bfloat16)],
         compiler_params=pltpu.CompilerParams(vmem_limit_bytes=16 * 1024 * 1024),
         name="pack",
     )(group, *[in_hbm(array) for array in (entries, lengths, histories, targets, item_pool)])
 
 
-def users_kernel(
-    places, blocks, first, last, id_ref, w_in, w_out, bias_in, *refs,
-):
+def users_kernel(places, blocks, id_ref, x_refs, w_in, w_out, unit_ref, sums, loss_ref, bias, scratch):
     count = len(places)
-    x_refs, unit_refs, refs = refs[:count], refs[count : count + blocks], refs[count + blocks :]
-    if not first:
-        loss_in, sums_in, refs = refs[0], refs[1 : 1 + blocks], refs[1 + blocks :]
-    loss_ref, out_refs, refs = refs[0], refs[1 : 1 + blocks], refs[1 + blocks :]
-    wide_sums, bias, scratch = refs[0], refs[1], refs[2:]
-    heads, length = bias_in.shape
-    sums = [
-        ref if ref.dtype == jnp.float32 else wide_sums.at[k - blocks // 2] for k, ref in enumerate(out_refs)
-    ]
-    loss_ref[...] = jnp.zeros_like(loss_ref) if first else loss_in[...]
-    for k in range(blocks):
-        sums[k][...] = jnp.zeros_like(sums[k]) if first else sums_in[k][...]
-    for h in range(heads):
-        wide = jnp.broadcast_to(0.5 * bias_in[h : h + 1, :], (length, length))
-        turned = pltpu.roll(wide, 0, 1, stride=1, stride_axis=0).T
-        bias[h] = jnp.concatenate([turned, turned], axis=1)
+    units = [unit_ref.at[id_ref[k]] for k in range(blocks)]
     for at in range(0, count, 8):
         users_step(
             x_refs[at : at + 8], [id_ref[blocks + k] for k in places[at : at + 8]],
-            [id_ref[k] for k in range(blocks)], w_in, w_out, unit_refs, loss_ref, sums, bias, *scratch,
+            [id_ref[k] for k in range(blocks)], w_in, w_out, units, loss_ref, sums, bias, *scratch,
         )
+
+
+def first_kernel(
+    places, blocks, own_count, id_ref, w_in_any, w_out_any, rel_any, unit_ref, *refs
+):
+    count = len(places)
+    x_any, refs = refs[:count], refs[count:]
+    loss_ref, sums, bias, refs = refs[0], refs[1 : 1 + blocks], refs[1 + blocks], refs[2 + blocks :]
+    w_in, w_out, rel, own_x, sems = refs[:5]
+    heads, length = rel.shape
+    moves = [(rel_any, rel), (w_in_any, w_in), (w_out_any, w_out)]
+    moves += [(x_any[k], own_x.at[k]) for k in range(own_count)]
+    copies = [pltpu.make_async_copy(*move, sems.at[k]) for k, move in enumerate(moves)]
+    for copy in copies:
+        copy.start()
+    loss_ref[...] = jnp.zeros_like(loss_ref)
+    for ref in sums:
+        ref[...] = jnp.zeros_like(ref)
+    copies[0].wait()
+    for h in range(heads):
+        wide = jnp.broadcast_to(0.5 * rel[h : h + 1, :], (length, length))
+        turned = pltpu.roll(wide, 0, 1, stride=1, stride_axis=0).T
+        bias[h] = jnp.concatenate([turned, turned], axis=1)
+    for copy in copies[1:]:
+        copy.wait()
+    x_refs = [own_x.at[k] for k in range(own_count)] + list(x_any[own_count:])
+    users_kernel(places, blocks, id_ref, x_refs, w_in, w_out, unit_ref, sums, loss_ref, bias, refs[5:])
+
+
+def second_kernel(places, blocks, id_ref, w_in, w_out, bias, unit_ref, loss_in, *refs):
+    count = len(places)
+    sums_in, x_refs, refs = refs[:blocks], refs[blocks : blocks + count], refs[blocks + count :]
+    loss_ref, out_refs, wide_sums = refs[0], refs[1 : 1 + blocks], refs[1 + blocks]
+    sums = [out_refs[k] if k < blocks // 2 else wide_sums.at[k - blocks // 2] for k in range(blocks)]
+    loss_ref[...] = loss_in[...]
     for k in range(blocks):
-        if sums[k] is not out_refs[k]:
-            out_refs[k][...] = sums[k][...].astype(out_refs[k].dtype)
+        sums[k][...] = sums_in[k][...]
+    users_kernel(
+        places, blocks, id_ref, x_refs, w_in, w_out, unit_ref, sums, loss_ref, bias, refs[2 + blocks :]
+    )
+    for k in range(blocks // 2, blocks):
+        out_refs[k][...] = sums[k][...].astype(out_refs[k].dtype)
 
 
 def users_step(
@@ -164,7 +189,6 @@
     width = w_out.shape[0]
     hdim = width // heads
     items = unit_refs[0].shape[0]
-    lines = tile // length
     per_step = len(x_refs)
 
     digits = [ref[width:, :].astype(jnp.float32) for ref in x_refs]
@@ -174,7 +198,7 @@
         starts.append(pl.multiple_of(end, chunk) if u else 0)
         end = end + (lens[u] + chunk - 1) // chunk * chunk
     end = pl.multiple_of(end, chunk)
-    tiles = (end + tile - 1) // tile
+    strips = (end + length - 1) // length
 
     place = lax.broadcasted_iota(jnp.int32, (1, length), 1)
     packed_tgt[...] = jnp.full_like(packed_tgt, -1)
@@ -197,11 +221,12 @@
 
     row = lax.broadcasted_iota(jnp.int32, (length, length), 0)
     col = lax.broadcasted_iota(jnp.int32, (length, length), 1)
-    item_id = lax.broadcasted_iota(jnp.int32, (items, tile), 0)
     rate = logit_scale * math.log2(math.e)
 
-    def one_tile(t, _):
-        first = pl.multiple_of(t * tile, tile)
+    def one_tile(strip, lines):
+        tile = lines * length
+        first = pl.multiple_of(strip * length, length)
+        item_id = lax.broadcasted_iota(jnp.int32, (items, tile), 0)
         x = events[pl.ds(first, tile), :].astype(jnp.float32)
         center, spread = center_and_spread(x)
         half_normed = (center * (0.5 * lax.rsqrt(spread + 1e-05))).astype(jnp.bfloat16)
@@ -221,8 +246,8 @@
             base = pl.multiple_of(first + k * length, length)
             sources = pl.ds(base, 2 * length)
             start = starts_ref[pl.ds(base, length), :]
-            ahead = packed_tgt[pl.ds(t * lines + k, 1), :] >= 0
-            here = packed_tgt[pl.ds(t * lines + k + 1, 1), :] >= 0
+            ahead = packed_tgt[pl.ds(strip + k, 1), :] >= 0
+            here = packed_tgt[pl.ds(strip + k + 1, 1), :] >= 0
             keep_ahead = (base - length + col >= start) & ahead
             keep_here = (col <= row) & (base + col >= start) & here
             keep = jnp.concatenate([keep_ahead, keep_here], axis=1)
@@ -246,7 +271,7 @@
         queries = (out * lax.rsqrt(square + 1e-06)).astype(jnp.bfloat16)
 
         target = jnp.concatenate(
-            [packed_tgt[pl.ds(t * lines + k + 1, 1), :] for k in range(lines)], axis=1
+            [packed_tgt[pl.ds(strip + k + 1, 1), :] for k in range(lines)], axis=1
         )
         total = jnp.zeros((1, tile), jnp.float32)
         target_dot = jnp.zeros((1, tile), jnp.float32)
@@ -255,23 +280,28 @@
                 unit_refs[j][...], queries, contract_last, preferred_element_type=jnp.float32
             )
             exps = jnp.exp2(dots * rate - rate)
-            exp_ref[j] = exps
+            exp_ref[j, :, :tile] = exps
             total += jnp.sum(exps, axis=0, keepdims=True)
             hit = item_id == target - block * items
             target_dot += jnp.sum(jnp.where(hit, dots, 0.0), axis=0, keepdims=True)
         loss = logit_scale + jnp.log(total) - logit_scale * target_dot
         for k in range(lines):
-            packed_loss[pl.ds(t * lines + k, 1), :] = loss[:, k * length : (k + 1) * length]
+            packed_loss[pl.ds(strip + k, 1), :] = loss[:, k * length : (k + 1) * length]
         share = jnp.where(target >= 0, 1.0 / total, 0.0)
         for j, block in enumerate(block_ids):
             hit = item_id == target - block * items
-            left = exp_ref[j] * share - jnp.where(hit, 1.0, 0.0)
-            residual[j] = left.astype(jnp.bfloat16)
+            left = exp_ref[j, :, :tile] * share - jnp.where(hit, 1.0, 0.0)
+            residual[j, :, :tile] = left.astype(jnp.bfloat16)
         for j in range(len(block_ids)):
-            sums[j][...] += jnp.dot(residual[j], queries, preferred_element_type=jnp.float32)
+            sums[j][...] += jnp.dot(residual[j, :, :tile], queries, preferred_element_type=jnp.float32)
+
+    def full_tile(t, _):
+        one_tile(t * (tile // length), tile // length)
         return 0
 
-    lax.fori_loop(0, tiles, one_tile, 0)
+    full = strips // (tile // length)
+    lax.fori_loop(0, full, full_tile, 0)
+    pl.when(strips % (tile // length) != 0)(lambda: one_tile(full * (tile // length), 1))
 
     for u in range(per_step):
         line, turn = starts[u] // length, lax.rem(starts[u], length)
@@ -282,44 +312,77 @@
         loss_ref[pl.ds(spots[u], 1), :] = jnp.where(place < lens[u], loss, 0.0)
 
 
-def users_call(ids, places, users, packed, units, w_in, w_out, rel_bias, carried, last):
-    heads, length = rel_bias.shape
-    width = w_out.shape[0]
-    blocks = len(units)
-    items = units[0].shape[0]
+def step_scratch(places, length, width, blocks, items):
     rows = -(-min(len(places), 8) * length // tile) * tile
     lines = -(-(rows // length + 2) // 8) * 8
-    whole = pl.BlockSpec(memory_space=pltpu.VMEM)
-    arrays = [w_in, w_out, rel_bias, *packed, *units, *carried]
-    narrow = lambda k: last and k >= blocks // 2
+    return [
+        pltpu.VMEM((blocks, items, tile), jnp.float32),
+        pltpu.VMEM((blocks, items, tile), jnp.bfloat16),
+        pltpu.VMEM((rows + tile, width), jnp.bfloat16),
+        pltpu.VMEM((rows + tile, length), jnp.int32),
+        pltpu.VMEM((length + rows + tile, width), jnp.bfloat16),
+        pltpu.VMEM((length + rows + tile, width), jnp.bfloat16),
+        pltpu.VMEM((lines, length), jnp.int32),
+        pltpu.VMEM((lines, length), jnp.float32),
+    ]
+
+
+scalars = pl.BlockSpec(memory_space=pltpu.SMEM)
+whole = pl.BlockSpec(memory_space=pltpu.VMEM)
+far_off = pl.BlockSpec(memory_space=pltpu.HBM)
+
+
+def first_call(ids, places, own_count, users, packed, units, w_in, w_out, rel_bias):
+    heads, length = rel_bias.shape
+    width, (blocks, items, _) = w_out.shape[0], units.shape
+    table = (heads, length, 2 * length)
     return pl.pallas_call(
-        functools.partial(users_kernel, places, blocks, not carried, last),
-        in_specs=[pl.BlockSpec(memory_space=pltpu.SMEM)] + [whole] * len(arrays),
+        functools.partial(first_kernel, places, blocks, own_count),
+        in_specs=[scalars] + [far_off] * 3 + [whole]
+        + [far_off] * own_count + [whole] * (len(places) - own_count),
+        out_specs=[whole] * (2 + blocks),
+        scratch_shapes=[
+            pltpu.VMEM(w_in.shape, jnp.bfloat16),
+            pltpu.VMEM(w_out.shape, jnp.bfloat16),
+            pltpu.VMEM(rel_bias.shape, jnp.float32),
+            pltpu.VMEM((own_count,) + packed[0].shape, jnp.bfloat16),
+            pltpu.SemaphoreType.DMA((3 + own_count,)),
+        ]
+        + step_scratch(places, length, width, blocks, items),
+        out_shape=[pltpu.VMEM((users, length), jnp.float32)]
+        + [pltpu.VMEM((items, width), jnp.float32)] * blocks
+        + [pltpu.VMEM(table, jnp.float32)],
+        compiler_params=pltpu.CompilerParams(vmem_limit_bytes=24 * 1024 * 1024),
+        name="first_users",
+    )(
+        ids, *[in_hbm(array) for array in (w_in, w_out, rel_bias)], in_vmem(units),
+        *[in_hbm(array) for array in packed[:own_count]], *[in_vmem(array) for array in packed[own_count:]],
+    )
+
+
+def second_call(ids, places, packed, units, w_in, w_out, loss, sums, bias):
+    items, width = sums[0].shape
+    length, blocks = bias.shape[1], len(sums)
+    arrays = [w_in, w_out, bias, units, loss, *sums, *packed]
+    return pl.pallas_call(
+        functools.partial(second_kernel, places, blocks),
+        in_specs=[scalars] + [whole] * len(arrays),
         out_specs=[whole] * (1 + blocks),
-        scratch_shapes=[
-            pltpu.VMEM((blocks // 2, items, width), jnp.float32),
-            pltpu.VMEM((heads, length, 2 * length), jnp.float32),
-            pltpu.VMEM((blocks, items, tile), jnp.float32),
-            pltpu.VMEM((blocks, items, tile), jnp.bfloat16),
-            pltpu.VMEM((rows + tile, width), jnp.bfloat16),
-            pltpu.VMEM((rows + tile, length), jnp.int32),
-            pltpu.VMEM((length + rows + tile, width), jnp.bfloat16),
-            pltpu.VMEM((length + rows + tile, width), jnp.bfloat16),
-            pltpu.VMEM((lines, length), jnp.int32),
-            pltpu.VMEM((lines, length), jnp.float32),
-        ],
-        out_shape=[pltpu.VMEM((users, length), jnp.float32)]
+        scratch_shapes=[pltpu.VMEM((blocks - blocks // 2, items, width), jnp.float32)]
+        + step_scratch(places, length, width, blocks, items),
+        out_shape=[jax.ShapeDtypeStruct(loss.shape, jnp.float32)]
         + [
-            pltpu.VMEM((items, width), jnp.bfloat16 if narrow(k) else jnp.float32) for k in range(blocks)
+            pltpu.VMEM((items, width), jnp.float32 if k < blocks // 2 else jnp.bfloat16)
+            for k in range(blocks)
         ],
         compiler_params=pltpu.CompilerParams(vmem_limit_bytes=24 * 1024 * 1024),
-        name="users",
+        name="second_users",
     )(ids, *[in_vmem(array) for array in arrays])
 
 
 def shards(histories, lengths, targets, send_list, w_in, w_out, rel_bias, item_pool):
     user_count = histories.shape[0]
-    groups = lax.axis_size("dp")
+    groups, blocks = lax.axis_size("dp"), lax.axis_size("blk")
     slots = user_count // groups
     group, mine = lax.axis_index("dp").astype(jnp.int32), lax.axis_index("blk").astype(jnp.int32)
 
@@ -327,14 +390,13 @@
         ((shift, slot) for shift in range(groups) for slot in range(slots)),
         key=lambda pair: (pair[0] != 0, abs(pair[0] - groups / 2)),
     )
-    *packed, unit = pack(
-        histories, lengths, targets, send_list, item_pool, work, groups, group.reshape(1)
-    )
-    over_unit = swap(unit, "blk", 2)
+    *packed, units = pack(
+        histories, lengths, targets, send_list, item_pool, work, groups, group.reshape(1), blocks
+    )
     packed = [
         users if shift == 0 else from_behind(users, "dp", shift) for users, (shift, _) in zip(packed, work)
     ]
-    units = [unit, over_unit, swap(unit, "blk", 1), swap(over_unit, "blk", 1)]
+    units = lax.all_to_all(units, "blk", split_axis=0, concat_axis=0, tiled=True)
 
     pool_float = item_pool.astype(jnp.float32)
     item_norm = jnp.sqrt(jnp.sum(pool_float * pool_float, axis=-1, keepdims=True) + 1e-06)
@@ -344,11 +406,11 @@
     ids = jnp.stack([mine, mine ^ 2, mine ^ 1, mine ^ 3, *came])
     half = user_count // 2
     order = tuple(range(user_count))
-    carried = users_call(
-        ids, order[:half], user_count, packed[:half], units, w_in, w_out, rel_bias, (), False
-    )
-    row_loss, own, over, side, far = users_call(
-        ids, order[half:], user_count, packed[half:], units, w_in, w_out, rel_bias, carried, True
+    loss, *sums, bias = first_call(
+        ids, order[:half], slots, user_count, packed[:half], units, w_in, w_out, rel_bias
+    )
+    row_loss, own, over, side, far = second_call(
+        ids, order[half:], packed[half:], units, w_in, w_out, loss, sums, bias
     )
     over = over + swap(far, "blk", 1).astype(jnp.float32)
     own = own + swap(side, "blk", 1).astype(jnp.float32)

time: 60.6 us -> 56 us (0.924); the launches traced: 61.3 us -> 54.9 us
  local copies, waits for them, and re-layouts: 5.86 us -> 0.13 us
  starting transfers between devices: 24.4 us -> 22.2 us
  Pallas kernels: 11.3 us -> 13.4 us
    unnamed x19 -> x20, local copies, waits for them, and re-layouts: 5.78 us -> 0.05 us
    all_to_all x0 -> x1, starting transfers between devices: none -> 4.38 us  [shards(): lax.all_to_all(units, 'blk', split_axis=0, concat_axis=0, tiled=True)]
    ppermute x6 -> x3, starting transfers between devices: 7.26 us -> 3.26 us  [swap(): return lax.ppermute(array, axis, [(i, i ^ bit) for i in range(devices)])]
    ppermute x7, starting transfers between devices: 17.1 us -> 14.6 us  [from_behind(): lax.ppermute(array, axis, [(i, (i + by) % devices) for i in range(devices)])]
    pallas_call x2, Pallas kernels: 8.33 us -> 10.1 us  [the longest x1 6.12 us: first_call(): pl.pallas_call(functools.partial(first_kernel, places, blocks, own_count)...]
    ppermute x7, waiting for transfers between devices: 10.4 us -> 9.39 us  [from_behind(): lax.ppermute(array, axis, [(i, (i + by) % devices) for i in range(devices)])]
    ppermute x6 -> x3, waiting for transfers between devices: 6.99 us -> 7.48 us  [swap(): return lax.ppermute(array, axis, [(i, i ^ bit) for i in range(devices)])]
  transfers between devices with their start and end apart: 13 -> 11, of which waited for: 5 -> 4; matrix products, arithmetic and copies ran while one was open for 1% -> 1% of each run, Pallas kernels for 7% -> 11%
where the time goes in v9:
time: 56 us; the launch traced here: 54.9 us
  starting transfers between devices  22.2 us (40%)
  waiting for transfers between devices  16.9 us (30%)
  Pallas kernels  13.4 us (24%)
  other arithmetic  1.5 us (3%)
  between operations  0.83 us (1%)
    ppermute x7, starting transfers between devices, from_behind(): lax.ppermute(array, axis, [(i, (i + by) % devices) for i in range(devices)])  14.6 us
    ppermute x7, waiting for transfers between devices, from_behind(): lax.ppermute(array, axis, [(i, (i + by) % devices) for i in range(devices)])  9.39 us
    ppermute x3, waiting for transfers between devices, swap(): return lax.ppermute(array, axis, [(i, i ^ bit) for i in range(devices)])  7.48 us
    pallas_call x1, Pallas kernels, first_call(): pl.pallas_call(functools.partial(first_kernel, places, blocks, own_count)...  6.12 us
    all_to_all x1, starting transfers between devices, shards(): lax.all_to_all(units, 'blk', split_axis=0, concat_axis=0, tiled=True)  4.38 us
    pallas_call x1, Pallas kernels, second_call(): pl.pallas_call(functools.partial(second_kernel, places, blocks), in_specs...  3.98 us
    pallas_call x1, Pallas kernels, pack(): pl.pallas_call(functools.partial(pack_kernel, work, groups), in_specs=[pl...  3.28 us
    ppermute x3, starting transfers between devices, swap(): return lax.ppermute(array, axis, [(i, i ^ bit) for i in range(devices)])  3.26 us
  transfers between devices with their start and end apart: 11, of which 4 were waited for; matrix products, arithmetic and copies ran while one was open for 1% of the time, Pallas kernels for 11%

profile of v9, /device:TPU:0, one launch (start us, length us, event | category | flops | bytes accessed | tf_op | source)
XLA Modules:
  0.0 54.9 jit_solution(363798819758568333)
XLA Ops:
  0.6 3.3 %pack.1 = (bf16[520,128]{1,0:T(8,128)(2,1)}, bf16[520,128]{1,0:T(8,128)(2,1)}, bf16[520,128]{1,0:T(8,128)(2,1)}, bf16[520,128]{1,0:T(8,128)(2,1)}, bf16[520,128]...) custom-call(s32[1]{0:T(128)} %bitcast.12.group_ref, ...), custom_call_target="tpu_custom_call" | custom-call | tf_op jit(solution)/shard_map/pack/pallas_call | solution.py:110
  3.9 0.0 copy-start.9
  3.9 0.0 copy-start.8
  3.9 0.0 copy-start.7
  4.0 0.0 copy-start.6
  4.0 0.0 copy-start.5
  4.0 0.0 copy-start.4
  4.0 0.0 copy-start.3
  4.0 4.4 %all-to-all-start = ((bf16[4,256,512]{2,1,0:T(8,128)(2,1)}), bf16[4,256,512]{2,1,0:T(8,128)(2,1)S(1)}, u32[]{:S(2)}, u32[]{:S(2)}) async-start(bf16[4,256,512]{2,1,0:T(8,128)(2,1)} %get-tuple-element.22), calls=%async_computation | async-start | bytes 2097152 | tf_op jit(solution)/shard_map/all_to_all | solution.py:399
  8.4 0.0 copy-done.9
  8.4 3.4 %collective-permute-start = (bf16[520,128]{1,0:T(8,128)(2,1)S(1)}, bf16[520,128]{1,0:T(8,128)(2,1)S(1)}, u32[]{:S(2)}, u32[]{:S(2)}) collective-permute-start(bf16[520,128]{1,0:T(8,128)(2,1)S(1)} %copy-done.9), channel_id=1, source_target_pairs={{0,16},{4,20},{8,24},{12,28},{16,0},{20,4},{24,8},{28,12},{1,17},{... | collective-permute-start | bytes 399368 | tf_op jit(solution)/shard_map/ppermute | solution.py:25
  11.8 0.0 copy-done.8
  11.8 2.5 %collective-permute-start.1 = (bf16[520,128]{1,0:T(8,128)(2,1)S(1)}, bf16[520,128]{1,0:T(8,128)(2,1)S(1)}, u32[]{:S(2)}, u32[]{:S(2)}) collective-permute-start(bf16[520,128]{1,0:T(8,128)(2,1)S(1)} %copy-done.8), channel_id=1, source_target_pairs={{0,12},{4,16},{8,20},{12,24},{16,28},{20,0},{24,4},{28,8},{1,13},{... | collective-permute-start | bytes 399368 | tf_op jit(solution)/shard_map/ppermute | solution.py:25
  14.3 0.0 copy-done.7
  14.3 1.3 %collective-permute-start.2 = (bf16[520,128]{1,0:T(8,128)(2,1)S(1)}, bf16[520,128]{1,0:T(8,128)(2,1)S(1)}, u32[]{:S(2)}, u32[]{:S(2)}) collective-permute-start(bf16[520,128]{1,0:T(8,128)(2,1)S(1)} %copy-done.7), channel_id=1, source_target_pairs={{0,20},{4,24},{8,28},{12,0},{16,4},{20,8},{24,12},{28,16},{1,21},{... | collective-permute-start | bytes 399368 | tf_op jit(solution)/shard_map/ppermute | solution.py:25
  15.6 0.0 copy-done.6
  15.6 1.6 %collective-permute-start.3 = (bf16[520,128]{1,0:T(8,128)(2,1)S(1)}, bf16[520,128]{1,0:T(8,128)(2,1)S(1)}, u32[]{:S(2)}, u32[]{:S(2)}) collective-permute-start(bf16[520,128]{1,0:T(8,128)(2,1)S(1)} %copy-done.6), channel_id=1, source_target_pairs={{0,8},{4,12},{8,16},{12,20},{16,24},{20,28},{24,0},{28,4},{1,9},{5... | collective-permute-start | bytes 399368 | tf_op jit(solution)/shard_map/ppermute | solution.py:25
  17.2 0.0 copy-done.5
  17.2 2.2 %collective-permute-start.4 = (bf16[520,128]{1,0:T(8,128)(2,1)S(1)}, bf16[520,128]{1,0:T(8,128)(2,1)S(1)}, u32[]{:S(2)}, u32[]{:S(2)}) collective-permute-start(bf16[520,128]{1,0:T(8,128)(2,1)S(1)} %copy-done.5), channel_id=1, source_target_pairs={{0,24},{4,28},{8,0},{12,4},{16,8},{20,12},{24,16},{28,20},{1,25},{... | collective-permute-start | bytes 399368 | tf_op jit(solution)/shard_map/ppermute | solution.py:25
  19.4 8.2 %collective-permute-done.refs_1_ = bf16[520,128]{1,0:T(8,128)(2,1)S(1)} collective-permute-done((bf16[520,128]{1,0:T(8,128)(2,1)S(1)}, bf16[520,128]{1,0:T(8,128)(2,1)S(1)}, u32[]{:S(2)}, u32[]{:S(2)}) %collective-permute-start) | collective-permute-done | bytes 133152 | tf_op jit(solution)/shard_map/ppermute | solution.py:25
  27.6 0.0 copy-done.4
  27.6 0.0 collective-permute-start.5
  27.6 1.2 %collective-permute-done.1.refs_2_ = bf16[520,128]{1,0:T(8,128)(2,1)S(1)} collective-permute-done((bf16[520,128]{1,0:T(8,128)(2,1)S(1)}, bf16[520,128]{1,0:T(8,128)(2,1)S(1)}, u32[]{:S(2)}, u32[]{:S(2)}) %collective-permute-start.1) | collective-permute-done | bytes 133152 | tf_op jit(solution)/shard_map/ppermute | solution.py:25
  28.8 0.0 copy-done.3
  28.8 3.5 %collective-permute-start.6 = (bf16[520,128]{1,0:T(8,128)(2,1)S(1)}, bf16[520,128]{1,0:T(8,128)(2,1)S(1)}, u32[]{:S(2)}, u32[]{:S(2)}) collective-permute-start(bf16[520,128]{1,0:T(8,128)(2,1)S(1)} %copy-done.3), channel_id=1, source_target_pairs={{0,28},{4,0},{8,4},{12,8},{16,12},{20,16},{24,20},{28,24},{1,29},{... | collective-permute-start | bytes 399368 | tf_op jit(solution)/shard_map/ppermute | solution.py:25
  32.3 0.1 stack.51.id_ref
  32.4 0.0 collective-permute-done.2.refs_3_
  32.4 0.0 all-to-all-done.unit_ref
  32.4 0.0 copy-start
  32.5 0.0 copy-start.1
  32.5 6.1 %first_users.1 = (f32[8,128]{1,0:T(8,128)S(1)}, f32[256,512]{1,0:T(8,128)S(1)}, f32[256,512]{1,0:T(8,128)S(1)}, f32[256,512]{1,0:T(8,128)S(1)}, f32[256,512]{1,0:T(8,128)S(1)}, /*index=5*/f32[4,128,256]{2,1,0:T(8,128)S(1)}) custom-call(s32[12]{0:T(128)S(1)} %stack.51.id_ref, bf16[512,2048]{1,0:T(8,128)(2,1)} %w_in.1, bf16[512,512]{1,0:T(8,128)(2,1)} %w_out.1, ...), custom_call_target="tpu_custom_call" | custom-call | tf_op jit(solution)/shard_map/first_users/pallas_call | solution.py:339
  38.6 0.0 collective-permute-done.3.refs_4_
  38.6 0.0 collective-permute-done.4.refs_5_
  38.6 0.0 collective-permute-done.5.refs_6_
  38.6 0.0 collective-permute-done.6.refs_7_
  38.6 0.0 copy-done
  38.7 0.0 copy-start.2
  38.7 4.0 %second_users.1 = (f32[8,128]{1,0:T(8,128)}, f32[256,512]{1,0:T(8,128)S(1)}, f32[256,512]{1,0:T(8,128)S(1)}, bf16[256,512]{1,0:T(8,128)(2,1)S(1)}, bf16[256,512]{1,0:T(8,128)(2,1)S(1)}) custom-call(s32[12]{0:T(128)S(1)} %stack.51.id_ref, bf16[512,2048]{1,0:T(8,128)(2,1)S(1)} %copy-done, bf16[512,512]{1,0:T(8,128)(2,1)S(1)} %copy-done.1, ...), custom_call_target="tpu_custom_call" | custom-call | tf_op jit(solution)/shard_map/second_users/pallas_call | solution.py:367
  42.6 0.0 collective-permute-start.8
  42.6 0.5 collective-permute-start.7
  43.2 1.0 %collective-permute-done.8 = bf16[256,512]{1,0:T(8,128)(2,1)S(1)} collective-permute-done((bf16[256,512]{1,0:T(8,128)(2,1)S(1)}, bf16[256,512]{1,0:T(8,128)(2,1)S(1)}, u32[]{:S(2)}, u32[]{:S(2)}) %collective-permute-start.8) | collective-permute-done | bytes 262176 | tf_op jit(solution)/shard_map/ppermute | solution.py:20
  44.2 0.1 add_convert_fusion
  44.3 2.8 %collective-permute-start.9 = (bf16[256,512]{1,0:T(8,128)(2,1)S(1)}, bf16[256,512]{1,0:T(8,128)(2,1)S(1)}, u32[]{:S(2)}, u32[]{:S(2)}) collective-permute-start(bf16[256,512]{1,0:T(8,128)(2,1)S(1)} %add_convert_fusion), channel_id=1, source_target_pairs={{0,2},{1,3},{2,0},{3,1},{4,6},{5,7},{6,4},{7,5},{8,10},{9,11},{10,... | collective-permute-start | bytes 786440 | tf_op jit(solution)/shard_map/ppermute | solution.py:20
  47.0 0.1 fusion
  47.1 0.0 collective-permute-done.7
  47.2 6.5 %collective-permute-done.9 = bf16[256,512]{1,0:T(8,128)(2,1)S(1)} collective-permute-done((bf16[256,512]{1,0:T(8,128)(2,1)S(1)}, bf16[256,512]{1,0:T(8,128)(2,1)S(1)}, u32[]{:S(2)}, u32[]{:S(2)}) %collective-permute-start.9) | collective-permute-done | bytes 262176 | tf_op jit(solution)/shard_map/ppermute | solution.py:20
  53.6 0.3 multiply_reduce_fusion
  53.9 1.0 %subtract_divide_fusion = f32[256,512]{1,0:T(8,128)} fusion(bf16[256,512]{1,0:T(8,128)(2,1)S(1)} %copy-done.2, f32[256]{0:T(256)S(1)} %multiply_reduce_fusion, f32[256]{0:T(256)S(1)} %add_sqrt_fusion, bf16[256,512]{1,0:T(8,128)(2,1)S(1)} %collective-permute-done.9, f32[256,512]{1,0:T(8,128)S(1)} %get-tuple-element.38, ...), kind=kLoop, calls=%fused_computation.3 | loop fusion | flops 1310720 | bytes 1837056 | tf_op jit(solution)/shard_map/div | solution.py:418
  (3 shorter events, 0.0 us)
Async XLA Ops:
  3.9 4.5 %copy-start.9 = (bf16[520,128]{1,0:T(8,128)(2,1)S(1)}, bf16[520,128]{1,0:T(8,128)(2,1)}, u32[]{:S(2)}) copy-start(bf16[520,128]{1,0:T(8,128)(2,1)} %get-tuple-element.24) | copy-start | bytes 399364
  3.9 7.8 %copy-start.8 = (bf16[520,128]{1,0:T(8,128)(2,1)S(1)}, bf16[520,128]{1,0:T(8,128)(2,1)}, u32[]{:S(2)}) copy-start(bf16[520,128]{1,0:T(8,128)(2,1)} %get-tuple-element.25) | copy-start | bytes 399364
  3.9 10.3 %copy-start.7 = (bf16[520,128]{1,0:T(8,128)(2,1)S(1)}, bf16[520,128]{1,0:T(8,128)(2,1)}, u32[]{:S(2)}) copy-start(bf16[520,128]{1,0:T(8,128)(2,1)} %get-tuple-element.26) | copy-start | bytes 399364
  4.0 11.7 %copy-start.6 = (bf16[520,128]{1,0:T(8,128)(2,1)S(1)}, bf16[520,128]{1,0:T(8,128)(2,1)}, u32[]{:S(2)}) copy-start(bf16[520,128]{1,0:T(8,128)(2,1)} %get-tuple-element.33) | copy-start | bytes 399364
  4.0 13.2 %copy-start.5 = (bf16[520,128]{1,0:T(8,128)(2,1)S(1)}, bf16[520,128]{1,0:T(8,128)(2,1)}, u32[]{:S(2)}) copy-start(bf16[520,128]{1,0:T(8,128)(2,1)} %get-tuple-element.34) | copy-start | bytes 399364
  4.0 23.6 %copy-start.4 = (bf16[520,128]{1,0:T(8,128)(2,1)S(1)}, bf16[520,128]{1,0:T(8,128)(2,1)}, u32[]{:S(2)}) copy-start(bf16[520,128]{1,0:T(8,128)(2,1)} %get-tuple-element.35) | copy-start | bytes 399364
  4.0 24.8 %copy-start.3 = (bf16[520,128]{1,0:T(8,128)(2,1)S(1)}, bf16[520,128]{1,0:T(8,128)(2,1)}, u32[]{:S(2)}) copy-start(bf16[520,128]{1,0:T(8,128)(2,1)} %get-tuple-element.36) | copy-start | bytes 399364
  4.0 28.4 %all-to-all-start = ((bf16[4,256,512]{2,1,0:T(8,128)(2,1)}), bf16[4,256,512]{2,1,0:T(8,128)(2,1)S(1)}, u32[]{:S(2)}, u32[]{:S(2)}) async-start(bf16[4,256,512]{2,1,0:T(8,128)(2,1)} %get-tuple-element.22), calls=%async_computation | async-start | bytes 2097152 | tf_op jit(solution)/shard_map/all_to_all | solution.py:399
  8.4 19.2 %collective-permute-start = (bf16[520,128]{1,0:T(8,128)(2,1)S(1)}, bf16[520,128]{1,0:T(8,128)(2,1)S(1)}, u32[]{:S(2)}, u32[]{:S(2)}) collective-permute-start(bf16[520,128]{1,0:T(8,128)(2,1)S(1)} %copy-done.9), channel_id=1, source_target_pairs={{0,16},{4,20},{8,24},{12,28},{16,0},{20,4},{24,8},{28,12},{1,17},{... | collective-permute-start | bytes 399368 | tf_op jit(solution)/shard_map/ppermute | solution.py:25
  11.8 17.0 %collective-permute-start.1 = (bf16[520,128]{1,0:T(8,128)(2,1)S(1)}, bf16[520,128]{1,0:T(8,128)(2,1)S(1)}, u32[]{:S(2)}, u32[]{:S(2)}) collective-permute-start(bf16[520,128]{1,0:T(8,128)(2,1)S(1)} %copy-done.8), channel_id=1, source_target_pairs={{0,12},{4,16},{8,20},{12,24},{16,28},{20,0},{24,4},{28,8},{1,13},{... | collective-permute-start | bytes 399368 | tf_op jit(solution)/shard_map/ppermute | solution.py:25
  14.3 18.1 %collective-permute-start.2 = (bf16[520,128]{1,0:T(8,128)(2,1)S(1)}, bf16[520,128]{1,0:T(8,128)(2,1)S(1)}, u32[]{:S(2)}, u32[]{:S(2)}) collective-permute-start(bf16[520,128]{1,0:T(8,128)(2,1)S(1)} %copy-done.7), channel_id=1, source_target_pairs={{0,20},{4,24},{8,28},{12,0},{16,4},{20,8},{24,12},{28,16},{1,21},{... | collective-permute-start | bytes 399368 | tf_op jit(solution)/shard_map/ppermute | solution.py:25
  15.6 23.0 %collective-permute-start.3 = (bf16[520,128]{1,0:T(8,128)(2,1)S(1)}, bf16[520,128]{1,0:T(8,128)(2,1)S(1)}, u32[]{:S(2)}, u32[]{:S(2)}) collective-permute-start(bf16[520,128]{1,0:T(8,128)(2,1)S(1)} %copy-done.6), channel_id=1, source_target_pairs={{0,8},{4,12},{8,16},{12,20},{16,24},{20,28},{24,0},{28,4},{1,9},{5... | collective-permute-start | bytes 399368 | tf_op jit(solution)/shard_map/ppermute | solution.py:25
  17.2 21.4 %collective-permute-start.4 = (bf16[520,128]{1,0:T(8,128)(2,1)S(1)}, bf16[520,128]{1,0:T(8,128)(2,1)S(1)}, u32[]{:S(2)}, u32[]{:S(2)}) collective-permute-start(bf16[520,128]{1,0:T(8,128)(2,1)S(1)} %copy-done.5), channel_id=1, source_target_pairs={{0,24},{4,28},{8,0},{12,4},{16,8},{20,12},{24,16},{28,20},{1,25},{... | collective-permute-start | bytes 399368 | tf_op jit(solution)/shard_map/ppermute | solution.py:25
  27.6 11.0 %collective-permute-start.5 = (bf16[520,128]{1,0:T(8,128)(2,1)S(1)}, bf16[520,128]{1,0:T(8,128)(2,1)S(1)}, u32[]{:S(2)}, u32[]{:S(2)}) collective-permute-start(bf16[520,128]{1,0:T(8,128)(2,1)S(1)} %copy-done.4), channel_id=1, source_target_pairs={{0,4},{4,8},{8,12},{12,16},{16,20},{20,24},{24,28},{28,0},{1,5},{5... | collective-permute-start | bytes 399368 | tf_op jit(solution)/shard_map/ppermute | solution.py:25
  28.8 9.8 %collective-permute-start.6 = (bf16[520,128]{1,0:T(8,128)(2,1)S(1)}, bf16[520,128]{1,0:T(8,128)(2,1)S(1)}, u32[]{:S(2)}, u32[]{:S(2)}) collective-permute-start(bf16[520,128]{1,0:T(8,128)(2,1)S(1)} %copy-done.3), channel_id=1, source_target_pairs={{0,28},{4,0},{8,4},{12,8},{16,12},{20,16},{24,20},{28,24},{1,29},{... | collective-permute-start | bytes 399368 | tf_op jit(solution)/shard_map/ppermute | solution.py:25
  32.4 6.2 %copy-start = (bf16[512,2048]{1,0:T(8,128)(2,1)S(1)}, bf16[512,2048]{1,0:T(8,128)(2,1)}, u32[]{:S(2)}) copy-start(bf16[512,2048]{1,0:T(8,128)(2,1)} %w_in.1) | copy-start | bytes 6291460
  32.5 6.2 %copy-start.1 = (bf16[512,512]{1,0:T(8,128)(2,1)S(1)}, bf16[512,512]{1,0:T(8,128)(2,1)}, u32[]{:S(2)}) copy-start(bf16[512,512]{1,0:T(8,128)(2,1)} %w_out.1) | copy-start | bytes 1572868
  38.7 8.4 %copy-start.2 = (bf16[256,512]{1,0:T(8,128)(2,1)S(1)}, bf16[256,512]{1,0:T(8,128)(2,1)}, u32[]{:S(2)}) copy-start(bf16[256,512]{1,0:T(8,128)(2,1)} %pool_any.1) | copy-start | bytes 786436
  42.6 1.5 %collective-permute-start.8 = (bf16[256,512]{1,0:T(8,128)(2,1)S(1)}, bf16[256,512]{1,0:T(8,128)(2,1)S(1)}, u32[]{:S(2)}, u32[]{:S(2)}) collective-permute-start(bf16[256,512]{1,0:T(8,128)(2,1)S(1)} %get-tuple-element.41), channel_id=1, source_target_pairs={{0,1},{1,0},{2,3},{3,2},{4,5},{5,4},{6,7},{7,6},{8,9},{9,8},{10,11... | collective-permute-start | bytes 786440 | tf_op jit(solution)/shard_map/ppermute | solution.py:20
  42.6 4.5 %collective-permute-start.7 = (bf16[256,512]{1,0:T(8,128)(2,1)S(1)}, bf16[256,512]{1,0:T(8,128)(2,1)S(1)}, u32[]{:S(2)}, u32[]{:S(2)}) collective-permute-start(bf16[256,512]{1,0:T(8,128)(2,1)S(1)} %get-tuple-element.39), channel_id=1, source_target_pairs={{0,1},{1,0},{2,3},{3,2},{4,5},{5,4},{6,7},{7,6},{8,9},{9,8},{10,11... | collective-permute-start | bytes 786440 | tf_op jit(solution)/shard_map/ppermute | solution.py:20
  44.3 9.4 %collective-permute-start.9 = (bf16[256,512]{1,0:T(8,128)(2,1)S(1)}, bf16[256,512]{1,0:T(8,128)(2,1)S(1)}, u32[]{:S(2)}, u32[]{:S(2)}) collective-permute-start(bf16[256,512]{1,0:T(8,128)(2,1)S(1)} %add_convert_fusion), channel_id=1, source_target_pairs={{0,2},{1,3},{2,0},{3,1},{4,6},{5,7},{6,4},{7,5},{8,10},{9,11},{10,... | collective-permute-start | bytes 786440 | tf_op jit(solution)/shard_map/ppermute | solution.py:20

commit v10 on v9

--- a/solution.py
+++ b/solution.py
@@ -45,10 +45,9 @@
 def pack_kernel(
     work, groups, group_ref, list_any, len_any, from_any, tgt_any, pool_any, *refs,
 ):
-    users = from_any.shape[0]
+    users, length, width = from_any.shape
     to_refs, unit_any = refs[:users], refs[users]
-    entries, lens, targets, pool, unit, buffer, sems, in_sems, out_sems = refs[users + 1 :]
-    users, length, width = from_any.shape
+    entries, lens, targets, pool, unit, sems, in_sems = refs[users + 1 :]
     pieces = width // length
     small = [
         pltpu.make_async_copy(source, target, sems.at[k])
@@ -58,20 +57,20 @@
     ]
     for copy in small:
         copy.start()
+    small[0].wait()
+    slots = users // groups
+    order = [entries[(group_ref[0] + shift) % groups * slots + slot] for shift, slot in work]
     copies_in = [
-        [
-            pltpu.make_async_copy(
-                from_any.at[u, :, pl.ds(c * length, length)],
-                buffer.at[u, pl.ds(c * length, length)],
-                in_sems.at[u, c],
-            )
-            for c in range(pieces)
-        ]
-        for u in range(users)
+        pltpu.make_async_copy(
+            from_any.at[order[k], :, pl.ds(c * length, length)],
+            to_refs[k].at[pl.ds(c * length, length)],
+            in_sems.at[k, c],
+        )
+        for k in range(users)
+        for c in range(pieces)
     ]
-    for copies in copies_in:
-        for copy in copies:
-            copy.start()
+    for copy in copies_in:
+        copy.start()
     small[3].wait()
     rows = pool[...].astype(jnp.float32)
     unit[...] = (rows * lax.rsqrt(jnp.sum(rows * rows, axis=-1, keepdims=True) + 1e-06)).astype(jnp.bfloat16)
@@ -83,46 +82,32 @@
     small[1].wait()
     small[2].wait()
     row = lax.broadcasted_iota(jnp.int32, (number_rows, length), 0)
-    for u in range(users):
-        target = targets[u : u + 1, :]
-        numbers = jnp.where(row == 0, lens[u], jnp.where(row == 1, target // 256, target % 256))
-        buffer[u, width:, :] = numbers.astype(jnp.float32).astype(jnp.bfloat16)
-    small[0].wait()
-    copies_out = []
-    for k, (shift, slot) in enumerate(work):
-        user = entries[(group_ref[0] + shift) % groups * (users // groups) + slot]
-        for c in range(pieces):
-            pltpu.make_async_copy(
-                from_any.at[user, :, pl.ds(c * length, length)],
-                buffer.at[user, pl.ds(c * length, length)],
-                in_sems.at[user, c],
-            ).wait()
-        copies_out.append(pltpu.make_async_copy(buffer.at[user], to_refs[k], out_sems.at[k]))
-        copies_out[k].start()
-    for copy in units_out + copies_out:
+    for k in range(users):
+        target = targets[pl.ds(order[k], 1), :]
+        numbers = jnp.where(row == 0, lens[order[k]], jnp.where(row == 1, target // 256, target % 256))
+        to_refs[k][width:, :] = numbers.astype(jnp.float32).astype(jnp.bfloat16)
+    for copy in copies_in + units_out:
         copy.wait()
 
 
 def pack(histories, lengths, targets, entries, item_pool, work, groups, group, blocks):
     users, length, width = histories.shape
-    shape = (users, width + number_rows, length)
+    shape = (width + number_rows, length)
     hbm = pl.BlockSpec(memory_space=pltpu.HBM)
     return pl.pallas_call(
         functools.partial(pack_kernel, work, groups),
         in_specs=[pl.BlockSpec(memory_space=pltpu.SMEM)] + [hbm] * 5,
-        out_specs=[hbm] * (users + 1),
+        out_specs=[pl.BlockSpec(memory_space=pltpu.VMEM)] * users + [hbm],
         scratch_shapes=[
             pltpu.SMEM(entries.shape, jnp.int32),
             pltpu.SMEM(lengths.shape, jnp.int32),
             pltpu.VMEM(targets.shape, jnp.int32),
             pltpu.VMEM(item_pool.shape, jnp.bfloat16),
             pltpu.VMEM(item_pool.shape, jnp.bfloat16),
-            pltpu.VMEM(shape, jnp.bfloat16),
             pltpu.SemaphoreType.DMA((4 + blocks,)),
             pltpu.SemaphoreType.DMA((users, width // length)),
-            pltpu.SemaphoreType.DMA((users,)),
         ],
-        out_shape=[pltpu.HBM(shape[1:], jnp.bfloat16)] * users
+        out_shape=[pltpu.VMEM(shape, jnp.bfloat16)] * users
         + [pltpu.HBM((blocks,) + item_pool.shape, jnp.bfloat16)],
         compiler_params=pltpu.CompilerParams(vmem_limit_bytes=16 * 1024 * 1024),
         name="pack",
@@ -140,15 +125,14 @@
 
 
 def first_kernel(
-    places, blocks, own_count, id_ref, w_in_any, w_out_any, rel_any, unit_ref, *refs
+    places, blocks, id_ref, w_in_any, w_out_any, rel_any, unit_ref, *refs
 ):
     count = len(places)
-    x_any, refs = refs[:count], refs[count:]
+    x_refs, refs = refs[:count], refs[count:]
     loss_ref, sums, bias, refs = refs[0], refs[1 : 1 + blocks], refs[1 + blocks], refs[2 + blocks :]
-    w_in, w_out, rel, own_x, sems = refs[:5]
+    w_in, w_out, rel, sems = refs[:4]
     heads, length = rel.shape
     moves = [(rel_any, rel), (w_in_any, w_in), (w_out_any, w_out)]
-    moves += [(x_any[k], own_x.at[k]) for k in range(own_count)]
     copies = [pltpu.make_async_copy(*move, sems.at[k]) for k, move in enumerate(moves)]
     for copy in copies:
         copy.start()
@@ -162,8 +146,7 @@
         bias[h] = jnp.concatenate([turned, turned], axis=1)
     for copy in copies[1:]:
         copy.wait()
-    x_refs = [own_x.at[k] for k in range(own_count)] + list(x_any[own_count:])
-    users_kernel(places, blocks, id_ref, x_refs, w_in, w_out, unit_ref, sums, loss_ref, bias, refs[5:])
+    users_kernel(places, blocks, id_ref, x_refs, w_in, w_out, unit_ref, sums, loss_ref, bias, refs[4:])
 
 
 def second_kernel(places, blocks, id_ref, w_in, w_out, bias, unit_ref, loss_in, *refs):
@@ -332,21 +315,19 @@
 far_off = pl.BlockSpec(memory_space=pltpu.HBM)
 
 
-def first_call(ids, places, own_count, users, packed, units, w_in, w_out, rel_bias):
+def first_call(ids, places, users, packed, units, w_in, w_out, rel_bias):
     heads, length = rel_bias.shape
     width, (blocks, items, _) = w_out.shape[0], units.shape
     table = (heads, length, 2 * length)
     return pl.pallas_call(
-        functools.partial(first_kernel, places, blocks, own_count),
-        in_specs=[scalars] + [far_off] * 3 + [whole]
-        + [far_off] * own_count + [whole] * (len(places) - own_count),
+        functools.partial(first_kernel, places, blocks),
+        in_specs=[scalars] + [far_off] * 3 + [whole] * (1 + len(places)),
         out_specs=[whole] * (2 + blocks),
         scratch_shapes=[
             pltpu.VMEM(w_in.shape, jnp.bfloat16),
             pltpu.VMEM(w_out.shape, jnp.bfloat16),
             pltpu.VMEM(rel_bias.shape, jnp.float32),
-            pltpu.VMEM((own_count,) + packed[0].shape, jnp.bfloat16),
-            pltpu.SemaphoreType.DMA((3 + own_count,)),
+            pltpu.SemaphoreType.DMA((3,)),
         ]
         + step_scratch(places, length, width, blocks, items),
         out_shape=[pltpu.VMEM((users, length), jnp.float32)]
@@ -356,7 +337,7 @@
         name="first_users",
     )(
         ids, *[in_hbm(array) for array in (w_in, w_out, rel_bias)], in_vmem(units),
-        *[in_hbm(array) for array in packed[:own_count]], *[in_vmem(array) for array in packed[own_count:]],
+        *[in_vmem(array) for array in packed],
     )
 
 
@@ -386,16 +367,19 @@
     slots = user_count // groups
     group, mine = lax.axis_index("dp").astype(jnp.int32), lax.axis_index("blk").astype(jnp.int32)
 
-    work = sorted(
-        ((shift, slot) for shift in range(groups) for slot in range(slots)),
-        key=lambda pair: (pair[0] != 0, abs(pair[0] - groups / 2)),
-    )
+    by_distance = sorted(range(1, groups), key=lambda shift: abs(shift - groups / 2))
+    early = [groups - by_distance[-1], *by_distance[: groups // 2 - 2]]
+    late = [shift for shift in by_distance if shift not in early]
+    work = [(shift, slot) for shift in [0, *early, *late] for slot in range(slots)]
     *packed, units = pack(
         histories, lengths, targets, send_list, item_pool, work, groups, group.reshape(1), blocks
     )
-    packed = [
-        users if shift == 0 else from_behind(users, "dp", shift) for users, (shift, _) in zip(packed, work)
-    ]
+    half = user_count // 2
+    for k in range(slots, user_count):
+        if k >= half:
+            before = slots * (1 if work[k][0] == late[1] else 2)
+            packed[before], packed[k] = lax.optimization_barrier((packed[before], packed[k]))
+        packed[k] = from_behind(packed[k], "dp", work[k][0])
     units = lax.all_to_all(units, "blk", split_axis=0, concat_axis=0, tiled=True)
 
     pool_float = item_pool.astype(jnp.float32)
@@ -404,10 +388,9 @@
 
     came = [((group - shift) % groups) * slots + slot for shift, slot in work]
     ids = jnp.stack([mine, mine ^ 2, mine ^ 1, mine ^ 3, *came])
-    half = user_count // 2
     order = tuple(range(user_count))
     loss, *sums, bias = first_call(
-        ids, order[:half], slots, user_count, packed[:half], units, w_in, w_out, rel_bias
+        ids, order[:half], user_count, packed[:half], units, w_in, w_out, rel_bias
     )
     row_loss, own, over, side, far = second_call(
         ids, order[half:], packed[half:], units, w_in, w_out, loss, sums, bias

time: 56 us -> 56.8 us (1.014)
  the two profiles are of different devices: /device:TPU:0 before, /device:TPU:6 now
where the time goes in v10:
time: 56.8 us; the launch traced here: 56.9 us
  waiting for transfers between devices  28 us (49%)
  Pallas kernels  13.3 us (23%)
  starting transfers between devices  13.2 us (23%)
  other arithmetic  1.48 us (3%)
  between operations  0.75 us (1%)
    ppermute x7, waiting for transfers between devices, from_behind(): lax.ppermute(array, axis, [(i, (i + by) % devices) for i in range(devices)])  18.8 us
    ppermute x3, waiting for transfers between devices, swap(): return lax.ppermute(array, axis, [(i, i ^ bit) for i in range(devices)])  9.2 us
    ppermute x7, starting transfers between devices, from_behind(): lax.ppermute(array, axis, [(i, (i + by) % devices) for i in range(devices)])  8.62 us
    pallas_call x1, Pallas kernels, first_call(): pl.pallas_call(functools.partial(first_kernel, places, blocks), in_specs=...  6.08 us
    pallas_call x1, Pallas kernels, second_call(): pl.pallas_call(functools.partial(second_kernel, places, blocks), in_specs...  4.77 us
    all_to_all x1, starting transfers between devices, shards(): lax.all_to_all(units, 'blk', split_axis=0, concat_axis=0, tiled=True)  4 us
    pallas_call x1, Pallas kernels, pack(): pl.pallas_call(functools.partial(pack_kernel, work, groups), in_specs=[pl...  2.44 us
  transfers between devices with their start and end apart: 11, of which 5 were waited for; matrix products, arithmetic and copies ran while one was open for 1% of the time, Pallas kernels for 11%

profile of v10, /device:TPU:6, one launch (start us, length us, event | category | flops | bytes accessed | tf_op | source)
XLA Modules:
  0.0 56.9 jit_solution(3393567988947359313)
XLA Ops:
  0.6 2.4 %pack.1 = (bf16[520,128]{1,0:T(8,128)(2,1)S(1)}, bf16[520,128]{1,0:T(8,128)(2,1)S(1)}, bf16[520,128]{1,0:T(8,128)(2,1)S(1)}, bf16[520,128]{1,0:T(8,128)(2,1)S(1)...) custom-call(s32[1]{0:T(128)} %bitcast.12.group_ref, ...), custom_call_target="tpu_custom_call" | custom-call | tf_op jit(solution)/shard_map/pack/pallas_call | solution.py:97
  3.1 4.0 %all-to-all-start = ((bf16[4,256,512]{2,1,0:T(8,128)(2,1)}), bf16[4,256,512]{2,1,0:T(8,128)(2,1)S(1)}, u32[]{:S(2)}, u32[]{:S(2)}) async-start(bf16[4,256,512]{2,1,0:T(8,128)(2,1)} %get-tuple-element.30), calls=%async_computation | async-start | bytes 2097152 | tf_op jit(solution)/shard_map/all_to_all | solution.py:383
  7.1 2.6 %collective-permute-start.1 = (bf16[520,128]{1,0:T(8,128)(2,1)S(1)}, bf16[520,128]{1,0:T(8,128)(2,1)S(1)}, u32[]{:S(2)}, u32[]{:S(2)}) collective-permute-start(bf16[520,128]{1,0:T(8,128)(2,1)S(1)} %get-tuple-element.35), channel_id=1, source_target_pairs={{0,16},{4,20},{8,24},{12,28},{16,0},{20,4},{24,8},{28,12},{1,17},{... | collective-permute-start | bytes 399368 | tf_op jit(solution)/shard_map/ppermute | solution.py:25
  9.7 1.5 %collective-permute-start = (bf16[520,128]{1,0:T(8,128)(2,1)S(1)}, bf16[520,128]{1,0:T(8,128)(2,1)S(1)}, u32[]{:S(2)}, u32[]{:S(2)}) collective-permute-start(bf16[520,128]{1,0:T(8,128)(2,1)S(1)} %get-tuple-element.32), channel_id=1, source_target_pairs={{0,4},{4,8},{8,12},{12,16},{16,20},{20,24},{24,28},{28,0},{1,5},{5... | collective-permute-start | bytes 399368 | tf_op jit(solution)/shard_map/ppermute | solution.py:25
  11.2 0.3 collective-permute-start.2
  11.5 11.5 %collective-permute-done.1.refs_2_ = bf16[520,128]{1,0:T(8,128)(2,1)S(1)} collective-permute-done((bf16[520,128]{1,0:T(8,128)(2,1)S(1)}, bf16[520,128]{1,0:T(8,128)(2,1)S(1)}, u32[]{:S(2)}, u32[]{:S(2)}) %collective-permute-start.1) | collective-permute-done | bytes 133152 | tf_op jit(solution)/shard_map/ppermute | solution.py:25
  22.9 0.0 collective-permute-done.refs_1_
  22.9 0.0 collective-permute-start.6
  22.9 0.0 collective-permute-start.5
  22.9 4.2 %collective-permute-start.3 = (bf16[520,128]{1,0:T(8,128)(2,1)S(1)}, bf16[520,128]{1,0:T(8,128)(2,1)S(1)}, u32[]{:S(2)}, u32[]{:S(2)}) collective-permute-start(bf16[520,128]{1,0:T(8,128)(2,1)S(1)} %get-tuple-element.49), channel_id=1, source_target_pairs={{0,20},{4,24},{8,28},{12,0},{16,4},{20,8},{24,12},{28,16},{1,21},{... | collective-permute-start | bytes 399368 | tf_op jit(solution)/shard_map/ppermute | solution.py:25
  27.2 0.0 collective-permute-start.4
  27.2 0.1 stack.51.id_ref
  27.3 0.0 collective-permute-done.2.refs_3_
  27.3 0.0 all-to-all-done.unit_ref
  27.3 0.0 copy-start
  27.3 0.0 copy-start.1
  27.3 6.1 %first_users.1 = (f32[8,128]{1,0:T(8,128)S(1)}, f32[256,512]{1,0:T(8,128)S(1)}, f32[256,512]{1,0:T(8,128)S(1)}, f32[256,512]{1,0:T(8,128)S(1)}, f32[256,512]{1,0:T(8,128)S(1)}, /*index=5*/f32[4,128,256]{2,1,0:T(8,128)S(1)}) custom-call(s32[12]{0:T(128)S(1)} %stack.51.id_ref, bf16[512,2048]{1,0:T(8,128)(2,1)} %w_in.1, bf16[512,512]{1,0:T(8,128)(2,1)} %w_out.1, ...), custom_call_target="tpu_custom_call" | custom-call | tf_op jit(solution)/shard_map/first_users/pallas_call | solution.py:322
  33.4 0.0 collective-permute-done.6.refs_7_
  33.4 0.0 collective-permute-done.5.refs_6_
  33.4 7.4 %collective-permute-done.3.refs_4_ = bf16[520,128]{1,0:T(8,128)(2,1)S(1)} collective-permute-done((bf16[520,128]{1,0:T(8,128)(2,1)S(1)}, bf16[520,128]{1,0:T(8,128)(2,1)S(1)}, u32[]{:S(2)}, u32[]{:S(2)}) %collective-permute-start.3) | collective-permute-done | bytes 133152 | tf_op jit(solution)/shard_map/ppermute | solution.py:25
  40.8 0.0 collective-permute-done.4.refs_5_
  40.8 0.0 copy-done
  40.8 0.0 copy-done.1
  40.8 0.0 copy-start.2
  40.8 4.8 %second_users.1 = (f32[8,128]{1,0:T(8,128)}, f32[256,512]{1,0:T(8,128)S(1)}, f32[256,512]{1,0:T(8,128)S(1)}, bf16[256,512]{1,0:T(8,128)(2,1)S(1)}, bf16[256,512]{1,0:T(8,128)(2,1)S(1)}) custom-call(s32[12]{0:T(128)S(1)} %stack.51.id_ref, bf16[512,2048]{1,0:T(8,128)(2,1)S(1)} %copy-done, bf16[512,512]{1,0:T(8,128)(2,1)S(1)} %copy-done.1, ...), custom_call_target="tpu_custom_call" | custom-call | tf_op jit(solution)/shard_map/second_users/pallas_call | solution.py:348
  45.6 0.0 collective-permute-start.8
  45.6 0.5 collective-permute-start.7
  46.1 1.0 %collective-permute-done.8 = bf16[256,512]{1,0:T(8,128)(2,1)S(1)} collective-permute-done((bf16[256,512]{1,0:T(8,128)(2,1)S(1)}, bf16[256,512]{1,0:T(8,128)(2,1)S(1)}, u32[]{:S(2)}, u32[]{:S(2)}) %collective-permute-start.8) | collective-permute-done | bytes 262176 | tf_op jit(solution)/shard_map/ppermute | solution.py:20
  47.1 0.1 add_convert_fusion
  47.2 0.1 collective-permute-start.9
  47.3 0.0 copy-done.2
  47.3 0.1 fusion
  47.4 0.1 collective-permute-done.7
  47.5 8.1 %collective-permute-done.9 = bf16[256,512]{1,0:T(8,128)(2,1)S(1)} collective-permute-done((bf16[256,512]{1,0:T(8,128)(2,1)S(1)}, bf16[256,512]{1,0:T(8,128)(2,1)S(1)}, u32[]{:S(2)}, u32[]{:S(2)}) %collective-permute-start.9) | collective-permute-done | bytes 262176 | tf_op jit(solution)/shard_map/ppermute | solution.py:20
  55.6 0.3 multiply_reduce_fusion
  55.9 1.0 %subtract_divide_fusion = f32[256,512]{1,0:T(8,128)} fusion(bf16[256,512]{1,0:T(8,128)(2,1)S(1)} %copy-done.2, f32[256]{0:T(256)S(1)} %multiply_reduce_fusion, f32[256]{0:T(256)S(1)} %add_sqrt_fusion, bf16[256,512]{1,0:T(8,128)(2,1)S(1)} %collective-permute-done.9, f32[256,512]{1,0:T(8,128)S(1)} %get-tuple-element.54, ...), kind=kLoop, calls=%fused_computation.3 | loop fusion | flops 1310720 | bytes 1837056 | tf_op jit(solution)/shard_map/div | solution.py:401
  (1 shorter events, 0.0 us)
Async XLA Ops:
  3.1 24.2 %all-to-all-start = ((bf16[4,256,512]{2,1,0:T(8,128)(2,1)}), bf16[4,256,512]{2,1,0:T(8,128)(2,1)S(1)}, u32[]{:S(2)}, u32[]{:S(2)}) async-start(bf16[4,256,512]{2,1,0:T(8,128)(2,1)} %get-tuple-element.30), calls=%async_computation | async-start | bytes 2097152 | tf_op jit(solution)/shard_map/all_to_all | solution.py:383
  7.1 15.8 %collective-permute-start.1 = (bf16[520,128]{1,0:T(8,128)(2,1)S(1)}, bf16[520,128]{1,0:T(8,128)(2,1)S(1)}, u32[]{:S(2)}, u32[]{:S(2)}) collective-permute-start(bf16[520,128]{1,0:T(8,128)(2,1)S(1)} %get-tuple-element.35), channel_id=1, source_target_pairs={{0,16},{4,20},{8,24},{12,28},{16,0},{20,4},{24,8},{28,12},{1,17},{... | collective-permute-start | bytes 399368 | tf_op jit(solution)/shard_map/ppermute | solution.py:25
  9.7 13.3 %collective-permute-start = (bf16[520,128]{1,0:T(8,128)(2,1)S(1)}, bf16[520,128]{1,0:T(8,128)(2,1)S(1)}, u32[]{:S(2)}, u32[]{:S(2)}) collective-permute-start(bf16[520,128]{1,0:T(8,128)(2,1)S(1)} %get-tuple-element.32), channel_id=1, source_target_pairs={{0,4},{4,8},{8,12},{12,16},{16,20},{20,24},{24,28},{28,0},{1,5},{5... | collective-permute-start | bytes 399368 | tf_op jit(solution)/shard_map/ppermute | solution.py:25
  11.2 16.0 %collective-permute-start.2 = (bf16[520,128]{1,0:T(8,128)(2,1)S(1)}, bf16[520,128]{1,0:T(8,128)(2,1)S(1)}, u32[]{:S(2)}, u32[]{:S(2)}) collective-permute-start(bf16[520,128]{1,0:T(8,128)(2,1)S(1)} %get-tuple-element.42), channel_id=1, source_target_pairs={{0,12},{4,16},{8,20},{12,24},{16,28},{20,0},{24,4},{28,8},{1,13},{... | collective-permute-start | bytes 399368 | tf_op jit(solution)/shard_map/ppermute | solution.py:25
  22.9 10.5 %collective-permute-start.6 = (bf16[520,128]{1,0:T(8,128)(2,1)S(1)}, bf16[520,128]{1,0:T(8,128)(2,1)S(1)}, u32[]{:S(2)}, u32[]{:S(2)}) collective-permute-start(bf16[520,128]{1,0:T(8,128)(2,1)S(1)} %get-tuple-element.52), channel_id=1, source_target_pairs={{0,28},{4,0},{8,4},{12,8},{16,12},{20,16},{24,20},{28,24},{1,29},{... | collective-permute-start | bytes 399368 | tf_op jit(solution)/shard_map/ppermute | solution.py:25
  22.9 10.5 %collective-permute-start.5 = (bf16[520,128]{1,0:T(8,128)(2,1)S(1)}, bf16[520,128]{1,0:T(8,128)(2,1)S(1)}, u32[]{:S(2)}, u32[]{:S(2)}) collective-permute-start(bf16[520,128]{1,0:T(8,128)(2,1)S(1)} %get-tuple-element.51), channel_id=1, source_target_pairs={{0,24},{4,28},{8,0},{12,4},{16,8},{20,12},{24,16},{28,20},{1,25},{... | collective-permute-start | bytes 399368 | tf_op jit(solution)/shard_map/ppermute | solution.py:25
  22.9 17.8 %collective-permute-start.3 = (bf16[520,128]{1,0:T(8,128)(2,1)S(1)}, bf16[520,128]{1,0:T(8,128)(2,1)S(1)}, u32[]{:S(2)}, u32[]{:S(2)}) collective-permute-start(bf16[520,128]{1,0:T(8,128)(2,1)S(1)} %get-tuple-element.49), channel_id=1, source_target_pairs={{0,20},{4,24},{8,28},{12,0},{16,4},{20,8},{24,12},{28,16},{1,21},{... | collective-permute-start | bytes 399368 | tf_op jit(solution)/shard_map/ppermute | solution.py:25
  27.2 13.6 %collective-permute-start.4 = (bf16[520,128]{1,0:T(8,128)(2,1)S(1)}, bf16[520,128]{1,0:T(8,128)(2,1)S(1)}, u32[]{:S(2)}, u32[]{:S(2)}) collective-permute-start(bf16[520,128]{1,0:T(8,128)(2,1)S(1)} %get-tuple-element.50), channel_id=1, source_target_pairs={{0,8},{4,12},{8,16},{12,20},{16,24},{20,28},{24,0},{28,4},{1,9},{5... | collective-permute-start | bytes 399368 | tf_op jit(solution)/shard_map/ppermute | solution.py:25
  27.3 13.5 %copy-start = (bf16[512,2048]{1,0:T(8,128)(2,1)S(1)}, bf16[512,2048]{1,0:T(8,128)(2,1)}, u32[]{:S(2)}) copy-start(bf16[512,2048]{1,0:T(8,128)(2,1)} %w_in.1) | copy-start | bytes 6291460
  27.3 13.5 %copy-start.1 = (bf16[512,512]{1,0:T(8,128)(2,1)S(1)}, bf16[512,512]{1,0:T(8,128)(2,1)}, u32[]{:S(2)}) copy-start(bf16[512,512]{1,0:T(8,128)(2,1)} %w_out.1) | copy-start | bytes 1572868
  40.8 6.5 %copy-start.2 = (bf16[256,512]{1,0:T(8,128)(2,1)S(1)}, bf16[256,512]{1,0:T(8,128)(2,1)}, u32[]{:S(2)}) copy-start(bf16[256,512]{1,0:T(8,128)(2,1)} %pool_any.1) | copy-start | bytes 786436
  45.6 1.5 %collective-permute-start.8 = (bf16[256,512]{1,0:T(8,128)(2,1)S(1)}, bf16[256,512]{1,0:T(8,128)(2,1)S(1)}, u32[]{:S(2)}, u32[]{:S(2)}) collective-permute-start(bf16[256,512]{1,0:T(8,128)(2,1)S(1)} %get-tuple-element.57), channel_id=1, source_target_pairs={{0,1},{1,0},{2,3},{3,2},{4,5},{5,4},{6,7},{7,6},{8,9},{9,8},{10,11... | collective-permute-start | bytes 786440 | tf_op jit(solution)/shard_map/ppermute | solution.py:20
  45.6 1.9 %collective-permute-start.7 = (bf16[256,512]{1,0:T(8,128)(2,1)S(1)}, bf16[256,512]{1,0:T(8,128)(2,1)S(1)}, u32[]{:S(2)}, u32[]{:S(2)}) collective-permute-start(bf16[256,512]{1,0:T(8,128)(2,1)S(1)} %get-tuple-element.55), channel_id=1, source_target_pairs={{0,1},{1,0},{2,3},{3,2},{4,5},{5,4},{6,7},{7,6},{8,9},{9,8},{10,11... | collective-permute-start | bytes 786440 | tf_op jit(solution)/shard_map/ppermute | solution.py:20
  47.2 8.4 %collective-permute-start.9 = (bf16[256,512]{1,0:T(8,128)(2,1)S(1)}, bf16[256,512]{1,0:T(8,128)(2,1)S(1)}, u32[]{:S(2)}, u32[]{:S(2)}) collective-permute-start(bf16[256,512]{1,0:T(8,128)(2,1)S(1)} %add_convert_fusion), channel_id=1, source_target_pairs={{0,2},{1,3},{2,0},{3,1},{4,6},{5,7},{6,4},{7,5},{8,10},{9,11},{10,... | collective-permute-start | bytes 786440 | tf_op jit(solution)/shard_map/ppermute | solution.py:20

commit v11 on v10

--- a/solution.py
+++ b/solution.py
@@ -124,29 +124,30 @@
         )
 
 
-def first_kernel(
-    places, blocks, id_ref, w_in_any, w_out_any, rel_any, unit_ref, *refs
-):
-    count = len(places)
-    x_refs, refs = refs[:count], refs[count:]
-    loss_ref, sums, bias, refs = refs[0], refs[1 : 1 + blocks], refs[1 + blocks], refs[2 + blocks :]
-    w_in, w_out, rel, sems = refs[:4]
-    heads, length = rel.shape
-    moves = [(rel_any, rel), (w_in_any, w_in), (w_out_any, w_out)]
-    copies = [pltpu.make_async_copy(*move, sems.at[k]) for k, move in enumerate(moves)]
+def load_kernel(w_in_any, w_out_any, rel, w_in, w_out, bias, sems):
+    copies = [
+        pltpu.make_async_copy(w_in_any, w_in, sems.at[0]),
+        pltpu.make_async_copy(w_out_any, w_out, sems.at[1]),
+    ]
     for copy in copies:
         copy.start()
-    loss_ref[...] = jnp.zeros_like(loss_ref)
-    for ref in sums:
-        ref[...] = jnp.zeros_like(ref)
-    copies[0].wait()
+    heads, length = rel.shape
     for h in range(heads):
         wide = jnp.broadcast_to(0.5 * rel[h : h + 1, :], (length, length))
         turned = pltpu.roll(wide, 0, 1, stride=1, stride_axis=0).T
         bias[h] = jnp.concatenate([turned, turned], axis=1)
-    for copy in copies[1:]:
+    for copy in copies:
         copy.wait()
-    users_kernel(places, blocks, id_ref, x_refs, w_in, w_out, unit_ref, sums, loss_ref, bias, refs[4:])
+
+
+def first_kernel(places, blocks, id_ref, w_in, w_out, bias, unit_ref, *refs):
+    count = len(places)
+    x_refs, refs = refs[:count], refs[count:]
+    loss_ref, sums, scratch = refs[0], refs[1 : 1 + blocks], refs[1 + blocks :]
+    loss_ref[...] = jnp.zeros_like(loss_ref)
+    for ref in sums:
+        ref[...] = jnp.zeros_like(ref)
+    users_kernel(places, blocks, id_ref, x_refs, w_in, w_out, unit_ref, sums, loss_ref, bias, scratch)
 
 
 def second_kernel(places, blocks, id_ref, w_in, w_out, bias, unit_ref, loss_in, *refs):
@@ -315,30 +316,36 @@
 far_off = pl.BlockSpec(memory_space=pltpu.HBM)
 
 
-def first_call(ids, places, users, packed, units, w_in, w_out, rel_bias):
+def load_call(w_in, w_out, rel_bias):
     heads, length = rel_bias.shape
+    return pl.pallas_call(
+        load_kernel,
+        in_specs=[far_off, far_off, whole],
+        out_specs=[whole] * 3,
+        scratch_shapes=[pltpu.SemaphoreType.DMA((2,))],
+        out_shape=[
+            pltpu.VMEM(w_in.shape, jnp.bfloat16),
+            pltpu.VMEM(w_out.shape, jnp.bfloat16),
+            pltpu.VMEM((heads, length, 2 * length), jnp.float32),
+        ],
+        name="load",
+    )(in_hbm(w_in), in_hbm(w_out), rel_bias)
+
+
+def first_call(ids, places, users, packed, units, w_in, w_out, bias):
+    length = bias.shape[1]
     width, (blocks, items, _) = w_out.shape[0], units.shape
-    table = (heads, length, 2 * length)
+    arrays = [w_in, w_out, bias, units, *packed]
     return pl.pallas_call(
         functools.partial(first_kernel, places, blocks),
-        in_specs=[scalars] + [far_off] * 3 + [whole] * (1 + len(places)),
-        out_specs=[whole] * (2 + blocks),
-        scratch_shapes=[
-            pltpu.VMEM(w_in.shape, jnp.bfloat16),
-            pltpu.VMEM(w_out.shape, jnp.bfloat16),
-            pltpu.VMEM(rel_bias.shape, jnp.float32),
-            pltpu.SemaphoreType.DMA((3,)),
-        ]
-        + step_scratch(places, length, width, blocks, items),
+        in_specs=[scalars] + [whole] * len(arrays),
+        out_specs=[whole] * (1 + blocks),
+        scratch_shapes=step_scratch(places, length, width, blocks, items),
         out_shape=[pltpu.VMEM((users, length), jnp.float32)]
-        + [pltpu.VMEM((items, width), jnp.float32)] * blocks
-        + [pltpu.VMEM(table, jnp.float32)],
+        + [pltpu.VMEM((items, width), jnp.float32)] * blocks,
         compiler_params=pltpu.CompilerParams(vmem_limit_bytes=24 * 1024 * 1024),
         name="first_users",
-    )(
-        ids, *[in_hbm(array) for array in (w_in, w_out, rel_bias)], in_vmem(units),
-        *[in_vmem(array) for array in packed],
-    )
+    )(ids, *[in_vmem(array) for array in arrays])
 
 
 def second_call(ids, places, packed, units, w_in, w_out, loss, sums, bias):
@@ -367,18 +374,20 @@
     slots = user_count // groups
     group, mine = lax.axis_index("dp").astype(jnp.int32), lax.axis_index("blk").astype(jnp.int32)
 
-    by_distance = sorted(range(1, groups), key=lambda shift: abs(shift - groups / 2))
-    early = [groups - by_distance[-1], *by_distance[: groups // 2 - 2]]
-    late = [shift for shift in by_distance if shift not in early]
-    work = [(shift, slot) for shift in [0, *early, *late] for slot in range(slots)]
+    work = sorted(
+        ((shift, slot) for shift in range(groups) for slot in range(slots)),
+        key=lambda pair: (pair[0] != 0, abs(pair[0] - groups / 2)),
+    )
     *packed, units = pack(
         histories, lengths, targets, send_list, item_pool, work, groups, group.reshape(1), blocks
     )
     half = user_count // 2
     for k in range(slots, user_count):
-        if k >= half:
-            before = slots * (1 if work[k][0] == late[1] else 2)
-            packed[before], packed[k] = lax.optimization_barrier((packed[before], packed[k]))
+        if k == user_count - 2 * slots:
+            packed[slots], w_in = lax.optimization_barrier((packed[slots], w_in))
+            w_in, w_out, bias = load_call(w_in, w_out, rel_bias)
+        if k >= user_count - 2 * slots:
+            packed[k], w_out = lax.optimization_barrier((packed[k], w_out))
         packed[k] = from_behind(packed[k], "dp", work[k][0])
     units = lax.all_to_all(units, "blk", split_axis=0, concat_axis=0, tiled=True)
 
@@ -389,9 +398,7 @@
     came = [((group - shift) % groups) * slots + slot for shift, slot in work]
     ids = jnp.stack([mine, mine ^ 2, mine ^ 1, mine ^ 3, *came])
     order = tuple(range(user_count))
-    loss, *sums, bias = first_call(
-        ids, order[:half], user_count, packed[:half], units, w_in, w_out, rel_bias
-    )
+    loss, *sums = first_call(ids, order[:half], user_count, packed[:half], units, w_in, w_out, bias)
     row_loss, own, over, side, far = second_call(
         ids, order[half:], packed[half:], units, w_in, w_out, loss, sums, bias
     )

time: 56.8 us -> 58.2 us (1.025)
  the two profiles are of different devices: /device:TPU:6 before, /device:TPU:0 now
where the time goes in v11:
time: 58.2 us; the launch traced here: 57.4 us
  starting transfers between devices  20.6 us (35%)
  waiting for transfers between devices  17.6 us (30%)
  Pallas kernels  15.4 us (26%)
  local copies, waits for them, and re-layouts  1.65 us (3%)
  other arithmetic  1.51 us (3%)
  between operations  0.75 us (1%)
    ppermute x7, starting transfers between devices, from_behind(): lax.ppermute(array, axis, [(i, (i + by) % devices) for i in range(devices)])  13.9 us
    ppermute x7, waiting for transfers between devices, from_behind(): lax.ppermute(array, axis, [(i, (i + by) % devices) for i in range(devices)])  10.1 us
    ppermute x3, waiting for transfers between devices, swap(): return lax.ppermute(array, axis, [(i, i ^ bit) for i in range(devices)])  7.48 us
    pallas_call x1, Pallas kernels, first_call(): pl.pallas_call(functools.partial(first_kernel, places, blocks), in_specs=...  4.95 us
    pallas_call x1, Pallas kernels, second_call(): pl.pallas_call(functools.partial(second_kernel, places, blocks), in_specs...  4.77 us
    all_to_all x1, starting transfers between devices, shards(): lax.all_to_all(units, 'blk', split_axis=0, concat_axis=0, tiled=True)  4.25 us
    pallas_call x1, Pallas kernels, pack(): pl.pallas_call(functools.partial(pack_kernel, work, groups), in_specs=[pl...  3.23 us
    ppermute x3, starting transfers between devices, swap(): return lax.ppermute(array, axis, [(i, i ^ bit) for i in range(devices)])  2.45 us
  transfers between devices with their start and end apart: 11, of which 4 were waited for; matrix products, arithmetic and copies ran while one was open for 1% of the time, Pallas kernels for 13%

profile of v11, /device:TPU:0, one launch (start us, length us, event | category | flops | bytes accessed | tf_op | source)
XLA Modules:
  0.0 57.4 jit_solution(17987787635843595572)
XLA Ops:
  0.6 3.2 %pack.1 = (bf16[520,128]{1,0:T(8,128)(2,1)S(1)}, bf16[520,128]{1,0:T(8,128)(2,1)S(1)}, bf16[520,128]{1,0:T(8,128)(2,1)}, bf16[520,128]{1,0:T(8,128)(2,1)}, bf16[...) custom-call(s32[1]{0:T(128)} %bitcast.12.group_ref, ...), custom_call_target="tpu_custom_call" | custom-call | tf_op jit(solution)/shard_map/pack/pallas_call | solution.py:97
  3.9 0.0 copy-start.2
  3.9 0.0 copy-start.3
  3.9 4.3 %all-to-all-start = ((bf16[4,256,512]{2,1,0:T(8,128)(2,1)}), bf16[4,256,512]{2,1,0:T(8,128)(2,1)}, u32[]{:S(2)}, u32[]{:S(2)}) async-start(bf16[4,256,512]{2,1,0:T(8,128)(2,1)} %get-tuple-element.39), calls=%async_computation | async-start | bytes 2097152 | tf_op jit(solution)/shard_map/all_to_all | solution.py:392
  8.2 4.1 %collective-permute-start = (bf16[520,128]{1,0:T(8,128)(2,1)S(1)}, bf16[520,128]{1,0:T(8,128)(2,1)S(1)}, u32[]{:S(2)}, u32[]{:S(2)}) collective-permute-start(bf16[520,128]{1,0:T(8,128)(2,1)S(1)} %get-tuple-element.30), channel_id=1, source_target_pairs={{0,16},{4,20},{8,24},{12,28},{16,0},{20,4},{24,8},{28,12},{1,17},{... | collective-permute-start | bytes 399368 | tf_op jit(solution)/shard_map/ppermute | solution.py:25
  12.3 2.5 %collective-permute-start.1 = (bf16[520,128]{1,0:T(8,128)(2,1)}, bf16[520,128]{1,0:T(8,128)(2,1)}, u32[]{:S(2)}, u32[]{:S(2)}) collective-permute-start(bf16[520,128]{1,0:T(8,128)(2,1)} %get-tuple-element.42), channel_id=1, source_target_pairs={{0,12},{4,16},{8,20},{12,24},{16,28},{20,0},{24,4},{28,8},{1,13},{... | collective-permute-start | bytes 399368 | tf_op jit(solution)/shard_map/ppermute | solution.py:25
  14.8 1.3 %collective-permute-start.2 = (bf16[520,128]{1,0:T(8,128)(2,1)}, bf16[520,128]{1,0:T(8,128)(2,1)}, u32[]{:S(2)}, u32[]{:S(2)}) collective-permute-start(bf16[520,128]{1,0:T(8,128)(2,1)} %get-tuple-element.43), channel_id=1, source_target_pairs={{0,20},{4,24},{8,28},{12,0},{16,4},{20,8},{24,12},{28,16},{1,21},{... | collective-permute-start | bytes 399368 | tf_op jit(solution)/shard_map/ppermute | solution.py:25
  16.1 1.6 %collective-permute-start.3 = (bf16[520,128]{1,0:T(8,128)(2,1)}, bf16[520,128]{1,0:T(8,128)(2,1)S(1)}, u32[]{:S(2)}, u32[]{:S(2)}) collective-permute-start(bf16[520,128]{1,0:T(8,128)(2,1)} %get-tuple-element.49), channel_id=1, source_target_pairs={{0,8},{4,12},{8,16},{12,20},{16,24},{20,28},{24,0},{28,4},{1,9},{5... | collective-permute-start | bytes 399368 | tf_op jit(solution)/shard_map/ppermute | solution.py:25
  17.7 2.2 %collective-permute-start.4 = (bf16[520,128]{1,0:T(8,128)(2,1)}, bf16[520,128]{1,0:T(8,128)(2,1)S(1)}, u32[]{:S(2)}, u32[]{:S(2)}) collective-permute-start(bf16[520,128]{1,0:T(8,128)(2,1)} %get-tuple-element.50), channel_id=1, source_target_pairs={{0,24},{4,28},{8,0},{12,4},{16,8},{20,12},{24,16},{28,20},{1,25},{... | collective-permute-start | bytes 399368 | tf_op jit(solution)/shard_map/ppermute | solution.py:25
  19.9 0.0 copy-done.2
  19.9 0.0 copy-done.3
  19.9 8.1 %collective-permute-done.refs_1_ = bf16[520,128]{1,0:T(8,128)(2,1)S(1)} collective-permute-done((bf16[520,128]{1,0:T(8,128)(2,1)S(1)}, bf16[520,128]{1,0:T(8,128)(2,1)S(1)}, u32[]{:S(2)}, u32[]{:S(2)}) %collective-permute-start) | collective-permute-done | bytes 133152 | tf_op jit(solution)/shard_map/ppermute | solution.py:25
  28.1 0.0 copy-start
  28.1 0.7 %copy-done = bf16[520,128]{1,0:T(8,128)(2,1)} copy-done((bf16[520,128]{1,0:T(8,128)(2,1)}, bf16[520,128]{1,0:T(8,128)(2,1)S(1)}, u32[]{:S(2)}) %copy-start) | copy-done | bytes 133144
  28.7 2.4 %load.1 = (bf16[512,2048]{1,0:T(8,128)(2,1)S(1)}, bf16[512,512]{1,0:T(8,128)(2,1)S(1)}, f32[4,128,256]{2,1,0:T(8,128)S(1)}) custom-call(bf16[512,2048]{1,0:T(8,128)(2,1)} %w_in_any, bf16[512,512]{1,0:T(8,128)(2,1)} %w_out_any.1, f32[4,128]{1,0:T(4,128)} %rel.1), custom_call_target="tpu_custom_call" | custom-call | tf_op jit(solution)/shard_map/load/pallas_call | solution.py:321
  31.1 2.0 %collective-permute-start.6 = (bf16[520,128]{1,0:T(8,128)(2,1)}, bf16[520,128]{1,0:T(8,128)(2,1)}, u32[]{:S(2)}, u32[]{:S(2)}) collective-permute-start(bf16[520,128]{1,0:T(8,128)(2,1)} %copy-done.3), channel_id=1, source_target_pairs={{0,28},{4,0},{8,4},{12,8},{16,12},{20,16},{24,20},{28,24},{1,29},{... | collective-permute-start | bytes 399368 | tf_op jit(solution)/shard_map/ppermute | solution.py:25
  33.1 0.0 collective-permute-done.1.refs_2_
  33.1 0.1 collective-permute-start.5
  33.2 0.1 stack.51.id_ref
  33.3 0.0 collective-permute-done.2.refs_3_
  33.3 0.0 all-to-all-done.unit_ref
  33.3 0.0 copy-start.1
  33.3 0.9 %copy-done.1 = bf16[520,128]{1,0:T(8,128)(2,1)S(1)} copy-done((bf16[520,128]{1,0:T(8,128)(2,1)S(1)}, bf16[520,128]{1,0:T(8,128)(2,1)}, u32[]{:S(2)}) %copy-start.1) | copy-done | bytes 133144
  34.2 5.0 %first_users.1 = (f32[8,128]{1,0:T(8,128)S(1)}, f32[256,512]{1,0:T(8,128)S(1)}, f32[256,512]{1,0:T(8,128)S(1)}, f32[256,512]{1,0:T(8,128)S(1)}, f32[256,512]{1,0:T(8,128)S(1)}) custom-call(s32[12]{0:T(128)S(1)} %stack.51.id_ref, bf16[512,2048]{1,0:T(8,128)(2,1)S(1)} %get-tuple-element.32.w_in, bf16[512,512]{1,0:T(8,128)(2,1)S(1)} %get-tuple-element.37.w_out, ...), custom_call_target="tpu_custom_call" | custom-call | tf_op jit(solution)/shard_map/first_users/pallas_call | solution.py:339
  39.2 0.0 collective-permute-done.3.refs_4_
  39.2 0.0 collective-permute-done.4.refs_5_
  39.2 0.0 collective-permute-done.6.refs_7_
  39.2 2.0 %collective-permute-done.5.refs_6_ = bf16[520,128]{1,0:T(8,128)(2,1)} collective-permute-done((bf16[520,128]{1,0:T(8,128)(2,1)}, bf16[520,128]{1,0:T(8,128)(2,1)}, u32[]{:S(2)}, u32[]{:S(2)}) %collective-permute-start.5) | collective-permute-done | bytes 133152 | tf_op jit(solution)/shard_map/ppermute | solution.py:25
  41.2 0.0 copy-start.4
  41.2 4.8 %second_users.1 = (f32[8,128]{1,0:T(8,128)}, f32[256,512]{1,0:T(8,128)S(1)}, f32[256,512]{1,0:T(8,128)S(1)}, bf16[256,512]{1,0:T(8,128)(2,1)S(1)}, bf16[256,512]{1,0:T(8,128)(2,1)S(1)}) custom-call(s32[12]{0:T(128)S(1)} %stack.51.id_ref, bf16[512,2048]{1,0:T(8,128)(2,1)S(1)} %get-tuple-element.32.w_in, bf16[512,512]{1,0:T(8,128)(2,1)S(1)} %get-tuple-element.37.w_out, ...), custom_call_target="tpu_custom_call" | custom-call | tf_op jit(solution)/shard_map/second_users/pallas_call | solution.py:355
  46.0 0.0 collective-permute-start.8
  46.0 0.5 collective-permute-start.7
  46.5 1.0 %collective-permute-done.8 = bf16[256,512]{1,0:T(8,128)(2,1)S(1)} collective-permute-done((bf16[256,512]{1,0:T(8,128)(2,1)S(1)}, bf16[256,512]{1,0:T(8,128)(2,1)S(1)}, u32[]{:S(2)}, u32[]{:S(2)}) %collective-permute-start.8) | collective-permute-done | bytes 262176 | tf_op jit(solution)/shard_map/ppermute | solution.py:20
  47.5 0.1 add_convert_fusion
  47.6 1.9 %collective-permute-start.9 = (bf16[256,512]{1,0:T(8,128)(2,1)S(1)}, bf16[256,512]{1,0:T(8,128)(2,1)S(1)}, u32[]{:S(2)}, u32[]{:S(2)}) collective-permute-start(bf16[256,512]{1,0:T(8,128)(2,1)S(1)} %add_convert_fusion), channel_id=1, source_target_pairs={{0,2},{1,3},{2,0},{3,1},{4,6},{5,7},{6,4},{7,5},{8,10},{9,11},{10,... | collective-permute-start | bytes 786440 | tf_op jit(solution)/shard_map/ppermute | solution.py:20
  49.5 0.0 copy-done.4
  49.5 0.1 fusion
  49.7 0.0 collective-permute-done.7
  49.7 6.5 %collective-permute-done.9 = bf16[256,512]{1,0:T(8,128)(2,1)S(1)} collective-permute-done((bf16[256,512]{1,0:T(8,128)(2,1)S(1)}, bf16[256,512]{1,0:T(8,128)(2,1)S(1)}, u32[]{:S(2)}, u32[]{:S(2)}) %collective-permute-start.9) | collective-permute-done | bytes 262176 | tf_op jit(solution)/shard_map/ppermute | solution.py:20
  56.1 0.3 multiply_reduce_fusion
  56.4 1.0 %subtract_divide_fusion = f32[256,512]{1,0:T(8,128)} fusion(bf16[256,512]{1,0:T(8,128)(2,1)S(1)} %copy-done.4, f32[256]{0:T(256)S(1)} %multiply_reduce_fusion, f32[256]{0:T(256)S(1)} %add_sqrt_fusion, bf16[256,512]{1,0:T(8,128)(2,1)S(1)} %collective-permute-done.9, f32[256,512]{1,0:T(8,128)S(1)} %get-tuple-element.54, ...), kind=kLoop, calls=%fused_computation.3 | loop fusion | flops 1310720 | bytes 1837056 | tf_op jit(solution)/shard_map/div | solution.py:408
  (1 shorter events, 0.0 us)
Async XLA Ops:
  3.9 16.1 %copy-start.2 = (bf16[520,128]{1,0:T(8,128)(2,1)}, bf16[520,128]{1,0:T(8,128)(2,1)S(1)}, u32[]{:S(2)}) copy-start(bf16[520,128]{1,0:T(8,128)(2,1)S(1)} %get-tuple-element.51) | copy-start | bytes 399364
  3.9 16.1 %copy-start.3 = (bf16[520,128]{1,0:T(8,128)(2,1)}, bf16[520,128]{1,0:T(8,128)(2,1)S(1)}, u32[]{:S(2)}) copy-start(bf16[520,128]{1,0:T(8,128)(2,1)S(1)} %get-tuple-element.52) | copy-start | bytes 399364
  3.9 29.4 %all-to-all-start = ((bf16[4,256,512]{2,1,0:T(8,128)(2,1)}), bf16[4,256,512]{2,1,0:T(8,128)(2,1)}, u32[]{:S(2)}, u32[]{:S(2)}) async-start(bf16[4,256,512]{2,1,0:T(8,128)(2,1)} %get-tuple-element.39), calls=%async_computation | async-start | bytes 2097152 | tf_op jit(solution)/shard_map/all_to_all | solution.py:392
  8.2 19.9 %collective-permute-start = (bf16[520,128]{1,0:T(8,128)(2,1)S(1)}, bf16[520,128]{1,0:T(8,128)(2,1)S(1)}, u32[]{:S(2)}, u32[]{:S(2)}) collective-permute-start(bf16[520,128]{1,0:T(8,128)(2,1)S(1)} %get-tuple-element.30), channel_id=1, source_target_pairs={{0,16},{4,20},{8,24},{12,28},{16,0},{20,4},{24,8},{28,12},{1,17},{... | collective-permute-start | bytes 399368 | tf_op jit(solution)/shard_map/ppermute | solution.py:25
  12.3 20.8 %collective-permute-start.1 = (bf16[520,128]{1,0:T(8,128)(2,1)}, bf16[520,128]{1,0:T(8,128)(2,1)}, u32[]{:S(2)}, u32[]{:S(2)}) collective-permute-start(bf16[520,128]{1,0:T(8,128)(2,1)} %get-tuple-element.42), channel_id=1, source_target_pairs={{0,12},{4,16},{8,20},{12,24},{16,28},{20,0},{24,4},{28,8},{1,13},{... | collective-permute-start | bytes 399368 | tf_op jit(solution)/shard_map/ppermute | solution.py:25
  14.8 18.5 %collective-permute-start.2 = (bf16[520,128]{1,0:T(8,128)(2,1)}, bf16[520,128]{1,0:T(8,128)(2,1)}, u32[]{:S(2)}, u32[]{:S(2)}) collective-permute-start(bf16[520,128]{1,0:T(8,128)(2,1)} %get-tuple-element.43), channel_id=1, source_target_pairs={{0,20},{4,24},{8,28},{12,0},{16,4},{20,8},{24,12},{28,16},{1,21},{... | collective-permute-start | bytes 399368 | tf_op jit(solution)/shard_map/ppermute | solution.py:25
  16.1 23.1 %collective-permute-start.3 = (bf16[520,128]{1,0:T(8,128)(2,1)}, bf16[520,128]{1,0:T(8,128)(2,1)S(1)}, u32[]{:S(2)}, u32[]{:S(2)}) collective-permute-start(bf16[520,128]{1,0:T(8,128)(2,1)} %get-tuple-element.49), channel_id=1, source_target_pairs={{0,8},{4,12},{8,16},{12,20},{16,24},{20,28},{24,0},{28,4},{1,9},{5... | collective-permute-start | bytes 399368 | tf_op jit(solution)/shard_map/ppermute | solution.py:25
  17.7 21.5 %collective-permute-start.4 = (bf16[520,128]{1,0:T(8,128)(2,1)}, bf16[520,128]{1,0:T(8,128)(2,1)S(1)}, u32[]{:S(2)}, u32[]{:S(2)}) collective-permute-start(bf16[520,128]{1,0:T(8,128)(2,1)} %get-tuple-element.50), channel_id=1, source_target_pairs={{0,24},{4,28},{8,0},{12,4},{16,8},{20,12},{24,16},{28,20},{1,25},{... | collective-permute-start | bytes 399368 | tf_op jit(solution)/shard_map/ppermute | solution.py:25
  28.1 0.7 %copy-start = (bf16[520,128]{1,0:T(8,128)(2,1)}, bf16[520,128]{1,0:T(8,128)(2,1)S(1)}, u32[]{:S(2)}) copy-start(bf16[520,128]{1,0:T(8,128)(2,1)S(1)} %collective-permute-done.refs_1_) | copy-start | bytes 399364
  31.1 8.1 %collective-permute-start.6 = (bf16[520,128]{1,0:T(8,128)(2,1)}, bf16[520,128]{1,0:T(8,128)(2,1)}, u32[]{:S(2)}, u32[]{:S(2)}) collective-permute-start(bf16[520,128]{1,0:T(8,128)(2,1)} %copy-done.3), channel_id=1, source_target_pairs={{0,28},{4,0},{8,4},{12,8},{16,12},{20,16},{24,20},{28,24},{1,29},{... | collective-permute-start | bytes 399368 | tf_op jit(solution)/shard_map/ppermute | solution.py:25
  33.1 8.1 %collective-permute-start.5 = (bf16[520,128]{1,0:T(8,128)(2,1)}, bf16[520,128]{1,0:T(8,128)(2,1)}, u32[]{:S(2)}, u32[]{:S(2)}) collective-permute-start(bf16[520,128]{1,0:T(8,128)(2,1)} %copy-done.2), channel_id=1, source_target_pairs={{0,4},{4,8},{8,12},{12,16},{16,20},{20,24},{24,28},{28,0},{1,5},{5... | collective-permute-start | bytes 399368 | tf_op jit(solution)/shard_map/ppermute | solution.py:25
  33.3 0.9 %copy-start.1 = (bf16[520,128]{1,0:T(8,128)(2,1)S(1)}, bf16[520,128]{1,0:T(8,128)(2,1)}, u32[]{:S(2)}) copy-start(bf16[520,128]{1,0:T(8,128)(2,1)} %copy-done) | copy-start | bytes 399364
  41.2 8.3 %copy-start.4 = (bf16[256,512]{1,0:T(8,128)(2,1)S(1)}, bf16[256,512]{1,0:T(8,128)(2,1)}, u32[]{:S(2)}) copy-start(bf16[256,512]{1,0:T(8,128)(2,1)} %pool_any.1) | copy-start | bytes 786436
  46.0 1.5 %collective-permute-start.8 = (bf16[256,512]{1,0:T(8,128)(2,1)S(1)}, bf16[256,512]{1,0:T(8,128)(2,1)S(1)}, u32[]{:S(2)}, u32[]{:S(2)}) collective-permute-start(bf16[256,512]{1,0:T(8,128)(2,1)S(1)} %get-tuple-element.57), channel_id=1, source_target_pairs={{0,1},{1,0},{2,3},{3,2},{4,5},{5,4},{6,7},{7,6},{8,9},{9,8},{10,11... | collective-permute-start | bytes 786440 | tf_op jit(solution)/shard_map/ppermute | solution.py:20
  46.0 3.7 %collective-permute-start.7 = (bf16[256,512]{1,0:T(8,128)(2,1)S(1)}, bf16[256,512]{1,0:T(8,128)(2,1)S(1)}, u32[]{:S(2)}, u32[]{:S(2)}) collective-permute-start(bf16[256,512]{1,0:T(8,128)(2,1)S(1)} %get-tuple-element.55), channel_id=1, source_target_pairs={{0,1},{1,0},{2,3},{3,2},{4,5},{5,4},{6,7},{7,6},{8,9},{9,8},{10,11... | collective-permute-start | bytes 786440 | tf_op jit(solution)/shard_map/ppermute | solution.py:20
  47.6 8.6 %collective-permute-start.9 = (bf16[256,512]{1,0:T(8,128)(2,1)S(1)}, bf16[256,512]{1,0:T(8,128)(2,1)S(1)}, u32[]{:S(2)}, u32[]{:S(2)}) collective-permute-start(bf16[256,512]{1,0:T(8,128)(2,1)S(1)} %add_convert_fusion), channel_id=1, source_target_pairs={{0,2},{1,3},{2,0},{3,1},{4,6},{5,7},{6,4},{7,5},{8,10},{9,11},{10,... | collective-permute-start | bytes 786440 | tf_op jit(solution)/shard_map/ppermute | solution.py:20

commit v12 on v10

--- a/solution.py
+++ b/solution.py
@@ -181,7 +181,7 @@
         starts.append(pl.multiple_of(end, chunk) if u else 0)
         end = end + (lens[u] + chunk - 1) // chunk * chunk
     end = pl.multiple_of(end, chunk)
-    strips = (end + length - 1) // length
+    tiles = (end + tile - 1) // tile
 
     place = lax.broadcasted_iota(jnp.int32, (1, length), 1)
     packed_tgt[...] = jnp.full_like(packed_tgt, -1)
@@ -206,9 +206,10 @@
     col = lax.broadcasted_iota(jnp.int32, (length, length), 1)
     rate = logit_scale * math.log2(math.e)
 
-    def one_tile(strip, lines):
-        tile = lines * length
-        first = pl.multiple_of(strip * length, length)
+    lines = tile // length
+
+    def one_tile(t, _):
+        first, strip = pl.multiple_of(t * tile, tile), t * lines
         item_id = lax.broadcasted_iota(jnp.int32, (items, tile), 0)
         x = events[pl.ds(first, tile), :].astype(jnp.float32)
         center, spread = center_and_spread(x)
@@ -263,7 +264,7 @@
                 unit_refs[j][...], queries, contract_last, preferred_element_type=jnp.float32
             )
             exps = jnp.exp2(dots * rate - rate)
-            exp_ref[j, :, :tile] = exps
+            exp_ref[j] = exps
             total += jnp.sum(exps, axis=0, keepdims=True)
             hit = item_id == target - block * items
             target_dot += jnp.sum(jnp.where(hit, dots, 0.0), axis=0, keepdims=True)
@@ -273,18 +274,13 @@
         share = jnp.where(target >= 0, 1.0 / total, 0.0)
         for j, block in enumerate(block_ids):
             hit = item_id == target - block * items
-            left = exp_ref[j, :, :tile] * share - jnp.where(hit, 1.0, 0.0)
-            residual[j, :, :tile] = left.astype(jnp.bfloat16)
+            left = exp_ref[j] * share - jnp.where(hit, 1.0, 0.0)
+            residual[j] = left.astype(jnp.bfloat16)
         for j in range(len(block_ids)):
-            sums[j][...] += jnp.dot(residual[j, :, :tile], queries, preferred_element_type=jnp.float32)
-
-    def full_tile(t, _):
-        one_tile(t * (tile // length), tile // length)
+            sums[j][...] += jnp.dot(residual[j], queries, preferred_element_type=jnp.float32)
         return 0
 
-    full = strips // (tile // length)
-    lax.fori_loop(0, full, full_tile, 0)
-    pl.when(strips % (tile // length) != 0)(lambda: one_tile(full * (tile // length), 1))
+    lax.fori_loop(0, tiles, one_tile, 0)
 
     for u in range(per_step):
         line, turn = starts[u] // length, lax.rem(starts[u], length)
@@ -367,19 +363,17 @@
     slots = user_count // groups
     group, mine = lax.axis_index("dp").astype(jnp.int32), lax.axis_index("blk").astype(jnp.int32)
 
-    by_distance = sorted(range(1, groups), key=lambda shift: abs(shift - groups / 2))
-    early = [groups - by_distance[-1], *by_distance[: groups // 2 - 2]]
-    late = [shift for shift in by_distance if shift not in early]
-    work = [(shift, slot) for shift in [0, *early, *late] for slot in range(slots)]
+    work = sorted(
+        ((shift, slot) for shift in range(groups) for slot in range(slots)),
+        key=lambda pair: (pair[0] != 0, pair[0] not in (1, groups - 1), abs(pair[0] - groups / 2)),
+    )
     *packed, units = pack(
         histories, lengths, targets, send_list, item_pool, work, groups, group.reshape(1), blocks
     )
     half = user_count // 2
-    for k in range(slots, user_count):
-        if k >= half:
-            before = slots * (1 if work[k][0] == late[1] else 2)
-            packed[before], packed[k] = lax.optimization_barrier((packed[before], packed[k]))
-        packed[k] = from_behind(packed[k], "dp", work[k][0])
+    packed = [
+        users if shift == 0 else from_behind(users, "dp", shift) for users, (shift, _) in zip(packed, work)
+    ]
     units = lax.all_to_all(units, "blk", split_axis=0, concat_axis=0, tiled=True)
 
     pool_float = item_pool.astype(jnp.float32)

time: 56.8 us -> 54.8 us (0.965)
  the two profiles are of different devices: /device:TPU:6 before, /device:TPU:0 now
where the time goes in v12:
time: 54.8 us; the launch traced here: 54.5 us
  starting transfers between devices  20.6 us (38%)
  waiting for transfers between devices  18.5 us (34%)
  Pallas kernels  13.1 us (24%)
  other arithmetic  1.52 us (3%)
  between operations  0.74 us (1%)
    ppermute x7, starting transfers between devices, from_behind(): lax.ppermute(array, axis, [(i, (i + by) % devices) for i in range(devices)])  14 us
    ppermute x7, waiting for transfers between devices, from_behind(): lax.ppermute(array, axis, [(i, (i + by) % devices) for i in range(devices)])  11 us
    ppermute x3, waiting for transfers between devices, swap(): return lax.ppermute(array, axis, [(i, i ^ bit) for i in range(devices)])  7.48 us
    pallas_call x1, Pallas kernels, first_call(): pl.pallas_call(functools.partial(first_kernel, places, blocks), in_specs=...  6 us
    pallas_call x1, Pallas kernels, second_call(): pl.pallas_call(functools.partial(second_kernel, places, blocks), in_specs...  4.63 us
    all_to_all x1, starting transfers between devices, shards(): lax.all_to_all(units, 'blk', split_axis=0, concat_axis=0, tiled=True)  4.25 us
    pallas_call x1, Pallas kernels, pack(): pl.pallas_call(functools.partial(pack_kernel, work, groups), in_specs=[pl...  2.44 us
    ppermute x3, starting transfers between devices, swap(): return lax.ppermute(array, axis, [(i, i ^ bit) for i in range(devices)])  2.36 us
  transfers between devices with their start and end apart: 11, of which 3 were waited for; matrix products, arithmetic and copies ran while one was open for 1% of the time, Pallas kernels for 11%

profile of v12, /device:TPU:0, one launch (start us, length us, event | category | flops | bytes accessed | tf_op | source)
XLA Modules:
  0.0 54.5 jit_solution(13795833076330961513)
XLA Ops:
  0.6 2.4 %pack.1 = (bf16[520,128]{1,0:T(8,128)(2,1)S(1)}, bf16[520,128]{1,0:T(8,128)(2,1)S(1)}, bf16[520,128]{1,0:T(8,128)(2,1)S(1)}, bf16[520,128]{1,0:T(8,128)(2,1)S(1)...) custom-call(s32[1]{0:T(128)} %bitcast.12.group_ref, ...), custom_call_target="tpu_custom_call" | custom-call | tf_op jit(solution)/shard_map/pack/pallas_call | solution.py:97
  3.1 4.2 %all-to-all-start = ((bf16[4,256,512]{2,1,0:T(8,128)(2,1)}), bf16[4,256,512]{2,1,0:T(8,128)(2,1)S(1)}, u32[]{:S(2)}, u32[]{:S(2)}) async-start(bf16[4,256,512]{2,1,0:T(8,128)(2,1)} %get-tuple-element.22), calls=%async_computation | async-start | bytes 2097152 | tf_op jit(solution)/shard_map/all_to_all | solution.py:377
  7.3 2.3 %collective-permute-start = (bf16[520,128]{1,0:T(8,128)(2,1)S(1)}, bf16[520,128]{1,0:T(8,128)(2,1)S(1)}, u32[]{:S(2)}, u32[]{:S(2)}) collective-permute-start(bf16[520,128]{1,0:T(8,128)(2,1)S(1)} %get-tuple-element.24), channel_id=1, source_target_pairs={{0,4},{4,8},{8,12},{12,16},{16,20},{20,24},{24,28},{28,0},{1,5},{5... | collective-permute-start | bytes 399368 | tf_op jit(solution)/shard_map/ppermute | solution.py:25
  9.6 3.1 %collective-permute-start.1 = (bf16[520,128]{1,0:T(8,128)(2,1)S(1)}, bf16[520,128]{1,0:T(8,128)(2,1)S(1)}, u32[]{:S(2)}, u32[]{:S(2)}) collective-permute-start(bf16[520,128]{1,0:T(8,128)(2,1)S(1)} %get-tuple-element.25), channel_id=1, source_target_pairs={{0,28},{4,0},{8,4},{12,8},{16,12},{20,16},{24,20},{28,24},{1,29},{... | collective-permute-start | bytes 399368 | tf_op jit(solution)/shard_map/ppermute | solution.py:25
  12.7 0.9 %collective-permute-start.2 = (bf16[520,128]{1,0:T(8,128)(2,1)S(1)}, bf16[520,128]{1,0:T(8,128)(2,1)S(1)}, u32[]{:S(2)}, u32[]{:S(2)}) collective-permute-start(bf16[520,128]{1,0:T(8,128)(2,1)S(1)} %get-tuple-element.26), channel_id=1, source_target_pairs={{0,16},{4,20},{8,24},{12,28},{16,0},{20,4},{24,8},{28,12},{1,17},{... | collective-permute-start | bytes 399368 | tf_op jit(solution)/shard_map/ppermute | solution.py:25
  13.6 1.6 %collective-permute-start.3 = (bf16[520,128]{1,0:T(8,128)(2,1)S(1)}, bf16[520,128]{1,0:T(8,128)(2,1)S(1)}, u32[]{:S(2)}, u32[]{:S(2)}) collective-permute-start(bf16[520,128]{1,0:T(8,128)(2,1)S(1)} %get-tuple-element.33), channel_id=1, source_target_pairs={{0,12},{4,16},{8,20},{12,24},{16,28},{20,0},{24,4},{28,8},{1,13},{... | collective-permute-start | bytes 399368 | tf_op jit(solution)/shard_map/ppermute | solution.py:25
  15.2 2.2 %collective-permute-start.4 = (bf16[520,128]{1,0:T(8,128)(2,1)S(1)}, bf16[520,128]{1,0:T(8,128)(2,1)S(1)}, u32[]{:S(2)}, u32[]{:S(2)}) collective-permute-start(bf16[520,128]{1,0:T(8,128)(2,1)S(1)} %get-tuple-element.34), channel_id=1, source_target_pairs={{0,20},{4,24},{8,28},{12,0},{16,4},{20,8},{24,12},{28,16},{1,21},{... | collective-permute-start | bytes 399368 | tf_op jit(solution)/shard_map/ppermute | solution.py:25
  17.5 0.0 collective-permute-done.refs_1_
  17.5 1.6 %collective-permute-start.5 = (bf16[520,128]{1,0:T(8,128)(2,1)S(1)}, bf16[520,128]{1,0:T(8,128)(2,1)S(1)}, u32[]{:S(2)}, u32[]{:S(2)}) collective-permute-start(bf16[520,128]{1,0:T(8,128)(2,1)S(1)} %get-tuple-element.35), channel_id=1, source_target_pairs={{0,8},{4,12},{8,16},{12,20},{16,24},{20,28},{24,0},{28,4},{1,9},{5... | collective-permute-start | bytes 399368 | tf_op jit(solution)/shard_map/ppermute | solution.py:25
  19.0 0.0 collective-permute-done.1.refs_2_
  19.0 2.3 %collective-permute-start.6 = (bf16[520,128]{1,0:T(8,128)(2,1)S(1)}, bf16[520,128]{1,0:T(8,128)(2,1)S(1)}, u32[]{:S(2)}, u32[]{:S(2)}) collective-permute-start(bf16[520,128]{1,0:T(8,128)(2,1)S(1)} %get-tuple-element.36), channel_id=1, source_target_pairs={{0,24},{4,28},{8,0},{12,4},{16,8},{20,12},{24,16},{28,20},{1,25},{... | collective-permute-start | bytes 399368 | tf_op jit(solution)/shard_map/ppermute | solution.py:25
  21.3 0.1 stack.51.id_ref
  21.4 11.0 %collective-permute-done.2.refs_3_ = bf16[520,128]{1,0:T(8,128)(2,1)S(1)} collective-permute-done((bf16[520,128]{1,0:T(8,128)(2,1)S(1)}, bf16[520,128]{1,0:T(8,128)(2,1)S(1)}, u32[]{:S(2)}, u32[]{:S(2)}) %collective-permute-start.2) | collective-permute-done | bytes 133152 | tf_op jit(solution)/shard_map/ppermute | solution.py:25
  32.4 0.0 all-to-all-done.unit_ref
  32.4 0.0 copy-start
  32.4 0.0 copy-start.1
  32.4 6.0 %first_users.1 = (f32[8,128]{1,0:T(8,128)S(1)}, f32[256,512]{1,0:T(8,128)S(1)}, f32[256,512]{1,0:T(8,128)S(1)}, f32[256,512]{1,0:T(8,128)S(1)}, f32[256,512]{1,0:T(8,128)S(1)}, /*index=5*/f32[4,128,256]{2,1,0:T(8,128)S(1)}) custom-call(s32[12]{0:T(128)S(1)} %stack.51.id_ref, bf16[512,2048]{1,0:T(8,128)(2,1)} %w_in.1, bf16[512,512]{1,0:T(8,128)(2,1)} %w_out.1, ...), custom_call_target="tpu_custom_call" | custom-call | tf_op jit(solution)/shard_map/first_users/pallas_call | solution.py:318
  38.5 0.0 collective-permute-done.3.refs_4_
  38.5 0.0 collective-permute-done.4.refs_5_
  38.5 0.0 collective-permute-done.5.refs_6_
  38.5 0.0 collective-permute-done.6.refs_7_
  38.5 0.0 copy-done
  38.5 0.0 copy-done.1
  38.5 0.0 copy-start.2
  38.5 4.6 %second_users.1 = (f32[8,128]{1,0:T(8,128)}, f32[256,512]{1,0:T(8,128)S(1)}, f32[256,512]{1,0:T(8,128)S(1)}, bf16[256,512]{1,0:T(8,128)(2,1)S(1)}, bf16[256,512]{1,0:T(8,128)(2,1)S(1)}) custom-call(s32[12]{0:T(128)S(1)} %stack.51.id_ref, bf16[512,2048]{1,0:T(8,128)(2,1)S(1)} %copy-done, bf16[512,512]{1,0:T(8,128)(2,1)S(1)} %copy-done.1, ...), custom_call_target="tpu_custom_call" | custom-call | tf_op jit(solution)/shard_map/second_users/pallas_call | solution.py:344
  43.2 0.0 collective-permute-start.8
  43.2 0.5 collective-permute-start.7
  43.7 1.0 %collective-permute-done.8 = bf16[256,512]{1,0:T(8,128)(2,1)S(1)} collective-permute-done((bf16[256,512]{1,0:T(8,128)(2,1)S(1)}, bf16[256,512]{1,0:T(8,128)(2,1)S(1)}, u32[]{:S(2)}, u32[]{:S(2)}) %collective-permute-start.8) | collective-permute-done | bytes 262176 | tf_op jit(solution)/shard_map/ppermute | solution.py:20
  44.7 0.1 add_convert_fusion
  44.8 1.9 %collective-permute-start.9 = (bf16[256,512]{1,0:T(8,128)(2,1)S(1)}, bf16[256,512]{1,0:T(8,128)(2,1)S(1)}, u32[]{:S(2)}, u32[]{:S(2)}) collective-permute-start(bf16[256,512]{1,0:T(8,128)(2,1)S(1)} %add_convert_fusion), channel_id=1, source_target_pairs={{0,2},{1,3},{2,0},{3,1},{4,6},{5,7},{6,4},{7,5},{8,10},{9,11},{10,... | collective-permute-start | bytes 786440 | tf_op jit(solution)/shard_map/ppermute | solution.py:20
  46.6 0.0 copy-done.2
  46.6 0.1 fusion
  46.8 0.0 collective-permute-done.7
  46.8 6.5 %collective-permute-done.9 = bf16[256,512]{1,0:T(8,128)(2,1)S(1)} collective-permute-done((bf16[256,512]{1,0:T(8,128)(2,1)S(1)}, bf16[256,512]{1,0:T(8,128)(2,1)S(1)}, u32[]{:S(2)}, u32[]{:S(2)}) %collective-permute-start.9) | collective-permute-done | bytes 262176 | tf_op jit(solution)/shard_map/ppermute | solution.py:20
  53.2 0.3 multiply_reduce_fusion
  53.5 1.0 %subtract_divide_fusion = f32[256,512]{1,0:T(8,128)} fusion(bf16[256,512]{1,0:T(8,128)(2,1)S(1)} %copy-done.2, f32[256]{0:T(256)S(1)} %multiply_reduce_fusion, f32[256]{0:T(256)S(1)} %add_sqrt_fusion, bf16[256,512]{1,0:T(8,128)(2,1)S(1)} %collective-permute-done.9, f32[256,512]{1,0:T(8,128)S(1)} %get-tuple-element.38, ...), kind=kLoop, calls=%fused_computation.3 | loop fusion | flops 1310720 | bytes 1837056 | tf_op jit(solution)/shard_map/div | solution.py:395
  (1 shorter events, 0.0 us)
Async XLA Ops:
  3.1 29.4 %all-to-all-start = ((bf16[4,256,512]{2,1,0:T(8,128)(2,1)}), bf16[4,256,512]{2,1,0:T(8,128)(2,1)S(1)}, u32[]{:S(2)}, u32[]{:S(2)}) async-start(bf16[4,256,512]{2,1,0:T(8,128)(2,1)} %get-tuple-element.22), calls=%async_computation | async-start | bytes 2097152 | tf_op jit(solution)/shard_map/all_to_all | solution.py:377
  7.3 10.1 %collective-permute-start = (bf16[520,128]{1,0:T(8,128)(2,1)S(1)}, bf16[520,128]{1,0:T(8,128)(2,1)S(1)}, u32[]{:S(2)}, u32[]{:S(2)}) collective-permute-start(bf16[520,128]{1,0:T(8,128)(2,1)S(1)} %get-tuple-element.24), channel_id=1, source_target_pairs={{0,4},{4,8},{8,12},{12,16},{16,20},{20,24},{24,28},{28,0},{1,5},{5... | collective-permute-start | bytes 399368 | tf_op jit(solution)/shard_map/ppermute | solution.py:25
  9.6 9.4 %collective-permute-start.1 = (bf16[520,128]{1,0:T(8,128)(2,1)S(1)}, bf16[520,128]{1,0:T(8,128)(2,1)S(1)}, u32[]{:S(2)}, u32[]{:S(2)}) collective-permute-start(bf16[520,128]{1,0:T(8,128)(2,1)S(1)} %get-tuple-element.25), channel_id=1, source_target_pairs={{0,28},{4,0},{8,4},{12,8},{16,12},{20,16},{24,20},{28,24},{1,29},{... | collective-permute-start | bytes 399368 | tf_op jit(solution)/shard_map/ppermute | solution.py:25
  12.7 19.7 %collective-permute-start.2 = (bf16[520,128]{1,0:T(8,128)(2,1)S(1)}, bf16[520,128]{1,0:T(8,128)(2,1)S(1)}, u32[]{:S(2)}, u32[]{:S(2)}) collective-permute-start(bf16[520,128]{1,0:T(8,128)(2,1)S(1)} %get-tuple-element.26), channel_id=1, source_target_pairs={{0,16},{4,20},{8,24},{12,28},{16,0},{20,4},{24,8},{28,12},{1,17},{... | collective-permute-start | bytes 399368 | tf_op jit(solution)/shard_map/ppermute | solution.py:25
  13.6 24.8 %collective-permute-start.3 = (bf16[520,128]{1,0:T(8,128)(2,1)S(1)}, bf16[520,128]{1,0:T(8,128)(2,1)S(1)}, u32[]{:S(2)}, u32[]{:S(2)}) collective-permute-start(bf16[520,128]{1,0:T(8,128)(2,1)S(1)} %get-tuple-element.33), channel_id=1, source_target_pairs={{0,12},{4,16},{8,20},{12,24},{16,28},{20,0},{24,4},{28,8},{1,13},{... | collective-permute-start | bytes 399368 | tf_op jit(solution)/shard_map/ppermute | solution.py:25
  15.2 23.2 %collective-permute-start.4 = (bf16[520,128]{1,0:T(8,128)(2,1)S(1)}, bf16[520,128]{1,0:T(8,128)(2,1)S(1)}, u32[]{:S(2)}, u32[]{:S(2)}) collective-permute-start(bf16[520,128]{1,0:T(8,128)(2,1)S(1)} %get-tuple-element.34), channel_id=1, source_target_pairs={{0,20},{4,24},{8,28},{12,0},{16,4},{20,8},{24,12},{28,16},{1,21},{... | collective-permute-start | bytes 399368 | tf_op jit(solution)/shard_map/ppermute | solution.py:25
  17.5 21.0 %collective-permute-start.5 = (bf16[520,128]{1,0:T(8,128)(2,1)S(1)}, bf16[520,128]{1,0:T(8,128)(2,1)S(1)}, u32[]{:S(2)}, u32[]{:S(2)}) collective-permute-start(bf16[520,128]{1,0:T(8,128)(2,1)S(1)} %get-tuple-element.35), channel_id=1, source_target_pairs={{0,8},{4,12},{8,16},{12,20},{16,24},{20,28},{24,0},{28,4},{1,9},{5... | collective-permute-start | bytes 399368 | tf_op jit(solution)/shard_map/ppermute | solution.py:25
  19.0 19.5 %collective-permute-start.6 = (bf16[520,128]{1,0:T(8,128)(2,1)S(1)}, bf16[520,128]{1,0:T(8,128)(2,1)S(1)}, u32[]{:S(2)}, u32[]{:S(2)}) collective-permute-start(bf16[520,128]{1,0:T(8,128)(2,1)S(1)} %get-tuple-element.36), channel_id=1, source_target_pairs={{0,24},{4,28},{8,0},{12,4},{16,8},{20,12},{24,16},{28,20},{1,25},{... | collective-permute-start | bytes 399368 | tf_op jit(solution)/shard_map/ppermute | solution.py:25
  32.4 6.1 %copy-start = (bf16[512,2048]{1,0:T(8,128)(2,1)S(1)}, bf16[512,2048]{1,0:T(8,128)(2,1)}, u32[]{:S(2)}) copy-start(bf16[512,2048]{1,0:T(8,128)(2,1)} %w_in.1) | copy-start | bytes 6291460
  32.4 6.1 %copy-start.1 = (bf16[512,512]{1,0:T(8,128)(2,1)S(1)}, bf16[512,512]{1,0:T(8,128)(2,1)}, u32[]{:S(2)}) copy-start(bf16[512,512]{1,0:T(8,128)(2,1)} %w_out.1) | copy-start | bytes 1572868
  38.5 8.1 %copy-start.2 = (bf16[256,512]{1,0:T(8,128)(2,1)S(1)}, bf16[256,512]{1,0:T(8,128)(2,1)}, u32[]{:S(2)}) copy-start(bf16[256,512]{1,0:T(8,128)(2,1)} %pool_any.1) | copy-start | bytes 786436
  43.2 1.5 %collective-permute-start.8 = (bf16[256,512]{1,0:T(8,128)(2,1)S(1)}, bf16[256,512]{1,0:T(8,128)(2,1)S(1)}, u32[]{:S(2)}, u32[]{:S(2)}) collective-permute-start(bf16[256,512]{1,0:T(8,128)(2,1)S(1)} %get-tuple-element.41), channel_id=1, source_target_pairs={{0,1},{1,0},{2,3},{3,2},{4,5},{5,4},{6,7},{7,6},{8,9},{9,8},{10,11... | collective-permute-start | bytes 786440 | tf_op jit(solution)/shard_map/ppermute | solution.py:20
  43.2 3.6 %collective-permute-start.7 = (bf16[256,512]{1,0:T(8,128)(2,1)S(1)}, bf16[256,512]{1,0:T(8,128)(2,1)S(1)}, u32[]{:S(2)}, u32[]{:S(2)}) collective-permute-start(bf16[256,512]{1,0:T(8,128)(2,1)S(1)} %get-tuple-element.39), channel_id=1, source_target_pairs={{0,1},{1,0},{2,3},{3,2},{4,5},{5,4},{6,7},{7,6},{8,9},{9,8},{10,11... | collective-permute-start | bytes 786440 | tf_op jit(solution)/shard_map/ppermute | solution.py:20
  44.8 8.5 %collective-permute-start.9 = (bf16[256,512]{1,0:T(8,128)(2,1)S(1)}, bf16[256,512]{1,0:T(8,128)(2,1)S(1)}, u32[]{:S(2)}, u32[]{:S(2)}) collective-permute-start(bf16[256,512]{1,0:T(8,128)(2,1)S(1)} %add_convert_fusion), channel_id=1, source_target_pairs={{0,2},{1,3},{2,0},{3,1},{4,6},{5,7},{6,4},{7,5},{8,10},{9,11},{10,... | collective-permute-start | bytes 786440 | tf_op jit(solution)/shard_map/ppermute | solution.py:20

commit v13 on v12

--- a/solution.py
+++ b/solution.py
@@ -363,10 +363,10 @@
     slots = user_count // groups
     group, mine = lax.axis_index("dp").astype(jnp.int32), lax.axis_index("blk").astype(jnp.int32)
 
-    work = sorted(
-        ((shift, slot) for shift in range(groups) for slot in range(slots)),
-        key=lambda pair: (pair[0] != 0, pair[0] not in (1, groups - 1), abs(pair[0] - groups / 2)),
-    )
+    near = sorted({0, 1, groups - 1, 2 % groups}, key=lambda shift: (shift != 0, shift == 2))
+    others = [shift for shift in range(groups) if shift not in near]
+    order = near + sorted(others, key=lambda shift: abs(shift - groups / 2))
+    work = [(shift, slot) for shift in order for slot in range(slots)]
     *packed, units = pack(
         histories, lengths, targets, send_list, item_pool, work, groups, group.reshape(1), blocks
     )

time: 54.8 us -> 51.1 us (0.932)
  the two profiles are of different devices: /device:TPU:0 before, /device:TPU:30 now
where the time goes in v13:
time: 51.1 us; the launch traced here: 50.9 us
  waiting for transfers between devices  22.5 us (44%)
  Pallas kernels  13.1 us (26%)
  starting transfers between devices  13 us (25%)
  other arithmetic  1.52 us (3%)
  between operations  0.7 us (1%)
    ppermute x7, waiting for transfers between devices, from_behind(): lax.ppermute(array, axis, [(i, (i + by) % devices) for i in range(devices)])  10.4 us
    ppermute x3, waiting for transfers between devices, swap(): return lax.ppermute(array, axis, [(i, i ^ bit) for i in range(devices)])  8.78 us
    ppermute x7, starting transfers between devices, from_behind(): lax.ppermute(array, axis, [(i, (i + by) % devices) for i in range(devices)])  7.95 us
    pallas_call x1, Pallas kernels, first_call(): pl.pallas_call(functools.partial(first_kernel, places, blocks), in_specs=...  6 us
    pallas_call x1, Pallas kernels, second_call(): pl.pallas_call(functools.partial(second_kernel, places, blocks), in_specs...  4.63 us
    all_to_all x1, starting transfers between devices, shards(): lax.all_to_all(units, 'blk', split_axis=0, concat_axis=0, tiled=True)  4 us
    all_to_all x1, waiting for transfers between devices, shards(): lax.all_to_all(units, 'blk', split_axis=0, concat_axis=0, tiled=True)  3.34 us
    pallas_call x1, Pallas kernels, pack(): pl.pallas_call(functools.partial(pack_kernel, work, groups), in_specs=[pl...  2.44 us
  transfers between devices with their start and end apart: 11, of which 6 were waited for; matrix products, arithmetic and copies ran while one was open for 1% of the time, Pallas kernels for 12%

profile of v13, /device:TPU:30, one launch (start us, length us, event | category | flops | bytes accessed | tf_op | source)
XLA Modules:
  0.0 50.9 jit_solution(14649417767428534493)
XLA Ops:
  0.6 2.4 %pack.1 = (bf16[520,128]{1,0:T(8,128)(2,1)S(1)}, bf16[520,128]{1,0:T(8,128)(2,1)S(1)}, bf16[520,128]{1,0:T(8,128)(2,1)S(1)}, bf16[520,128]{1,0:T(8,128)(2,1)S(1)...) custom-call(s32[1]{0:T(128)} %bitcast.12.group_ref, ...), custom_call_target="tpu_custom_call" | custom-call | tf_op jit(solution)/shard_map/pack/pallas_call | solution.py:97
  3.1 4.0 %all-to-all-start = ((bf16[4,256,512]{2,1,0:T(8,128)(2,1)}), bf16[4,256,512]{2,1,0:T(8,128)(2,1)S(1)}, u32[]{:S(2)}, u32[]{:S(2)}) async-start(bf16[4,256,512]{2,1,0:T(8,128)(2,1)} %get-tuple-element.22), calls=%async_computation | async-start | bytes 2097152 | tf_op jit(solution)/shard_map/all_to_all | solution.py:377
  7.1 0.0 collective-permute-start
  7.1 2.0 %collective-permute-start.1 = (bf16[520,128]{1,0:T(8,128)(2,1)S(1)}, bf16[520,128]{1,0:T(8,128)(2,1)S(1)}, u32[]{:S(2)}, u32[]{:S(2)}) collective-permute-start(bf16[520,128]{1,0:T(8,128)(2,1)S(1)} %get-tuple-element.25), channel_id=1, source_target_pairs={{0,28},{4,0},{8,4},{12,8},{16,12},{20,16},{24,20},{28,24},{1,29},{... | collective-permute-start | bytes 399368 | tf_op jit(solution)/shard_map/ppermute | solution.py:25
  9.1 0.2 collective-permute-start.2
  9.3 1.7 %collective-permute-start.3 = (bf16[520,128]{1,0:T(8,128)(2,1)S(1)}, bf16[520,128]{1,0:T(8,128)(2,1)S(1)}, u32[]{:S(2)}, u32[]{:S(2)}) collective-permute-start(bf16[520,128]{1,0:T(8,128)(2,1)S(1)} %get-tuple-element.33), channel_id=1, source_target_pairs={{0,16},{4,20},{8,24},{12,28},{16,0},{20,4},{24,8},{28,12},{1,17},{... | collective-permute-start | bytes 399368 | tf_op jit(solution)/shard_map/ppermute | solution.py:25
  11.0 3.7 %collective-permute-start.4 = (bf16[520,128]{1,0:T(8,128)(2,1)S(1)}, bf16[520,128]{1,0:T(8,128)(2,1)S(1)}, u32[]{:S(2)}, u32[]{:S(2)}) collective-permute-start(bf16[520,128]{1,0:T(8,128)(2,1)S(1)} %get-tuple-element.34), channel_id=1, source_target_pairs={{0,12},{4,16},{8,20},{12,24},{16,28},{20,0},{24,4},{28,8},{1,13},{... | collective-permute-start | bytes 399368 | tf_op jit(solution)/shard_map/ppermute | solution.py:25
  14.7 0.0 collective-permute-done.refs_1_
  14.7 0.1 collective-permute-start.5
  14.8 1.4 %collective-permute-done.1.refs_2_ = bf16[520,128]{1,0:T(8,128)(2,1)S(1)} collective-permute-done((bf16[520,128]{1,0:T(8,128)(2,1)S(1)}, bf16[520,128]{1,0:T(8,128)(2,1)S(1)}, u32[]{:S(2)}, u32[]{:S(2)}) %collective-permute-start.1) | collective-permute-done | bytes 133152 | tf_op jit(solution)/shard_map/ppermute | solution.py:25
  16.2 0.2 collective-permute-start.6
  16.4 0.1 stack.51.id_ref
  16.5 0.0 collective-permute-done.2.refs_3_
  16.5 3.3 %all-to-all-done.unit_ref = bf16[4,256,512]{2,1,0:T(8,128)(2,1)S(1)} async-done(((bf16[4,256,512]{2,1,0:T(8,128)(2,1)}), bf16[4,256,512]{2,1,0:T(8,128)(2,1)S(1)}, u32[]{:S(2)}, u32[]{:S(2)}) %all-to-all-start) | async-done | bytes 1048608 | tf_op jit(solution)/shard_map/all_to_all | solution.py:377
  19.9 0.0 copy-start
  19.9 0.0 copy-start.1
  19.9 6.0 %first_users.1 = (f32[8,128]{1,0:T(8,128)S(1)}, f32[256,512]{1,0:T(8,128)S(1)}, f32[256,512]{1,0:T(8,128)S(1)}, f32[256,512]{1,0:T(8,128)S(1)}, f32[256,512]{1,0:T(8,128)S(1)}, /*index=5*/f32[4,128,256]{2,1,0:T(8,128)S(1)}) custom-call(s32[12]{0:T(128)S(1)} %stack.51.id_ref, bf16[512,2048]{1,0:T(8,128)(2,1)} %w_in.1, bf16[512,512]{1,0:T(8,128)(2,1)} %w_out.1, ...), custom_call_target="tpu_custom_call" | custom-call | tf_op jit(solution)/shard_map/first_users/pallas_call | solution.py:318
  25.9 4.6 %collective-permute-done.3.refs_4_ = bf16[520,128]{1,0:T(8,128)(2,1)S(1)} collective-permute-done((bf16[520,128]{1,0:T(8,128)(2,1)S(1)}, bf16[520,128]{1,0:T(8,128)(2,1)S(1)}, u32[]{:S(2)}, u32[]{:S(2)}) %collective-permute-start.3) | collective-permute-done | bytes 133152 | tf_op jit(solution)/shard_map/ppermute | solution.py:25
  30.5 0.0 collective-permute-done.4.refs_5_
  30.5 4.4 %collective-permute-done.5.refs_6_ = bf16[520,128]{1,0:T(8,128)(2,1)S(1)} collective-permute-done((bf16[520,128]{1,0:T(8,128)(2,1)S(1)}, bf16[520,128]{1,0:T(8,128)(2,1)S(1)}, u32[]{:S(2)}, u32[]{:S(2)}) %collective-permute-start.5) | collective-permute-done | bytes 133152 | tf_op jit(solution)/shard_map/ppermute | solution.py:25
  34.9 0.0 collective-permute-done.6.refs_7_
  34.9 0.0 copy-done
  34.9 0.0 copy-done.1
  34.9 0.0 copy-start.2
  34.9 4.6 %second_users.1 = (f32[8,128]{1,0:T(8,128)}, f32[256,512]{1,0:T(8,128)S(1)}, f32[256,512]{1,0:T(8,128)S(1)}, bf16[256,512]{1,0:T(8,128)(2,1)S(1)}, bf16[256,512]{1,0:T(8,128)(2,1)S(1)}) custom-call(s32[12]{0:T(128)S(1)} %stack.51.id_ref, bf16[512,2048]{1,0:T(8,128)(2,1)S(1)} %copy-done, bf16[512,512]{1,0:T(8,128)(2,1)S(1)} %copy-done.1, ...), custom_call_target="tpu_custom_call" | custom-call | tf_op jit(solution)/shard_map/second_users/pallas_call | solution.py:344
  39.5 0.0 collective-permute-start.8
  39.5 0.5 collective-permute-start.7
  40.0 1.0 %collective-permute-done.8 = bf16[256,512]{1,0:T(8,128)(2,1)S(1)} collective-permute-done((bf16[256,512]{1,0:T(8,128)(2,1)S(1)}, bf16[256,512]{1,0:T(8,128)(2,1)S(1)}, u32[]{:S(2)}, u32[]{:S(2)}) %collective-permute-start.8) | collective-permute-done | bytes 262176 | tf_op jit(solution)/shard_map/ppermute | solution.py:20
  41.1 0.1 add_convert_fusion
  41.1 0.5 collective-permute-start.9
  41.6 0.0 copy-done.2
  41.6 0.1 fusion
  41.8 0.0 collective-permute-done.7
  41.8 7.7 %collective-permute-done.9 = bf16[256,512]{1,0:T(8,128)(2,1)S(1)} collective-permute-done((bf16[256,512]{1,0:T(8,128)(2,1)S(1)}, bf16[256,512]{1,0:T(8,128)(2,1)S(1)}, u32[]{:S(2)}, u32[]{:S(2)}) %collective-permute-start.9) | collective-permute-done | bytes 262176 | tf_op jit(solution)/shard_map/ppermute | solution.py:20
  49.6 0.3 multiply_reduce_fusion
  49.8 1.0 %subtract_divide_fusion = f32[256,512]{1,0:T(8,128)} fusion(bf16[256,512]{1,0:T(8,128)(2,1)S(1)} %copy-done.2, f32[256]{0:T(256)S(1)} %multiply_reduce_fusion, f32[256]{0:T(256)S(1)} %add_sqrt_fusion, bf16[256,512]{1,0:T(8,128)(2,1)S(1)} %collective-permute-done.9, f32[256,512]{1,0:T(8,128)S(1)} %get-tuple-element.38, ...), kind=kLoop, calls=%fused_computation.3 | loop fusion | flops 1310720 | bytes 1837056 | tf_op jit(solution)/shard_map/div | solution.py:395
  (1 shorter events, 0.0 us)
Async XLA Ops:
  3.1 16.8 %all-to-all-start = ((bf16[4,256,512]{2,1,0:T(8,128)(2,1)}), bf16[4,256,512]{2,1,0:T(8,128)(2,1)S(1)}, u32[]{:S(2)}, u32[]{:S(2)}) async-start(bf16[4,256,512]{2,1,0:T(8,128)(2,1)} %get-tuple-element.22), calls=%async_computation | async-start | bytes 2097152 | tf_op jit(solution)/shard_map/all_to_all | solution.py:377
  7.1 7.7 %collective-permute-start = (bf16[520,128]{1,0:T(8,128)(2,1)S(1)}, bf16[520,128]{1,0:T(8,128)(2,1)S(1)}, u32[]{:S(2)}, u32[]{:S(2)}) collective-permute-start(bf16[520,128]{1,0:T(8,128)(2,1)S(1)} %get-tuple-element.24), channel_id=1, source_target_pairs={{0,4},{4,8},{8,12},{12,16},{16,20},{20,24},{24,28},{28,0},{1,5},{5... | collective-permute-start | bytes 399368 | tf_op jit(solution)/shard_map/ppermute | solution.py:25
  7.1 9.1 %collective-permute-start.1 = (bf16[520,128]{1,0:T(8,128)(2,1)S(1)}, bf16[520,128]{1,0:T(8,128)(2,1)S(1)}, u32[]{:S(2)}, u32[]{:S(2)}) collective-permute-start(bf16[520,128]{1,0:T(8,128)(2,1)S(1)} %get-tuple-element.25), channel_id=1, source_target_pairs={{0,28},{4,0},{8,4},{12,8},{16,12},{20,16},{24,20},{28,24},{1,29},{... | collective-permute-start | bytes 399368 | tf_op jit(solution)/shard_map/ppermute | solution.py:25
  9.1 7.4 %collective-permute-start.2 = (bf16[520,128]{1,0:T(8,128)(2,1)S(1)}, bf16[520,128]{1,0:T(8,128)(2,1)S(1)}, u32[]{:S(2)}, u32[]{:S(2)}) collective-permute-start(bf16[520,128]{1,0:T(8,128)(2,1)S(1)} %get-tuple-element.26), channel_id=1, source_target_pairs={{0,8},{4,12},{8,16},{12,20},{16,24},{20,28},{24,0},{28,4},{1,9},{5... | collective-permute-start | bytes 399368 | tf_op jit(solution)/shard_map/ppermute | solution.py:25
  9.3 21.1 %collective-permute-start.3 = (bf16[520,128]{1,0:T(8,128)(2,1)S(1)}, bf16[520,128]{1,0:T(8,128)(2,1)S(1)}, u32[]{:S(2)}, u32[]{:S(2)}) collective-permute-start(bf16[520,128]{1,0:T(8,128)(2,1)S(1)} %get-tuple-element.33), channel_id=1, source_target_pairs={{0,16},{4,20},{8,24},{12,28},{16,0},{20,4},{24,8},{28,12},{1,17},{... | collective-permute-start | bytes 399368 | tf_op jit(solution)/shard_map/ppermute | solution.py:25
  11.0 19.4 %collective-permute-start.4 = (bf16[520,128]{1,0:T(8,128)(2,1)S(1)}, bf16[520,128]{1,0:T(8,128)(2,1)S(1)}, u32[]{:S(2)}, u32[]{:S(2)}) collective-permute-start(bf16[520,128]{1,0:T(8,128)(2,1)S(1)} %get-tuple-element.34), channel_id=1, source_target_pairs={{0,12},{4,16},{8,20},{12,24},{16,28},{20,0},{24,4},{28,8},{1,13},{... | collective-permute-start | bytes 399368 | tf_op jit(solution)/shard_map/ppermute | solution.py:25
  14.7 20.1 %collective-permute-start.5 = (bf16[520,128]{1,0:T(8,128)(2,1)S(1)}, bf16[520,128]{1,0:T(8,128)(2,1)S(1)}, u32[]{:S(2)}, u32[]{:S(2)}) collective-permute-start(bf16[520,128]{1,0:T(8,128)(2,1)S(1)} %get-tuple-element.35), channel_id=1, source_target_pairs={{0,20},{4,24},{8,28},{12,0},{16,4},{20,8},{24,12},{28,16},{1,21},{... | collective-permute-start | bytes 399368 | tf_op jit(solution)/shard_map/ppermute | solution.py:25
  16.2 18.7 %collective-permute-start.6 = (bf16[520,128]{1,0:T(8,128)(2,1)S(1)}, bf16[520,128]{1,0:T(8,128)(2,1)S(1)}, u32[]{:S(2)}, u32[]{:S(2)}) collective-permute-start(bf16[520,128]{1,0:T(8,128)(2,1)S(1)} %get-tuple-element.36), channel_id=1, source_target_pairs={{0,24},{4,28},{8,0},{12,4},{16,8},{20,12},{24,16},{28,20},{1,25},{... | collective-permute-start | bytes 399368 | tf_op jit(solution)/shard_map/ppermute | solution.py:25
  19.9 15.0 %copy-start = (bf16[512,2048]{1,0:T(8,128)(2,1)S(1)}, bf16[512,2048]{1,0:T(8,128)(2,1)}, u32[]{:S(2)}) copy-start(bf16[512,2048]{1,0:T(8,128)(2,1)} %w_in.1) | copy-start | bytes 6291460
  19.9 15.0 %copy-start.1 = (bf16[512,512]{1,0:T(8,128)(2,1)S(1)}, bf16[512,512]{1,0:T(8,128)(2,1)}, u32[]{:S(2)}) copy-start(bf16[512,512]{1,0:T(8,128)(2,1)} %w_out.1) | copy-start | bytes 1572868
  34.9 6.8 %copy-start.2 = (bf16[256,512]{1,0:T(8,128)(2,1)S(1)}, bf16[256,512]{1,0:T(8,128)(2,1)}, u32[]{:S(2)}) copy-start(bf16[256,512]{1,0:T(8,128)(2,1)} %pool_any.1) | copy-start | bytes 786436
  39.5 1.5 %collective-permute-start.8 = (bf16[256,512]{1,0:T(8,128)(2,1)S(1)}, bf16[256,512]{1,0:T(8,128)(2,1)S(1)}, u32[]{:S(2)}, u32[]{:S(2)}) collective-permute-start(bf16[256,512]{1,0:T(8,128)(2,1)S(1)} %get-tuple-element.41), channel_id=1, source_target_pairs={{0,1},{1,0},{2,3},{3,2},{4,5},{5,4},{6,7},{7,6},{8,9},{9,8},{10,11... | collective-permute-start | bytes 786440 | tf_op jit(solution)/shard_map/ppermute | solution.py:20
  39.5 2.3 %collective-permute-start.7 = (bf16[256,512]{1,0:T(8,128)(2,1)S(1)}, bf16[256,512]{1,0:T(8,128)(2,1)S(1)}, u32[]{:S(2)}, u32[]{:S(2)}) collective-permute-start(bf16[256,512]{1,0:T(8,128)(2,1)S(1)} %get-tuple-element.39), channel_id=1, source_target_pairs={{0,1},{1,0},{2,3},{3,2},{4,5},{5,4},{6,7},{7,6},{8,9},{9,8},{10,11... | collective-permute-start | bytes 786440 | tf_op jit(solution)/shard_map/ppermute | solution.py:20
  41.1 8.4 %collective-permute-start.9 = (bf16[256,512]{1,0:T(8,128)(2,1)S(1)}, bf16[256,512]{1,0:T(8,128)(2,1)S(1)}, u32[]{:S(2)}, u32[]{:S(2)}) collective-permute-start(bf16[256,512]{1,0:T(8,128)(2,1)S(1)} %add_convert_fusion), channel_id=1, source_target_pairs={{0,2},{1,3},{2,0},{3,1},{4,6},{5,7},{6,4},{7,5},{8,10},{9,11},{10,... | collective-permute-start | bytes 786440 | tf_op jit(solution)/shard_map/ppermute | solution.py:20

commit v14 on v13

--- a/solution.py
+++ b/solution.py
@@ -114,22 +114,19 @@
     )(group, *[in_hbm(array) for array in (entries, lengths, histories, targets, item_pool)])
 
 
-def users_kernel(places, blocks, id_ref, x_refs, w_in, w_out, unit_ref, sums, loss_ref, bias, scratch):
-    count = len(places)
-    units = [unit_ref.at[id_ref[k]] for k in range(blocks)]
-    for at in range(0, count, 8):
+def users_kernel(places, id_ref, x_refs, w_in, w_out, unit_ref, sums_in, sums, loss_ref, bias, scratch):
+    blocks = unit_ref.shape[0]
+    for at in range(0, len(places), 8):
         users_step(
             x_refs[at : at + 8], [id_ref[blocks + k] for k in places[at : at + 8]],
-            [id_ref[k] for k in range(blocks)], w_in, w_out, units, loss_ref, sums, bias, *scratch,
+            w_in, w_out, unit_ref, sums if at else sums_in, sums, loss_ref, bias, *scratch,
         )
 
 
-def first_kernel(
-    places, blocks, id_ref, w_in_any, w_out_any, rel_any, unit_ref, *refs
-):
+def first_kernel(places, id_ref, w_in_any, w_out_any, rel_any, unit_ref, *refs):
     count = len(places)
     x_refs, refs = refs[:count], refs[count:]
-    loss_ref, sums, bias, refs = refs[0], refs[1 : 1 + blocks], refs[1 + blocks], refs[2 + blocks :]
+    loss_ref, sums, bias, refs = refs[0], refs[1], refs[2], refs[3:]
     w_in, w_out, rel, sems = refs[:4]
     heads, length = rel.shape
     moves = [(rel_any, rel), (w_in_any, w_in), (w_out_any, w_out)]
@@ -137,8 +134,6 @@
     for copy in copies:
         copy.start()
     loss_ref[...] = jnp.zeros_like(loss_ref)
-    for ref in sums:
-        ref[...] = jnp.zeros_like(ref)
     copies[0].wait()
     for h in range(heads):
         wide = jnp.broadcast_to(0.5 * rel[h : h + 1, :], (length, length))
@@ -146,32 +141,27 @@
         bias[h] = jnp.concatenate([turned, turned], axis=1)
     for copy in copies[1:]:
         copy.wait()
-    users_kernel(places, blocks, id_ref, x_refs, w_in, w_out, unit_ref, sums, loss_ref, bias, refs[4:])
-
-
-def second_kernel(places, blocks, id_ref, w_in, w_out, bias, unit_ref, loss_in, *refs):
+    users_kernel(places, id_ref, x_refs, w_in, w_out, unit_ref, None, sums, loss_ref, bias, refs[4:])
+
+
+def second_kernel(places, id_ref, w_in, w_out, bias, unit_ref, loss_in, sums_in, *refs):
     count = len(places)
-    sums_in, x_refs, refs = refs[:blocks], refs[blocks : blocks + count], refs[blocks + count :]
-    loss_ref, out_refs, wide_sums = refs[0], refs[1 : 1 + blocks], refs[1 + blocks]
-    sums = [out_refs[k] if k < blocks // 2 else wide_sums.at[k - blocks // 2] for k in range(blocks)]
+    x_refs, refs = refs[:count], refs[count:]
+    loss_ref, out_refs, sums, scratch = refs[0], refs[1:5], refs[5], refs[6:]
     loss_ref[...] = loss_in[...]
-    for k in range(blocks):
-        sums[k][...] = sums_in[k][...]
-    users_kernel(
-        places, blocks, id_ref, x_refs, w_in, w_out, unit_ref, sums, loss_ref, bias, refs[2 + blocks :]
-    )
-    for k in range(blocks // 2, blocks):
-        out_refs[k][...] = sums[k][...].astype(out_refs[k].dtype)
+    users_kernel(places, id_ref, x_refs, w_in, w_out, unit_ref, sums_in, sums, loss_ref, bias, scratch)
+    for k, ref in enumerate(out_refs):
+        ref[...] = sums[id_ref[k]].astype(ref.dtype)
 
 
 def users_step(
-    x_refs, spots, block_ids, w_in, w_out, unit_refs, loss_ref, sums, bias,
+    x_refs, spots, w_in, w_out, unit_ref, sums_in, sums, loss_ref, bias,
     exp_ref, residual, events, starts_ref, key, value, packed_tgt, packed_loss,
 ):
     heads, length, _ = bias.shape
     width = w_out.shape[0]
     hdim = width // heads
-    items = unit_refs[0].shape[0]
+    blocks, items, _ = unit_ref.shape
     per_step = len(x_refs)
 
     digits = [ref[width:, :].astype(jnp.float32) for ref in x_refs]
@@ -185,8 +175,6 @@
 
     place = lax.broadcasted_iota(jnp.int32, (1, length), 1)
     packed_tgt[...] = jnp.full_like(packed_tgt, -1)
-    key[:length, :] = jnp.zeros((length, width), key.dtype)
-    value[:length, :] = jnp.zeros((length, width), value.dtype)
     for u in range(per_step):
         starts_ref[pl.ds(starts[u], length), :] = jnp.full((length, length), starts[u], jnp.int32)
     for u in range(per_step):
@@ -208,8 +196,11 @@
 
     lines = tile // length
 
-    def one_tile(t, _):
-        first, strip = pl.multiple_of(t * tile, tile), t * lines
+    def one_tile(t):
+        opening = isinstance(t, int)
+        first, strip = t * tile, t * lines
+        if not opening:
+            first = pl.multiple_of(first, tile)
         item_id = lax.broadcasted_iota(jnp.int32, (items, tile), 0)
         x = events[pl.ds(first, tile), :].astype(jnp.float32)
         center, spread = center_and_spread(x)
@@ -227,14 +218,17 @@
         value[pl.ds(first + length, tile), :] = values
         mixed = []
         for k in range(lines):
-            base = pl.multiple_of(first + k * length, length)
-            sources = pl.ds(base, 2 * length)
+            base = first + k * length
+            if not opening:
+                base = pl.multiple_of(base, length)
             start = starts_ref[pl.ds(base, length), :]
-            ahead = packed_tgt[pl.ds(strip + k, 1), :] >= 0
             here = packed_tgt[pl.ds(strip + k + 1, 1), :] >= 0
-            keep_ahead = (base - length + col >= start) & ahead
-            keep_here = (col <= row) & (base + col >= start) & here
-            keep = jnp.concatenate([keep_ahead, keep_here], axis=1)
+            keep = (col <= row) & (base + col >= start) & here
+            sources, seen = pl.ds(base + length, length), slice(length, 2 * length)
+            if not (opening and k == 0):
+                ahead = packed_tgt[pl.ds(strip + k, 1), :] >= 0
+                keep = jnp.concatenate([(base - length + col >= start) & ahead, keep], axis=1)
+                sources, seen = pl.ds(base, 2 * length), slice(0, 2 * length)
             by_head = []
             for h in range(heads):
                 cols = slice(h * hdim, (h + 1) * hdim)
@@ -242,7 +236,7 @@
                     query[k * length : (k + 1) * length, cols], key[sources, cols], contract_last,
                     preferred_element_type=jnp.float32,
                 )
-                attn = half_silu(scores * (0.5 / math.sqrt(hdim)) + bias[h])
+                attn = half_silu(scores * (0.5 / math.sqrt(hdim)) + bias[h, :, seen])
                 attn = jnp.where(keep, attn, 0.0).astype(jnp.bfloat16)
                 by_head.append(jnp.dot(attn, value[sources, cols], preferred_element_type=jnp.float32))
             mixed.append(jnp.concatenate(by_head, axis=1))
@@ -259,28 +253,34 @@
         )
         total = jnp.zeros((1, tile), jnp.float32)
         target_dot = jnp.zeros((1, tile), jnp.float32)
-        for j, block in enumerate(block_ids):
+        for j in range(blocks):
             dots = lax.dot_general(
-                unit_refs[j][...], queries, contract_last, preferred_element_type=jnp.float32
+                unit_ref[j], queries, contract_last, preferred_element_type=jnp.float32
             )
             exps = jnp.exp2(dots * rate - rate)
             exp_ref[j] = exps
             total += jnp.sum(exps, axis=0, keepdims=True)
-            hit = item_id == target - block * items
+            hit = item_id == target - j * items
             target_dot += jnp.sum(jnp.where(hit, dots, 0.0), axis=0, keepdims=True)
         loss = logit_scale + jnp.log(total) - logit_scale * target_dot
         for k in range(lines):
             packed_loss[pl.ds(strip + k, 1), :] = loss[:, k * length : (k + 1) * length]
         share = jnp.where(target >= 0, 1.0 / total, 0.0)
-        for j, block in enumerate(block_ids):
-            hit = item_id == target - block * items
+        for j in range(blocks):
+            hit = item_id == target - j * items
             left = exp_ref[j] * share - jnp.where(hit, 1.0, 0.0)
             residual[j] = left.astype(jnp.bfloat16)
-        for j in range(len(block_ids)):
-            sums[j][...] += jnp.dot(residual[j], queries, preferred_element_type=jnp.float32)
+        before = sums_in if opening else sums
+        for j in range(blocks):
+            part = jnp.dot(residual[j], queries, preferred_element_type=jnp.float32)
+            sums[j] = part if before is None else before[j] + part
+
+    def later_tile(t, _):
+        one_tile(t)
         return 0
 
-    lax.fori_loop(0, tiles, one_tile, 0)
+    one_tile(0)
+    lax.fori_loop(1, tiles, later_tile, 0)
 
     for u in range(per_step):
         line, turn = starts[u] // length, lax.rem(starts[u], length)
@@ -314,11 +314,10 @@
 def first_call(ids, places, users, packed, units, w_in, w_out, rel_bias):
     heads, length = rel_bias.shape
     width, (blocks, items, _) = w_out.shape[0], units.shape
-    table = (heads, length, 2 * length)
     return pl.pallas_call(
-        functools.partial(first_kernel, places, blocks),
+        functools.partial(first_kernel, places),
         in_specs=[scalars] + [far_off] * 3 + [whole] * (1 + len(places)),
-        out_specs=[whole] * (2 + blocks),
+        out_specs=[whole] * 3,
         scratch_shapes=[
             pltpu.VMEM(w_in.shape, jnp.bfloat16),
             pltpu.VMEM(w_out.shape, jnp.bfloat16),
@@ -326,9 +325,11 @@
             pltpu.SemaphoreType.DMA((3,)),
         ]
         + step_scratch(places, length, width, blocks, items),
-        out_shape=[pltpu.VMEM((users, length), jnp.float32)]
-        + [pltpu.VMEM((items, width), jnp.float32)] * blocks
-        + [pltpu.VMEM(table, jnp.float32)],
+        out_shape=[
+            pltpu.VMEM((users, length), jnp.float32),
+            pltpu.VMEM((blocks, items, width), jnp.float32),
+            pltpu.VMEM((heads, length, 2 * length), jnp.float32),
+        ],
         compiler_params=pltpu.CompilerParams(vmem_limit_bytes=24 * 1024 * 1024),
         name="first_users",
     )(
@@ -338,20 +339,18 @@
 
 
 def second_call(ids, places, packed, units, w_in, w_out, loss, sums, bias):
-    items, width = sums[0].shape
-    length, blocks = bias.shape[1], len(sums)
-    arrays = [w_in, w_out, bias, units, loss, *sums, *packed]
+    blocks, items, width = sums.shape
+    length = bias.shape[1]
+    arrays = [w_in, w_out, bias, units, loss, sums, *packed]
     return pl.pallas_call(
-        functools.partial(second_kernel, places, blocks),
+        functools.partial(second_kernel, places),
         in_specs=[scalars] + [whole] * len(arrays),
-        out_specs=[whole] * (1 + blocks),
-        scratch_shapes=[pltpu.VMEM((blocks - blocks // 2, items, width), jnp.float32)]
+        out_specs=[whole] * 5,
+        scratch_shapes=[pltpu.VMEM(sums.shape, jnp.float32)]
         + step_scratch(places, length, width, blocks, items),
         out_shape=[jax.ShapeDtypeStruct(loss.shape, jnp.float32)]
-        + [
-            pltpu.VMEM((items, width), jnp.float32 if k < blocks // 2 else jnp.bfloat16)
-            for k in range(blocks)
-        ],
+        + [pltpu.VMEM((items, width), jnp.float32)] * 2
+        + [pltpu.VMEM((items, width), jnp.bfloat16)] * 2,
         compiler_params=pltpu.CompilerParams(vmem_limit_bytes=24 * 1024 * 1024),
         name="second_users",
     )(ids, *[in_vmem(array) for array in arrays])
@@ -383,7 +382,7 @@
     came = [((group - shift) % groups) * slots + slot for shift, slot in work]
     ids = jnp.stack([mine, mine ^ 2, mine ^ 1, mine ^ 3, *came])
     order = tuple(range(user_count))
-    loss, *sums, bias = first_call(
+    loss, sums, bias = first_call(
         ids, order[:half], user_count, packed[:half], units, w_in, w_out, rel_bias
     )
     row_loss, own, over, side, far = second_call(

time: 51.1 us -> 51.8 us (1.014)
  Pallas kernels: 13.1 us -> 14.2 us
    pallas_call x2, Pallas kernels: 10.6 us -> 11.7 us  [the longest x1 6.44 us: first_call(): pl.pallas_call(functools.partial(first_kernel, places), in_specs=[scalars...]
  transfers between devices with their start and end apart: 11 -> 11, of which waited for: 6 -> 6; matrix products, arithmetic and copies ran while one was open for 1% -> 1% of each run, Pallas kernels for 12% -> 13%
where the time goes in v14:
time: 51.8 us; the launch traced here: 51.5 us
  waiting for transfers between devices  22.1 us (43%)
  Pallas kernels  14.2 us (27%)
  starting transfers between devices  13 us (25%)
  other arithmetic  1.48 us (3%)
  between operations  0.7 us (1%)
    ppermute x7, waiting for transfers between devices, from_behind(): lax.ppermute(array, axis, [(i, (i + by) % devices) for i in range(devices)])  9.94 us
    ppermute x3, waiting for transfers between devices, swap(): return lax.ppermute(array, axis, [(i, i ^ bit) for i in range(devices)])  8.79 us
    ppermute x7, starting transfers between devices, from_behind(): lax.ppermute(array, axis, [(i, (i + by) % devices) for i in range(devices)])  7.95 us
    pallas_call x1, Pallas kernels, first_call(): pl.pallas_call(functools.partial(first_kernel, places), in_specs=[scalars...  6.44 us
    pallas_call x1, Pallas kernels, second_call(): pl.pallas_call(functools.partial(second_kernel, places), in_specs=[scalar...  5.31 us
    all_to_all x1, starting transfers between devices, shards(): lax.all_to_all(units, 'blk', split_axis=0, concat_axis=0, tiled=True)  4 us
    all_to_all x1, waiting for transfers between devices, shards(): lax.all_to_all(units, 'blk', split_axis=0, concat_axis=0, tiled=True)  3.34 us
    pallas_call x1, Pallas kernels, pack(): pl.pallas_call(functools.partial(pack_kernel, work, groups), in_specs=[pl...  2.44 us
  transfers between devices with their start and end apart: 11, of which 6 were waited for; matrix products, arithmetic and copies ran while one was open for 1% of the time, Pallas kernels for 13%

profile of v14, /device:TPU:30, one launch (start us, length us, event | category | flops | bytes accessed | tf_op | source)
XLA Modules:
  0.0 51.5 jit_solution(11285779447593558417)
XLA Ops:
  0.6 2.4 %pack.1 = (bf16[520,128]{1,0:T(8,128)(2,1)S(1)}, bf16[520,128]{1,0:T(8,128)(2,1)S(1)}, bf16[520,128]{1,0:T(8,128)(2,1)S(1)}, bf16[520,128]{1,0:T(8,128)(2,1)S(1)...) custom-call(s32[1]{0:T(128)} %bitcast.12.group_ref, ...), custom_call_target="tpu_custom_call" | custom-call | tf_op jit(solution)/shard_map/pack/pallas_call | solution.py:97
  3.1 4.0 %all-to-all-start = ((bf16[4,256,512]{2,1,0:T(8,128)(2,1)}), bf16[4,256,512]{2,1,0:T(8,128)(2,1)S(1)}, u32[]{:S(2)}, u32[]{:S(2)}) async-start(bf16[4,256,512]{2,1,0:T(8,128)(2,1)} %get-tuple-element.19), calls=%async_computation | async-start | bytes 2097152 | tf_op jit(solution)/shard_map/all_to_all | solution.py:376
  7.1 0.0 collective-permute-start
  7.1 2.0 %collective-permute-start.1 = (bf16[520,128]{1,0:T(8,128)(2,1)S(1)}, bf16[520,128]{1,0:T(8,128)(2,1)S(1)}, u32[]{:S(2)}, u32[]{:S(2)}) collective-permute-start(bf16[520,128]{1,0:T(8,128)(2,1)S(1)} %get-tuple-element.22), channel_id=1, source_target_pairs={{0,28},{4,0},{8,4},{12,8},{16,12},{20,16},{24,20},{28,24},{1,29},{... | collective-permute-start | bytes 399368 | tf_op jit(solution)/shard_map/ppermute | solution.py:25
  9.1 0.2 collective-permute-start.2
  9.3 1.7 %collective-permute-start.3 = (bf16[520,128]{1,0:T(8,128)(2,1)S(1)}, bf16[520,128]{1,0:T(8,128)(2,1)S(1)}, u32[]{:S(2)}, u32[]{:S(2)}) collective-permute-start(bf16[520,128]{1,0:T(8,128)(2,1)S(1)} %get-tuple-element.27), channel_id=1, source_target_pairs={{0,16},{4,20},{8,24},{12,28},{16,0},{20,4},{24,8},{28,12},{1,17},{... | collective-permute-start | bytes 399368 | tf_op jit(solution)/shard_map/ppermute | solution.py:25
  11.0 3.7 %collective-permute-start.4 = (bf16[520,128]{1,0:T(8,128)(2,1)S(1)}, bf16[520,128]{1,0:T(8,128)(2,1)S(1)}, u32[]{:S(2)}, u32[]{:S(2)}) collective-permute-start(bf16[520,128]{1,0:T(8,128)(2,1)S(1)} %get-tuple-element.28), channel_id=1, source_target_pairs={{0,12},{4,16},{8,20},{12,24},{16,28},{20,0},{24,4},{28,8},{1,13},{... | collective-permute-start | bytes 399368 | tf_op jit(solution)/shard_map/ppermute | solution.py:25
  14.7 0.0 collective-permute-done.refs_1_
  14.7 0.1 collective-permute-start.5
  14.8 1.4 %collective-permute-done.1.refs_2_ = bf16[520,128]{1,0:T(8,128)(2,1)S(1)} collective-permute-done((bf16[520,128]{1,0:T(8,128)(2,1)S(1)}, bf16[520,128]{1,0:T(8,128)(2,1)S(1)}, u32[]{:S(2)}, u32[]{:S(2)}) %collective-permute-start.1) | collective-permute-done | bytes 133152 | tf_op jit(solution)/shard_map/ppermute | solution.py:25
  16.2 0.2 collective-permute-start.6
  16.4 0.1 stack.51.id_ref
  16.5 0.0 collective-permute-done.2.refs_3_
  16.5 3.3 %all-to-all-done.unit_ref = bf16[4,256,512]{2,1,0:T(8,128)(2,1)S(1)} async-done(((bf16[4,256,512]{2,1,0:T(8,128)(2,1)}), bf16[4,256,512]{2,1,0:T(8,128)(2,1)S(1)}, u32[]{:S(2)}, u32[]{:S(2)}) %all-to-all-start) | async-done | bytes 1048608 | tf_op jit(solution)/shard_map/all_to_all | solution.py:376
  19.9 0.0 copy-start
  19.9 0.0 copy-start.1
  19.9 6.4 %first_users.1 = (f32[8,128]{1,0:T(8,128)S(1)}, f32[4,256,512]{2,1,0:T(8,128)S(1)}, f32[4,128,256]{2,1,0:T(8,128)S(1)}) custom-call(s32[12]{0:T(128)S(1)} %stack.51.id_ref, bf16[512,2048]{1,0:T(8,128)(2,1)} %w_in.1, bf16[512,512]{1,0:T(8,128)(2,1)} %w_out.1, f32[4,128]{1,0:T(4,128)} %rel_any.1, bf16[4,256,512]{2,1,0:T(8,128)(2,1)S(1)} %all-to-all-done.unit_ref, ...), custom_call_target="tpu_custom_call" | custom-call | tf_op jit(solution)/shard_map/first_users/pallas_call | solution.py:317
  26.3 4.1 %collective-permute-done.3.refs_0_ = bf16[520,128]{1,0:T(8,128)(2,1)S(1)} collective-permute-done((bf16[520,128]{1,0:T(8,128)(2,1)S(1)}, bf16[520,128]{1,0:T(8,128)(2,1)S(1)}, u32[]{:S(2)}, u32[]{:S(2)}) %collective-permute-start.3) | collective-permute-done | bytes 133152 | tf_op jit(solution)/shard_map/ppermute | solution.py:25
  30.5 0.0 collective-permute-done.4.refs_1_
  30.5 4.4 %collective-permute-done.5.refs_2_ = bf16[520,128]{1,0:T(8,128)(2,1)S(1)} collective-permute-done((bf16[520,128]{1,0:T(8,128)(2,1)S(1)}, bf16[520,128]{1,0:T(8,128)(2,1)S(1)}, u32[]{:S(2)}, u32[]{:S(2)}) %collective-permute-start.5) | collective-permute-done | bytes 133152 | tf_op jit(solution)/shard_map/ppermute | solution.py:25
  34.9 0.0 collective-permute-done.6.refs_3_
  34.9 0.0 copy-done
  34.9 0.0 copy-done.1
  34.9 0.0 copy-start.2
  34.9 5.3 %second_users.1 = (f32[8,128]{1,0:T(8,128)}, f32[256,512]{1,0:T(8,128)S(1)}, f32[256,512]{1,0:T(8,128)S(1)}, bf16[256,512]{1,0:T(8,128)(2,1)S(1)}, bf16[256,512]{1,0:T(8,128)(2,1)S(1)}) custom-call(s32[12]{0:T(128)S(1)} %stack.51.id_ref, bf16[512,2048]{1,0:T(8,128)(2,1)S(1)} %copy-done, bf16[512,512]{1,0:T(8,128)(2,1)S(1)} %copy-done.1, ...), custom_call_target="tpu_custom_call" | custom-call | tf_op jit(solution)/shard_map/second_users/pallas_call | solution.py:345
  40.2 0.0 collective-permute-start.8
  40.2 0.5 collective-permute-start.7
  40.7 1.0 %collective-permute-done.8 = bf16[256,512]{1,0:T(8,128)(2,1)S(1)} collective-permute-done((bf16[256,512]{1,0:T(8,128)(2,1)S(1)}, bf16[256,512]{1,0:T(8,128)(2,1)S(1)}, u32[]{:S(2)}, u32[]{:S(2)}) %collective-permute-start.8) | collective-permute-done | bytes 262176 | tf_op jit(solution)/shard_map/ppermute | solution.py:20
  41.7 0.1 add_convert_fusion
  41.8 0.5 collective-permute-start.9
  42.3 0.0 copy-done.2
  42.3 0.1 fusion
  42.5 0.0 collective-permute-done.7
  42.5 7.8 %collective-permute-done.9 = bf16[256,512]{1,0:T(8,128)(2,1)S(1)} collective-permute-done((bf16[256,512]{1,0:T(8,128)(2,1)S(1)}, bf16[256,512]{1,0:T(8,128)(2,1)S(1)}, u32[]{:S(2)}, u32[]{:S(2)}) %collective-permute-start.9) | collective-permute-done | bytes 262176 | tf_op jit(solution)/shard_map/ppermute | solution.py:20
  50.2 0.3 multiply_reduce_fusion
  50.5 1.0 %subtract_divide_fusion = f32[256,512]{1,0:T(8,128)} fusion(bf16[256,512]{1,0:T(8,128)(2,1)S(1)} %copy-done.2, f32[256]{0:T(256)S(1)} %multiply_reduce_fusion, f32[256]{0:T(256)S(1)} %add_sqrt_fusion, bf16[256,512]{1,0:T(8,128)(2,1)S(1)} %collective-permute-done.9, f32[256,512]{1,0:T(8,128)S(1)} %get-tuple-element.32, ...), kind=kLoop, calls=%fused_computation.3 | loop fusion | flops 1310720 | bytes 1837056 | tf_op jit(solution)/shard_map/div | solution.py:394
  (1 shorter events, 0.0 us)
Async XLA Ops:
  3.1 16.8 %all-to-all-start = ((bf16[4,256,512]{2,1,0:T(8,128)(2,1)}), bf16[4,256,512]{2,1,0:T(8,128)(2,1)S(1)}, u32[]{:S(2)}, u32[]{:S(2)}) async-start(bf16[4,256,512]{2,1,0:T(8,128)(2,1)} %get-tuple-element.19), calls=%async_computation | async-start | bytes 2097152 | tf_op jit(solution)/shard_map/all_to_all | solution.py:376
  7.1 7.7 %collective-permute-start = (bf16[520,128]{1,0:T(8,128)(2,1)S(1)}, bf16[520,128]{1,0:T(8,128)(2,1)S(1)}, u32[]{:S(2)}, u32[]{:S(2)}) collective-permute-start(bf16[520,128]{1,0:T(8,128)(2,1)S(1)} %get-tuple-element.21), channel_id=1, source_target_pairs={{0,4},{4,8},{8,12},{12,16},{16,20},{20,24},{24,28},{28,0},{1,5},{5... | collective-permute-start | bytes 399368 | tf_op jit(solution)/shard_map/ppermute | solution.py:25
  7.1 9.1 %collective-permute-start.1 = (bf16[520,128]{1,0:T(8,128)(2,1)S(1)}, bf16[520,128]{1,0:T(8,128)(2,1)S(1)}, u32[]{:S(2)}, u32[]{:S(2)}) collective-permute-start(bf16[520,128]{1,0:T(8,128)(2,1)S(1)} %get-tuple-element.22), channel_id=1, source_target_pairs={{0,28},{4,0},{8,4},{12,8},{16,12},{20,16},{24,20},{28,24},{1,29},{... | collective-permute-start | bytes 399368 | tf_op jit(solution)/shard_map/ppermute | solution.py:25
  9.1 7.4 %collective-permute-start.2 = (bf16[520,128]{1,0:T(8,128)(2,1)S(1)}, bf16[520,128]{1,0:T(8,128)(2,1)S(1)}, u32[]{:S(2)}, u32[]{:S(2)}) collective-permute-start(bf16[520,128]{1,0:T(8,128)(2,1)S(1)} %get-tuple-element.23), channel_id=1, source_target_pairs={{0,8},{4,12},{8,16},{12,20},{16,24},{20,28},{24,0},{28,4},{1,9},{5... | collective-permute-start | bytes 399368 | tf_op jit(solution)/shard_map/ppermute | solution.py:25
  9.3 21.1 %collective-permute-start.3 = (bf16[520,128]{1,0:T(8,128)(2,1)S(1)}, bf16[520,128]{1,0:T(8,128)(2,1)S(1)}, u32[]{:S(2)}, u32[]{:S(2)}) collective-permute-start(bf16[520,128]{1,0:T(8,128)(2,1)S(1)} %get-tuple-element.27), channel_id=1, source_target_pairs={{0,16},{4,20},{8,24},{12,28},{16,0},{20,4},{24,8},{28,12},{1,17},{... | collective-permute-start | bytes 399368 | tf_op jit(solution)/shard_map/ppermute | solution.py:25
  11.0 19.4 %collective-permute-start.4 = (bf16[520,128]{1,0:T(8,128)(2,1)S(1)}, bf16[520,128]{1,0:T(8,128)(2,1)S(1)}, u32[]{:S(2)}, u32[]{:S(2)}) collective-permute-start(bf16[520,128]{1,0:T(8,128)(2,1)S(1)} %get-tuple-element.28), channel_id=1, source_target_pairs={{0,12},{4,16},{8,20},{12,24},{16,28},{20,0},{24,4},{28,8},{1,13},{... | collective-permute-start | bytes 399368 | tf_op jit(solution)/shard_map/ppermute | solution.py:25
  14.7 20.1 %collective-permute-start.5 = (bf16[520,128]{1,0:T(8,128)(2,1)S(1)}, bf16[520,128]{1,0:T(8,128)(2,1)S(1)}, u32[]{:S(2)}, u32[]{:S(2)}) collective-permute-start(bf16[520,128]{1,0:T(8,128)(2,1)S(1)} %get-tuple-element.29), channel_id=1, source_target_pairs={{0,20},{4,24},{8,28},{12,0},{16,4},{20,8},{24,12},{28,16},{1,21},{... | collective-permute-start | bytes 399368 | tf_op jit(solution)/shard_map/ppermute | solution.py:25
  16.2 18.7 %collective-permute-start.6 = (bf16[520,128]{1,0:T(8,128)(2,1)S(1)}, bf16[520,128]{1,0:T(8,128)(2,1)S(1)}, u32[]{:S(2)}, u32[]{:S(2)}) collective-permute-start(bf16[520,128]{1,0:T(8,128)(2,1)S(1)} %get-tuple-element.30), channel_id=1, source_target_pairs={{0,24},{4,28},{8,0},{12,4},{16,8},{20,12},{24,16},{28,20},{1,25},{... | collective-permute-start | bytes 399368 | tf_op jit(solution)/shard_map/ppermute | solution.py:25
  19.9 15.0 %copy-start = (bf16[512,2048]{1,0:T(8,128)(2,1)S(1)}, bf16[512,2048]{1,0:T(8,128)(2,1)}, u32[]{:S(2)}) copy-start(bf16[512,2048]{1,0:T(8,128)(2,1)} %w_in.1) | copy-start | bytes 6291460
  19.9 15.0 %copy-start.1 = (bf16[512,512]{1,0:T(8,128)(2,1)S(1)}, bf16[512,512]{1,0:T(8,128)(2,1)}, u32[]{:S(2)}) copy-start(bf16[512,512]{1,0:T(8,128)(2,1)} %w_out.1) | copy-start | bytes 1572868
  34.9 7.4 %copy-start.2 = (bf16[256,512]{1,0:T(8,128)(2,1)S(1)}, bf16[256,512]{1,0:T(8,128)(2,1)}, u32[]{:S(2)}) copy-start(bf16[256,512]{1,0:T(8,128)(2,1)} %pool_any.1) | copy-start | bytes 786436
  40.2 1.5 %collective-permute-start.8 = (bf16[256,512]{1,0:T(8,128)(2,1)S(1)}, bf16[256,512]{1,0:T(8,128)(2,1)S(1)}, u32[]{:S(2)}, u32[]{:S(2)}) collective-permute-start(bf16[256,512]{1,0:T(8,128)(2,1)S(1)} %get-tuple-element.35), channel_id=1, source_target_pairs={{0,1},{1,0},{2,3},{3,2},{4,5},{5,4},{6,7},{7,6},{8,9},{9,8},{10,11... | collective-permute-start | bytes 786440 | tf_op jit(solution)/shard_map/ppermute | solution.py:20
  40.2 2.3 %collective-permute-start.7 = (bf16[256,512]{1,0:T(8,128)(2,1)S(1)}, bf16[256,512]{1,0:T(8,128)(2,1)S(1)}, u32[]{:S(2)}, u32[]{:S(2)}) collective-permute-start(bf16[256,512]{1,0:T(8,128)(2,1)S(1)} %get-tuple-element.33), channel_id=1, source_target_pairs={{0,1},{1,0},{2,3},{3,2},{4,5},{5,4},{6,7},{7,6},{8,9},{9,8},{10,11... | collective-permute-start | bytes 786440 | tf_op jit(solution)/shard_map/ppermute | solution.py:20
  41.8 8.4 %collective-permute-start.9 = (bf16[256,512]{1,0:T(8,128)(2,1)S(1)}, bf16[256,512]{1,0:T(8,128)(2,1)S(1)}, u32[]{:S(2)}, u32[]{:S(2)}) collective-permute-start(bf16[256,512]{1,0:T(8,128)(2,1)S(1)} %add_convert_fusion), channel_id=1, source_target_pairs={{0,2},{1,3},{2,0},{3,1},{4,6},{5,7},{6,4},{7,5},{8,10},{9,11},{10,... | collective-permute-start | bytes 786440 | tf_op jit(solution)/shard_map/ppermute | solution.py:20

commit v15 on v14

--- a/solution.py
+++ b/solution.py
@@ -114,12 +114,12 @@
     )(group, *[in_hbm(array) for array in (entries, lengths, histories, targets, item_pool)])
 
 
-def users_kernel(places, id_ref, x_refs, w_in, w_out, unit_ref, sums_in, sums, loss_ref, bias, scratch):
+def users_kernel(places, id_ref, x_refs, w_in, w_out, unit_ref, sums, loss_ref, bias, scratch):
     blocks = unit_ref.shape[0]
     for at in range(0, len(places), 8):
         users_step(
             x_refs[at : at + 8], [id_ref[blocks + k] for k in places[at : at + 8]],
-            w_in, w_out, unit_ref, sums if at else sums_in, sums, loss_ref, bias, *scratch,
+            w_in, w_out, unit_ref, sums, loss_ref, bias, *scratch,
         )
 
 
@@ -134,6 +134,7 @@
     for copy in copies:
         copy.start()
     loss_ref[...] = jnp.zeros_like(loss_ref)
+    sums[...] = jnp.zeros_like(sums)
     copies[0].wait()
     for h in range(heads):
         wide = jnp.broadcast_to(0.5 * rel[h : h + 1, :], (length, length))
@@ -141,7 +142,7 @@
         bias[h] = jnp.concatenate([turned, turned], axis=1)
     for copy in copies[1:]:
         copy.wait()
-    users_kernel(places, id_ref, x_refs, w_in, w_out, unit_ref, None, sums, loss_ref, bias, refs[4:])
+    users_kernel(places, id_ref, x_refs, w_in, w_out, unit_ref, sums, loss_ref, bias, refs[4:])
 
 
 def second_kernel(places, id_ref, w_in, w_out, bias, unit_ref, loss_in, sums_in, *refs):
@@ -149,13 +150,14 @@
     x_refs, refs = refs[:count], refs[count:]
     loss_ref, out_refs, sums, scratch = refs[0], refs[1:5], refs[5], refs[6:]
     loss_ref[...] = loss_in[...]
-    users_kernel(places, id_ref, x_refs, w_in, w_out, unit_ref, sums_in, sums, loss_ref, bias, scratch)
+    sums[...] = sums_in[...]
+    users_kernel(places, id_ref, x_refs, w_in, w_out, unit_ref, sums, loss_ref, bias, scratch)
     for k, ref in enumerate(out_refs):
         ref[...] = sums[id_ref[k]].astype(ref.dtype)
 
 
 def users_step(
-    x_refs, spots, w_in, w_out, unit_ref, sums_in, sums, loss_ref, bias,
+    x_refs, spots, w_in, w_out, unit_ref, sums, loss_ref, bias,
     exp_ref, residual, events, starts_ref, key, value, packed_tgt, packed_loss,
 ):
     heads, length, _ = bias.shape
@@ -175,6 +177,8 @@
 
     place = lax.broadcasted_iota(jnp.int32, (1, length), 1)
     packed_tgt[...] = jnp.full_like(packed_tgt, -1)
+    key[:length, :] = jnp.zeros((length, width), key.dtype)
+    value[:length, :] = jnp.zeros((length, width), value.dtype)
     for u in range(per_step):
         starts_ref[pl.ds(starts[u], length), :] = jnp.full((length, length), starts[u], jnp.int32)
     for u in range(per_step):
@@ -196,11 +200,8 @@
 
     lines = tile // length
 
-    def one_tile(t):
-        opening = isinstance(t, int)
-        first, strip = t * tile, t * lines
-        if not opening:
-            first = pl.multiple_of(first, tile)
+    def one_tile(t, _):
+        first, strip = pl.multiple_of(t * tile, tile), t * lines
         item_id = lax.broadcasted_iota(jnp.int32, (items, tile), 0)
         x = events[pl.ds(first, tile), :].astype(jnp.float32)
         center, spread = center_and_spread(x)
@@ -218,17 +219,14 @@
         value[pl.ds(first + length, tile), :] = values
         mixed = []
         for k in range(lines):
-            base = first + k * length
-            if not opening:
-                base = pl.multiple_of(base, length)
+            base = pl.multiple_of(first + k * length, length)
+            sources = pl.ds(base, 2 * length)
             start = starts_ref[pl.ds(base, length), :]
+            ahead = packed_tgt[pl.ds(strip + k, 1), :] >= 0
             here = packed_tgt[pl.ds(strip + k + 1, 1), :] >= 0
-            keep = (col <= row) & (base + col >= start) & here
-            sources, seen = pl.ds(base + length, length), slice(length, 2 * length)
-            if not (opening and k == 0):
-                ahead = packed_tgt[pl.ds(strip + k, 1), :] >= 0
-                keep = jnp.concatenate([(base - length + col >= start) & ahead, keep], axis=1)
-                sources, seen = pl.ds(base, 2 * length), slice(0, 2 * length)
+            keep_ahead = (base - length + col >= start) & ahead
+            keep_here = (col <= row) & (base + col >= start) & here
+            keep = jnp.concatenate([keep_ahead, keep_here], axis=1)
             by_head = []
             for h in range(heads):
                 cols = slice(h * hdim, (h + 1) * hdim)
@@ -236,7 +234,7 @@
                     query[k * length : (k + 1) * length, cols], key[sources, cols], contract_last,
                     preferred_element_type=jnp.float32,
                 )
-                attn = half_silu(scores * (0.5 / math.sqrt(hdim)) + bias[h, :, seen])
+                attn = half_silu(scores * (0.5 / math.sqrt(hdim)) + bias[h])
                 attn = jnp.where(keep, attn, 0.0).astype(jnp.bfloat16)
                 by_head.append(jnp.dot(attn, value[sources, cols], preferred_element_type=jnp.float32))
             mixed.append(jnp.concatenate(by_head, axis=1))
@@ -270,17 +268,11 @@
             hit = item_id == target - j * items
             left = exp_ref[j] * share - jnp.where(hit, 1.0, 0.0)
             residual[j] = left.astype(jnp.bfloat16)
-        before = sums_in if opening else sums
         for j in range(blocks):
-            part = jnp.dot(residual[j], queries, preferred_element_type=jnp.float32)
-            sums[j] = part if before is None else before[j] + part
-
-    def later_tile(t, _):
-        one_tile(t)
+            sums[j] += jnp.dot(residual[j], queries, preferred_element_type=jnp.float32)
         return 0
 
-    one_tile(0)
-    lax.fori_loop(1, tiles, later_tile, 0)
+    lax.fori_loop(0, tiles, one_tile, 0)
 
     for u in range(per_step):
         line, turn = starts[u] // length, lax.rem(starts[u], length)

time: 51.8 us -> 52.2 us (level)
  the two profiles are of different devices: /device:TPU:30 before, /device:TPU:18 now
where the time goes in v15:
time: 52.2 us; the launch traced here: 52.4 us
  waiting for transfers between devices  21.3 us (41%)
  Pallas kernels  16.2 us (31%)
  starting transfers between devices  12.6 us (24%)
  other arithmetic  1.48 us (3%)
  between operations  0.75 us (1%)
    ppermute x7, waiting for transfers between devices, from_behind(): lax.ppermute(array, axis, [(i, (i + by) % devices) for i in range(devices)])  12.1 us
    ppermute x3, waiting for transfers between devices, swap(): return lax.ppermute(array, axis, [(i, i ^ bit) for i in range(devices)])  9.2 us
    pallas_call x1, Pallas kernels, first_call(): pl.pallas_call(functools.partial(first_kernel, places), in_specs=[scalars...  9.09 us
    ppermute x7, starting transfers between devices, from_behind(): lax.ppermute(array, axis, [(i, (i + by) % devices) for i in range(devices)])  8.52 us
    pallas_call x1, Pallas kernels, second_call(): pl.pallas_call(functools.partial(second_kernel, places), in_specs=[scalar...  4.66 us
    all_to_all x1, starting transfers between devices, shards(): lax.all_to_all(units, 'blk', split_axis=0, concat_axis=0, tiled=True)  3.53 us
    pallas_call x1, Pallas kernels, pack(): pl.pallas_call(functools.partial(pack_kernel, work, groups), in_specs=[pl...  2.44 us
  transfers between devices with their start and end apart: 11, of which 6 were waited for; matrix products, arithmetic and copies ran while one was open for 1% of the time, Pallas kernels for 17%

profile of v15, /device:TPU:18, one launch (start us, length us, event | category | flops | bytes accessed | tf_op | source)
XLA Modules:
  0.0 52.4 jit_solution(15742560642116116063)
XLA Ops:
  0.6 2.4 %pack.1 = (bf16[520,128]{1,0:T(8,128)(2,1)S(1)}, bf16[520,128]{1,0:T(8,128)(2,1)S(1)}, bf16[520,128]{1,0:T(8,128)(2,1)S(1)}, bf16[520,128]{1,0:T(8,128)(2,1)S(1)...) custom-call(s32[1]{0:T(128)} %bitcast.12.group_ref, ...), custom_call_target="tpu_custom_call" | custom-call | tf_op jit(solution)/shard_map/pack/pallas_call | solution.py:97
  3.1 3.5 %all-to-all-start = ((bf16[4,256,512]{2,1,0:T(8,128)(2,1)}), bf16[4,256,512]{2,1,0:T(8,128)(2,1)S(1)}, u32[]{:S(2)}, u32[]{:S(2)}) async-start(bf16[4,256,512]{2,1,0:T(8,128)(2,1)} %get-tuple-element.19), calls=%async_computation | async-start | bytes 2097152 | tf_op jit(solution)/shard_map/all_to_all | solution.py:368
  6.6 1.6 %collective-permute-start = (bf16[520,128]{1,0:T(8,128)(2,1)S(1)}, bf16[520,128]{1,0:T(8,128)(2,1)S(1)}, u32[]{:S(2)}, u32[]{:S(2)}) collective-permute-start(bf16[520,128]{1,0:T(8,128)(2,1)S(1)} %get-tuple-element.21), channel_id=1, source_target_pairs={{0,4},{4,8},{8,12},{12,16},{16,20},{20,24},{24,28},{28,0},{1,5},{5... | collective-permute-start | bytes 399368 | tf_op jit(solution)/shard_map/ppermute | solution.py:25
  8.2 0.5 collective-permute-start.1
  8.7 1.6 %collective-permute-start.2 = (bf16[520,128]{1,0:T(8,128)(2,1)S(1)}, bf16[520,128]{1,0:T(8,128)(2,1)S(1)}, u32[]{:S(2)}, u32[]{:S(2)}) collective-permute-start(bf16[520,128]{1,0:T(8,128)(2,1)S(1)} %get-tuple-element.23), channel_id=1, source_target_pairs={{0,8},{4,12},{8,16},{12,20},{16,24},{20,28},{24,0},{28,4},{1,9},{5... | collective-permute-start | bytes 399368 | tf_op jit(solution)/shard_map/ppermute | solution.py:25
  10.3 0.3 collective-permute-start.3
  10.6 3.5 %collective-permute-start.4 = (bf16[520,128]{1,0:T(8,128)(2,1)S(1)}, bf16[520,128]{1,0:T(8,128)(2,1)S(1)}, u32[]{:S(2)}, u32[]{:S(2)}) collective-permute-start(bf16[520,128]{1,0:T(8,128)(2,1)S(1)} %get-tuple-element.28), channel_id=1, source_target_pairs={{0,12},{4,16},{8,20},{12,24},{16,28},{20,0},{24,4},{28,8},{1,13},{... | collective-permute-start | bytes 399368 | tf_op jit(solution)/shard_map/ppermute | solution.py:25
  14.1 1.2 %collective-permute-done.refs_1_ = bf16[520,128]{1,0:T(8,128)(2,1)S(1)} collective-permute-done((bf16[520,128]{1,0:T(8,128)(2,1)S(1)}, bf16[520,128]{1,0:T(8,128)(2,1)S(1)}, u32[]{:S(2)}, u32[]{:S(2)}) %collective-permute-start) | collective-permute-done | bytes 133152 | tf_op jit(solution)/shard_map/ppermute | solution.py:25
  15.2 0.0 collective-permute-start.5
  15.2 0.3 collective-permute-done.1.refs_2_
  15.5 1.1 %collective-permute-start.6 = (bf16[520,128]{1,0:T(8,128)(2,1)S(1)}, bf16[520,128]{1,0:T(8,128)(2,1)S(1)}, u32[]{:S(2)}, u32[]{:S(2)}) collective-permute-start(bf16[520,128]{1,0:T(8,128)(2,1)S(1)} %get-tuple-element.30), channel_id=1, source_target_pairs={{0,24},{4,28},{8,0},{12,4},{16,8},{20,12},{24,16},{28,20},{1,25},{... | collective-permute-start | bytes 399368 | tf_op jit(solution)/shard_map/ppermute | solution.py:25
  16.6 0.1 stack.51.id_ref
  16.7 10.6 %collective-permute-done.2.refs_3_ = bf16[520,128]{1,0:T(8,128)(2,1)S(1)} collective-permute-done((bf16[520,128]{1,0:T(8,128)(2,1)S(1)}, bf16[520,128]{1,0:T(8,128)(2,1)S(1)}, u32[]{:S(2)}, u32[]{:S(2)}) %collective-permute-start.2) | collective-permute-done | bytes 133152 | tf_op jit(solution)/shard_map/ppermute | solution.py:25
  27.3 0.0 all-to-all-done.unit_ref
  27.3 0.0 copy-start
  27.3 0.0 copy-start.1
  27.3 9.1 %first_users.1 = (f32[8,128]{1,0:T(8,128)S(1)}, f32[4,256,512]{2,1,0:T(8,128)S(1)}, f32[4,128,256]{2,1,0:T(8,128)S(1)}) custom-call(s32[12]{0:T(128)S(1)} %stack.51.id_ref, bf16[512,2048]{1,0:T(8,128)(2,1)} %w_in.1, bf16[512,512]{1,0:T(8,128)(2,1)} %w_out.1, f32[4,128]{1,0:T(4,128)} %rel_any.1, bf16[4,256,512]{2,1,0:T(8,128)(2,1)S(1)} %all-to-all-done.unit_ref, ...), custom_call_target="tpu_custom_call" | custom-call | tf_op jit(solution)/shard_map/first_users/pallas_call | solution.py:309
  36.4 0.0 collective-permute-done.3.refs_0_
  36.4 0.0 collective-permute-done.4.refs_1_
  36.4 0.0 collective-permute-done.5.refs_2_
  36.4 0.0 collective-permute-done.6.refs_3_
  36.4 0.0 copy-done
  36.5 0.0 copy-done.1
  36.5 0.0 copy-start.2
  36.5 4.7 %second_users.1 = (f32[8,128]{1,0:T(8,128)}, f32[256,512]{1,0:T(8,128)S(1)}, f32[256,512]{1,0:T(8,128)S(1)}, bf16[256,512]{1,0:T(8,128)(2,1)S(1)}, bf16[256,512]{1,0:T(8,128)(2,1)S(1)}) custom-call(s32[12]{0:T(128)S(1)} %stack.51.id_ref, bf16[512,2048]{1,0:T(8,128)(2,1)S(1)} %copy-done, bf16[512,512]{1,0:T(8,128)(2,1)S(1)} %copy-done.1, ...), custom_call_target="tpu_custom_call" | custom-call | tf_op jit(solution)/shard_map/second_users/pallas_call | solution.py:337
  41.1 0.0 collective-permute-start.8
  41.1 0.5 collective-permute-start.7
  41.6 1.0 %collective-permute-done.8 = bf16[256,512]{1,0:T(8,128)(2,1)S(1)} collective-permute-done((bf16[256,512]{1,0:T(8,128)(2,1)S(1)}, bf16[256,512]{1,0:T(8,128)(2,1)S(1)}, u32[]{:S(2)}, u32[]{:S(2)}) %collective-permute-start.8) | collective-permute-done | bytes 262176 | tf_op jit(solution)/shard_map/ppermute | solution.py:20
  42.7 0.1 add_convert_fusion
  42.8 0.1 collective-permute-start.9
  42.8 0.0 copy-done.2
  42.8 0.1 fusion
  43.0 0.1 collective-permute-done.7
  43.0 8.1 %collective-permute-done.9 = bf16[256,512]{1,0:T(8,128)(2,1)S(1)} collective-permute-done((bf16[256,512]{1,0:T(8,128)(2,1)S(1)}, bf16[256,512]{1,0:T(8,128)(2,1)S(1)}, u32[]{:S(2)}, u32[]{:S(2)}) %collective-permute-start.9) | collective-permute-done | bytes 262176 | tf_op jit(solution)/shard_map/ppermute | solution.py:20
  51.2 0.3 multiply_reduce_fusion
  51.4 1.0 %subtract_divide_fusion = f32[256,512]{1,0:T(8,128)} fusion(bf16[256,512]{1,0:T(8,128)(2,1)S(1)} %copy-done.2, f32[256]{0:T(256)S(1)} %multiply_reduce_fusion, f32[256]{0:T(256)S(1)} %add_sqrt_fusion, bf16[256,512]{1,0:T(8,128)(2,1)S(1)} %collective-permute-done.9, f32[256,512]{1,0:T(8,128)S(1)} %get-tuple-element.32, ...), kind=kLoop, calls=%fused_computation.3 | loop fusion | flops 1310720 | bytes 1837056 | tf_op jit(solution)/shard_map/div | solution.py:386
  (1 shorter events, 0.0 us)
Async XLA Ops:
  3.1 24.2 %all-to-all-start = ((bf16[4,256,512]{2,1,0:T(8,128)(2,1)}), bf16[4,256,512]{2,1,0:T(8,128)(2,1)S(1)}, u32[]{:S(2)}, u32[]{:S(2)}) async-start(bf16[4,256,512]{2,1,0:T(8,128)(2,1)} %get-tuple-element.19), calls=%async_computation | async-start | bytes 2097152 | tf_op jit(solution)/shard_map/all_to_all | solution.py:368
  6.6 8.6 %collective-permute-start = (bf16[520,128]{1,0:T(8,128)(2,1)S(1)}, bf16[520,128]{1,0:T(8,128)(2,1)S(1)}, u32[]{:S(2)}, u32[]{:S(2)}) collective-permute-start(bf16[520,128]{1,0:T(8,128)(2,1)S(1)} %get-tuple-element.21), channel_id=1, source_target_pairs={{0,4},{4,8},{8,12},{12,16},{16,20},{20,24},{24,28},{28,0},{1,5},{5... | collective-permute-start | bytes 399368 | tf_op jit(solution)/shard_map/ppermute | solution.py:25
  8.2 7.3 %collective-permute-start.1 = (bf16[520,128]{1,0:T(8,128)(2,1)S(1)}, bf16[520,128]{1,0:T(8,128)(2,1)S(1)}, u32[]{:S(2)}, u32[]{:S(2)}) collective-permute-start(bf16[520,128]{1,0:T(8,128)(2,1)S(1)} %get-tuple-element.22), channel_id=1, source_target_pairs={{0,28},{4,0},{8,4},{12,8},{16,12},{20,16},{24,20},{28,24},{1,29},{... | collective-permute-start | bytes 399368 | tf_op jit(solution)/shard_map/ppermute | solution.py:25
  8.7 18.6 %collective-permute-start.2 = (bf16[520,128]{1,0:T(8,128)(2,1)S(1)}, bf16[520,128]{1,0:T(8,128)(2,1)S(1)}, u32[]{:S(2)}, u32[]{:S(2)}) collective-permute-start(bf16[520,128]{1,0:T(8,128)(2,1)S(1)} %get-tuple-element.23), channel_id=1, source_target_pairs={{0,8},{4,12},{8,16},{12,20},{16,24},{20,28},{24,0},{28,4},{1,9},{5... | collective-permute-start | bytes 399368 | tf_op jit(solution)/shard_map/ppermute | solution.py:25
  10.3 26.1 %collective-permute-start.3 = (bf16[520,128]{1,0:T(8,128)(2,1)S(1)}, bf16[520,128]{1,0:T(8,128)(2,1)S(1)}, u32[]{:S(2)}, u32[]{:S(2)}) collective-permute-start(bf16[520,128]{1,0:T(8,128)(2,1)S(1)} %get-tuple-element.27), channel_id=1, source_target_pairs={{0,16},{4,20},{8,24},{12,28},{16,0},{20,4},{24,8},{28,12},{1,17},{... | collective-permute-start | bytes 399368 | tf_op jit(solution)/shard_map/ppermute | solution.py:25
  10.6 25.8 %collective-permute-start.4 = (bf16[520,128]{1,0:T(8,128)(2,1)S(1)}, bf16[520,128]{1,0:T(8,128)(2,1)S(1)}, u32[]{:S(2)}, u32[]{:S(2)}) collective-permute-start(bf16[520,128]{1,0:T(8,128)(2,1)S(1)} %get-tuple-element.28), channel_id=1, source_target_pairs={{0,12},{4,16},{8,20},{12,24},{16,28},{20,0},{24,4},{28,8},{1,13},{... | collective-permute-start | bytes 399368 | tf_op jit(solution)/shard_map/ppermute | solution.py:25
  15.2 21.2 %collective-permute-start.5 = (bf16[520,128]{1,0:T(8,128)(2,1)S(1)}, bf16[520,128]{1,0:T(8,128)(2,1)S(1)}, u32[]{:S(2)}, u32[]{:S(2)}) collective-permute-start(bf16[520,128]{1,0:T(8,128)(2,1)S(1)} %get-tuple-element.29), channel_id=1, source_target_pairs={{0,20},{4,24},{8,28},{12,0},{16,4},{20,8},{24,12},{28,16},{1,21},{... | collective-permute-start | bytes 399368 | tf_op jit(solution)/shard_map/ppermute | solution.py:25
  15.5 20.9 %collective-permute-start.6 = (bf16[520,128]{1,0:T(8,128)(2,1)S(1)}, bf16[520,128]{1,0:T(8,128)(2,1)S(1)}, u32[]{:S(2)}, u32[]{:S(2)}) collective-permute-start(bf16[520,128]{1,0:T(8,128)(2,1)S(1)} %get-tuple-element.30), channel_id=1, source_target_pairs={{0,24},{4,28},{8,0},{12,4},{16,8},{20,12},{24,16},{28,20},{1,25},{... | collective-permute-start | bytes 399368 | tf_op jit(solution)/shard_map/ppermute | solution.py:25
  27.3 9.1 %copy-start = (bf16[512,2048]{1,0:T(8,128)(2,1)S(1)}, bf16[512,2048]{1,0:T(8,128)(2,1)}, u32[]{:S(2)}) copy-start(bf16[512,2048]{1,0:T(8,128)(2,1)} %w_in.1) | copy-start | bytes 6291460
  27.3 9.2 %copy-start.1 = (bf16[512,512]{1,0:T(8,128)(2,1)S(1)}, bf16[512,512]{1,0:T(8,128)(2,1)}, u32[]{:S(2)}) copy-start(bf16[512,512]{1,0:T(8,128)(2,1)} %w_out.1) | copy-start | bytes 1572868
  36.5 6.4 %copy-start.2 = (bf16[256,512]{1,0:T(8,128)(2,1)S(1)}, bf16[256,512]{1,0:T(8,128)(2,1)}, u32[]{:S(2)}) copy-start(bf16[256,512]{1,0:T(8,128)(2,1)} %pool_any.1) | copy-start | bytes 786436
  41.1 1.5 %collective-permute-start.8 = (bf16[256,512]{1,0:T(8,128)(2,1)S(1)}, bf16[256,512]{1,0:T(8,128)(2,1)S(1)}, u32[]{:S(2)}, u32[]{:S(2)}) collective-permute-start(bf16[256,512]{1,0:T(8,128)(2,1)S(1)} %get-tuple-element.35), channel_id=1, source_target_pairs={{0,1},{1,0},{2,3},{3,2},{4,5},{5,4},{6,7},{7,6},{8,9},{9,8},{10,11... | collective-permute-start | bytes 786440 | tf_op jit(solution)/shard_map/ppermute | solution.py:20
  41.1 1.9 %collective-permute-start.7 = (bf16[256,512]{1,0:T(8,128)(2,1)S(1)}, bf16[256,512]{1,0:T(8,128)(2,1)S(1)}, u32[]{:S(2)}, u32[]{:S(2)}) collective-permute-start(bf16[256,512]{1,0:T(8,128)(2,1)S(1)} %get-tuple-element.33), channel_id=1, source_target_pairs={{0,1},{1,0},{2,3},{3,2},{4,5},{5,4},{6,7},{7,6},{8,9},{9,8},{10,11... | collective-permute-start | bytes 786440 | tf_op jit(solution)/shard_map/ppermute | solution.py:20
  42.8 8.4 %collective-permute-start.9 = (bf16[256,512]{1,0:T(8,128)(2,1)S(1)}, bf16[256,512]{1,0:T(8,128)(2,1)S(1)}, u32[]{:S(2)}, u32[]{:S(2)}) collective-permute-start(bf16[256,512]{1,0:T(8,128)(2,1)S(1)} %add_convert_fusion), channel_id=1, source_target_pairs={{0,2},{1,3},{2,0},{3,1},{4,6},{5,7},{6,4},{7,5},{8,10},{9,11},{10,... | collective-permute-start | bytes 786440 | tf_op jit(solution)/shard_map/ppermute | solution.py:20

commit v16 on v15

--- a/solution.py
+++ b/solution.py
@@ -43,7 +43,7 @@
 
 
 def pack_kernel(
-    work, groups, group_ref, list_any, len_any, from_any, tgt_any, pool_any, *refs,
+    work, groups, list_any, len_any, from_any, tgt_any, pool_any, *refs,
 ):
     users, length, width = from_any.shape
     to_refs, unit_any = refs[:users], refs[users]
@@ -59,7 +59,8 @@
         copy.start()
     small[0].wait()
     slots = users // groups
-    order = [entries[(group_ref[0] + shift) % groups * slots + slot] for shift, slot in work]
+    group = lax.axis_index("dp")
+    order = [entries[lax.rem(group + shift, groups) * slots + slot] for shift, slot in work]
     copies_in = [
         pltpu.make_async_copy(
             from_any.at[order[k], :, pl.ds(c * length, length)],
@@ -90,13 +91,13 @@
         copy.wait()
 
 
-def pack(histories, lengths, targets, entries, item_pool, work, groups, group, blocks):
+def pack(histories, lengths, targets, entries, item_pool, work, groups, blocks):
     users, length, width = histories.shape
     shape = (width + number_rows, length)
     hbm = pl.BlockSpec(memory_space=pltpu.HBM)
     return pl.pallas_call(
         functools.partial(pack_kernel, work, groups),
-        in_specs=[pl.BlockSpec(memory_space=pltpu.SMEM)] + [hbm] * 5,
+        in_specs=[hbm] * 5,
         out_specs=[pl.BlockSpec(memory_space=pltpu.VMEM)] * users + [hbm],
         scratch_shapes=[
             pltpu.SMEM(entries.shape, jnp.int32),
@@ -111,20 +112,22 @@
         + [pltpu.HBM((blocks,) + item_pool.shape, jnp.bfloat16)],
         compiler_params=pltpu.CompilerParams(vmem_limit_bytes=16 * 1024 * 1024),
         name="pack",
-    )(group, *[in_hbm(array) for array in (entries, lengths, histories, targets, item_pool)])
-
-
-def users_kernel(places, id_ref, x_refs, w_in, w_out, unit_ref, sums, loss_ref, bias, scratch):
-    blocks = unit_ref.shape[0]
-    for at in range(0, len(places), 8):
+    )(*[in_hbm(array) for array in (entries, lengths, histories, targets, item_pool)])
+
+
+def users_kernel(work, groups, x_refs, w_in, w_out, unit_ref, sums, loss_ref, bias, scratch):
+    slots = loss_ref.shape[0] // groups
+    group = lax.axis_index("dp")
+    spots = [lax.rem(group + groups - shift, groups) * slots + slot for shift, slot in work]
+    for at in range(0, len(work), 8):
         users_step(
-            x_refs[at : at + 8], [id_ref[blocks + k] for k in places[at : at + 8]],
+            x_refs[at : at + 8], spots[at : at + 8],
             w_in, w_out, unit_ref, sums, loss_ref, bias, *scratch,
         )
 
 
-def first_kernel(places, id_ref, w_in_any, w_out_any, rel_any, unit_ref, *refs):
-    count = len(places)
+def first_kernel(work, groups, w_in_any, w_out_any, rel_any, unit_ref, *refs):
+    count = len(work)
     x_refs, refs = refs[:count], refs[count:]
     loss_ref, sums, bias, refs = refs[0], refs[1], refs[2], refs[3:]
     w_in, w_out, rel, sems = refs[:4]
@@ -142,18 +145,19 @@
         bias[h] = jnp.concatenate([turned, turned], axis=1)
     for copy in copies[1:]:
         copy.wait()
-    users_kernel(places, id_ref, x_refs, w_in, w_out, unit_ref, sums, loss_ref, bias, refs[4:])
-
-
-def second_kernel(places, id_ref, w_in, w_out, bias, unit_ref, loss_in, sums_in, *refs):
-    count = len(places)
+    users_kernel(work, groups, x_refs, w_in, w_out, unit_ref, sums, loss_ref, bias, refs[4:])
+
+
+def second_kernel(work, groups, w_in, w_out, bias, unit_ref, loss_in, sums_in, *refs):
+    count = len(work)
     x_refs, refs = refs[:count], refs[count:]
     loss_ref, out_refs, sums, scratch = refs[0], refs[1:5], refs[5], refs[6:]
     loss_ref[...] = loss_in[...]
     sums[...] = sums_in[...]
-    users_kernel(places, id_ref, x_refs, w_in, w_out, unit_ref, sums, loss_ref, bias, scratch)
-    for k, ref in enumerate(out_refs):
-        ref[...] = sums[id_ref[k]].astype(ref.dtype)
+    users_kernel(work, groups, x_refs, w_in, w_out, unit_ref, sums, loss_ref, bias, scratch)
+    mine = lax.axis_index("blk")
+    for bits, ref in zip((0, 2, 1, 3), out_refs):
+        ref[...] = sums[mine ^ bits].astype(ref.dtype)
 
 
 def users_step(
@@ -283,8 +287,8 @@
         loss_ref[pl.ds(spots[u], 1), :] = jnp.where(place < lens[u], loss, 0.0)
 
 
-def step_scratch(places, length, width, blocks, items):
-    rows = -(-min(len(places), 8) * length // tile) * tile
+def step_scratch(count, length, width, blocks, items):
+    rows = -(-min(count, 8) * length // tile) * tile
     lines = -(-(rows // length + 2) // 8) * 8
     return [
         pltpu.VMEM((blocks, items, tile), jnp.float32),
@@ -298,17 +302,16 @@
     ]
 
 
-scalars = pl.BlockSpec(memory_space=pltpu.SMEM)
 whole = pl.BlockSpec(memory_space=pltpu.VMEM)
 far_off = pl.BlockSpec(memory_space=pltpu.HBM)
 
 
-def first_call(ids, places, users, packed, units, w_in, w_out, rel_bias):
+def first_call(work, groups, users, packed, units, w_in, w_out, rel_bias):
     heads, length = rel_bias.shape
     width, (blocks, items, _) = w_out.shape[0], units.shape
     return pl.pallas_call(
-        functools.partial(first_kernel, places),
-        in_specs=[scalars] + [far_off] * 3 + [whole] * (1 + len(places)),
+        functools.partial(first_kernel, work, groups),
+        in_specs=[far_off] * 3 + [whole] * (1 + len(work)),
         out_specs=[whole] * 3,
         scratch_shapes=[
             pltpu.VMEM(w_in.shape, jnp.bfloat16),
@@ -316,7 +319,7 @@
             pltpu.VMEM(rel_bias.shape, jnp.float32),
             pltpu.SemaphoreType.DMA((3,)),
         ]
-        + step_scratch(places, length, width, blocks, items),
+        + step_scratch(len(work), length, width, blocks, items),
         out_shape=[
             pltpu.VMEM((users, length), jnp.float32),
             pltpu.VMEM((blocks, items, width), jnp.float32),
@@ -325,41 +328,40 @@
         compiler_params=pltpu.CompilerParams(vmem_limit_bytes=24 * 1024 * 1024),
         name="first_users",
     )(
-        ids, *[in_hbm(array) for array in (w_in, w_out, rel_bias)], in_vmem(units),
+        *[in_hbm(array) for array in (w_in, w_out, rel_bias)], in_vmem(units),
         *[in_vmem(array) for array in packed],
     )
 
 
-def second_call(ids, places, packed, units, w_in, w_out, loss, sums, bias):
+def second_call(work, groups, packed, units, w_in, w_out, loss, sums, bias):
     blocks, items, width = sums.shape
     length = bias.shape[1]
     arrays = [w_in, w_out, bias, units, loss, sums, *packed]
     return pl.pallas_call(
-        functools.partial(second_kernel, places),
-        in_specs=[scalars] + [whole] * len(arrays),
+        functools.partial(second_kernel, work, groups),
+        in_specs=[whole] * len(arrays),
         out_specs=[whole] * 5,
         scratch_shapes=[pltpu.VMEM(sums.shape, jnp.float32)]
-        + step_scratch(places, length, width, blocks, items),
-        out_shape=[jax.ShapeDtypeStruct(loss.shape, jnp.float32)]
+        + step_scratch(len(work), length, width, blocks, items),
+        out_shape=[pltpu.VMEM(loss.shape, jnp.float32)]
         + [pltpu.VMEM((items, width), jnp.float32)] * 2
         + [pltpu.VMEM((items, width), jnp.bfloat16)] * 2,
         compiler_params=pltpu.CompilerParams(vmem_limit_bytes=24 * 1024 * 1024),
         name="second_users",
-    )(ids, *[in_vmem(array) for array in arrays])
+    )(*[in_vmem(array) for array in arrays])
 
 
 def shards(histories, lengths, targets, send_list, w_in, w_out, rel_bias, item_pool):
     user_count = histories.shape[0]
     groups, blocks = lax.axis_size("dp"), lax.axis_size("blk")
     slots = user_count // groups
-    group, mine = lax.axis_index("dp").astype(jnp.int32), lax.axis_index("blk").astype(jnp.int32)
 
     near = sorted({0, 1, groups - 1, 2 % groups}, key=lambda shift: (shift != 0, shift == 2))
     others = [shift for shift in range(groups) if shift not in near]
     order = near + sorted(others, key=lambda shift: abs(shift - groups / 2))
     work = [(shift, slot) for shift in order for slot in range(slots)]
     *packed, units = pack(
-        histories, lengths, targets, send_list, item_pool, work, groups, group.reshape(1), blocks
+        histories, lengths, targets, send_list, item_pool, work, groups, blocks
     )
     half = user_count // 2
     packed = [
@@ -371,14 +373,11 @@
     item_norm = jnp.sqrt(jnp.sum(pool_float * pool_float, axis=-1, keepdims=True) + 1e-06)
     unit_rows = pool_float / item_norm
 
-    came = [((group - shift) % groups) * slots + slot for shift, slot in work]
-    ids = jnp.stack([mine, mine ^ 2, mine ^ 1, mine ^ 3, *came])
-    order = tuple(range(user_count))
     loss, sums, bias = first_call(
-        ids, order[:half], user_count, packed[:half], units, w_in, w_out, rel_bias
+        work[:half], groups, user_count, packed[:half], units, w_in, w_out, rel_bias
     )
     row_loss, own, over, side, far = second_call(
-        ids, order[half:], packed[half:], units, w_in, w_out, loss, sums, bias
+        work[half:], groups, packed[half:], units, w_in, w_out, loss, sums, bias
     )
     over = over + swap(far, "blk", 1).astype(jnp.float32)
     own = own + swap(side, "blk", 1).astype(jnp.float32)

time: 52.2 us -> 50.7 us (0.971)
  starting transfers between devices: 12.6 us -> 17.7 us
  Pallas kernels: 16.2 us -> 11.3 us
  waiting for transfers between devices: 21.3 us -> 19.1 us
    ppermute x3, starting transfers between devices: 0.58 us -> 5.66 us  [swap(): return lax.ppermute(array, axis, [(i, i ^ bit) for i in range(devices)])]
    pallas_call x3, Pallas kernels: 16.2 us -> 11.3 us  [the longest x1 5.32 us: first_call(): pl.pallas_call(functools.partial(first_kernel, work, groups), in_specs=[f...]
    ppermute x3, waiting for transfers between devices: 9.2 us -> 6.89 us  [swap(): return lax.ppermute(array, axis, [(i, i ^ bit) for i in range(devices)])]
    unnamed x6 -> x7, local copies, waits for them, and re-layouts: 0.01 us -> 0.61 us
  transfers between devices with their start and end apart: 11 -> 11, of which waited for: 6 -> 5; matrix products, arithmetic and copies ran while one was open for 1% -> 2% of each run, Pallas kernels for 17% -> 10%
where the time goes in v16:
time: 50.7 us; the launch traced here: 50.9 us
  waiting for transfers between devices  19.1 us (38%)
  starting transfers between devices  17.7 us (35%)
  Pallas kernels  11.3 us (22%)
  other arithmetic  1.5 us (3%)
  between operations  0.75 us (1%)
  local copies, waits for them, and re-layouts  0.61 us (1%)
    ppermute x7, waiting for transfers between devices, from_behind(): lax.ppermute(array, axis, [(i, (i + by) % devices) for i in range(devices)])  12.2 us
    ppermute x7, starting transfers between devices, from_behind(): lax.ppermute(array, axis, [(i, (i + by) % devices) for i in range(devices)])  8.52 us
    ppermute x3, waiting for transfers between devices, swap(): return lax.ppermute(array, axis, [(i, i ^ bit) for i in range(devices)])  6.89 us
    ppermute x3, starting transfers between devices, swap(): return lax.ppermute(array, axis, [(i, i ^ bit) for i in range(devices)])  5.66 us
    pallas_call x1, Pallas kernels, first_call(): pl.pallas_call(functools.partial(first_kernel, work, groups), in_specs=[f...  5.32 us
    all_to_all x1, starting transfers between devices, shards(): lax.all_to_all(units, 'blk', split_axis=0, concat_axis=0, tiled=True)  3.53 us
    pallas_call x1, Pallas kernels, second_call(): pl.pallas_call(functools.partial(second_kernel, work, groups), in_specs=[...  3.52 us
    pallas_call x1, Pallas kernels, pack(): pl.pallas_call(functools.partial(pack_kernel, work, groups), in_specs=[hb...  2.44 us
  transfers between devices with their start and end apart: 11, of which 5 were waited for; matrix products, arithmetic and copies ran while one was open for 2% of the time, Pallas kernels for 10%

profile of v16, /device:TPU:18, one launch (start us, length us, event | category | flops | bytes accessed | tf_op | source)
XLA Modules:
  0.0 50.9 jit_solution(374209101582795829)
XLA Ops:
  0.6 2.4 %pack.1 = (bf16[520,128]{1,0:T(8,128)(2,1)S(1)}, bf16[520,128]{1,0:T(8,128)(2,1)S(1)}, bf16[520,128]{1,0:T(8,128)(2,1)S(1)}, bf16[520,128]{1,0:T(8,128)(2,1)S(1)...) custom-call(s32[8]{0:T(128)} %list_any.1, ...), custom_call_target="tpu_custom_call" | custom-call | tf_op jit(solution)/shard_map/pack/pallas_call | solution.py:98
  3.1 3.5 %all-to-all-start = ((bf16[4,256,512]{2,1,0:T(8,128)(2,1)}), bf16[4,256,512]{2,1,0:T(8,128)(2,1)S(1)}, u32[]{:S(2)}, u32[]{:S(2)}) async-start(bf16[4,256,512]{2,1,0:T(8,128)(2,1)} %get-tuple-element.19), calls=%async_computation | async-start | bytes 2097152 | tf_op jit(solution)/shard_map/all_to_all | solution.py:370
  6.6 1.6 %collective-permute-start = (bf16[520,128]{1,0:T(8,128)(2,1)S(1)}, bf16[520,128]{1,0:T(8,128)(2,1)S(1)}, u32[]{:S(2)}, u32[]{:S(2)}) collective-permute-start(bf16[520,128]{1,0:T(8,128)(2,1)S(1)} %get-tuple-element.21), channel_id=1, source_target_pairs={{0,4},{4,8},{8,12},{12,16},{16,20},{20,24},{24,28},{28,0},{1,5},{5... | collective-permute-start | bytes 399368 | tf_op jit(solution)/shard_map/ppermute | solution.py:25
  8.2 0.5 collective-permute-start.1
  8.7 1.6 %collective-permute-start.2 = (bf16[520,128]{1,0:T(8,128)(2,1)S(1)}, bf16[520,128]{1,0:T(8,128)(2,1)S(1)}, u32[]{:S(2)}, u32[]{:S(2)}) collective-permute-start(bf16[520,128]{1,0:T(8,128)(2,1)S(1)} %get-tuple-element.23), channel_id=1, source_target_pairs={{0,8},{4,12},{8,16},{12,20},{16,24},{20,28},{24,0},{28,4},{1,9},{5... | collective-permute-start | bytes 399368 | tf_op jit(solution)/shard_map/ppermute | solution.py:25
  10.3 0.3 collective-permute-start.3
  10.6 3.5 %collective-permute-start.4 = (bf16[520,128]{1,0:T(8,128)(2,1)S(1)}, bf16[520,128]{1,0:T(8,128)(2,1)S(1)}, u32[]{:S(2)}, u32[]{:S(2)}) collective-permute-start(bf16[520,128]{1,0:T(8,128)(2,1)S(1)} %get-tuple-element.28), channel_id=1, source_target_pairs={{0,12},{4,16},{8,20},{12,24},{16,28},{20,0},{24,4},{28,8},{1,13},{... | collective-permute-start | bytes 399368 | tf_op jit(solution)/shard_map/ppermute | solution.py:25
  14.1 1.2 %collective-permute-done.refs_1_ = bf16[520,128]{1,0:T(8,128)(2,1)S(1)} collective-permute-done((bf16[520,128]{1,0:T(8,128)(2,1)S(1)}, bf16[520,128]{1,0:T(8,128)(2,1)S(1)}, u32[]{:S(2)}, u32[]{:S(2)}) %collective-permute-start) | collective-permute-done | bytes 133152 | tf_op jit(solution)/shard_map/ppermute | solution.py:25
  15.2 0.0 collective-permute-start.5
  15.2 0.3 collective-permute-done.1.refs_2_
  15.5 1.1 %collective-permute-start.6 = (bf16[520,128]{1,0:T(8,128)(2,1)S(1)}, bf16[520,128]{1,0:T(8,128)(2,1)S(1)}, u32[]{:S(2)}, u32[]{:S(2)}) collective-permute-start(bf16[520,128]{1,0:T(8,128)(2,1)S(1)} %get-tuple-element.30), channel_id=1, source_target_pairs={{0,24},{4,28},{8,0},{12,4},{16,8},{20,12},{24,16},{28,20},{1,25},{... | collective-permute-start | bytes 399368 | tf_op jit(solution)/shard_map/ppermute | solution.py:25
  16.6 10.7 %collective-permute-done.2.refs_3_ = bf16[520,128]{1,0:T(8,128)(2,1)S(1)} collective-permute-done((bf16[520,128]{1,0:T(8,128)(2,1)S(1)}, bf16[520,128]{1,0:T(8,128)(2,1)S(1)}, u32[]{:S(2)}, u32[]{:S(2)}) %collective-permute-start.2) | collective-permute-done | bytes 133152 | tf_op jit(solution)/shard_map/ppermute | solution.py:25
  27.3 0.0 all-to-all-done.unit_ref
  27.3 0.0 copy-start
  27.3 0.0 copy-start.1
  27.3 5.3 %first_users.1 = (f32[8,128]{1,0:T(8,128)S(1)}, f32[4,256,512]{2,1,0:T(8,128)S(1)}, f32[4,128,256]{2,1,0:T(8,128)S(1)}) custom-call(bf16[512,2048]{1,0:T(8,128)(2,1)} %w_in.1, bf16[512,512]{1,0:T(8,128)(2,1)} %w_out.1, f32[4,128]{1,0:T(4,128)} %rel_any.1, bf16[4,256,512]{2,1,0:T(8,128)(2,1)S(1)} %all-to-all-done.unit_ref, ...), custom_call_target="tpu_custom_call" | custom-call | tf_op jit(solution)/shard_map/first_users/pallas_call | solution.py:312
  32.6 0.0 collective-permute-done.3.refs_0_
  32.6 0.0 collective-permute-done.4.refs_1_
  32.6 0.0 collective-permute-done.5.refs_2_
  32.7 0.0 collective-permute-done.6.refs_3_
  32.7 0.0 copy-done
  32.7 0.0 copy-done.1
  32.7 0.0 copy-start.2
  32.7 3.5 %second_users.1 = (f32[8,128]{1,0:T(8,128)S(1)}, f32[256,512]{1,0:T(8,128)S(1)}, f32[256,512]{1,0:T(8,128)S(1)}, bf16[256,512]{1,0:T(8,128)(2,1)S(1)}, bf16[256,512]{1,0:T(8,128)(2,1)S(1)}) custom-call(bf16[512,2048]{1,0:T(8,128)(2,1)S(1)} %copy-done, bf16[512,512]{1,0:T(8,128)(2,1)S(1)} %copy-done.1, f32[4,128,256]{2,1,0:T(8,128)S(1)} %get-tuple-element.24.bias, ...), custom_call_target="tpu_custom_call" | custom-call | tf_op jit(solution)/shard_map/second_users/pallas_call | solution.py:340
  36.2 0.1 collective-permute-start.8
  36.3 0.5 collective-permute-start.7
  36.8 1.0 %collective-permute-done.8 = bf16[256,512]{1,0:T(8,128)(2,1)S(1)} collective-permute-done((bf16[256,512]{1,0:T(8,128)(2,1)S(1)}, bf16[256,512]{1,0:T(8,128)(2,1)S(1)}, u32[]{:S(2)}, u32[]{:S(2)}) %collective-permute-start.8) | collective-permute-done | bytes 262176 | tf_op jit(solution)/shard_map/ppermute | solution.py:20
  37.8 0.1 add_convert_fusion
  37.9 5.1 %collective-permute-start.9 = (bf16[256,512]{1,0:T(8,128)(2,1)S(1)}, bf16[256,512]{1,0:T(8,128)(2,1)S(1)}, u32[]{:S(2)}, u32[]{:S(2)}) collective-permute-start(bf16[256,512]{1,0:T(8,128)(2,1)S(1)} %add_convert_fusion), channel_id=1, source_target_pairs={{0,2},{1,3},{2,0},{3,1},{4,6},{5,7},{6,4},{7,5},{8,10},{9,11},{10,... | collective-permute-start | bytes 786440 | tf_op jit(solution)/shard_map/ppermute | solution.py:20
  43.0 0.0 copy-done.2
  43.0 0.1 fusion
  43.1 0.6 %copy.10 = f32[8,128]{1,0:T(8,128)} copy(f32[8,128]{1,0:T(8,128)S(1)} %get-tuple-element.36) | data formatting | bytes 8192
  43.7 0.0 collective-permute-done.7
  43.7 5.9 %collective-permute-done.9 = bf16[256,512]{1,0:T(8,128)(2,1)S(1)} collective-permute-done((bf16[256,512]{1,0:T(8,128)(2,1)S(1)}, bf16[256,512]{1,0:T(8,128)(2,1)S(1)}, u32[]{:S(2)}, u32[]{:S(2)}) %collective-permute-start.9) | collective-permute-done | bytes 262176 | tf_op jit(solution)/shard_map/ppermute | solution.py:20
  49.6 0.3 multiply_reduce_fusion
  49.9 1.0 %subtract_divide_fusion = f32[256,512]{1,0:T(8,128)} fusion(bf16[256,512]{1,0:T(8,128)(2,1)S(1)} %copy-done.2, f32[256]{0:T(256)S(1)} %multiply_reduce_fusion, f32[256]{0:T(256)S(1)} %add_sqrt_fusion, bf16[256,512]{1,0:T(8,128)(2,1)S(1)} %collective-permute-done.9, f32[256,512]{1,0:T(8,128)S(1)} %get-tuple-element.32, ...), kind=kLoop, calls=%fused_computation.3 | loop fusion | flops 1310720 | bytes 1837056 | tf_op jit(solution)/shard_map/div | solution.py:385
  (1 shorter events, 0.0 us)
Async XLA Ops:
  3.1 24.2 %all-to-all-start = ((bf16[4,256,512]{2,1,0:T(8,128)(2,1)}), bf16[4,256,512]{2,1,0:T(8,128)(2,1)S(1)}, u32[]{:S(2)}, u32[]{:S(2)}) async-start(bf16[4,256,512]{2,1,0:T(8,128)(2,1)} %get-tuple-element.19), calls=%async_computation | async-start | bytes 2097152 | tf_op jit(solution)/shard_map/all_to_all | solution.py:370
  6.6 8.6 %collective-permute-start = (bf16[520,128]{1,0:T(8,128)(2,1)S(1)}, bf16[520,128]{1,0:T(8,128)(2,1)S(1)}, u32[]{:S(2)}, u32[]{:S(2)}) collective-permute-start(bf16[520,128]{1,0:T(8,128)(2,1)S(1)} %get-tuple-element.21), channel_id=1, source_target_pairs={{0,4},{4,8},{8,12},{12,16},{16,20},{20,24},{24,28},{28,0},{1,5},{5... | collective-permute-start | bytes 399368 | tf_op jit(solution)/shard_map/ppermute | solution.py:25
  8.2 7.3 %collective-permute-start.1 = (bf16[520,128]{1,0:T(8,128)(2,1)S(1)}, bf16[520,128]{1,0:T(8,128)(2,1)S(1)}, u32[]{:S(2)}, u32[]{:S(2)}) collective-permute-start(bf16[520,128]{1,0:T(8,128)(2,1)S(1)} %get-tuple-element.22), channel_id=1, source_target_pairs={{0,28},{4,0},{8,4},{12,8},{16,12},{20,16},{24,20},{28,24},{1,29},{... | collective-permute-start | bytes 399368 | tf_op jit(solution)/shard_map/ppermute | solution.py:25
  8.7 18.6 %collective-permute-start.2 = (bf16[520,128]{1,0:T(8,128)(2,1)S(1)}, bf16[520,128]{1,0:T(8,128)(2,1)S(1)}, u32[]{:S(2)}, u32[]{:S(2)}) collective-permute-start(bf16[520,128]{1,0:T(8,128)(2,1)S(1)} %get-tuple-element.23), channel_id=1, source_target_pairs={{0,8},{4,12},{8,16},{12,20},{16,24},{20,28},{24,0},{28,4},{1,9},{5... | collective-permute-start | bytes 399368 | tf_op jit(solution)/shard_map/ppermute | solution.py:25
  10.3 22.4 %collective-permute-start.3 = (bf16[520,128]{1,0:T(8,128)(2,1)S(1)}, bf16[520,128]{1,0:T(8,128)(2,1)S(1)}, u32[]{:S(2)}, u32[]{:S(2)}) collective-permute-start(bf16[520,128]{1,0:T(8,128)(2,1)S(1)} %get-tuple-element.27), channel_id=1, source_target_pairs={{0,16},{4,20},{8,24},{12,28},{16,0},{20,4},{24,8},{28,12},{1,17},{... | collective-permute-start | bytes 399368 | tf_op jit(solution)/shard_map/ppermute | solution.py:25
  10.6 22.0 %collective-permute-start.4 = (bf16[520,128]{1,0:T(8,128)(2,1)S(1)}, bf16[520,128]{1,0:T(8,128)(2,1)S(1)}, u32[]{:S(2)}, u32[]{:S(2)}) collective-permute-start(bf16[520,128]{1,0:T(8,128)(2,1)S(1)} %get-tuple-element.28), channel_id=1, source_target_pairs={{0,12},{4,16},{8,20},{12,24},{16,28},{20,0},{24,4},{28,8},{1,13},{... | collective-permute-start | bytes 399368 | tf_op jit(solution)/shard_map/ppermute | solution.py:25
  15.2 17.4 %collective-permute-start.5 = (bf16[520,128]{1,0:T(8,128)(2,1)S(1)}, bf16[520,128]{1,0:T(8,128)(2,1)S(1)}, u32[]{:S(2)}, u32[]{:S(2)}) collective-permute-start(bf16[520,128]{1,0:T(8,128)(2,1)S(1)} %get-tuple-element.29), channel_id=1, source_target_pairs={{0,20},{4,24},{8,28},{12,0},{16,4},{20,8},{24,12},{28,16},{1,21},{... | collective-permute-start | bytes 399368 | tf_op jit(solution)/shard_map/ppermute | solution.py:25
  15.5 17.1 %collective-permute-start.6 = (bf16[520,128]{1,0:T(8,128)(2,1)S(1)}, bf16[520,128]{1,0:T(8,128)(2,1)S(1)}, u32[]{:S(2)}, u32[]{:S(2)}) collective-permute-start(bf16[520,128]{1,0:T(8,128)(2,1)S(1)} %get-tuple-element.30), channel_id=1, source_target_pairs={{0,24},{4,28},{8,0},{12,4},{16,8},{20,12},{24,16},{28,20},{1,25},{... | collective-permute-start | bytes 399368 | tf_op jit(solution)/shard_map/ppermute | solution.py:25
  27.3 5.4 %copy-start = (bf16[512,2048]{1,0:T(8,128)(2,1)S(1)}, bf16[512,2048]{1,0:T(8,128)(2,1)}, u32[]{:S(2)}) copy-start(bf16[512,2048]{1,0:T(8,128)(2,1)} %w_in.1) | copy-start | bytes 6291460
  27.3 5.4 %copy-start.1 = (bf16[512,512]{1,0:T(8,128)(2,1)S(1)}, bf16[512,512]{1,0:T(8,128)(2,1)}, u32[]{:S(2)}) copy-start(bf16[512,512]{1,0:T(8,128)(2,1)} %w_out.1) | copy-start | bytes 1572868
  32.7 10.3 %copy-start.2 = (bf16[256,512]{1,0:T(8,128)(2,1)S(1)}, bf16[256,512]{1,0:T(8,128)(2,1)}, u32[]{:S(2)}) copy-start(bf16[256,512]{1,0:T(8,128)(2,1)} %pool_any.1) | copy-start | bytes 786436
  36.2 1.6 %collective-permute-start.8 = (bf16[256,512]{1,0:T(8,128)(2,1)S(1)}, bf16[256,512]{1,0:T(8,128)(2,1)S(1)}, u32[]{:S(2)}, u32[]{:S(2)}) collective-permute-start(bf16[256,512]{1,0:T(8,128)(2,1)S(1)} %get-tuple-element.35), channel_id=1, source_target_pairs={{0,1},{1,0},{2,3},{3,2},{4,5},{5,4},{6,7},{7,6},{8,9},{9,8},{10,11... | collective-permute-start | bytes 786440 | tf_op jit(solution)/shard_map/ppermute | solution.py:20
  36.3 7.4 %collective-permute-start.7 = (bf16[256,512]{1,0:T(8,128)(2,1)S(1)}, bf16[256,512]{1,0:T(8,128)(2,1)S(1)}, u32[]{:S(2)}, u32[]{:S(2)}) collective-permute-start(bf16[256,512]{1,0:T(8,128)(2,1)S(1)} %get-tuple-element.33), channel_id=1, source_target_pairs={{0,1},{1,0},{2,3},{3,2},{4,5},{5,4},{6,7},{7,6},{8,9},{9,8},{10,11... | collective-permute-start | bytes 786440 | tf_op jit(solution)/shard_map/ppermute | solution.py:20
  37.9 11.7 %collective-permute-start.9 = (bf16[256,512]{1,0:T(8,128)(2,1)S(1)}, bf16[256,512]{1,0:T(8,128)(2,1)S(1)}, u32[]{:S(2)}, u32[]{:S(2)}) collective-permute-start(bf16[256,512]{1,0:T(8,128)(2,1)S(1)} %add_convert_fusion), channel_id=1, source_target_pairs={{0,2},{1,3},{2,0},{3,1},{4,6},{5,7},{6,4},{7,5},{8,10},{9,11},{10,... | collective-permute-start | bytes 786440 | tf_op jit(solution)/shard_map/ppermute | solution.py:20

commit v17 on v16

--- a/solution.py
+++ b/solution.py
@@ -47,8 +47,7 @@
 ):
     users, length, width = from_any.shape
     to_refs, unit_any = refs[:users], refs[users]
-    entries, lens, targets, pool, unit, sems, in_sems = refs[users + 1 :]
-    pieces = width // length
+    entries, lens, targets, pool, unit, events, sems, in_sems = refs[users + 1 :]
     small = [
         pltpu.make_async_copy(source, target, sems.at[k])
         for k, (source, target) in enumerate(
@@ -57,18 +56,8 @@
     ]
     for copy in small:
         copy.start()
-    small[0].wait()
-    slots = users // groups
-    group = lax.axis_index("dp")
-    order = [entries[lax.rem(group + shift, groups) * slots + slot] for shift, slot in work]
     copies_in = [
-        pltpu.make_async_copy(
-            from_any.at[order[k], :, pl.ds(c * length, length)],
-            to_refs[k].at[pl.ds(c * length, length)],
-            in_sems.at[k, c],
-        )
-        for k in range(users)
-        for c in range(pieces)
+        pltpu.make_async_copy(from_any.at[u], events.at[u], in_sems.at[u]) for u in range(users)
     ]
     for copy in copies_in:
         copy.start()
@@ -80,14 +69,22 @@
     ]
     for copy in units_out:
         copy.start()
-    small[1].wait()
-    small[2].wait()
+    for copy in small[:3]:
+        copy.wait()
+    slots = users // groups
+    group = lax.axis_index("dp")
+    order = [entries[lax.rem(group + shift, groups) * slots + slot] for shift, slot in work]
     row = lax.broadcasted_iota(jnp.int32, (number_rows, length), 0)
     for k in range(users):
         target = targets[pl.ds(order[k], 1), :]
         numbers = jnp.where(row == 0, lens[order[k]], jnp.where(row == 1, target // 256, target % 256))
         to_refs[k][width:, :] = numbers.astype(jnp.float32).astype(jnp.bfloat16)
-    for copy in copies_in + units_out:
+    for copy in copies_in:
+        copy.wait()
+    for k in range(users):
+        for c in range(0, width, length):
+            to_refs[k][c : c + length, :] = events[order[k], :, c : c + length]
+    for copy in units_out:
         copy.wait()
 
 
@@ -105,8 +102,9 @@
             pltpu.VMEM(targets.shape, jnp.int32),
             pltpu.VMEM(item_pool.shape, jnp.bfloat16),
             pltpu.VMEM(item_pool.shape, jnp.bfloat16),
+            pltpu.VMEM(histories.shape, jnp.bfloat16),
             pltpu.SemaphoreType.DMA((4 + blocks,)),
-            pltpu.SemaphoreType.DMA((users, width // length)),
+            pltpu.SemaphoreType.DMA((users,)),
         ],
         out_shape=[pltpu.VMEM(shape, jnp.bfloat16)] * users
         + [pltpu.HBM((blocks,) + item_pool.shape, jnp.bfloat16)],

time: 50.7 us -> 50.2 us (level)
  the two profiles are of different devices: /device:TPU:18 before, /device:TPU:30 now
where the time goes in v17:
time: 50.2 us; the launch traced here: 50 us
  waiting for transfers between devices  22.7 us (45%)
  starting transfers between devices  13 us (26%)
  Pallas kernels  11.4 us (23%)
  other arithmetic  1.5 us (3%)
  between operations  0.7 us (1%)
  local copies, waits for them, and re-layouts  0.61 us (1%)
    ppermute x7, waiting for transfers between devices, from_behind(): lax.ppermute(array, axis, [(i, (i + by) % devices) for i in range(devices)])  11.1 us
    ppermute x3, waiting for transfers between devices, swap(): return lax.ppermute(array, axis, [(i, i ^ bit) for i in range(devices)])  8.21 us
    ppermute x7, starting transfers between devices, from_behind(): lax.ppermute(array, axis, [(i, (i + by) % devices) for i in range(devices)])  7.95 us
    pallas_call x1, Pallas kernels, first_call(): pl.pallas_call(functools.partial(first_kernel, work, groups), in_specs=[f...  5.32 us
    all_to_all x1, starting transfers between devices, shards(): lax.all_to_all(units, 'blk', split_axis=0, concat_axis=0, tiled=True)  4 us
    pallas_call x1, Pallas kernels, second_call(): pl.pallas_call(functools.partial(second_kernel, work, groups), in_specs=[...  3.51 us
    all_to_all x1, waiting for transfers between devices, shards(): lax.all_to_all(units, 'blk', split_axis=0, concat_axis=0, tiled=True)  3.44 us
    pallas_call x1, Pallas kernels, pack(): pl.pallas_call(functools.partial(pack_kernel, work, groups), in_specs=[hb...  2.6 us
  transfers between devices with their start and end apart: 11, of which 6 were waited for; matrix products, arithmetic and copies ran while one was open for 2% of the time, Pallas kernels for 11%

profile of v17, /device:TPU:30, one launch (start us, length us, event | category | flops | bytes accessed | tf_op | source)
XLA Modules:
  0.0 50.0 jit_solution(7112055687096120361)
XLA Ops:
  0.6 2.6 %pack.1 = (bf16[520,128]{1,0:T(8,128)(2,1)S(1)}, bf16[520,128]{1,0:T(8,128)(2,1)S(1)}, bf16[520,128]{1,0:T(8,128)(2,1)S(1)}, bf16[520,128]{1,0:T(8,128)(2,1)S(1)...) custom-call(s32[8]{0:T(128)} %list_any.1, ...), custom_call_target="tpu_custom_call" | custom-call | tf_op jit(solution)/shard_map/pack/pallas_call | solution.py:95
  3.2 4.0 %all-to-all-start = ((bf16[4,256,512]{2,1,0:T(8,128)(2,1)}), bf16[4,256,512]{2,1,0:T(8,128)(2,1)S(1)}, u32[]{:S(2)}, u32[]{:S(2)}) async-start(bf16[4,256,512]{2,1,0:T(8,128)(2,1)} %get-tuple-element.19), calls=%async_computation | async-start | bytes 2097152 | tf_op jit(solution)/shard_map/all_to_all | solution.py:368
  7.2 0.0 collective-permute-start
  7.2 2.0 %collective-permute-start.1 = (bf16[520,128]{1,0:T(8,128)(2,1)S(1)}, bf16[520,128]{1,0:T(8,128)(2,1)S(1)}, u32[]{:S(2)}, u32[]{:S(2)}) collective-permute-start(bf16[520,128]{1,0:T(8,128)(2,1)S(1)} %get-tuple-element.22), channel_id=1, source_target_pairs={{0,28},{4,0},{8,4},{12,8},{16,12},{20,16},{24,20},{28,24},{1,29},{... | collective-permute-start | bytes 399368 | tf_op jit(solution)/shard_map/ppermute | solution.py:25
  9.3 0.2 collective-permute-start.2
  9.5 1.7 %collective-permute-start.3 = (bf16[520,128]{1,0:T(8,128)(2,1)S(1)}, bf16[520,128]{1,0:T(8,128)(2,1)S(1)}, u32[]{:S(2)}, u32[]{:S(2)}) collective-permute-start(bf16[520,128]{1,0:T(8,128)(2,1)S(1)} %get-tuple-element.27), channel_id=1, source_target_pairs={{0,16},{4,20},{8,24},{12,28},{16,0},{20,4},{24,8},{28,12},{1,17},{... | collective-permute-start | bytes 399368 | tf_op jit(solution)/shard_map/ppermute | solution.py:25
  11.2 3.7 %collective-permute-start.4 = (bf16[520,128]{1,0:T(8,128)(2,1)S(1)}, bf16[520,128]{1,0:T(8,128)(2,1)S(1)}, u32[]{:S(2)}, u32[]{:S(2)}) collective-permute-start(bf16[520,128]{1,0:T(8,128)(2,1)S(1)} %get-tuple-element.28), channel_id=1, source_target_pairs={{0,12},{4,16},{8,20},{12,24},{16,28},{20,0},{24,4},{28,8},{1,13},{... | collective-permute-start | bytes 399368 | tf_op jit(solution)/shard_map/ppermute | solution.py:25
  14.9 0.0 collective-permute-done.refs_1_
  14.9 0.1 collective-permute-start.5
  15.0 1.4 %collective-permute-done.1.refs_2_ = bf16[520,128]{1,0:T(8,128)(2,1)S(1)} collective-permute-done((bf16[520,128]{1,0:T(8,128)(2,1)S(1)}, bf16[520,128]{1,0:T(8,128)(2,1)S(1)}, u32[]{:S(2)}, u32[]{:S(2)}) %collective-permute-start.1) | collective-permute-done | bytes 133152 | tf_op jit(solution)/shard_map/ppermute | solution.py:25
  16.4 0.2 collective-permute-start.6
  16.6 0.0 collective-permute-done.2.refs_3_
  16.6 3.4 %all-to-all-done.unit_ref = bf16[4,256,512]{2,1,0:T(8,128)(2,1)S(1)} async-done(((bf16[4,256,512]{2,1,0:T(8,128)(2,1)}), bf16[4,256,512]{2,1,0:T(8,128)(2,1)S(1)}, u32[]{:S(2)}, u32[]{:S(2)}) %all-to-all-start) | async-done | bytes 1048608 | tf_op jit(solution)/shard_map/all_to_all | solution.py:368
  20.0 0.0 copy-start
  20.0 0.0 copy-start.1
  20.0 5.3 %first_users.1 = (f32[8,128]{1,0:T(8,128)S(1)}, f32[4,256,512]{2,1,0:T(8,128)S(1)}, f32[4,128,256]{2,1,0:T(8,128)S(1)}) custom-call(bf16[512,2048]{1,0:T(8,128)(2,1)} %w_in.1, bf16[512,512]{1,0:T(8,128)(2,1)} %w_out.1, f32[4,128]{1,0:T(4,128)} %rel_any.1, bf16[4,256,512]{2,1,0:T(8,128)(2,1)S(1)} %all-to-all-done.unit_ref, ...), custom_call_target="tpu_custom_call" | custom-call | tf_op jit(solution)/shard_map/first_users/pallas_call | solution.py:310
  25.4 5.3 %collective-permute-done.3.refs_0_ = bf16[520,128]{1,0:T(8,128)(2,1)S(1)} collective-permute-done((bf16[520,128]{1,0:T(8,128)(2,1)S(1)}, bf16[520,128]{1,0:T(8,128)(2,1)S(1)}, u32[]{:S(2)}, u32[]{:S(2)}) %collective-permute-start.3) | collective-permute-done | bytes 133152 | tf_op jit(solution)/shard_map/ppermute | solution.py:25
  30.6 0.0 collective-permute-done.4.refs_1_
  30.6 4.4 %collective-permute-done.5.refs_2_ = bf16[520,128]{1,0:T(8,128)(2,1)S(1)} collective-permute-done((bf16[520,128]{1,0:T(8,128)(2,1)S(1)}, bf16[520,128]{1,0:T(8,128)(2,1)S(1)}, u32[]{:S(2)}, u32[]{:S(2)}) %collective-permute-start.5) | collective-permute-done | bytes 133152 | tf_op jit(solution)/shard_map/ppermute | solution.py:25
  35.0 0.0 collective-permute-done.6.refs_3_
  35.0 0.0 copy-done
  35.0 0.0 copy-done.1
  35.0 0.0 copy-start.2
  35.0 3.5 %second_users.1 = (f32[8,128]{1,0:T(8,128)S(1)}, f32[256,512]{1,0:T(8,128)S(1)}, f32[256,512]{1,0:T(8,128)S(1)}, bf16[256,512]{1,0:T(8,128)(2,1)S(1)}, bf16[256,512]{1,0:T(8,128)(2,1)S(1)}) custom-call(bf16[512,2048]{1,0:T(8,128)(2,1)S(1)} %copy-done, bf16[512,512]{1,0:T(8,128)(2,1)S(1)} %copy-done.1, f32[4,128,256]{2,1,0:T(8,128)S(1)} %get-tuple-element.24.bias, ...), custom_call_target="tpu_custom_call" | custom-call | tf_op jit(solution)/shard_map/second_users/pallas_call | solution.py:338
  38.6 0.1 collective-permute-start.8
  38.6 0.5 collective-permute-start.7
  39.1 1.0 %collective-permute-done.8 = bf16[256,512]{1,0:T(8,128)(2,1)S(1)} collective-permute-done((bf16[256,512]{1,0:T(8,128)(2,1)S(1)}, bf16[256,512]{1,0:T(8,128)(2,1)S(1)}, u32[]{:S(2)}, u32[]{:S(2)}) %collective-permute-start.8) | collective-permute-done | bytes 262176 | tf_op jit(solution)/shard_map/ppermute | solution.py:20
  40.2 0.1 add_convert_fusion
  40.3 0.5 collective-permute-start.9
  40.7 0.0 copy-done.2
  40.7 0.1 fusion
  40.9 0.6 %copy.10 = f32[8,128]{1,0:T(8,128)} copy(f32[8,128]{1,0:T(8,128)S(1)} %get-tuple-element.36) | data formatting | bytes 8192
  41.5 0.0 collective-permute-done.7
  41.5 7.2 %collective-permute-done.9 = bf16[256,512]{1,0:T(8,128)(2,1)S(1)} collective-permute-done((bf16[256,512]{1,0:T(8,128)(2,1)S(1)}, bf16[256,512]{1,0:T(8,128)(2,1)S(1)}, u32[]{:S(2)}, u32[]{:S(2)}) %collective-permute-start.9) | collective-permute-done | bytes 262176 | tf_op jit(solution)/shard_map/ppermute | solution.py:20
  48.7 0.3 multiply_reduce_fusion
  48.9 1.0 %subtract_divide_fusion = f32[256,512]{1,0:T(8,128)} fusion(bf16[256,512]{1,0:T(8,128)(2,1)S(1)} %copy-done.2, f32[256]{0:T(256)S(1)} %multiply_reduce_fusion, f32[256]{0:T(256)S(1)} %add_sqrt_fusion, bf16[256,512]{1,0:T(8,128)(2,1)S(1)} %collective-permute-done.9, f32[256,512]{1,0:T(8,128)S(1)} %get-tuple-element.32, ...), kind=kLoop, calls=%fused_computation.3 | loop fusion | flops 1310720 | bytes 1837056 | tf_op jit(solution)/shard_map/div | solution.py:383
  (1 shorter events, 0.0 us)
Async XLA Ops:
  3.2 16.8 %all-to-all-start = ((bf16[4,256,512]{2,1,0:T(8,128)(2,1)}), bf16[4,256,512]{2,1,0:T(8,128)(2,1)S(1)}, u32[]{:S(2)}, u32[]{:S(2)}) async-start(bf16[4,256,512]{2,1,0:T(8,128)(2,1)} %get-tuple-element.19), calls=%async_computation | async-start | bytes 2097152 | tf_op jit(solution)/shard_map/all_to_all | solution.py:368
  7.2 7.7 %collective-permute-start = (bf16[520,128]{1,0:T(8,128)(2,1)S(1)}, bf16[520,128]{1,0:T(8,128)(2,1)S(1)}, u32[]{:S(2)}, u32[]{:S(2)}) collective-permute-start(bf16[520,128]{1,0:T(8,128)(2,1)S(1)} %get-tuple-element.21), channel_id=1, source_target_pairs={{0,4},{4,8},{8,12},{12,16},{16,20},{20,24},{24,28},{28,0},{1,5},{5... | collective-permute-start | bytes 399368 | tf_op jit(solution)/shard_map/ppermute | solution.py:25
  7.2 9.1 %collective-permute-start.1 = (bf16[520,128]{1,0:T(8,128)(2,1)S(1)}, bf16[520,128]{1,0:T(8,128)(2,1)S(1)}, u32[]{:S(2)}, u32[]{:S(2)}) collective-permute-start(bf16[520,128]{1,0:T(8,128)(2,1)S(1)} %get-tuple-element.22), channel_id=1, source_target_pairs={{0,28},{4,0},{8,4},{12,8},{16,12},{20,16},{24,20},{28,24},{1,29},{... | collective-permute-start | bytes 399368 | tf_op jit(solution)/shard_map/ppermute | solution.py:25
  9.3 7.3 %collective-permute-start.2 = (bf16[520,128]{1,0:T(8,128)(2,1)S(1)}, bf16[520,128]{1,0:T(8,128)(2,1)S(1)}, u32[]{:S(2)}, u32[]{:S(2)}) collective-permute-start(bf16[520,128]{1,0:T(8,128)(2,1)S(1)} %get-tuple-element.23), channel_id=1, source_target_pairs={{0,8},{4,12},{8,16},{12,20},{16,24},{20,28},{24,0},{28,4},{1,9},{5... | collective-permute-start | bytes 399368 | tf_op jit(solution)/shard_map/ppermute | solution.py:25
  9.5 21.1 %collective-permute-start.3 = (bf16[520,128]{1,0:T(8,128)(2,1)S(1)}, bf16[520,128]{1,0:T(8,128)(2,1)S(1)}, u32[]{:S(2)}, u32[]{:S(2)}) collective-permute-start(bf16[520,128]{1,0:T(8,128)(2,1)S(1)} %get-tuple-element.27), channel_id=1, source_target_pairs={{0,16},{4,20},{8,24},{12,28},{16,0},{20,4},{24,8},{28,12},{1,17},{... | collective-permute-start | bytes 399368 | tf_op jit(solution)/shard_map/ppermute | solution.py:25
  11.2 19.4 %collective-permute-start.4 = (bf16[520,128]{1,0:T(8,128)(2,1)S(1)}, bf16[520,128]{1,0:T(8,128)(2,1)S(1)}, u32[]{:S(2)}, u32[]{:S(2)}) collective-permute-start(bf16[520,128]{1,0:T(8,128)(2,1)S(1)} %get-tuple-element.28), channel_id=1, source_target_pairs={{0,12},{4,16},{8,20},{12,24},{16,28},{20,0},{24,4},{28,8},{1,13},{... | collective-permute-start | bytes 399368 | tf_op jit(solution)/shard_map/ppermute | solution.py:25
  14.9 20.1 %collective-permute-start.5 = (bf16[520,128]{1,0:T(8,128)(2,1)S(1)}, bf16[520,128]{1,0:T(8,128)(2,1)S(1)}, u32[]{:S(2)}, u32[]{:S(2)}) collective-permute-start(bf16[520,128]{1,0:T(8,128)(2,1)S(1)} %get-tuple-element.29), channel_id=1, source_target_pairs={{0,20},{4,24},{8,28},{12,0},{16,4},{20,8},{24,12},{28,16},{1,21},{... | collective-permute-start | bytes 399368 | tf_op jit(solution)/shard_map/ppermute | solution.py:25
  16.4 18.7 %collective-permute-start.6 = (bf16[520,128]{1,0:T(8,128)(2,1)S(1)}, bf16[520,128]{1,0:T(8,128)(2,1)S(1)}, u32[]{:S(2)}, u32[]{:S(2)}) collective-permute-start(bf16[520,128]{1,0:T(8,128)(2,1)S(1)} %get-tuple-element.30), channel_id=1, source_target_pairs={{0,24},{4,28},{8,0},{12,4},{16,8},{20,12},{24,16},{28,20},{1,25},{... | collective-permute-start | bytes 399368 | tf_op jit(solution)/shard_map/ppermute | solution.py:25
  20.0 15.0 %copy-start = (bf16[512,2048]{1,0:T(8,128)(2,1)S(1)}, bf16[512,2048]{1,0:T(8,128)(2,1)}, u32[]{:S(2)}) copy-start(bf16[512,2048]{1,0:T(8,128)(2,1)} %w_in.1) | copy-start | bytes 6291460
  20.0 15.0 %copy-start.1 = (bf16[512,512]{1,0:T(8,128)(2,1)S(1)}, bf16[512,512]{1,0:T(8,128)(2,1)}, u32[]{:S(2)}) copy-start(bf16[512,512]{1,0:T(8,128)(2,1)} %w_out.1) | copy-start | bytes 1572868
  35.0 5.7 %copy-start.2 = (bf16[256,512]{1,0:T(8,128)(2,1)S(1)}, bf16[256,512]{1,0:T(8,128)(2,1)}, u32[]{:S(2)}) copy-start(bf16[256,512]{1,0:T(8,128)(2,1)} %pool_any.1) | copy-start | bytes 786436
  38.6 1.6 %collective-permute-start.8 = (bf16[256,512]{1,0:T(8,128)(2,1)S(1)}, bf16[256,512]{1,0:T(8,128)(2,1)S(1)}, u32[]{:S(2)}, u32[]{:S(2)}) collective-permute-start(bf16[256,512]{1,0:T(8,128)(2,1)S(1)} %get-tuple-element.35), channel_id=1, source_target_pairs={{0,1},{1,0},{2,3},{3,2},{4,5},{5,4},{6,7},{7,6},{8,9},{9,8},{10,11... | collective-permute-start | bytes 786440 | tf_op jit(solution)/shard_map/ppermute | solution.py:20
  38.6 2.8 %collective-permute-start.7 = (bf16[256,512]{1,0:T(8,128)(2,1)S(1)}, bf16[256,512]{1,0:T(8,128)(2,1)S(1)}, u32[]{:S(2)}, u32[]{:S(2)}) collective-permute-start(bf16[256,512]{1,0:T(8,128)(2,1)S(1)} %get-tuple-element.33), channel_id=1, source_target_pairs={{0,1},{1,0},{2,3},{3,2},{4,5},{5,4},{6,7},{7,6},{8,9},{9,8},{10,11... | collective-permute-start | bytes 786440 | tf_op jit(solution)/shard_map/ppermute | solution.py:20
  40.3 8.4 %collective-permute-start.9 = (bf16[256,512]{1,0:T(8,128)(2,1)S(1)}, bf16[256,512]{1,0:T(8,128)(2,1)S(1)}, u32[]{:S(2)}, u32[]{:S(2)}) collective-permute-start(bf16[256,512]{1,0:T(8,128)(2,1)S(1)} %add_convert_fusion), channel_id=1, source_target_pairs={{0,2},{1,3},{2,0},{3,1},{4,6},{5,7},{6,4},{7,5},{8,10},{9,11},{10,... | collective-permute-start | bytes 786440 | tf_op jit(solution)/shard_map/ppermute | solution.py:20

commit v18 on v16

--- a/solution.py
+++ b/solution.py
@@ -10,7 +10,7 @@
 
 logit_scale = 20.0
 contract_last = (((1,), (1,)), ((), ()))
-tile = 256
+first_tile, second_tile = 384, 256
 chunk = 16
 number_rows = 8
 
@@ -55,7 +55,7 @@
             ((list_any, entries), (len_any, lens), (tgt_any, targets), (pool_any, pool))
         )
     ]
-    for copy in small:
+    for copy in reversed(small):
         copy.start()
     small[0].wait()
     slots = users // groups
@@ -115,13 +115,13 @@
     )(*[in_hbm(array) for array in (entries, lengths, histories, targets, item_pool)])
 
 
-def users_kernel(work, groups, x_refs, w_in, w_out, unit_ref, sums, loss_ref, bias, scratch):
+def users_kernel(tile, work, groups, x_refs, w_in, w_out, unit_ref, sums, loss_ref, bias, scratch):
     slots = loss_ref.shape[0] // groups
     group = lax.axis_index("dp")
     spots = [lax.rem(group + groups - shift, groups) * slots + slot for shift, slot in work]
     for at in range(0, len(work), 8):
         users_step(
-            x_refs[at : at + 8], spots[at : at + 8],
+            tile, x_refs[at : at + 8], spots[at : at + 8],
             w_in, w_out, unit_ref, sums, loss_ref, bias, *scratch,
         )
 
@@ -145,7 +145,7 @@
         bias[h] = jnp.concatenate([turned, turned], axis=1)
     for copy in copies[1:]:
         copy.wait()
-    users_kernel(work, groups, x_refs, w_in, w_out, unit_ref, sums, loss_ref, bias, refs[4:])
+    users_kernel(first_tile, work, groups, x_refs, w_in, w_out, unit_ref, sums, loss_ref, bias, refs[4:])
 
 
 def second_kernel(work, groups, w_in, w_out, bias, unit_ref, loss_in, sums_in, *refs):
@@ -154,14 +154,14 @@
     loss_ref, out_refs, sums, scratch = refs[0], refs[1:5], refs[5], refs[6:]
     loss_ref[...] = loss_in[...]
     sums[...] = sums_in[...]
-    users_kernel(work, groups, x_refs, w_in, w_out, unit_ref, sums, loss_ref, bias, scratch)
+    users_kernel(second_tile, work, groups, x_refs, w_in, w_out, unit_ref, sums, loss_ref, bias, scratch)
     mine = lax.axis_index("blk")
     for bits, ref in zip((0, 2, 1, 3), out_refs):
         ref[...] = sums[mine ^ bits].astype(ref.dtype)
 
 
 def users_step(
-    x_refs, spots, w_in, w_out, unit_ref, sums, loss_ref, bias,
+    tile, x_refs, spots, w_in, w_out, unit_ref, sums, loss_ref, bias,
     exp_ref, residual, events, starts_ref, key, value, packed_tgt, packed_loss,
 ):
     heads, length, _ = bias.shape
@@ -287,7 +287,7 @@
         loss_ref[pl.ds(spots[u], 1), :] = jnp.where(place < lens[u], loss, 0.0)
 
 
-def step_scratch(count, length, width, blocks, items):
+def step_scratch(tile, count, length, width, blocks, items):
     rows = -(-min(count, 8) * length // tile) * tile
     lines = -(-(rows // length + 2) // 8) * 8
     return [
@@ -319,7 +319,7 @@
             pltpu.VMEM(rel_bias.shape, jnp.float32),
             pltpu.SemaphoreType.DMA((3,)),
         ]
-        + step_scratch(len(work), length, width, blocks, items),
+        + step_scratch(first_tile, len(work), length, width, blocks, items),
         out_shape=[
             pltpu.VMEM((users, length), jnp.float32),
             pltpu.VMEM((blocks, items, width), jnp.float32),
@@ -342,7 +342,7 @@
         in_specs=[whole] * len(arrays),
         out_specs=[whole] * 5,
         scratch_shapes=[pltpu.VMEM(sums.shape, jnp.float32)]
-        + step_scratch(len(work), length, width, blocks, items),
+        + step_scratch(second_tile, len(work), length, width, blocks, items),
         out_shape=[pltpu.VMEM(loss.shape, jnp.float32)]
         + [pltpu.VMEM((items, width), jnp.float32)] * 2
         + [pltpu.VMEM((items, width), jnp.bfloat16)] * 2,

time: 50.7 us -> 50.3 us (level)
  the two profiles are of different devices: /device:TPU:18 before, /device:TPU:30 now
where the time goes in v18:
time: 50.3 us; the launch traced here: 50 us
  waiting for transfers between devices  21.4 us (43%)
  starting transfers between devices  13 us (26%)
  Pallas kernels  12.7 us (25%)
  other arithmetic  1.5 us (3%)
  between operations  0.7 us (1%)
  local copies, waits for them, and re-layouts  0.61 us (1%)
    ppermute x7, waiting for transfers between devices, from_behind(): lax.ppermute(array, axis, [(i, (i + by) % devices) for i in range(devices)])  9.8 us
    ppermute x3, waiting for transfers between devices, swap(): return lax.ppermute(array, axis, [(i, i ^ bit) for i in range(devices)])  8.21 us
    ppermute x7, starting transfers between devices, from_behind(): lax.ppermute(array, axis, [(i, (i + by) % devices) for i in range(devices)])  7.95 us
    pallas_call x1, Pallas kernels, first_call(): pl.pallas_call(functools.partial(first_kernel, work, groups), in_specs=[f...  6.58 us
    all_to_all x1, starting transfers between devices, shards(): lax.all_to_all(units, 'blk', split_axis=0, concat_axis=0, tiled=True)  4 us
    pallas_call x1, Pallas kernels, second_call(): pl.pallas_call(functools.partial(second_kernel, work, groups), in_specs=[...  3.51 us
    all_to_all x1, waiting for transfers between devices, shards(): lax.all_to_all(units, 'blk', split_axis=0, concat_axis=0, tiled=True)  3.44 us
    pallas_call x1, Pallas kernels, pack(): pl.pallas_call(functools.partial(pack_kernel, work, groups), in_specs=[hb...  2.61 us
  transfers between devices with their start and end apart: 11, of which 6 were waited for; matrix products, arithmetic and copies ran while one was open for 2% of the time, Pallas kernels for 13%

profile of v18, /device:TPU:30, one launch (start us, length us, event | category | flops | bytes accessed | tf_op | source)
XLA Modules:
  0.0 50.0 jit_solution(11854270029888636688)
XLA Ops:
  0.6 2.6 %pack.1 = (bf16[520,128]{1,0:T(8,128)(2,1)S(1)}, bf16[520,128]{1,0:T(8,128)(2,1)S(1)}, bf16[520,128]{1,0:T(8,128)(2,1)S(1)}, bf16[520,128]{1,0:T(8,128)(2,1)S(1)...) custom-call(s32[8]{0:T(128)} %list_any.1, ...), custom_call_target="tpu_custom_call" | custom-call | tf_op jit(solution)/shard_map/pack/pallas_call | solution.py:98
  3.2 4.0 %all-to-all-start = ((bf16[4,256,512]{2,1,0:T(8,128)(2,1)}), bf16[4,256,512]{2,1,0:T(8,128)(2,1)S(1)}, u32[]{:S(2)}, u32[]{:S(2)}) async-start(bf16[4,256,512]{2,1,0:T(8,128)(2,1)} %get-tuple-element.19), calls=%async_computation | async-start | bytes 2097152 | tf_op jit(solution)/shard_map/all_to_all | solution.py:370
  7.2 0.0 collective-permute-start
  7.3 2.0 %collective-permute-start.1 = (bf16[520,128]{1,0:T(8,128)(2,1)S(1)}, bf16[520,128]{1,0:T(8,128)(2,1)S(1)}, u32[]{:S(2)}, u32[]{:S(2)}) collective-permute-start(bf16[520,128]{1,0:T(8,128)(2,1)S(1)} %get-tuple-element.22), channel_id=1, source_target_pairs={{0,28},{4,0},{8,4},{12,8},{16,12},{20,16},{24,20},{28,24},{1,29},{... | collective-permute-start | bytes 399368 | tf_op jit(solution)/shard_map/ppermute | solution.py:25
  9.3 0.2 collective-permute-start.2
  9.5 1.7 %collective-permute-start.3 = (bf16[520,128]{1,0:T(8,128)(2,1)S(1)}, bf16[520,128]{1,0:T(8,128)(2,1)S(1)}, u32[]{:S(2)}, u32[]{:S(2)}) collective-permute-start(bf16[520,128]{1,0:T(8,128)(2,1)S(1)} %get-tuple-element.27), channel_id=1, source_target_pairs={{0,16},{4,20},{8,24},{12,28},{16,0},{20,4},{24,8},{28,12},{1,17},{... | collective-permute-start | bytes 399368 | tf_op jit(solution)/shard_map/ppermute | solution.py:25
  11.2 3.7 %collective-permute-start.4 = (bf16[520,128]{1,0:T(8,128)(2,1)S(1)}, bf16[520,128]{1,0:T(8,128)(2,1)S(1)}, u32[]{:S(2)}, u32[]{:S(2)}) collective-permute-start(bf16[520,128]{1,0:T(8,128)(2,1)S(1)} %get-tuple-element.28), channel_id=1, source_target_pairs={{0,12},{4,16},{8,20},{12,24},{16,28},{20,0},{24,4},{28,8},{1,13},{... | collective-permute-start | bytes 399368 | tf_op jit(solution)/shard_map/ppermute | solution.py:25
  14.9 0.0 collective-permute-done.refs_1_
  14.9 0.1 collective-permute-start.5
  15.0 1.4 %collective-permute-done.1.refs_2_ = bf16[520,128]{1,0:T(8,128)(2,1)S(1)} collective-permute-done((bf16[520,128]{1,0:T(8,128)(2,1)S(1)}, bf16[520,128]{1,0:T(8,128)(2,1)S(1)}, u32[]{:S(2)}, u32[]{:S(2)}) %collective-permute-start.1) | collective-permute-done | bytes 133152 | tf_op jit(solution)/shard_map/ppermute | solution.py:25
  16.4 0.2 collective-permute-start.6
  16.6 0.0 collective-permute-done.2.refs_3_
  16.6 3.4 %all-to-all-done.unit_ref = bf16[4,256,512]{2,1,0:T(8,128)(2,1)S(1)} async-done(((bf16[4,256,512]{2,1,0:T(8,128)(2,1)}), bf16[4,256,512]{2,1,0:T(8,128)(2,1)S(1)}, u32[]{:S(2)}, u32[]{:S(2)}) %all-to-all-start) | async-done | bytes 1048608 | tf_op jit(solution)/shard_map/all_to_all | solution.py:370
  20.0 0.0 copy-start
  20.1 0.0 copy-start.1
  20.1 6.6 %first_users.1 = (f32[8,128]{1,0:T(8,128)S(1)}, f32[4,256,512]{2,1,0:T(8,128)S(1)}, f32[4,128,256]{2,1,0:T(8,128)S(1)}) custom-call(bf16[512,2048]{1,0:T(8,128)(2,1)} %w_in.1, bf16[512,512]{1,0:T(8,128)(2,1)} %w_out.1, f32[4,128]{1,0:T(4,128)} %rel_any.1, bf16[4,256,512]{2,1,0:T(8,128)(2,1)S(1)} %all-to-all-done.unit_ref, ...), custom_call_target="tpu_custom_call" | custom-call | tf_op jit(solution)/shard_map/first_users/pallas_call | solution.py:312
  26.6 4.0 %collective-permute-done.3.refs_0_ = bf16[520,128]{1,0:T(8,128)(2,1)S(1)} collective-permute-done((bf16[520,128]{1,0:T(8,128)(2,1)S(1)}, bf16[520,128]{1,0:T(8,128)(2,1)S(1)}, u32[]{:S(2)}, u32[]{:S(2)}) %collective-permute-start.3) | collective-permute-done | bytes 133152 | tf_op jit(solution)/shard_map/ppermute | solution.py:25
  30.6 0.0 collective-permute-done.4.refs_1_
  30.6 4.4 %collective-permute-done.5.refs_2_ = bf16[520,128]{1,0:T(8,128)(2,1)S(1)} collective-permute-done((bf16[520,128]{1,0:T(8,128)(2,1)S(1)}, bf16[520,128]{1,0:T(8,128)(2,1)S(1)}, u32[]{:S(2)}, u32[]{:S(2)}) %collective-permute-start.5) | collective-permute-done | bytes 133152 | tf_op jit(solution)/shard_map/ppermute | solution.py:25
  35.0 0.0 collective-permute-done.6.refs_3_
  35.0 0.0 copy-done
  35.0 0.0 copy-done.1
  35.0 0.0 copy-start.2
  35.1 3.5 %second_users.1 = (f32[8,128]{1,0:T(8,128)S(1)}, f32[256,512]{1,0:T(8,128)S(1)}, f32[256,512]{1,0:T(8,128)S(1)}, bf16[256,512]{1,0:T(8,128)(2,1)S(1)}, bf16[256,512]{1,0:T(8,128)(2,1)S(1)}) custom-call(bf16[512,2048]{1,0:T(8,128)(2,1)S(1)} %copy-done, bf16[512,512]{1,0:T(8,128)(2,1)S(1)} %copy-done.1, f32[4,128,256]{2,1,0:T(8,128)S(1)} %get-tuple-element.24.bias, ...), custom_call_target="tpu_custom_call" | custom-call | tf_op jit(solution)/shard_map/second_users/pallas_call | solution.py:340
  38.6 0.1 collective-permute-start.8
  38.7 0.5 collective-permute-start.7
  39.2 1.0 %collective-permute-done.8 = bf16[256,512]{1,0:T(8,128)(2,1)S(1)} collective-permute-done((bf16[256,512]{1,0:T(8,128)(2,1)S(1)}, bf16[256,512]{1,0:T(8,128)(2,1)S(1)}, u32[]{:S(2)}, u32[]{:S(2)}) %collective-permute-start.8) | collective-permute-done | bytes 262176 | tf_op jit(solution)/shard_map/ppermute | solution.py:20
  40.2 0.1 add_convert_fusion
  40.3 0.5 collective-permute-start.9
  40.8 0.0 copy-done.2
  40.8 0.1 fusion
  40.9 0.6 %copy.10 = f32[8,128]{1,0:T(8,128)} copy(f32[8,128]{1,0:T(8,128)S(1)} %get-tuple-element.36) | data formatting | bytes 8192
  41.5 0.0 collective-permute-done.7
  41.5 7.2 %collective-permute-done.9 = bf16[256,512]{1,0:T(8,128)(2,1)S(1)} collective-permute-done((bf16[256,512]{1,0:T(8,128)(2,1)S(1)}, bf16[256,512]{1,0:T(8,128)(2,1)S(1)}, u32[]{:S(2)}, u32[]{:S(2)}) %collective-permute-start.9) | collective-permute-done | bytes 262176 | tf_op jit(solution)/shard_map/ppermute | solution.py:20
  48.7 0.3 multiply_reduce_fusion
  48.9 1.0 %subtract_divide_fusion = f32[256,512]{1,0:T(8,128)} fusion(bf16[256,512]{1,0:T(8,128)(2,1)S(1)} %copy-done.2, f32[256]{0:T(256)S(1)} %multiply_reduce_fusion, f32[256]{0:T(256)S(1)} %add_sqrt_fusion, bf16[256,512]{1,0:T(8,128)(2,1)S(1)} %collective-permute-done.9, f32[256,512]{1,0:T(8,128)S(1)} %get-tuple-element.32, ...), kind=kLoop, calls=%fused_computation.3 | loop fusion | flops 1310720 | bytes 1837056 | tf_op jit(solution)/shard_map/div | solution.py:385
  (1 shorter events, 0.0 us)
Async XLA Ops:
  3.2 16.8 %all-to-all-start = ((bf16[4,256,512]{2,1,0:T(8,128)(2,1)}), bf16[4,256,512]{2,1,0:T(8,128)(2,1)S(1)}, u32[]{:S(2)}, u32[]{:S(2)}) async-start(bf16[4,256,512]{2,1,0:T(8,128)(2,1)} %get-tuple-element.19), calls=%async_computation | async-start | bytes 2097152 | tf_op jit(solution)/shard_map/all_to_all | solution.py:370
  7.2 7.7 %collective-permute-start = (bf16[520,128]{1,0:T(8,128)(2,1)S(1)}, bf16[520,128]{1,0:T(8,128)(2,1)S(1)}, u32[]{:S(2)}, u32[]{:S(2)}) collective-permute-start(bf16[520,128]{1,0:T(8,128)(2,1)S(1)} %get-tuple-element.21), channel_id=1, source_target_pairs={{0,4},{4,8},{8,12},{12,16},{16,20},{20,24},{24,28},{28,0},{1,5},{5... | collective-permute-start | bytes 399368 | tf_op jit(solution)/shard_map/ppermute | solution.py:25
  7.3 9.1 %collective-permute-start.1 = (bf16[520,128]{1,0:T(8,128)(2,1)S(1)}, bf16[520,128]{1,0:T(8,128)(2,1)S(1)}, u32[]{:S(2)}, u32[]{:S(2)}) collective-permute-start(bf16[520,128]{1,0:T(8,128)(2,1)S(1)} %get-tuple-element.22), channel_id=1, source_target_pairs={{0,28},{4,0},{8,4},{12,8},{16,12},{20,16},{24,20},{28,24},{1,29},{... | collective-permute-start | bytes 399368 | tf_op jit(solution)/shard_map/ppermute | solution.py:25
  9.3 7.3 %collective-permute-start.2 = (bf16[520,128]{1,0:T(8,128)(2,1)S(1)}, bf16[520,128]{1,0:T(8,128)(2,1)S(1)}, u32[]{:S(2)}, u32[]{:S(2)}) collective-permute-start(bf16[520,128]{1,0:T(8,128)(2,1)S(1)} %get-tuple-element.23), channel_id=1, source_target_pairs={{0,8},{4,12},{8,16},{12,20},{16,24},{20,28},{24,0},{28,4},{1,9},{5... | collective-permute-start | bytes 399368 | tf_op jit(solution)/shard_map/ppermute | solution.py:25
  9.5 21.1 %collective-permute-start.3 = (bf16[520,128]{1,0:T(8,128)(2,1)S(1)}, bf16[520,128]{1,0:T(8,128)(2,1)S(1)}, u32[]{:S(2)}, u32[]{:S(2)}) collective-permute-start(bf16[520,128]{1,0:T(8,128)(2,1)S(1)} %get-tuple-element.27), channel_id=1, source_target_pairs={{0,16},{4,20},{8,24},{12,28},{16,0},{20,4},{24,8},{28,12},{1,17},{... | collective-permute-start | bytes 399368 | tf_op jit(solution)/shard_map/ppermute | solution.py:25
  11.2 19.4 %collective-permute-start.4 = (bf16[520,128]{1,0:T(8,128)(2,1)S(1)}, bf16[520,128]{1,0:T(8,128)(2,1)S(1)}, u32[]{:S(2)}, u32[]{:S(2)}) collective-permute-start(bf16[520,128]{1,0:T(8,128)(2,1)S(1)} %get-tuple-element.28), channel_id=1, source_target_pairs={{0,12},{4,16},{8,20},{12,24},{16,28},{20,0},{24,4},{28,8},{1,13},{... | collective-permute-start | bytes 399368 | tf_op jit(solution)/shard_map/ppermute | solution.py:25
  14.9 20.1 %collective-permute-start.5 = (bf16[520,128]{1,0:T(8,128)(2,1)S(1)}, bf16[520,128]{1,0:T(8,128)(2,1)S(1)}, u32[]{:S(2)}, u32[]{:S(2)}) collective-permute-start(bf16[520,128]{1,0:T(8,128)(2,1)S(1)} %get-tuple-element.29), channel_id=1, source_target_pairs={{0,20},{4,24},{8,28},{12,0},{16,4},{20,8},{24,12},{28,16},{1,21},{... | collective-permute-start | bytes 399368 | tf_op jit(solution)/shard_map/ppermute | solution.py:25
  16.4 18.7 %collective-permute-start.6 = (bf16[520,128]{1,0:T(8,128)(2,1)S(1)}, bf16[520,128]{1,0:T(8,128)(2,1)S(1)}, u32[]{:S(2)}, u32[]{:S(2)}) collective-permute-start(bf16[520,128]{1,0:T(8,128)(2,1)S(1)} %get-tuple-element.30), channel_id=1, source_target_pairs={{0,24},{4,28},{8,0},{12,4},{16,8},{20,12},{24,16},{28,20},{1,25},{... | collective-permute-start | bytes 399368 | tf_op jit(solution)/shard_map/ppermute | solution.py:25
  20.0 15.0 %copy-start = (bf16[512,2048]{1,0:T(8,128)(2,1)S(1)}, bf16[512,2048]{1,0:T(8,128)(2,1)}, u32[]{:S(2)}) copy-start(bf16[512,2048]{1,0:T(8,128)(2,1)} %w_in.1) | copy-start | bytes 6291460
  20.1 15.0 %copy-start.1 = (bf16[512,512]{1,0:T(8,128)(2,1)S(1)}, bf16[512,512]{1,0:T(8,128)(2,1)}, u32[]{:S(2)}) copy-start(bf16[512,512]{1,0:T(8,128)(2,1)} %w_out.1) | copy-start | bytes 1572868
  35.0 5.7 %copy-start.2 = (bf16[256,512]{1,0:T(8,128)(2,1)S(1)}, bf16[256,512]{1,0:T(8,128)(2,1)}, u32[]{:S(2)}) copy-start(bf16[256,512]{1,0:T(8,128)(2,1)} %pool_any.1) | copy-start | bytes 786436
  38.6 1.6 %collective-permute-start.8 = (bf16[256,512]{1,0:T(8,128)(2,1)S(1)}, bf16[256,512]{1,0:T(8,128)(2,1)S(1)}, u32[]{:S(2)}, u32[]{:S(2)}) collective-permute-start(bf16[256,512]{1,0:T(8,128)(2,1)S(1)} %get-tuple-element.35), channel_id=1, source_target_pairs={{0,1},{1,0},{2,3},{3,2},{4,5},{5,4},{6,7},{7,6},{8,9},{9,8},{10,11... | collective-permute-start | bytes 786440 | tf_op jit(solution)/shard_map/ppermute | solution.py:20
  38.7 2.8 %collective-permute-start.7 = (bf16[256,512]{1,0:T(8,128)(2,1)S(1)}, bf16[256,512]{1,0:T(8,128)(2,1)S(1)}, u32[]{:S(2)}, u32[]{:S(2)}) collective-permute-start(bf16[256,512]{1,0:T(8,128)(2,1)S(1)} %get-tuple-element.33), channel_id=1, source_target_pairs={{0,1},{1,0},{2,3},{3,2},{4,5},{5,4},{6,7},{7,6},{8,9},{9,8},{10,11... | collective-permute-start | bytes 786440 | tf_op jit(solution)/shard_map/ppermute | solution.py:20
  40.3 8.4 %collective-permute-start.9 = (bf16[256,512]{1,0:T(8,128)(2,1)S(1)}, bf16[256,512]{1,0:T(8,128)(2,1)S(1)}, u32[]{:S(2)}, u32[]{:S(2)}) collective-permute-start(bf16[256,512]{1,0:T(8,128)(2,1)S(1)} %add_convert_fusion), channel_id=1, source_target_pairs={{0,2},{1,3},{2,0},{3,1},{4,6},{5,7},{6,4},{7,5},{8,10},{9,11},{10,... | collective-permute-start | bytes 786440 | tf_op jit(solution)/shard_map/ppermute | solution.py:20

commit v19 on v18

--- a/solution.py
+++ b/solution.py
@@ -55,7 +55,7 @@
             ((list_any, entries), (len_any, lens), (tgt_any, targets), (pool_any, pool))
         )
     ]
-    for copy in reversed(small):
+    for copy in small:
         copy.start()
     small[0].wait()
     slots = users // groups
@@ -370,8 +370,8 @@
     units = lax.all_to_all(units, "blk", split_axis=0, concat_axis=0, tiled=True)
 
     pool_float = item_pool.astype(jnp.float32)
-    item_norm = jnp.sqrt(jnp.sum(pool_float * pool_float, axis=-1, keepdims=True) + 1e-06)
-    unit_rows = pool_float / item_norm
+    inverse_norm = lax.rsqrt(jnp.sum(pool_float * pool_float, axis=-1, keepdims=True) + 1e-06)
+    unit_rows = pool_float * inverse_norm
 
     loss, sums, bias = first_call(
         work[:half], groups, user_count, packed[:half], units, w_in, w_out, rel_bias
@@ -384,7 +384,7 @@
     item_sum = logit_scale * (own + swap(over.astype(jnp.bfloat16), "blk", 2).astype(jnp.float32))
     pool_grad = (
         item_sum - unit_rows * jnp.sum(unit_rows * item_sum, axis=-1, keepdims=True)
-    ) / item_norm
+    ) * inverse_norm
     return (row_loss, pool_grad)
 
 

time: 50.3 us -> 50.1 us (level)
    div x1 -> x0, other arithmetic: 1.02 us -> none  [shards(): (item_sum - unit_rows * jnp.sum(unit_rows * item_sum, axis=-1, keepdims=T...]
    mul x0 -> x1, other arithmetic: none -> 1 us  [shards(): (item_sum - unit_rows * jnp.sum(unit_rows * item_sum, axis=-1, keepdims=T...]
where the time goes in v19:
time: 50.1 us; the launch traced here: 49.8 us
  waiting for transfers between devices  21.4 us (43%)
  starting transfers between devices  13 us (26%)
  Pallas kernels  12.5 us (25%)
  other arithmetic  1.48 us (3%)
  between operations  0.7 us (1%)
  local copies, waits for them, and re-layouts  0.61 us (1%)
    ppermute x7, waiting for transfers between devices, from_behind(): lax.ppermute(array, axis, [(i, (i + by) % devices) for i in range(devices)])  9.79 us
    ppermute x3, waiting for transfers between devices, swap(): return lax.ppermute(array, axis, [(i, i ^ bit) for i in range(devices)])  8.21 us
    ppermute x7, starting transfers between devices, from_behind(): lax.ppermute(array, axis, [(i, (i + by) % devices) for i in range(devices)])  7.95 us
    pallas_call x1, Pallas kernels, first_call(): pl.pallas_call(functools.partial(first_kernel, work, groups), in_specs=[f...  6.59 us
    all_to_all x1, starting transfers between devices, shards(): lax.all_to_all(units, 'blk', split_axis=0, concat_axis=0, tiled=True)  4 us
    pallas_call x1, Pallas kernels, second_call(): pl.pallas_call(functools.partial(second_kernel, work, groups), in_specs=[...  3.51 us
    all_to_all x1, waiting for transfers between devices, shards(): lax.all_to_all(units, 'blk', split_axis=0, concat_axis=0, tiled=True)  3.44 us
    pallas_call x1, Pallas kernels, pack(): pl.pallas_call(functools.partial(pack_kernel, work, groups), in_specs=[hb...  2.44 us
  transfers between devices with their start and end apart: 11, of which 6 were waited for; matrix products, arithmetic and copies ran while one was open for 2% of the time, Pallas kernels for 13%

profile of v19, /device:TPU:30, one launch (start us, length us, event | category | flops | bytes accessed | tf_op | source)
XLA Modules:
  0.0 49.8 jit_solution(15542415831893151235)
XLA Ops:
  0.6 2.4 %pack.1 = (bf16[520,128]{1,0:T(8,128)(2,1)S(1)}, bf16[520,128]{1,0:T(8,128)(2,1)S(1)}, bf16[520,128]{1,0:T(8,128)(2,1)S(1)}, bf16[520,128]{1,0:T(8,128)(2,1)S(1)...) custom-call(s32[8]{0:T(128)} %list_any.1, ...), custom_call_target="tpu_custom_call" | custom-call | tf_op jit(solution)/shard_map/pack/pallas_call | solution.py:98
  3.1 4.0 %all-to-all-start = ((bf16[4,256,512]{2,1,0:T(8,128)(2,1)}), bf16[4,256,512]{2,1,0:T(8,128)(2,1)S(1)}, u32[]{:S(2)}, u32[]{:S(2)}) async-start(bf16[4,256,512]{2,1,0:T(8,128)(2,1)} %get-tuple-element.19), calls=%async_computation | async-start | bytes 2097152 | tf_op jit(solution)/shard_map/all_to_all | solution.py:370
  7.1 0.0 collective-permute-start
  7.1 2.0 %collective-permute-start.1 = (bf16[520,128]{1,0:T(8,128)(2,1)S(1)}, bf16[520,128]{1,0:T(8,128)(2,1)S(1)}, u32[]{:S(2)}, u32[]{:S(2)}) collective-permute-start(bf16[520,128]{1,0:T(8,128)(2,1)S(1)} %get-tuple-element.22), channel_id=1, source_target_pairs={{0,28},{4,0},{8,4},{12,8},{16,12},{20,16},{24,20},{28,24},{1,29},{... | collective-permute-start | bytes 399368 | tf_op jit(solution)/shard_map/ppermute | solution.py:25
  9.1 0.2 collective-permute-start.2
  9.3 1.7 %collective-permute-start.3 = (bf16[520,128]{1,0:T(8,128)(2,1)S(1)}, bf16[520,128]{1,0:T(8,128)(2,1)S(1)}, u32[]{:S(2)}, u32[]{:S(2)}) collective-permute-start(bf16[520,128]{1,0:T(8,128)(2,1)S(1)} %get-tuple-element.27), channel_id=1, source_target_pairs={{0,16},{4,20},{8,24},{12,28},{16,0},{20,4},{24,8},{28,12},{1,17},{... | collective-permute-start | bytes 399368 | tf_op jit(solution)/shard_map/ppermute | solution.py:25
  11.0 3.7 %collective-permute-start.4 = (bf16[520,128]{1,0:T(8,128)(2,1)S(1)}, bf16[520,128]{1,0:T(8,128)(2,1)S(1)}, u32[]{:S(2)}, u32[]{:S(2)}) collective-permute-start(bf16[520,128]{1,0:T(8,128)(2,1)S(1)} %get-tuple-element.28), channel_id=1, source_target_pairs={{0,12},{4,16},{8,20},{12,24},{16,28},{20,0},{24,4},{28,8},{1,13},{... | collective-permute-start | bytes 399368 | tf_op jit(solution)/shard_map/ppermute | solution.py:25
  14.7 0.0 collective-permute-done.refs_1_
  14.7 0.1 collective-permute-start.5
  14.8 1.4 %collective-permute-done.1.refs_2_ = bf16[520,128]{1,0:T(8,128)(2,1)S(1)} collective-permute-done((bf16[520,128]{1,0:T(8,128)(2,1)S(1)}, bf16[520,128]{1,0:T(8,128)(2,1)S(1)}, u32[]{:S(2)}, u32[]{:S(2)}) %collective-permute-start.1) | collective-permute-done | bytes 133152 | tf_op jit(solution)/shard_map/ppermute | solution.py:25
  16.2 0.2 collective-permute-start.6
  16.4 0.0 collective-permute-done.2.refs_3_
  16.4 3.4 %all-to-all-done.unit_ref = bf16[4,256,512]{2,1,0:T(8,128)(2,1)S(1)} async-done(((bf16[4,256,512]{2,1,0:T(8,128)(2,1)}), bf16[4,256,512]{2,1,0:T(8,128)(2,1)S(1)}, u32[]{:S(2)}, u32[]{:S(2)}) %all-to-all-start) | async-done | bytes 1048608 | tf_op jit(solution)/shard_map/all_to_all | solution.py:370
  19.9 0.0 copy-start
  19.9 0.0 copy-start.1
  19.9 6.6 %first_users.1 = (f32[8,128]{1,0:T(8,128)S(1)}, f32[4,256,512]{2,1,0:T(8,128)S(1)}, f32[4,128,256]{2,1,0:T(8,128)S(1)}) custom-call(bf16[512,2048]{1,0:T(8,128)(2,1)} %w_in.1, bf16[512,512]{1,0:T(8,128)(2,1)} %w_out.1, f32[4,128]{1,0:T(4,128)} %rel_any.1, bf16[4,256,512]{2,1,0:T(8,128)(2,1)S(1)} %all-to-all-done.unit_ref, ...), custom_call_target="tpu_custom_call" | custom-call | tf_op jit(solution)/shard_map/first_users/pallas_call | solution.py:312
  26.5 4.0 %collective-permute-done.3.refs_0_ = bf16[520,128]{1,0:T(8,128)(2,1)S(1)} collective-permute-done((bf16[520,128]{1,0:T(8,128)(2,1)S(1)}, bf16[520,128]{1,0:T(8,128)(2,1)S(1)}, u32[]{:S(2)}, u32[]{:S(2)}) %collective-permute-start.3) | collective-permute-done | bytes 133152 | tf_op jit(solution)/shard_map/ppermute | solution.py:25
  30.5 0.0 collective-permute-done.4.refs_1_
  30.5 4.4 %collective-permute-done.5.refs_2_ = bf16[520,128]{1,0:T(8,128)(2,1)S(1)} collective-permute-done((bf16[520,128]{1,0:T(8,128)(2,1)S(1)}, bf16[520,128]{1,0:T(8,128)(2,1)S(1)}, u32[]{:S(2)}, u32[]{:S(2)}) %collective-permute-start.5) | collective-permute-done | bytes 133152 | tf_op jit(solution)/shard_map/ppermute | solution.py:25
  34.9 0.0 collective-permute-done.6.refs_3_
  34.9 0.0 copy-done
  34.9 0.0 copy-done.1
  34.9 0.0 copy-start.2
  34.9 3.5 %second_users.1 = (f32[8,128]{1,0:T(8,128)S(1)}, f32[256,512]{1,0:T(8,128)S(1)}, f32[256,512]{1,0:T(8,128)S(1)}, bf16[256,512]{1,0:T(8,128)(2,1)S(1)}, bf16[256,512]{1,0:T(8,128)(2,1)S(1)}) custom-call(bf16[512,2048]{1,0:T(8,128)(2,1)S(1)} %copy-done, bf16[512,512]{1,0:T(8,128)(2,1)S(1)} %copy-done.1, f32[4,128,256]{2,1,0:T(8,128)S(1)} %get-tuple-element.24.bias, ...), custom_call_target="tpu_custom_call" | custom-call | tf_op jit(solution)/shard_map/second_users/pallas_call | solution.py:340
  38.4 0.1 collective-permute-start.8
  38.5 0.5 collective-permute-start.7
  39.0 1.0 %collective-permute-done.8 = bf16[256,512]{1,0:T(8,128)(2,1)S(1)} collective-permute-done((bf16[256,512]{1,0:T(8,128)(2,1)S(1)}, bf16[256,512]{1,0:T(8,128)(2,1)S(1)}, u32[]{:S(2)}, u32[]{:S(2)}) %collective-permute-start.8) | collective-permute-done | bytes 262176 | tf_op jit(solution)/shard_map/ppermute | solution.py:20
  40.0 0.1 add_convert_fusion
  40.1 0.5 collective-permute-start.9
  40.6 0.0 copy-done.2
  40.6 0.1 fusion.5
  40.7 0.6 %copy.10 = f32[8,128]{1,0:T(8,128)} copy(f32[8,128]{1,0:T(8,128)S(1)} %get-tuple-element.36) | data formatting | bytes 8192
  41.3 0.0 collective-permute-done.7
  41.3 7.2 %collective-permute-done.9 = bf16[256,512]{1,0:T(8,128)(2,1)S(1)} collective-permute-done((bf16[256,512]{1,0:T(8,128)(2,1)S(1)}, bf16[256,512]{1,0:T(8,128)(2,1)S(1)}, u32[]{:S(2)}, u32[]{:S(2)}) %collective-permute-start.9) | collective-permute-done | bytes 262176 | tf_op jit(solution)/shard_map/ppermute | solution.py:20
  48.5 0.3 fusion.2
  48.8 1.0 %fusion.4 = f32[256,512]{1,0:T(8,128)} fusion(bf16[256,512]{1,0:T(8,128)(2,1)S(1)} %copy-done.2, f32[256]{0:T(256)S(1)} %fusion.2, f32[256]{0:T(256)S(1)} %add_rsqrt_fusion, bf16[256,512]{1,0:T(8,128)(2,1)S(1)} %collective-permute-done.9, f32[256,512]{1,0:T(8,128)S(1)} %get-tuple-element.32, bf16[256,512]{1,0:T(8,128)(2,1)S(1)} %collective-permute-done.7), kind=kLoop, calls=%fused_computation.6 | loop fusion | flops 1310720 | bytes 1837056 | tf_op jit(solution)/shard_map/mul | solution.py:385
  (1 shorter events, 0.0 us)
Async XLA Ops:
  3.1 16.8 %all-to-all-start = ((bf16[4,256,512]{2,1,0:T(8,128)(2,1)}), bf16[4,256,512]{2,1,0:T(8,128)(2,1)S(1)}, u32[]{:S(2)}, u32[]{:S(2)}) async-start(bf16[4,256,512]{2,1,0:T(8,128)(2,1)} %get-tuple-element.19), calls=%async_computation | async-start | bytes 2097152 | tf_op jit(solution)/shard_map/all_to_all | solution.py:370
  7.1 7.7 %collective-permute-start = (bf16[520,128]{1,0:T(8,128)(2,1)S(1)}, bf16[520,128]{1,0:T(8,128)(2,1)S(1)}, u32[]{:S(2)}, u32[]{:S(2)}) collective-permute-start(bf16[520,128]{1,0:T(8,128)(2,1)S(1)} %get-tuple-element.21), channel_id=1, source_target_pairs={{0,4},{4,8},{8,12},{12,16},{16,20},{20,24},{24,28},{28,0},{1,5},{5... | collective-permute-start | bytes 399368 | tf_op jit(solution)/shard_map/ppermute | solution.py:25
  7.1 9.1 %collective-permute-start.1 = (bf16[520,128]{1,0:T(8,128)(2,1)S(1)}, bf16[520,128]{1,0:T(8,128)(2,1)S(1)}, u32[]{:S(2)}, u32[]{:S(2)}) collective-permute-start(bf16[520,128]{1,0:T(8,128)(2,1)S(1)} %get-tuple-element.22), channel_id=1, source_target_pairs={{0,28},{4,0},{8,4},{12,8},{16,12},{20,16},{24,20},{28,24},{1,29},{... | collective-permute-start | bytes 399368 | tf_op jit(solution)/shard_map/ppermute | solution.py:25
  9.1 7.3 %collective-permute-start.2 = (bf16[520,128]{1,0:T(8,128)(2,1)S(1)}, bf16[520,128]{1,0:T(8,128)(2,1)S(1)}, u32[]{:S(2)}, u32[]{:S(2)}) collective-permute-start(bf16[520,128]{1,0:T(8,128)(2,1)S(1)} %get-tuple-element.23), channel_id=1, source_target_pairs={{0,8},{4,12},{8,16},{12,20},{16,24},{20,28},{24,0},{28,4},{1,9},{5... | collective-permute-start | bytes 399368 | tf_op jit(solution)/shard_map/ppermute | solution.py:25
  9.3 21.1 %collective-permute-start.3 = (bf16[520,128]{1,0:T(8,128)(2,1)S(1)}, bf16[520,128]{1,0:T(8,128)(2,1)S(1)}, u32[]{:S(2)}, u32[]{:S(2)}) collective-permute-start(bf16[520,128]{1,0:T(8,128)(2,1)S(1)} %get-tuple-element.27), channel_id=1, source_target_pairs={{0,16},{4,20},{8,24},{12,28},{16,0},{20,4},{24,8},{28,12},{1,17},{... | collective-permute-start | bytes 399368 | tf_op jit(solution)/shard_map/ppermute | solution.py:25
  11.0 19.4 %collective-permute-start.4 = (bf16[520,128]{1,0:T(8,128)(2,1)S(1)}, bf16[520,128]{1,0:T(8,128)(2,1)S(1)}, u32[]{:S(2)}, u32[]{:S(2)}) collective-permute-start(bf16[520,128]{1,0:T(8,128)(2,1)S(1)} %get-tuple-element.28), channel_id=1, source_target_pairs={{0,12},{4,16},{8,20},{12,24},{16,28},{20,0},{24,4},{28,8},{1,13},{... | collective-permute-start | bytes 399368 | tf_op jit(solution)/shard_map/ppermute | solution.py:25
  14.7 20.1 %collective-permute-start.5 = (bf16[520,128]{1,0:T(8,128)(2,1)S(1)}, bf16[520,128]{1,0:T(8,128)(2,1)S(1)}, u32[]{:S(2)}, u32[]{:S(2)}) collective-permute-start(bf16[520,128]{1,0:T(8,128)(2,1)S(1)} %get-tuple-element.29), channel_id=1, source_target_pairs={{0,20},{4,24},{8,28},{12,0},{16,4},{20,8},{24,12},{28,16},{1,21},{... | collective-permute-start | bytes 399368 | tf_op jit(solution)/shard_map/ppermute | solution.py:25
  16.2 18.7 %collective-permute-start.6 = (bf16[520,128]{1,0:T(8,128)(2,1)S(1)}, bf16[520,128]{1,0:T(8,128)(2,1)S(1)}, u32[]{:S(2)}, u32[]{:S(2)}) collective-permute-start(bf16[520,128]{1,0:T(8,128)(2,1)S(1)} %get-tuple-element.30), channel_id=1, source_target_pairs={{0,24},{4,28},{8,0},{12,4},{16,8},{20,12},{24,16},{28,20},{1,25},{... | collective-permute-start | bytes 399368 | tf_op jit(solution)/shard_map/ppermute | solution.py:25
  19.9 15.0 %copy-start = (bf16[512,2048]{1,0:T(8,128)(2,1)S(1)}, bf16[512,2048]{1,0:T(8,128)(2,1)}, u32[]{:S(2)}) copy-start(bf16[512,2048]{1,0:T(8,128)(2,1)} %w_in.1) | copy-start | bytes 6291460
  19.9 15.0 %copy-start.1 = (bf16[512,512]{1,0:T(8,128)(2,1)S(1)}, bf16[512,512]{1,0:T(8,128)(2,1)}, u32[]{:S(2)}) copy-start(bf16[512,512]{1,0:T(8,128)(2,1)} %w_out.1) | copy-start | bytes 1572868
  34.9 5.7 %copy-start.2 = (bf16[256,512]{1,0:T(8,128)(2,1)S(1)}, bf16[256,512]{1,0:T(8,128)(2,1)}, u32[]{:S(2)}) copy-start(bf16[256,512]{1,0:T(8,128)(2,1)} %pool_any.1) | copy-start | bytes 786436
  38.4 1.6 %collective-permute-start.8 = (bf16[256,512]{1,0:T(8,128)(2,1)S(1)}, bf16[256,512]{1,0:T(8,128)(2,1)S(1)}, u32[]{:S(2)}, u32[]{:S(2)}) collective-permute-start(bf16[256,512]{1,0:T(8,128)(2,1)S(1)} %get-tuple-element.35), channel_id=1, source_target_pairs={{0,1},{1,0},{2,3},{3,2},{4,5},{5,4},{6,7},{7,6},{8,9},{9,8},{10,11... | collective-permute-start | bytes 786440 | tf_op jit(solution)/shard_map/ppermute | solution.py:20
  38.5 2.8 %collective-permute-start.7 = (bf16[256,512]{1,0:T(8,128)(2,1)S(1)}, bf16[256,512]{1,0:T(8,128)(2,1)S(1)}, u32[]{:S(2)}, u32[]{:S(2)}) collective-permute-start(bf16[256,512]{1,0:T(8,128)(2,1)S(1)} %get-tuple-element.33), channel_id=1, source_target_pairs={{0,1},{1,0},{2,3},{3,2},{4,5},{5,4},{6,7},{7,6},{8,9},{9,8},{10,11... | collective-permute-start | bytes 786440 | tf_op jit(solution)/shard_map/ppermute | solution.py:20
  40.1 8.4 %collective-permute-start.9 = (bf16[256,512]{1,0:T(8,128)(2,1)S(1)}, bf16[256,512]{1,0:T(8,128)(2,1)S(1)}, u32[]{:S(2)}, u32[]{:S(2)}) collective-permute-start(bf16[256,512]{1,0:T(8,128)(2,1)S(1)} %add_convert_fusion), channel_id=1, source_target_pairs={{0,2},{1,3},{2,0},{3,1},{4,6},{5,7},{6,4},{7,5},{8,10},{9,11},{10,... | collective-permute-start | bytes 786440 | tf_op jit(solution)/shard_map/ppermute | solution.py:20

commit v20 on v19

--- a/solution.py
+++ b/solution.py
@@ -351,6 +351,34 @@
     )(*[in_vmem(array) for array in arrays])
 
 
+def finish_kernel(own, side, over, pool, out_any, out, sems):
+    quarter = own.shape[0] // 4
+    copies = []
+    for k in range(4):
+        rows = slice(k * quarter, (k + 1) * quarter)
+        items = pool[rows].astype(jnp.float32)
+        inverse = lax.rsqrt(jnp.sum(items * items, axis=-1, keepdims=True) + 1e-06)
+        unit = items * inverse
+        total = logit_scale * (own[rows] + side[rows].astype(jnp.float32) + over[rows].astype(jnp.float32))
+        out[rows] = (total - unit * jnp.sum(unit * total, axis=-1, keepdims=True)) * inverse
+        part = pl.ds(k * quarter, quarter)
+        copies.append(pltpu.make_async_copy(out.at[part], out_any.at[part], sems.at[k]))
+        copies[k].start()
+    for copy in copies:
+        copy.wait()
+
+
+def finish(own, side, over, pool):
+    return pl.pallas_call(
+        finish_kernel,
+        in_specs=[whole] * 4,
+        out_specs=far_off,
+        scratch_shapes=[pltpu.VMEM(own.shape, jnp.float32), pltpu.SemaphoreType.DMA((4,))],
+        out_shape=jax.ShapeDtypeStruct(own.shape, jnp.float32),
+        name="finish",
+    )(*[in_vmem(array) for array in (own, side, over, pool)])
+
+
 def shards(histories, lengths, targets, send_list, w_in, w_out, rel_bias, item_pool):
     user_count = histories.shape[0]
     groups, blocks = lax.axis_size("dp"), lax.axis_size("blk")
@@ -369,10 +397,6 @@
     ]
     units = lax.all_to_all(units, "blk", split_axis=0, concat_axis=0, tiled=True)
 
-    pool_float = item_pool.astype(jnp.float32)
-    inverse_norm = lax.rsqrt(jnp.sum(pool_float * pool_float, axis=-1, keepdims=True) + 1e-06)
-    unit_rows = pool_float * inverse_norm
-
     loss, sums, bias = first_call(
         work[:half], groups, user_count, packed[:half], units, w_in, w_out, rel_bias
     )
@@ -380,11 +404,8 @@
         work[half:], groups, packed[half:], units, w_in, w_out, loss, sums, bias
     )
     over = over + swap(far, "blk", 1).astype(jnp.float32)
-    own = own + swap(side, "blk", 1).astype(jnp.float32)
-    item_sum = logit_scale * (own + swap(over.astype(jnp.bfloat16), "blk", 2).astype(jnp.float32))
-    pool_grad = (
-        item_sum - unit_rows * jnp.sum(unit_rows * item_sum, axis=-1, keepdims=True)
-    ) * inverse_norm
+    side = swap(side, "blk", 1)
+    pool_grad = finish(own, side, swap(over.astype(jnp.bfloat16), "blk", 2), item_pool)
     return (row_loss, pool_grad)
 
 

time: 50.1 us -> 49.8 us (level)
  the two profiles are of different devices: /device:TPU:30 before, /device:TPU:12 now
where the time goes in v20:
time: 49.8 us; the launch traced here: 49.6 us
  waiting for transfers between devices  17.6 us (35%)
  starting transfers between devices  17 us (34%)
  Pallas kernels  13.6 us (27%)
  between operations  0.69 us (1%)
  local copies, waits for them, and re-layouts  0.6 us (1%)
    ppermute x7, starting transfers between devices, from_behind(): lax.ppermute(array, axis, [(i, (i + by) % devices) for i in range(devices)])  11.9 us
    ppermute x7, waiting for transfers between devices, from_behind(): lax.ppermute(array, axis, [(i, (i + by) % devices) for i in range(devices)])  8.65 us
    ppermute x3, waiting for transfers between devices, swap(): return lax.ppermute(array, axis, [(i, i ^ bit) for i in range(devices)])  8.36 us
    pallas_call x1, Pallas kernels, first_call(): pl.pallas_call(functools.partial(first_kernel, work, groups), in_specs=[f...  6.63 us
    all_to_all x1, starting transfers between devices, shards(): lax.all_to_all(units, 'blk', split_axis=0, concat_axis=0, tiled=True)  4 us
    pallas_call x1, Pallas kernels, second_call(): pl.pallas_call(functools.partial(second_kernel, work, groups), in_specs=[...  3.51 us
    pallas_call x1, Pallas kernels, pack(): pl.pallas_call(functools.partial(pack_kernel, work, groups), in_specs=[hb...  2.45 us
    ppermute x3, starting transfers between devices, swap(): return lax.ppermute(array, axis, [(i, i ^ bit) for i in range(devices)])  1.05 us
  transfers between devices with their start and end apart: 11, of which 7 were waited for; matrix products, arithmetic and copies ran while one was open for 1% of the time, Pallas kernels for 13%

profile of v20, /device:TPU:12, one launch (start us, length us, event | category | flops | bytes accessed | tf_op | source)
XLA Modules:
  0.0 49.6 jit_solution(10183710834682598708)
XLA Ops:
  0.6 2.4 %pack.1 = (bf16[520,128]{1,0:T(8,128)(2,1)S(1)}, bf16[520,128]{1,0:T(8,128)(2,1)S(1)}, bf16[520,128]{1,0:T(8,128)(2,1)S(1)}, bf16[520,128]{1,0:T(8,128)(2,1)S(1)...) custom-call(s32[8]{0:T(128)} %list_any.1, ...), custom_call_target="tpu_custom_call" | custom-call | tf_op jit(solution)/shard_map/pack/pallas_call | solution.py:98
  3.1 4.0 %all-to-all-start = ((bf16[4,256,512]{2,1,0:T(8,128)(2,1)}), bf16[4,256,512]{2,1,0:T(8,128)(2,1)S(1)}, u32[]{:S(2)}, u32[]{:S(2)}) async-start(bf16[4,256,512]{2,1,0:T(8,128)(2,1)} %get-tuple-element.19), calls=%async_computation | async-start | bytes 2097152 | tf_op jit(solution)/shard_map/all_to_all | solution.py:398
  7.1 1.5 %collective-permute-start = (bf16[520,128]{1,0:T(8,128)(2,1)S(1)}, bf16[520,128]{1,0:T(8,128)(2,1)S(1)}, u32[]{:S(2)}, u32[]{:S(2)}) collective-permute-start(bf16[520,128]{1,0:T(8,128)(2,1)S(1)} %get-tuple-element.21), channel_id=1, source_target_pairs={{0,4},{4,8},{8,12},{12,16},{16,20},{20,24},{24,28},{28,0},{1,5},{5... | collective-permute-start | bytes 399368 | tf_op jit(solution)/shard_map/ppermute | solution.py:25
  8.6 1.4 %collective-permute-start.1 = (bf16[520,128]{1,0:T(8,128)(2,1)S(1)}, bf16[520,128]{1,0:T(8,128)(2,1)S(1)}, u32[]{:S(2)}, u32[]{:S(2)}) collective-permute-start(bf16[520,128]{1,0:T(8,128)(2,1)S(1)} %get-tuple-element.22), channel_id=1, source_target_pairs={{0,28},{4,0},{8,4},{12,8},{16,12},{20,16},{24,20},{28,24},{1,29},{... | collective-permute-start | bytes 399368 | tf_op jit(solution)/shard_map/ppermute | solution.py:25
  10.0 1.6 %collective-permute-start.2 = (bf16[520,128]{1,0:T(8,128)(2,1)S(1)}, bf16[520,128]{1,0:T(8,128)(2,1)S(1)}, u32[]{:S(2)}, u32[]{:S(2)}) collective-permute-start(bf16[520,128]{1,0:T(8,128)(2,1)S(1)} %get-tuple-element.23), channel_id=1, source_target_pairs={{0,8},{4,12},{8,16},{12,20},{16,24},{20,28},{24,0},{28,4},{1,9},{5... | collective-permute-start | bytes 399368 | tf_op jit(solution)/shard_map/ppermute | solution.py:25
  11.6 2.8 %collective-permute-start.3 = (bf16[520,128]{1,0:T(8,128)(2,1)S(1)}, bf16[520,128]{1,0:T(8,128)(2,1)S(1)}, u32[]{:S(2)}, u32[]{:S(2)}) collective-permute-start(bf16[520,128]{1,0:T(8,128)(2,1)S(1)} %get-tuple-element.27), channel_id=1, source_target_pairs={{0,16},{4,20},{8,24},{12,28},{16,0},{20,4},{24,8},{28,12},{1,17},{... | collective-permute-start | bytes 399368 | tf_op jit(solution)/shard_map/ppermute | solution.py:25
  14.4 0.0 collective-permute-start.4
  14.4 0.0 collective-permute-done.refs_1_
  14.4 3.8 %collective-permute-start.5 = (bf16[520,128]{1,0:T(8,128)(2,1)S(1)}, bf16[520,128]{1,0:T(8,128)(2,1)S(1)}, u32[]{:S(2)}, u32[]{:S(2)}) collective-permute-start(bf16[520,128]{1,0:T(8,128)(2,1)S(1)} %get-tuple-element.29), channel_id=1, source_target_pairs={{0,20},{4,24},{8,28},{12,0},{16,4},{20,8},{24,12},{28,16},{1,21},{... | collective-permute-start | bytes 399368 | tf_op jit(solution)/shard_map/ppermute | solution.py:25
  18.3 0.0 collective-permute-done.1.refs_2_
  18.3 0.8 %collective-permute-start.6 = (bf16[520,128]{1,0:T(8,128)(2,1)S(1)}, bf16[520,128]{1,0:T(8,128)(2,1)S(1)}, u32[]{:S(2)}, u32[]{:S(2)}) collective-permute-start(bf16[520,128]{1,0:T(8,128)(2,1)S(1)} %get-tuple-element.30), channel_id=1, source_target_pairs={{0,24},{4,28},{8,0},{12,4},{16,8},{20,12},{24,16},{28,20},{1,25},{... | collective-permute-start | bytes 399368 | tf_op jit(solution)/shard_map/ppermute | solution.py:25
  19.0 0.3 collective-permute-done.2.refs_3_
  19.3 0.6 %all-to-all-done.unit_ref = bf16[4,256,512]{2,1,0:T(8,128)(2,1)S(1)} async-done(((bf16[4,256,512]{2,1,0:T(8,128)(2,1)}), bf16[4,256,512]{2,1,0:T(8,128)(2,1)S(1)}, u32[]{:S(2)}, u32[]{:S(2)}) %all-to-all-start) | async-done | bytes 1048608 | tf_op jit(solution)/shard_map/all_to_all | solution.py:398
  19.9 0.0 copy-start
  19.9 0.0 copy-start.1
  19.9 6.6 %first_users.1 = (f32[8,128]{1,0:T(8,128)S(1)}, f32[4,256,512]{2,1,0:T(8,128)S(1)}, f32[4,128,256]{2,1,0:T(8,128)S(1)}) custom-call(bf16[512,2048]{1,0:T(8,128)(2,1)} %w_in.1, bf16[512,512]{1,0:T(8,128)(2,1)} %w_out.1, f32[4,128]{1,0:T(4,128)} %rel_any.1, bf16[4,256,512]{2,1,0:T(8,128)(2,1)S(1)} %all-to-all-done.unit_ref, ...), custom_call_target="tpu_custom_call" | custom-call | tf_op jit(solution)/shard_map/first_users/pallas_call | solution.py:312
  26.5 0.0 collective-permute-done.3.refs_0_
  26.5 5.3 %collective-permute-done.4.refs_1_ = bf16[520,128]{1,0:T(8,128)(2,1)S(1)} collective-permute-done((bf16[520,128]{1,0:T(8,128)(2,1)S(1)}, bf16[520,128]{1,0:T(8,128)(2,1)S(1)}, u32[]{:S(2)}, u32[]{:S(2)}) %collective-permute-start.4) | collective-permute-done | bytes 133152 | tf_op jit(solution)/shard_map/ppermute | solution.py:25
  31.9 2.2 %collective-permute-done.5.refs_2_ = bf16[520,128]{1,0:T(8,128)(2,1)S(1)} collective-permute-done((bf16[520,128]{1,0:T(8,128)(2,1)S(1)}, bf16[520,128]{1,0:T(8,128)(2,1)S(1)}, u32[]{:S(2)}, u32[]{:S(2)}) %collective-permute-start.5) | collective-permute-done | bytes 133152 | tf_op jit(solution)/shard_map/ppermute | solution.py:25
  34.1 0.8 %collective-permute-done.6.refs_3_ = bf16[520,128]{1,0:T(8,128)(2,1)S(1)} collective-permute-done((bf16[520,128]{1,0:T(8,128)(2,1)S(1)}, bf16[520,128]{1,0:T(8,128)(2,1)S(1)}, u32[]{:S(2)}, u32[]{:S(2)}) %collective-permute-start.6) | collective-permute-done | bytes 133152 | tf_op jit(solution)/shard_map/ppermute | solution.py:25
  34.9 0.0 copy-done
  34.9 0.0 copy-done.1
  34.9 0.0 copy-start.2
  34.9 3.5 %second_users.1 = (f32[8,128]{1,0:T(8,128)S(1)}, f32[256,512]{1,0:T(8,128)S(1)}, f32[256,512]{1,0:T(8,128)S(1)}, bf16[256,512]{1,0:T(8,128)(2,1)S(1)}, bf16[256,512]{1,0:T(8,128)(2,1)S(1)}) custom-call(bf16[512,2048]{1,0:T(8,128)(2,1)S(1)} %copy-done, bf16[512,512]{1,0:T(8,128)(2,1)S(1)} %copy-done.1, f32[4,128,256]{2,1,0:T(8,128)S(1)} %get-tuple-element.24.bias, ...), custom_call_target="tpu_custom_call" | custom-call | tf_op jit(solution)/shard_map/second_users/pallas_call | solution.py:340
  38.4 0.1 collective-permute-start.8
  38.5 0.5 %collective-permute-start.7 = (bf16[256,512]{1,0:T(8,128)(2,1)S(1)}, bf16[256,512]{1,0:T(8,128)(2,1)S(1)}, u32[]{:S(2)}, u32[]{:S(2)}) collective-permute-start(bf16[256,512]{1,0:T(8,128)(2,1)S(1)} %get-tuple-element.33), channel_id=1, source_target_pairs={{0,1},{1,0},{2,3},{3,2},{4,5},{5,4},{6,7},{7,6},{8,9},{9,8},{10,11... | collective-permute-start | bytes 786440 | tf_op jit(solution)/shard_map/ppermute | solution.py:20
  39.0 1.0 %collective-permute-done.8 = bf16[256,512]{1,0:T(8,128)(2,1)S(1)} collective-permute-done((bf16[256,512]{1,0:T(8,128)(2,1)S(1)}, bf16[256,512]{1,0:T(8,128)(2,1)S(1)}, u32[]{:S(2)}, u32[]{:S(2)}) %collective-permute-start.8) | collective-permute-done | bytes 262176 | tf_op jit(solution)/shard_map/ppermute | solution.py:20
  40.0 0.1 add_convert_fusion
  40.1 0.5 collective-permute-start.9
  40.6 0.6 %copy.10 = f32[8,128]{1,0:T(8,128)} copy(f32[8,128]{1,0:T(8,128)S(1)} %get-tuple-element.36) | data formatting | bytes 8192
  41.2 0.0 collective-permute-done.7.side
  41.2 7.3 %collective-permute-done.9.over = bf16[256,512]{1,0:T(8,128)(2,1)S(1)} collective-permute-done((bf16[256,512]{1,0:T(8,128)(2,1)S(1)}, bf16[256,512]{1,0:T(8,128)(2,1)S(1)}, u32[]{:S(2)}, u32[]{:S(2)}) %collective-permute-start.9) | collective-permute-done | bytes 262176 | tf_op jit(solution)/shard_map/ppermute | solution.py:20
  48.5 0.0 copy-done.2
  48.5 1.0 %finish.1 = f32[256,512]{1,0:T(8,128)} custom-call(f32[256,512]{1,0:T(8,128)S(1)} %get-tuple-element.32.own, bf16[256,512]{1,0:T(8,128)(2,1)S(1)} %collective-permute-done.7.side, bf16[256,512]{1,0:T(8,128)(2,1)S(1)} %collective-permute-done.9.over, bf16[256,512]{1,0:T(8,128)(2,1)S(1)} %copy-done.2), custom_call_target="tpu_custom_call" | custom-call | tf_op jit(solution)/shard_map/finish/pallas_call | solution.py:372
Async XLA Ops:
  3.1 16.8 %all-to-all-start = ((bf16[4,256,512]{2,1,0:T(8,128)(2,1)}), bf16[4,256,512]{2,1,0:T(8,128)(2,1)S(1)}, u32[]{:S(2)}, u32[]{:S(2)}) async-start(bf16[4,256,512]{2,1,0:T(8,128)(2,1)} %get-tuple-element.19), calls=%async_computation | async-start | bytes 2097152 | tf_op jit(solution)/shard_map/all_to_all | solution.py:398
  7.1 7.4 %collective-permute-start = (bf16[520,128]{1,0:T(8,128)(2,1)S(1)}, bf16[520,128]{1,0:T(8,128)(2,1)S(1)}, u32[]{:S(2)}, u32[]{:S(2)}) collective-permute-start(bf16[520,128]{1,0:T(8,128)(2,1)S(1)} %get-tuple-element.21), channel_id=1, source_target_pairs={{0,4},{4,8},{8,12},{12,16},{16,20},{20,24},{24,28},{28,0},{1,5},{5... | collective-permute-start | bytes 399368 | tf_op jit(solution)/shard_map/ppermute | solution.py:25
  8.6 9.7 %collective-permute-start.1 = (bf16[520,128]{1,0:T(8,128)(2,1)S(1)}, bf16[520,128]{1,0:T(8,128)(2,1)S(1)}, u32[]{:S(2)}, u32[]{:S(2)}) collective-permute-start(bf16[520,128]{1,0:T(8,128)(2,1)S(1)} %get-tuple-element.22), channel_id=1, source_target_pairs={{0,28},{4,0},{8,4},{12,8},{16,12},{20,16},{24,20},{28,24},{1,29},{... | collective-permute-start | bytes 399368 | tf_op jit(solution)/shard_map/ppermute | solution.py:25
  10.0 9.3 %collective-permute-start.2 = (bf16[520,128]{1,0:T(8,128)(2,1)S(1)}, bf16[520,128]{1,0:T(8,128)(2,1)S(1)}, u32[]{:S(2)}, u32[]{:S(2)}) collective-permute-start(bf16[520,128]{1,0:T(8,128)(2,1)S(1)} %get-tuple-element.23), channel_id=1, source_target_pairs={{0,8},{4,12},{8,16},{12,20},{16,24},{20,28},{24,0},{28,4},{1,9},{5... | collective-permute-start | bytes 399368 | tf_op jit(solution)/shard_map/ppermute | solution.py:25
  11.6 14.9 %collective-permute-start.3 = (bf16[520,128]{1,0:T(8,128)(2,1)S(1)}, bf16[520,128]{1,0:T(8,128)(2,1)S(1)}, u32[]{:S(2)}, u32[]{:S(2)}) collective-permute-start(bf16[520,128]{1,0:T(8,128)(2,1)S(1)} %get-tuple-element.27), channel_id=1, source_target_pairs={{0,16},{4,20},{8,24},{12,28},{16,0},{20,4},{24,8},{28,12},{1,17},{... | collective-permute-start | bytes 399368 | tf_op jit(solution)/shard_map/ppermute | solution.py:25
  14.4 17.4 %collective-permute-start.4 = (bf16[520,128]{1,0:T(8,128)(2,1)S(1)}, bf16[520,128]{1,0:T(8,128)(2,1)S(1)}, u32[]{:S(2)}, u32[]{:S(2)}) collective-permute-start(bf16[520,128]{1,0:T(8,128)(2,1)S(1)} %get-tuple-element.28), channel_id=1, source_target_pairs={{0,12},{4,16},{8,20},{12,24},{16,28},{20,0},{24,4},{28,8},{1,13},{... | collective-permute-start | bytes 399368 | tf_op jit(solution)/shard_map/ppermute | solution.py:25
  14.4 19.7 %collective-permute-start.5 = (bf16[520,128]{1,0:T(8,128)(2,1)S(1)}, bf16[520,128]{1,0:T(8,128)(2,1)S(1)}, u32[]{:S(2)}, u32[]{:S(2)}) collective-permute-start(bf16[520,128]{1,0:T(8,128)(2,1)S(1)} %get-tuple-element.29), channel_id=1, source_target_pairs={{0,20},{4,24},{8,28},{12,0},{16,4},{20,8},{24,12},{28,16},{1,21},{... | collective-permute-start | bytes 399368 | tf_op jit(solution)/shard_map/ppermute | solution.py:25
  18.3 16.6 %collective-permute-start.6 = (bf16[520,128]{1,0:T(8,128)(2,1)S(1)}, bf16[520,128]{1,0:T(8,128)(2,1)S(1)}, u32[]{:S(2)}, u32[]{:S(2)}) collective-permute-start(bf16[520,128]{1,0:T(8,128)(2,1)S(1)} %get-tuple-element.30), channel_id=1, source_target_pairs={{0,24},{4,28},{8,0},{12,4},{16,8},{20,12},{24,16},{28,20},{1,25},{... | collective-permute-start | bytes 399368 | tf_op jit(solution)/shard_map/ppermute | solution.py:25
  19.9 15.0 %copy-start = (bf16[512,2048]{1,0:T(8,128)(2,1)S(1)}, bf16[512,2048]{1,0:T(8,128)(2,1)}, u32[]{:S(2)}) copy-start(bf16[512,2048]{1,0:T(8,128)(2,1)} %w_in.1) | copy-start | bytes 6291460
  19.9 15.0 %copy-start.1 = (bf16[512,512]{1,0:T(8,128)(2,1)S(1)}, bf16[512,512]{1,0:T(8,128)(2,1)}, u32[]{:S(2)}) copy-start(bf16[512,512]{1,0:T(8,128)(2,1)} %w_out.1) | copy-start | bytes 1572868
  34.9 13.6 %copy-start.2 = (bf16[256,512]{1,0:T(8,128)(2,1)S(1)}, bf16[256,512]{1,0:T(8,128)(2,1)}, u32[]{:S(2)}) copy-start(bf16[256,512]{1,0:T(8,128)(2,1)} %pool.1) | copy-start | bytes 786436
  38.4 1.6 %collective-permute-start.8 = (bf16[256,512]{1,0:T(8,128)(2,1)S(1)}, bf16[256,512]{1,0:T(8,128)(2,1)S(1)}, u32[]{:S(2)}, u32[]{:S(2)}) collective-permute-start(bf16[256,512]{1,0:T(8,128)(2,1)S(1)} %get-tuple-element.35), channel_id=1, source_target_pairs={{0,1},{1,0},{2,3},{3,2},{4,5},{5,4},{6,7},{7,6},{8,9},{9,8},{10,11... | collective-permute-start | bytes 786440 | tf_op jit(solution)/shard_map/ppermute | solution.py:20
  38.5 2.7 %collective-permute-start.7 = (bf16[256,512]{1,0:T(8,128)(2,1)S(1)}, bf16[256,512]{1,0:T(8,128)(2,1)S(1)}, u32[]{:S(2)}, u32[]{:S(2)}) collective-permute-start(bf16[256,512]{1,0:T(8,128)(2,1)S(1)} %get-tuple-element.33), channel_id=1, source_target_pairs={{0,1},{1,0},{2,3},{3,2},{4,5},{5,4},{6,7},{7,6},{8,9},{9,8},{10,11... | collective-permute-start | bytes 786440 | tf_op jit(solution)/shard_map/ppermute | solution.py:20
  40.1 8.4 %collective-permute-start.9 = (bf16[256,512]{1,0:T(8,128)(2,1)S(1)}, bf16[256,512]{1,0:T(8,128)(2,1)S(1)}, u32[]{:S(2)}, u32[]{:S(2)}) collective-permute-start(bf16[256,512]{1,0:T(8,128)(2,1)S(1)} %add_convert_fusion), channel_id=1, source_target_pairs={{0,2},{1,3},{2,0},{3,1},{4,6},{5,7},{6,4},{7,5},{8,10},{9,11},{10,... | collective-permute-start | bytes 786440 | tf_op jit(solution)/shard_map/ppermute | solution.py:20
